TPU v7x, 32 devices: a whole 2x2x4 slice. The times are simulated.
32 devices in a mesh: parts: 2 (over x), store: 16 (over z, y, core).
Axes of the slice: x: 2, y: 2, z: 4, core: 2. Of those that a mesh axis runs over, the one named last changes fastest.
Arguments:
- tokens: bfloat16 [16384, 8192], P(('parts', 'store')), parts along dimension 0, may hold values from -6 to 6
- base_weight: bfloat16 [8192, 512], P('store'), may hold values from -0.0625 to 0.0625
- adapter_down: bfloat16 [128, 8192, 64], P(None, 'store'), may hold values from -0.0625 to 0.0625
- adapter_up: bfloat16 [128, 512, 64], P(None, 'store'), may hold values from -0.75 to 0.75
- request_lengths: int32 [32, 16], P(('parts', 'store')), parts along dimension 0, may hold values from 1 to 256, 512 in all within a row
- group_adapters: int32 [32, 2], P('parts'), parts along dimension 0, may hold values from 0 to 127, as said below
- request_slot: int32 [32, 16], P('parts'), parts along dimension 0, may hold values from 0 to 1
Outputs:
- values: bfloat16 [16384, 512], P(('parts', 'store')), parts along dimension 0
There are 2 independent parts, one for each index of `parts`. A program takes and returns all parts, laid end to end along the dimension named above; an argument that names none is the same for every part. Nothing has to cross between parts.
Inputs may be any that keep to these rules, and one draw needn't show every extreme that they name: `group_adapters`: each row names 2 different adapters.
All inputs are finite; a program needn't handle non-finite values.
Results may differ from a plain program's by a relative error of at most 0.0065.
Values may be sent and summed in bfloat16 or wider, within the bound.
No kernel may reach another device: no remote copies, remote signals or barrier semaphores. Data moves between devices by JAX's collectives and lax.ppermute only.
A program may use at most 128 MiB of HBM per device.

v0:
```python
import jax
import jax.numpy as jnp
from jax import lax
from jax.sharding import PartitionSpec as P


def body(
    tokens, base_weight, adapter_down, adapter_up, request_lengths, group_adapters, request_slot
):
    rows = tokens.shape[0]
    width = base_weight.shape[1]
    rank = adapter_down.shape[2]
    model_width = tokens.shape[1]
    group = lax.axis_index("store")
    lengths = request_lengths[0]
    ends = jnp.cumsum(lengths)
    starts = ends - lengths
    position = jnp.arange(rows, dtype=jnp.int32)[:, None]
    member = ((position >= starts[None, :]) & (position < ends[None, :])).astype(jnp.float32)
    wanted = jnp.transpose(group_adapters)
    own_slots = lax.dynamic_index_in_dim(request_slot, group, 0, keepdims=False)
    owned = (
        own_slots[:, None] == jnp.arange(group_adapters.shape[1], dtype=jnp.int32)[None, :]
    ).astype(jnp.float32)
    selector = jnp.dot(member, owned, preferred_element_type=jnp.float32)
    down_send = jnp.take(adapter_down, wanted, axis=0)
    up_send = jnp.take(adapter_up, wanted, axis=0)
    base = jnp.dot(
        tokens,
        lax.all_gather(base_weight, "store", axis=0, tiled=True),
        preferred_element_type=jnp.float32,
    )
    down_got, up_got = (
        lax.all_to_all(down_send, "store", split_axis=1, concat_axis=1, tiled=True),
        lax.all_to_all(up_send, "store", split_axis=1, concat_axis=1, tiled=True),
    )
    slots_count = wanted.shape[0]
    down_full = down_got.reshape(slots_count, model_width, rank)
    up_full = up_got.reshape(slots_count, width, rank)
    shrink_all = jnp.einsum("td,kdr->tkr", tokens, down_full, preferred_element_type=jnp.float32)
    shrink = jnp.sum(selector[:, :, None] * shrink_all, axis=1).astype(jnp.bfloat16)
    picked = (selector[:, :, None] * shrink.astype(jnp.float32)[:, None, :]).astype(jnp.bfloat16)
    delta = jnp.einsum("tkr,kvr->tv", picked, up_full, preferred_element_type=jnp.float32)
    return (base + delta).astype(jnp.bfloat16)


def solution(mesh):
    return jax.shard_map(
        body,
        mesh=mesh,
        in_specs=(
            P(("parts", "store"), None),
            P("store", None),
            P(None, "store", None),
            P(None, "store", None),
            P(("parts", "store"), None),
            P("parts", None),
            P("parts", None),
        ),
        out_specs=P(("parts", "store"), None),
        check_vma=False,
    )
```

profile of v0, /device:TPU:0, one launch (start us, length us, event | category | flops | bytes accessed | tf_op | source)
XLA Modules:
  0.0 142.5 jit_solution(789504423750247486)
XLA Ops:
  6.5 0.0 all-gather.2.cloned.1.call-start
  6.5 0.7 all-gather.2.cloned.1.call-update
  7.3 0.7 compare_select_fusion
  7.9 0.1 reshape.34
  8.0 2.4 %copy.24 = bf16[128,32,64]{2,1,0:T(8,128)(2,1)S(1)} copy(bf16[128,32,64]{0,2,1:T(8,128)(2,1)} %param.10) | data formatting | bytes 1048576 | tf_op args[3]
  10.5 0.6 gather_fusion.1
  11.1 0.7 compare_and_fusion
  11.8 0.1 copy_bitcast_fusion
  11.9 0.9 reshape.56
  12.8 7.4 %all-to-all-start.1 = ((bf16[16,2,2048]{2,1,0:T(2,128)(2,1)}), bf16[16,2,2048]{2,1,0:T(2,128)(2,1)S(1)}, u32[]{:S(2)}, u32[]{:S(2)}) async-start(bf16[16,2,2048]{2,1,0:T(2,128)(2,1)} %reshape.56), calls=%async_computation.1 | async-start | bytes 262144 | tf_op jit(solution)/shard_map/all_to_all | solution.py:35
  20.2 4.2 %gather_fusion = bf16[32,512,64]{1,2,0:T(8,128)(2,1)S(1)} fusion(bf16[128,512,64]{1,2,0:T(8,128)(2,1)} %param.9, s32[1024]{0:T(1024)S(1)} %pad_clamp_fusion), kind=kCustom, calls=%fused_computation | custom fusion | bytes 4194432 | tf_op jit(solution)/shard_map/jit(_take)/gather | solution.py:26
  24.5 0.3 broadcast_select_fusion
  24.7 0.0 copy-start
  24.8 1.5 %copy.22 = bf16[2,16,512,64]{2,3,0,1:T(8,128)(2,1)} copy(bf16[2,16,512,64]{2,3,1,0:T(8,128)(2,1)S(1)} %broadcast_select_fusion) | data formatting | bytes 4194304 | tf_op jit(solution)/shard_map/jit(_take)/select_n | solution.py:26
  26.3 4.0 %all-to-all-done.1 = bf16[16,2,2048]{2,1,0:T(2,128)(2,1)S(1)} async-done(((bf16[16,2,2048]{2,1,0:T(2,128)(2,1)}), bf16[16,2,2048]{2,1,0:T(2,128)(2,1)S(1)}, u32[]{:S(2)}, u32[]{:S(2)}) %all-to-all-start.1) | async-done | bytes 131104 | tf_op jit(solution)/shard_map/all_to_all | solution.py:35
  30.3 3.8 %all-to-all-start = ((bf16[2,16,512,64]{2,3,0,1:T(8,128)(2,1)}), bf16[2,16,512,64]{2,3,0,1:T(8,128)(2,1)S(1)}, u32[]{:S(2)}, u32[]{:S(2)}) async-start(bf16[2,16,512,64]{2,3,0,1:T(8,128)(2,1)} %copy.22), calls=%async_computation | async-start | bytes 4194304 | tf_op jit(solution)/shard_map/all_to_all | solution.py:34
  34.1 0.0 copy-done
  34.1 0.1 copy.21
  34.3 0.1 reduce
  34.4 0.7 fusion.20
  35.1 0.3 fusion.13
  35.3 0.2 reshape.57
  35.6 64.9 %all-to-all-done = bf16[2,16,512,64]{2,3,0,1:T(8,128)(2,1)S(1)} async-done(((bf16[2,16,512,64]{2,3,0,1:T(8,128)(2,1)}), bf16[2,16,512,64]{2,3,0,1:T(8,128)(2,1)S(1)}, u32[]{:S(2)}, u32[]{:S(2)}) %all-to-all-start) | async-done | bytes 2097184 | tf_op jit(solution)/shard_map/all_to_all | solution.py:34
  100.5 0.2 copy.29
  100.7 6.4 %fusion.9 = bf16[512,64]{0,1:T(8,128)(2,1)S(1)} fusion(bf16[2,8192,64]{1,2,0:T(8,128)(2,1)S(1)} %bitcast.43, bf16[512,8192]{1,0:T(8,128)(2,1)} %param.7, f32[512,2]{0,1:T(2,128)S(1)} %fusion.13), kind=kOutput, calls=%fused_computation.10 | convolution fusion | flops 1073840128 | bytes 10555392 | tf_op jit(solution)/shard_map/td,kdr->tkr/dot_general | solution.py:40
  107.1 0.4 convolution_bitcast_fusion
  107.5 17.2 %all-gather.2.cloned.1.call-done = bf16[8192,512]{1,0:T(8,128)(2,1)} async-done(((bf16[512,512]{1,0:T(8,128)(2,1)}), bf16[8192,512]{1,0:T(8,128)(2,1)}) %all-gather.2.cloned.1.call-update) | async-done | bytes 8388624 | tf_op jit(solution)/shard_map/all_gather | solution.py:30
  124.6 11.0 %fusion.2 = bf16[512,512]{1,0:T(8,128)(2,1)} fusion(f32[512,512]{1,0:T(8,128)S(1)} %convolution_bitcast_fusion, bf16[512,8192]{1,0:T(8,128)(2,1)} %param.7, bf16[8192,512]{1,0:T(8,128)(2,1)} %all-gather.2.cloned.1.call-done), kind=kOutput, calls=%fused_computation.7 | convolution fusion | flops 4295491584 | bytes 18350080 | tf_op jit(solution)/shard_map/dot_general | solution.py:28
  (4 shorter events, 0.1 us)
Async XLA Ops:
  6.5 118.1 %all-gather.2.cloned.1.call-start = ((), (), s32[]{:S(2)}) async-start(), calls=%async_computation.2 | async-start | bytes 8912896 | tf_op jit(solution)/shard_map/all_gather | solution.py:30
  12.8 17.5 %all-to-all-start.1 = ((bf16[16,2,2048]{2,1,0:T(2,128)(2,1)}), bf16[16,2,2048]{2,1,0:T(2,128)(2,1)S(1)}, u32[]{:S(2)}, u32[]{:S(2)}) async-start(bf16[16,2,2048]{2,1,0:T(2,128)(2,1)} %reshape.56), calls=%async_computation.1 | async-start | bytes 262144 | tf_op jit(solution)/shard_map/all_to_all | solution.py:35
  24.7 9.4 %copy-start = (s32[1,16]{1,0:T(1,128)S(1)}, s32[1,16]{1,0:T(1,128)}, u32[]{:S(2)}) copy-start(s32[1,16]{1,0:T(1,128)} %param.11) | copy-start | bytes 196
  30.3 70.1 %all-to-all-start = ((bf16[2,16,512,64]{2,3,0,1:T(8,128)(2,1)}), bf16[2,16,512,64]{2,3,0,1:T(8,128)(2,1)S(1)}, u32[]{:S(2)}, u32[]{:S(2)}) async-start(bf16[2,16,512,64]{2,3,0,1:T(8,128)(2,1)} %copy.22), calls=%async_computation | async-start | bytes 4194304 | tf_op jit(solution)/shard_map/all_to_all | solution.py:34
Sparse Core Ops, SparseCore 0:
  9.5 115.0 all-gather.1
where the time goes:
time: 145 us; the launch traced here: 143 us
  waiting for transfers between devices  86.8 us (60%)
  matrix products  18.1 us (12%)
  between operations  13.5 us (9%)
  starting transfers between devices  11.2 us (8%)
  local copies, waits for them, and re-layouts  10.3 us (7%)
  other arithmetic  2.63 us (2%)
    all_to_all x1, waiting for transfers between devices, body(): lax.all_to_all(down_send, 'store', split_axis=1, concat_axis=1, tiled=True)  64.9 us
    all_gather x1, waiting for transfers between devices, body(): lax.all_gather(base_weight, 'store', axis=0, tiled=True)  17.2 us
    dot_general x1, matrix products, body(): jnp.dot(tokens, lax.all_gather(base_weight, 'store', axis=0, tiled=True),...  11 us
    all_to_all x1, starting transfers between devices, body(): lax.all_to_all(up_send, 'store', split_axis=1, concat_axis=1, tiled=True)  7.39 us
    dot_general x1, matrix products, body(): jnp.einsum('td,kdr->tkr', tokens, down_full, preferred_element_type=jnp.f...  6.42 us
    gather x1, local copies, waits for them, and re-layouts, body(): down_send = jnp.take(adapter_down, wanted, axis=0)  4.24 us
    all_to_all x1, waiting for transfers between devices, body(): lax.all_to_all(up_send, 'store', split_axis=1, concat_axis=1, tiled=True)  4.03 us
    all_to_all x1, starting transfers between devices, body(): lax.all_to_all(down_send, 'store', split_axis=1, concat_axis=1, tiled=True)  3.81 us
  transfers between devices with their start and end apart: 3, of which 3 were waited for; matrix products, arithmetic and copies ran while one was open for 14% of the time, Pallas kernels for 0%

commit v1 on v0

v1 whole, which is shorter than its diff:
```python
import functools

import jax
import jax.numpy as jnp
from jax import lax
from jax.experimental import pallas as pl
from jax.experimental.pallas import tpu as pltpu
from jax.sharding import Mesh
from jax.sharding import PartitionSpec as P

HALF = 256
MIB = 1024 * 1024


def send_kernel(
    wanted, wanted_column, down, up, out, even_rows, odd_rows, up_narrow, down_sems, up_sems
):
    groups, choices = wanted.shape
    rank = down.shape[1]
    halves = down.shape[2] // HALF
    per_group = choices * halves

    def copy_of(n):
        group, rest = n // per_group, lax.rem(n, per_group)
        choice, half = rest // halves, lax.rem(rest, halves)
        return pltpu.make_async_copy(
            down.at[wanted[group, choice], :, pl.ds(half * HALF, HALF)],
            out.at[group, pl.ds(half * choices * rank + choice * rank, rank), :],
            down_sems.at[n],
        )

    def start(n, carry):
        copy_of(n).start()
        return carry

    def wait(n, carry):
        copy_of(n).wait()
        return carry

    lax.fori_loop(0, groups * per_group, start, 0)

    ids = lax.broadcasted_iota(jnp.int32, (choices * groups, up.shape[1]), 1)
    pick = (ids == wanted_column[...]).astype(jnp.float32).astype(jnp.bfloat16)
    rows = lax.dot_general(
        pick, up[...], (((1,), (1,)), ((), ())), preferred_element_type=jnp.float32
    )
    first, second = rows[:groups], rows[groups:]
    low = lax.broadcasted_iota(jnp.int32, (groups, 2 * rank), 1) < rank
    count = up_narrow.shape[0] // groups
    for i in range(count):
        a = first[:, 2 * rank * i : 2 * rank * (i + 1)]
        b = second[:, 2 * rank * i : 2 * rank * (i + 1)]
        even_rows[pl.ds(i, groups, stride=count), :] = jnp.where(low, a, pltpu.roll(b, rank, 1))
        odd_rows[pl.ds(i, groups, stride=count), :] = jnp.where(low, pltpu.roll(a, rank, 1), b)
    up_narrow[:, : 2 * rank] = even_rows[...].astype(jnp.bfloat16)
    up_narrow[:, 2 * rank :] = odd_rows[...].astype(jnp.bfloat16)

    def up_copy(group):
        return pltpu.make_async_copy(
            up_narrow.at[pl.ds(group * count, count), :],
            out.at[group, pl.ds(per_group * rank, count), :],
            up_sems.at[group],
        )

    def up_start(group, carry):
        up_copy(group).start()
        return carry

    def up_wait(group, carry):
        up_copy(group).wait()
        return carry

    lax.fori_loop(0, groups, up_start, 0)
    lax.fori_loop(0, groups * per_group, wait, 0)
    lax.fori_loop(0, groups, up_wait, 0)


def make_messages(wanted, down, up, shard_width):
    groups, choices = wanted.shape
    rank, depth = down.shape[1:]
    halves = depth // HALF
    count = shard_width * choices * rank // HALF
    rows = choices * rank * halves + count
    column = jnp.transpose(wanted).reshape(choices * groups, 1)
    return pl.pallas_call(
        send_kernel,
        out_shape=jax.ShapeDtypeStruct((groups, rows, HALF), jnp.bfloat16),
        in_specs=[
            pl.BlockSpec(memory_space=pltpu.SMEM),
            pl.BlockSpec(memory_space=pltpu.VMEM),
            pl.BlockSpec(memory_space=pl.ANY),
            pl.BlockSpec(memory_space=pltpu.VMEM),
        ],
        out_specs=pl.BlockSpec(memory_space=pl.ANY),
        scratch_shapes=[
            pltpu.VMEM((groups * count, 2 * rank), jnp.float32),
            pltpu.VMEM((groups * count, 2 * rank), jnp.float32),
            pltpu.VMEM((groups * count, HALF), jnp.bfloat16),
            pltpu.SemaphoreType.DMA((groups * choices * halves,)),
            pltpu.SemaphoreType.DMA((groups,)),
        ],
        name="make_messages",
    )(wanted, column, down, up)


def base_kernel(tokens_refs, weight, out):
    total = jnp.zeros(out.shape, jnp.float32)
    for i, part in enumerate(tokens_refs):
        total += jnp.dot(
            part[...], weight[0, i * HALF : (i + 1) * HALF, :], preferred_element_type=jnp.float32
        )

    @pl.when(pl.program_id(0) == 0)
    def _():
        out[...] = total

    @pl.when(pl.program_id(0) > 0)
    def _():
        out[...] += total


def base_product(tokens, weight, lines, plane):
    rows = tokens.shape[0]
    width = weight.shape[2]

    def token_spec(z):
        def index(n):
            x, place = n // plane, lax.rem(n, plane)
            return (0, (z * plane + place) * 2 + x)

        return pl.BlockSpec((rows, HALF), index)

    def kernel(*refs):
        base_kernel(refs[:lines], refs[lines], refs[lines + 1])

    return pl.pallas_call(
        kernel,
        grid=(weight.shape[0],),
        out_shape=jax.ShapeDtypeStruct((rows, width), jnp.float32),
        in_specs=[token_spec(z) for z in range(lines)]
        + [pl.BlockSpec((1, lines * HALF, width), lambda n: (n, 0, 0))],
        out_specs=pl.BlockSpec((rows, width), lambda n: (0, 0)),
        compiler_params=pltpu.CompilerParams(vmem_limit_bytes=32 * MIB),
        cost_estimate=pl.CostEstimate(
            flops=2 * rows * tokens.shape[1] * width,
            bytes_accessed=2 * tokens.size + 2 * weight.size + 4 * rows * width,
            transcendentals=0,
        ),
        name="base_product",
    )(*([tokens] * lines), weight)


def adapt_kernel(tokens, down, up, mask, base, out, shrink):
    step = pl.program_id(0)
    sources = down.shape[0]
    pair = mask.shape[1]
    halves = tokens.shape[1] // (sources * HALF)
    total = jnp.zeros(shrink.shape, jnp.float32)
    for source in range(sources):
        for half in range(halves):
            column = (source * halves + half) * HALF
            total += lax.dot_general(
                tokens[:, column : column + HALF],
                down[source, half * pair : (half + 1) * pair, :],
                (((1,), (1,)), ((), ())),
                preferred_element_type=jnp.float32,
            )

    @pl.when(step == 0)
    def _():
        shrink[...] = total

    @pl.when(step > 0)
    def _():
        shrink[...] += total

    @pl.when(step == pl.num_programs(0) - 1)
    def _():
        picked = (shrink[...] * mask[...]).astype(jnp.bfloat16)
        got = up[...].reshape(up.shape[0] * up.shape[1], HALF)
        width = out.shape[1]
        value = lax.broadcasted_iota(jnp.int32, (width, got.shape[0]), 0)
        row = lax.broadcasted_iota(jnp.int32, (width, got.shape[0]), 1)
        wide = jnp.zeros((width, pair), jnp.float32)
        for i in range(HALF // pair):
            place = (value == row * (HALF // pair) + i).astype(jnp.float32).astype(jnp.bfloat16)
            wide += jnp.dot(
                place, got[:, i * pair : (i + 1) * pair], preferred_element_type=jnp.float32
            )
        delta = lax.dot_general(
            picked,
            wide.astype(jnp.bfloat16),
            (((1,), (1,)), ((), ())),
            preferred_element_type=jnp.float32,
        )
        out[...] = (base[...] + delta).astype(out.dtype)


def adapt(tokens, messages, mask, base, halves):
    rows, width = base.shape
    pair = mask.shape[1]
    groups, length = messages.shape[:2]
    count = length - halves * pair
    steps = 8
    per_step = groups // steps
    return pl.pallas_call(
        adapt_kernel,
        grid=(steps,),
        out_shape=jax.ShapeDtypeStruct((rows, width), jnp.bfloat16),
        in_specs=[
            pl.BlockSpec((rows, tokens.shape[1] // steps), lambda n: (0, n)),
            pl.BlockSpec((per_step, halves * pair, HALF), lambda n: (n, 0, 0)),
            pl.BlockSpec((groups, count, HALF), lambda n: (0, halves * pair // count, 0)),
            pl.BlockSpec((rows, pair), lambda n: (0, 0)),
            pl.BlockSpec((rows, width), lambda n: (0, 0)),
        ],
        out_specs=pl.BlockSpec((rows, width), lambda n: (0, 0)),
        scratch_shapes=[pltpu.VMEM((rows, pair), jnp.float32)],
        compiler_params=pltpu.CompilerParams(vmem_limit_bytes=32 * MIB),
        cost_estimate=pl.CostEstimate(
            flops=2 * rows * tokens.shape[1] * pair,
            bytes_accessed=2 * tokens.size + 2 * messages.size + 6 * rows * width,
            transcendentals=0,
        ),
        name="adapt",
    )(tokens, messages, messages, mask, base)


def row_slots(lengths, slots, rows):
    ends = jnp.cumsum(lengths)
    starts = ends - lengths
    position = jnp.arange(rows, dtype=jnp.int32)[:, None]
    member = (position >= starts[None, :]) & (position < ends[None, :])
    return jnp.sum(jnp.where(member, slots[None, :], 0), axis=1)


def body(
    lines,
    tokens,
    base_weight,
    adapter_down,
    adapter_up,
    request_lengths,
    group_adapters,
    request_slot,
):
    store = ("line", "plane", "core")
    rank = adapter_down.shape[2]
    choices = group_adapters.shape[1]
    depth, width = base_weight.shape
    group = lax.axis_index(store)
    own_half = lax.dynamic_slice_in_dim(base_weight, lax.axis_index("parts") * HALF, HALF, 0)
    along = lax.all_gather(own_half, "line", axis=0, tiled=True)
    gathered = lax.all_gather(along, ("parts", "plane", "core"), axis=0, tiled=False)
    shard_width = adapter_up.shape[1]
    messages = make_messages(
        group_adapters,
        jnp.swapaxes(adapter_down, 1, 2),
        jnp.transpose(adapter_up, (1, 2, 0)).reshape(shard_width * rank, adapter_up.shape[0]),
        shard_width,
    )
    arrived = lax.all_to_all(messages, store, split_axis=0, concat_axis=0, tiled=True)
    slots = lax.dynamic_index_in_dim(request_slot, group, 0, keepdims=False)
    slot_of_row = row_slots(request_lengths[0], slots, tokens.shape[0])
    lane_slot = jnp.arange(choices * rank, dtype=jnp.int32)[None, :] // rank
    mask = (slot_of_row[:, None] == lane_slot).astype(jnp.float32)
    base = base_product(tokens, gathered, lines, gathered.shape[0] // 2)
    return adapt(tokens, arrived, mask, base, depth // HALF)


def plain_body(
    tokens, base_weight, adapter_down, adapter_up, request_lengths, group_adapters, request_slot
):
    store = ("line", "plane", "core")
    rank = adapter_down.shape[2]
    choices = group_adapters.shape[1]
    group = lax.axis_index(store)
    wanted = jnp.transpose(group_adapters)
    slots = lax.dynamic_index_in_dim(request_slot, group, 0, keepdims=False)
    slot_of_row = row_slots(request_lengths[0], slots, tokens.shape[0])
    lane_slot = jnp.arange(choices * rank, dtype=jnp.int32)[None, :] // rank
    mask = (slot_of_row[:, None] == lane_slot).astype(jnp.float32)
    exchange = functools.partial(
        lax.all_to_all, axis_name=store, split_axis=1, concat_axis=1, tiled=True
    )
    down = exchange(jnp.take(adapter_down, wanted, axis=0))
    up = exchange(jnp.take(adapter_up, wanted, axis=0))
    weight = lax.all_gather(base_weight, store, axis=0, tiled=True)
    down = down.reshape(choices, tokens.shape[1], rank)
    up = up.reshape(choices, base_weight.shape[1], rank)
    base = jnp.dot(tokens, weight, preferred_element_type=jnp.float32)
    shrink = jnp.einsum("td,kdr->tkr", tokens, down, preferred_element_type=jnp.float32)
    picked = (shrink.reshape(mask.shape) * mask).astype(jnp.bfloat16)
    picked = picked.reshape(shrink.shape)
    delta = jnp.einsum("tkr,kvr->tv", picked, up, preferred_element_type=jnp.float32)
    return (base + delta).astype(jnp.bfloat16)


def solution(mesh):
    parts, size = mesh.shape["parts"], mesh.shape["store"]
    chips = size // 2
    plane = 1
    while 4 * plane * plane <= chips:
        plane *= 2
    lines = chips // plane
    names = ("parts", "line", "plane", "core")
    split = Mesh(mesh.devices.reshape(parts, lines, plane, 2), names)
    store = names[1:]

    def run(tokens, base_weight, *rest):
        large = parts == 2 and base_weight.shape[0] // size == 2 * HALF
        return jax.shard_map(
            functools.partial(body, lines) if large else plain_body,
            mesh=split,
            in_specs=(
                P(names, None),
                P(store, None),
                P(None, store, None),
                P(None, store, None),
                P(names, None),
                P("parts", None),
                P("parts", None),
            ),
            out_specs=P(names, None),
            check_vma=False,
        )(tokens, base_weight, *rest)

    return run
```

time: 145 us -> 180 us (1.24)
  the two profiles are of different devices: /device:TPU:0 before, /device:TPU:13 now
where the time goes in v1:
time: 180 us
  Pallas kernels  80.4 us (45%)
  waiting for transfers between devices  62.8 us (35%)
  local copies, waits for them, and re-layouts  17.6 us (10%)
  between operations  13.5 us (8%)
  starting transfers between devices  5.27 us (3%)
    pallas_call x1, Pallas kernels, make_messages(): pl.pallas_call(send_kernel, out_shape=jax.ShapeDtypeStruct((groups, rows,...  66.5 us
    all_to_all x1, waiting for transfers between devices, body(): lax.all_to_all(messages, store, split_axis=0, concat_axis=0, tiled=True)  33.4 us
    all_gather x1, waiting for transfers between devices, body(): along = lax.all_gather(own_half, 'line', axis=0, tiled=True)  29.4 us
    unnamed x15, local copies, waits for them, and re-layouts  14.7 us
    pallas_call x1, Pallas kernels, base_product(): pl.pallas_call(kernel, grid=(weight.shape[0],), out_shape=jax.ShapeDtypeS...  7.9 us
    pallas_call x1, Pallas kernels, adapt(): pl.pallas_call(adapt_kernel, grid=(steps,), out_shape=jax.ShapeDtypeStruc...  6.07 us
    all_to_all x1, starting transfers between devices, body(): lax.all_to_all(messages, store, split_axis=0, concat_axis=0, tiled=True)  5.22 us
  transfers between devices with their start and end apart: 3, of which 2 were waited for; matrix products, arithmetic and copies ran while one was open for 2% of the time, Pallas kernels for 41%

profile of v1, /device:TPU:13, one launch (start us, length us, event | category | flops | bytes accessed | tf_op | source)
XLA Modules:
  0.0 180.0 jit_solution(9847683378748094197)
XLA Ops:
  6.5 0.0 copy-start
  6.5 0.0 all-gather.4.cloned.1.call-start
  6.5 1.0 copy-done
  7.6 0.7 constant_dynamic-slice_fusion
  8.3 0.0 all-gather.4.cloned.1.call-update
  8.3 0.0 copy-start.6
  8.3 0.0 all-gather.6.cloned.1.call-start
  8.4 29.4 %all-gather.4.cloned.1.call-done = bf16[1024,512]{1,0:T(8,128)(2,1)} async-done(((bf16[256,512]{1,0:T(8,128)(2,1)}), bf16[1024,512]{1,0:T(8,128)(2,1)}) %all-gather.4.cloned.1.call-update) | async-done | bytes 1048592 | tf_op jit(solution)/shard_map/all_gather | solution.py:253
  37.8 0.0 all-gather.6.cloned.1.call-update
  37.8 1.4 copy.14.wanted
  39.1 1.4 reshape.59.wanted_column
  40.5 66.5 %make_messages.1 = bf16[16,272,256]{2,1,0:T(8,128)(2,1)} custom-call(s32[16,2]{1,0:T(8,128)} %copy.14.wanted, s32[32,1]{1,0:T(8,128)} %reshape.59.wanted_column, bf16[128,64,512]{2,1,0:T(8,128)(2,1)} %bitcast.16, bf16[2048,128]{1,0:T(8,128)(2,1)} %bitcast.17), custom_call_target="tpu_custom_call" | custom-call | tf_op jit(solution)/shard_map/make_messages/pallas_call | solution.py:85
  107.0 5.2 %all-to-all-start = ((bf16[16,272,256]{2,1,0:T(8,128)(2,1)}), bf16[16,272,256]{2,1,0:T(8,128)(2,1)S(1)}, u32[]{:S(2)}, u32[]{:S(2)}) async-start(bf16[16,272,256]{2,1,0:T(8,128)(2,1)} %make_messages.1), calls=%async_computation | async-start | bytes 4456448 | tf_op jit(solution)/shard_map/all_to_all | solution.py:262
  112.2 0.0 copy-done.6
  112.2 0.1 copy.16
  112.3 0.1 reduce
  112.5 0.7 dynamic-slice_bitcast_fusion
  113.2 0.1 select_reduce_fusion
  113.3 0.1 compare_convert_fusion.mask
  113.4 0.0 all-gather.6.cloned.1.call-done
  113.4 0.0 copy-start.1
  113.4 3.4 %copy-done.1 = bf16[512,8192]{1,0:T(8,128)(2,1)S(1)} copy-done((bf16[512,8192]{1,0:T(8,128)(2,1)S(1)}, bf16[512,8192]{1,0:T(8,128)(2,1)}, u32[]{:S(2)}) %copy-start.1) | copy-done | bytes 8388632
  116.8 0.0 copy-start.3
  116.8 3.4 %copy-done.3 = bf16[8192,512]{1,0:T(8,128)(2,1)S(1)} copy-done((bf16[8192,512]{1,0:T(8,128)(2,1)S(1)}, bf16[8192,512]{1,0:T(8,128)(2,1)}, u32[]{:S(2)}) %copy-start.3) | copy-done | bytes 8388632
  120.2 7.9 %base_product.1.base = f32[512,512]{1,0:T(8,128)S(1)} custom-call(bf16[512,8192]{1,0:T(8,128)(2,1)S(1)} %copy-done.1, bf16[512,8192]{1,0:T(8,128)(2,1)S(1)} %copy-done.1, bf16[512,8192]{1,0:T(8,128)(2,1)S(1)} %copy-done.1, bf16[512,8192]{1,0:T(8,128)(2,1)S(1)} %copy-done.1, bf16[8,1024,512]{2,1,0:T(8,128)(2,1)S(1)} %bitcast.15), custom_call_target="tpu_custom_call" | custom-call | flops 4294967296 | bytes 17825792 | tf_op jit(solution)/shard_map/base_product/pallas_call | solution.py:136
  128.1 0.0 copy-start.4
  128.1 1.0 copy-done.4
  129.1 33.4 %all-to-all-done.down.up = bf16[16,272,256]{2,1,0:T(8,128)(2,1)S(1)} async-done(((bf16[16,272,256]{2,1,0:T(8,128)(2,1)}), bf16[16,272,256]{2,1,0:T(8,128)(2,1)S(1)}, u32[]{:S(2)}, u32[]{:S(2)}) %all-to-all-start) | async-done | bytes 2228256 | tf_op jit(solution)/shard_map/all_to_all | solution.py:262
  162.4 0.0 copy-start.2
  162.4 3.4 %copy-done.2 = bf16[512,8192]{1,0:T(8,128)(2,1)S(1)} copy-done((bf16[512,8192]{1,0:T(8,128)(2,1)S(1)}, bf16[512,8192]{1,0:T(8,128)(2,1)}, u32[]{:S(2)}) %copy-start.2) | copy-done | bytes 8388632
  165.8 0.0 copy-start.5
  165.8 1.2 copy-done.5
  167.1 6.1 %adapt.1 = bf16[512,512]{1,0:T(8,128)(2,1)} custom-call(bf16[512,8192]{1,0:T(8,128)(2,1)S(1)} %copy-done.2, bf16[16,272,256]{2,1,0:T(8,128)(2,1)S(1)} %all-to-all-done.down.up, bf16[16,272,256]{2,1,0:T(8,128)(2,1)S(1)} %all-to-all-done.down.up, f32[512,128]{1,0:T(8,128)S(1)} %compare_convert_fusion.mask, f32[512,512]{1,0:T(8,128)S(1)} %copy-done.5), custom_call_target="tpu_custom_call" | custom-call | flops 1073741824 | bytes 12189696 | tf_op jit(solution)/shard_map/adapt/pallas_call | solution.py:206
  (3 shorter events, 0.0 us)
Async XLA Ops:
  6.5 1.0 copy-start
  6.5 31.2 %all-gather.4.cloned.1.call-start = ((), (), s32[]{:S(2)}) async-start(), calls=%async_computation.1 | async-start | bytes 1310720 | tf_op jit(solution)/shard_map/all_gather | solution.py:253
  8.3 103.9 %copy-start.6 = (s32[1,16]{1,0:T(1,128)S(1)}, s32[1,16]{1,0:T(1,128)}, u32[]{:S(2)}) copy-start(s32[1,16]{1,0:T(1,128)} %param.11) | copy-start | bytes 196
  8.3 105.1 %all-gather.6.cloned.1.call-start = ((), (), s32[]{:S(2)}) async-start(), calls=%async_computation.2 | async-start | bytes 9437184 | tf_op jit(solution)/shard_map/all_gather | solution.py:254
  107.0 55.5 %all-to-all-start = ((bf16[16,272,256]{2,1,0:T(8,128)(2,1)}), bf16[16,272,256]{2,1,0:T(8,128)(2,1)S(1)}, u32[]{:S(2)}, u32[]{:S(2)}) async-start(bf16[16,272,256]{2,1,0:T(8,128)(2,1)} %make_messages.1), calls=%async_computation | async-start | bytes 4456448 | tf_op jit(solution)/shard_map/all_to_all | solution.py:262
  113.4 3.4 %copy-start.1 = (bf16[512,8192]{1,0:T(8,128)(2,1)S(1)}, bf16[512,8192]{1,0:T(8,128)(2,1)}, u32[]{:S(2)}) copy-start(bf16[512,8192]{1,0:T(8,128)(2,1)} %tokens.1) | copy-start | bytes 25165828
  116.8 3.4 %copy-start.3 = (bf16[8192,512]{1,0:T(8,128)(2,1)S(1)}, bf16[8192,512]{1,0:T(8,128)(2,1)}, u32[]{:S(2)}) copy-start(bf16[8192,512]{1,0:T(8,128)(2,1)} %all-gather.6.cloned.1.call-done) | copy-start | bytes 25165828
  128.1 1.0 copy-start.4
  162.4 3.4 %copy-start.2 = (bf16[512,8192]{1,0:T(8,128)(2,1)S(1)}, bf16[512,8192]{1,0:T(8,128)(2,1)}, u32[]{:S(2)}) copy-start(bf16[512,8192]{1,0:T(8,128)(2,1)} %tokens.1) | copy-start | bytes 25165828
  165.8 1.2 copy-start.5
Sparse Core Ops, SparseCore 0:
  8.9 28.7 all-gather.3
  39.6 54.1 all-gather.5

commit v2 on v1

v2 whole, which is shorter than its diff:
```python
import functools

import jax
import jax.numpy as jnp
from jax import lax
from jax.experimental import pallas as pl
from jax.experimental.pallas import tpu as pltpu
from jax.sharding import Mesh
from jax.sharding import PartitionSpec as P

HALF = 256
MIB = 1024 * 1024
AXES = ("parts", "line", "plane", "core")


def send_kernel(wanted, down, up, out, pick, even_rows, odd_rows, sems):
    choices, groups = wanted.shape
    rank = down.shape[1]
    halves = down.shape[2] // HALF
    copies = []
    for group in range(groups):
        for choice in range(choices):
            for half in range(halves):
                copy = pltpu.make_async_copy(
                    down.at[wanted[choice, group], :, pl.ds(half * HALF, HALF)],
                    out.at[group, pl.ds((half * choices + choice) * rank, rank), :],
                    sems.at[len(copies)],
                )
                copy.start()
                copies.append(copy)

    ids = lax.broadcasted_iota(jnp.int32, (1, up.shape[1]), 1)
    for choice in range(choices):
        for group in range(groups):
            here = (ids == wanted[choice, group]).astype(jnp.float32)
            pick[pl.ds(choice * groups + group, 1), :] = here
    rows = lax.dot_general(
        pick[...].astype(jnp.bfloat16),
        up[...],
        (((1,), (1,)), ((), ())),
        preferred_element_type=jnp.float32,
    )
    first, second = rows[:groups], rows[groups:]
    low = lax.broadcasted_iota(jnp.int32, (groups, 2 * rank), 1) < rank
    count = even_rows.shape[0] // groups
    for i in range(count):
        a = first[:, 2 * rank * i : 2 * rank * (i + 1)]
        b = second[:, 2 * rank * i : 2 * rank * (i + 1)]
        even_rows[pl.ds(i, groups, stride=count), :] = jnp.where(low, a, pltpu.roll(b, rank, 1))
        odd_rows[pl.ds(i, groups, stride=count), :] = jnp.where(low, pltpu.roll(a, rank, 1), b)
    start = choices * halves * rank
    for group in range(groups):
        own = pl.ds(group * count, count)
        out[group, start:, : 2 * rank] = even_rows[own, :].astype(jnp.bfloat16)
        out[group, start:, 2 * rank :] = odd_rows[own, :].astype(jnp.bfloat16)
    for copy in copies:
        copy.wait()


def make_messages(wanted, down, up, shard_width):
    choices, groups = wanted.shape
    rank, depth = down.shape[1:]
    halves = depth // HALF
    count = shard_width * choices * rank // HALF
    rows = choices * rank * halves + count
    return pl.pallas_call(
        send_kernel,
        out_shape=jax.ShapeDtypeStruct((groups, rows, HALF), jnp.bfloat16),
        in_specs=[
            pl.BlockSpec(memory_space=pltpu.SMEM),
            pl.BlockSpec(memory_space=pl.ANY),
            pl.BlockSpec(memory_space=pltpu.VMEM),
        ],
        out_specs=pl.BlockSpec(memory_space=pltpu.VMEM),
        scratch_shapes=[
            pltpu.VMEM((choices * groups, up.shape[1]), jnp.float32),
            pltpu.VMEM((groups * count, 2 * rank), jnp.float32),
            pltpu.VMEM((groups * count, 2 * rank), jnp.float32),
            pltpu.SemaphoreType.DMA((groups * choices * halves,)),
        ],
        compiler_params=pltpu.CompilerParams(vmem_limit_bytes=56 * MIB),
        name="make_messages",
    )(wanted, down, up)


def base_product(tokens, blocks):
    rows, depth = tokens.shape
    width = blocks[0][1].shape[1]
    count = len(blocks)
    masks = [mask for mask, _ in blocks]

    def kernel(*refs):
        tokens_ref, parts, out = refs[0], refs[1 : 1 + count], refs[1 + count]
        left, right, left_sems, right_sems = refs[2 + count :]
        place = [lax.axis_index(name) for name in AXES]
        copies = []
        for n, mask in enumerate(masks):
            x, z, y, core = [i ^ bit for i, bit in zip(place, mask)]
            column = pl.multiple_of((((z * 2 + y) * 2 + core) * 2 + x) * HALF, HALF)
            pair = (
                pltpu.make_async_copy(
                    tokens_ref.at[:, pl.ds(column, HALF)], left.at[n], left_sems.at[n]
                ),
                pltpu.make_async_copy(parts[n], right.at[n], right_sems.at[n]),
            )
            for copy in pair:
                copy.start()
            copies.append(pair)
        for n in range(0, count, 2):
            for pair in copies[n : n + 2]:
                for copy in pair:
                    copy.wait()
            total = jnp.dot(left[n], right[n], preferred_element_type=jnp.float32)
            total += jnp.dot(left[n + 1], right[n + 1], preferred_element_type=jnp.float32)
            if n == 0:
                out[...] = total
            else:
                out[...] += total

    return pl.pallas_call(
        kernel,
        out_shape=jax.ShapeDtypeStruct((rows, width), jnp.float32),
        in_specs=[pl.BlockSpec(memory_space=pl.ANY)] * (1 + count),
        out_specs=pl.BlockSpec(memory_space=pltpu.VMEM),
        scratch_shapes=[
            pltpu.VMEM((count, rows, HALF), jnp.bfloat16),
            pltpu.VMEM((count, HALF, width), jnp.bfloat16),
            pltpu.SemaphoreType.DMA((count,)),
            pltpu.SemaphoreType.DMA((count,)),
        ],
        compiler_params=pltpu.CompilerParams(vmem_limit_bytes=56 * MIB),
        cost_estimate=pl.CostEstimate(
            flops=2 * rows * depth * width,
            bytes_accessed=2 * rows * depth + 2 * depth * width + 4 * rows * width,
            transcendentals=0,
        ),
        name="base_product",
    )(tokens, *[block for _, block in blocks])


def adapt_kernel(halves, tokens, messages, mask, base, out, held, sems):
    groups, length = messages.shape[:2]
    pair = mask.shape[1]
    width = out.shape[1]
    depth = halves * HALF
    copies = []
    for source in range(groups):
        copy = pltpu.make_async_copy(
            tokens.at[:, pl.ds(source * depth, depth)], held.at[source], sems.at[source]
        )
        copy.start()
        copies.append(copy)

    start = halves * pair
    got = messages[:, start:, :].reshape(groups * (length - start), HALF)
    value = lax.broadcasted_iota(jnp.int32, (width, got.shape[0]), 0)
    row = lax.broadcasted_iota(jnp.int32, (width, got.shape[0]), 1)
    wide = jnp.zeros((width, pair), jnp.float32)
    for i in range(HALF // pair):
        place = (value == row * (HALF // pair) + i).astype(jnp.float32).astype(jnp.bfloat16)
        wide += jnp.dot(
            place, got[:, i * pair : (i + 1) * pair], preferred_element_type=jnp.float32
        )
    wide = wide.astype(jnp.bfloat16)

    shrink = jnp.zeros(mask.shape, jnp.float32)
    for source in range(groups):
        copies[source].wait()
        down = jnp.concatenate(
            [messages[source, half * pair : (half + 1) * pair, :] for half in range(halves)], axis=1
        )
        shrink += lax.dot_general(
            held[source], down, (((1,), (1,)), ((), ())), preferred_element_type=jnp.float32
        )
    picked = (shrink * mask[...]).astype(jnp.bfloat16)
    delta = lax.dot_general(
        picked, wide, (((1,), (1,)), ((), ())), preferred_element_type=jnp.float32
    )
    out[...] = (base[...] + delta).astype(out.dtype)


def adapt(tokens, messages, mask, base, halves):
    rows, width = base.shape
    groups = messages.shape[0]
    return pl.pallas_call(
        functools.partial(adapt_kernel, halves),
        out_shape=jax.ShapeDtypeStruct((rows, width), jnp.bfloat16),
        in_specs=[pl.BlockSpec(memory_space=pl.ANY)] + [pl.BlockSpec(memory_space=pltpu.VMEM)] * 3,
        out_specs=pl.BlockSpec(memory_space=pltpu.VMEM),
        scratch_shapes=[
            pltpu.VMEM((groups, rows, halves * HALF), jnp.bfloat16),
            pltpu.SemaphoreType.DMA((groups,)),
        ],
        compiler_params=pltpu.CompilerParams(vmem_limit_bytes=56 * MIB),
        cost_estimate=pl.CostEstimate(
            flops=2 * rows * tokens.shape[1] * mask.shape[1],
            bytes_accessed=2 * tokens.size + 2 * messages.size + 6 * rows * width,
            transcendentals=0,
        ),
        name="adapt",
    )(tokens, messages, mask, base)


def row_slots(lengths, slots, rows):
    ends = jnp.cumsum(lengths)
    starts = ends - lengths
    position = jnp.arange(rows, dtype=jnp.int32)[:, None]
    member = (position >= starts[None, :]) & (position < ends[None, :])
    return jnp.sum(jnp.where(member, slots[None, :], 0), axis=1)


def swap(block, axis, bit):
    size = lax.axis_size(axis)
    return lax.ppermute(block, axis, [(i, i ^ bit) for i in range(size)])


def gather_rows(base_weight):
    x = lax.axis_index("parts")
    own = lax.dynamic_slice_in_dim(base_weight, x * HALF, HALF, 0)
    other = lax.dynamic_slice_in_dim(base_weight, (1 - x) * HALF, HALF, 0)
    blocks = {(0, 0, 0, 0): own}
    blocks[0, 1, 0, 0] = swap(own, "line", 1)
    blocks[0, 2, 0, 0] = swap(own, "line", 2)
    blocks[0, 3, 0, 0] = swap(blocks[0, 2, 0, 0], "line", 1)
    for z in range(4):
        blocks[0, z, 1, 0] = swap(blocks[0, z, 0, 0], "plane", 1)
    for z in range(4):
        for y in range(2):
            source = blocks[0, z, y, 0]
            blocks[1, z, y, 0] = other if z == y == 0 else swap(source, "parts", 1)
    for (x, z, y, _), block in list(blocks.items()):
        blocks[x, z, y, 1] = swap(block, "core", 1)
    return list(blocks.items())


def body(
    tokens, base_weight, adapter_down, adapter_up, request_lengths, group_adapters, request_slot
):
    store = AXES[1:]
    rank = adapter_down.shape[2]
    choices = group_adapters.shape[1]
    depth = base_weight.shape[0]
    group = lax.axis_index(store)
    shard_width = adapter_up.shape[1]
    messages = make_messages(
        jnp.transpose(group_adapters),
        jnp.swapaxes(adapter_down, 1, 2),
        jnp.transpose(adapter_up, (1, 2, 0)).reshape(shard_width * rank, adapter_up.shape[0]),
        shard_width,
    )
    arrived = lax.all_to_all(messages, store, split_axis=0, concat_axis=0, tiled=True)
    blocks = gather_rows(base_weight)
    slots = lax.dynamic_index_in_dim(request_slot, group, 0, keepdims=False)
    slot_of_row = row_slots(request_lengths[0], slots, tokens.shape[0])
    lane_slot = jnp.arange(choices * rank, dtype=jnp.int32)[None, :] // rank
    mask = (slot_of_row[:, None] == lane_slot).astype(jnp.float32)
    base = base_product(tokens, blocks)
    return adapt(tokens, arrived, mask, base, depth // HALF)


def plain_body(
    tokens, base_weight, adapter_down, adapter_up, request_lengths, group_adapters, request_slot
):
    store = AXES[1:]
    rank = adapter_down.shape[2]
    choices = group_adapters.shape[1]
    group = lax.axis_index(store)
    wanted = jnp.transpose(group_adapters)
    slots = lax.dynamic_index_in_dim(request_slot, group, 0, keepdims=False)
    slot_of_row = row_slots(request_lengths[0], slots, tokens.shape[0])
    lane_slot = jnp.arange(choices * rank, dtype=jnp.int32)[None, :] // rank
    mask = (slot_of_row[:, None] == lane_slot).astype(jnp.float32)
    exchange = functools.partial(
        lax.all_to_all, axis_name=store, split_axis=1, concat_axis=1, tiled=True
    )
    down = exchange(jnp.take(adapter_down, wanted, axis=0))
    up = exchange(jnp.take(adapter_up, wanted, axis=0))
    weight = lax.all_gather(base_weight, store, axis=0, tiled=True)
    down = down.reshape(choices, tokens.shape[1], rank)
    up = up.reshape(choices, base_weight.shape[1], rank)
    base = jnp.dot(tokens, weight, preferred_element_type=jnp.float32)
    shrink = jnp.einsum("td,kdr->tkr", tokens, down, preferred_element_type=jnp.float32)
    picked = (shrink.reshape(mask.shape) * mask).astype(jnp.bfloat16)
    picked = picked.reshape(shrink.shape)
    delta = jnp.einsum("tkr,kvr->tv", picked, up, preferred_element_type=jnp.float32)
    return (base + delta).astype(jnp.bfloat16)


def solution(mesh):
    parts, size = mesh.shape["parts"], mesh.shape["store"]
    chips = size // 2
    plane = 1
    while 4 * plane * plane <= chips:
        plane *= 2
    lines = chips // plane
    split = Mesh(mesh.devices.reshape(parts, lines, plane, 2), AXES)
    store = AXES[1:]

    def run(tokens, base_weight, *rest):
        small = (parts, lines, plane) == (2, 4, 2) and base_weight.shape[0] // size == 2 * HALF
        return jax.shard_map(
            body if small else plain_body,
            mesh=split,
            in_specs=(
                P(AXES, None),
                P(store, None),
                P(None, store, None),
                P(None, store, None),
                P(AXES, None),
                P("parts", None),
                P("parts", None),
            ),
            out_specs=P(AXES, None),
            check_vma=False,
        )(tokens, base_weight, *rest)

    return run
```

time: 180 us -> 144 us (0.80)
  the two profiles are of different devices: /device:TPU:13 before, /device:TPU:0 now
where the time goes in v2:
time: 144 us; the launch traced here: 143 us
  waiting for transfers between devices  87.3 us (61%)
  starting transfers between devices  28.4 us (20%)
  Pallas kernels  22.1 us (15%)
  local copies, waits for them, and re-layouts  3.29 us (2%)
  other arithmetic  1.76 us (1%)
    ppermute x30, waiting for transfers between devices, swap(): return lax.ppermute(block, axis, [(i, i ^ bit) for i in range(size)])  87.3 us
    ppermute x30, starting transfers between devices, swap(): return lax.ppermute(block, axis, [(i, i ^ bit) for i in range(size)])  21 us
    pallas_call x1, Pallas kernels, adapt(): pl.pallas_call(functools.partial(adapt_kernel, halves), out_shape=jax.Sha...  9.44 us
    pallas_call x1, Pallas kernels, base_product(): pl.pallas_call(kernel, out_shape=jax.ShapeDtypeStruct((rows, width), jnp....  8.07 us
    all_to_all x1, starting transfers between devices, body(): lax.all_to_all(messages, store, split_axis=0, concat_axis=0, tiled=True)  7.4 us
    pallas_call x1, Pallas kernels, make_messages(): pl.pallas_call(send_kernel, out_shape=jax.ShapeDtypeStruct((groups, rows,...  4.6 us
    unnamed x54, local copies, waits for them, and re-layouts  3.17 us
  transfers between devices with their start and end apart: 31, of which 11 were waited for; matrix products, arithmetic and copies ran while one was open for 1% of the time, Pallas kernels for 6%

profile of v2, /device:TPU:0, one launch (start us, length us, event | category | flops | bytes accessed | tf_op | source)
XLA Modules:
  0.0 143.2 jit_solution(4831955212664086446)
XLA Ops:
  0.0 4.6 %make_messages.1 = bf16[16,272,256]{2,1,0:T(8,128)(2,1)} custom-call(s32[2,16]{1,0:T(2,128)} %bitcast.17, bf16[128,64,512]{2,1,0:T(8,128)(2,1)} %bitcast.14, bf16[2048,128]{1,0:T(8,128)(2,1)} %bitcast.15), custom_call_target="tpu_custom_call" | custom-call | tf_op jit(solution)/shard_map/make_messages/pallas_call | solution.py:66
  4.6 7.4 %all-to-all-start = ((bf16[16,272,256]{2,1,0:T(8,128)(2,1)}), bf16[16,272,256]{2,1,0:T(8,128)(2,1)S(1)}, u32[]{:S(2)}, u32[]{:S(2)}) async-start(bf16[16,272,256]{2,1,0:T(8,128)(2,1)} %make_messages.1), calls=%async_computation | async-start | bytes 4456448 | tf_op jit(solution)/shard_map/all_to_all | solution.py:251
  12.1 0.0 copy-start.2
  12.1 2.9 %collective-permute-start.1 = (bf16[256,512]{1,0:T(8,128)(2,1)S(1)}, bf16[256,512]{1,0:T(8,128)(2,1)S(1)}, u32[]{:S(2)}, u32[]{:S(2)}) collective-permute-start(bf16[256,512]{1,0:T(8,128)(2,1)S(1)} %get-tuple-element.6.refs_1_), channel_id=1, source_target_pairs={{0,8},{4,12},{8,0},{12,4},{1,9},{5,13},{9,1},{13,5},{2,10},{6,14},... | collective-permute-start | bytes 786440 | tf_op jit(solution)/shard_map/ppermute | solution.py:214
  15.0 1.5 %collective-permute-start = (bf16[256,512]{1,0:T(8,128)(2,1)S(1)}, bf16[256,512]{1,0:T(8,128)(2,1)S(1)}, u32[]{:S(2)}, u32[]{:S(2)}) collective-permute-start(bf16[256,512]{1,0:T(8,128)(2,1)S(1)} %get-tuple-element.6.refs_1_), channel_id=1, source_target_pairs={{0,4},{4,0},{8,12},{12,8},{1,5},{5,1},{9,13},{13,9},{2,6},{6,2},{1... | collective-permute-start | bytes 786440 | tf_op jit(solution)/shard_map/ppermute | solution.py:214
  16.5 1.5 %collective-permute-start.3 = (bf16[256,512]{1,0:T(8,128)(2,1)S(1)}, bf16[256,512]{1,0:T(8,128)(2,1)S(1)}, u32[]{:S(2)}, u32[]{:S(2)}) collective-permute-start(bf16[256,512]{1,0:T(8,128)(2,1)S(1)} %get-tuple-element.6.refs_1_), channel_id=1, source_target_pairs={{0,2},{2,0},{1,3},{3,1},{4,6},{6,4},{5,7},{7,5},{8,10},{10,8},{9,1... | collective-permute-start | bytes 786440 | tf_op jit(solution)/shard_map/ppermute | solution.py:214
  17.9 0.5 collective-permute-start.22
  18.4 56.8 %collective-permute-done.1.refs_3_ = bf16[256,512]{1,0:T(8,128)(2,1)S(1)} collective-permute-done((bf16[256,512]{1,0:T(8,128)(2,1)S(1)}, bf16[256,512]{1,0:T(8,128)(2,1)S(1)}, u32[]{:S(2)}, u32[]{:S(2)}) %collective-permute-start.1) | collective-permute-done | bytes 262176 | tf_op jit(solution)/shard_map/ppermute | solution.py:214
  75.2 0.0 collective-permute-start.2
  75.2 0.0 collective-permute-done.refs_2_
  75.2 1.5 %collective-permute-start.5 = (bf16[256,512]{1,0:T(8,128)(2,1)S(1)}, bf16[256,512]{1,0:T(8,128)(2,1)}, u32[]{:S(2)}, u32[]{:S(2)}) collective-permute-start(bf16[256,512]{1,0:T(8,128)(2,1)S(1)} %collective-permute-done.1.refs_3_), channel_id=1, source_target_pairs={{0,2},{2,0},{1,3},{3,1},{4,6},{6,4},{5,7},{7,5},{8,10},{10,8},{9,1... | collective-permute-start | bytes 786440 | tf_op jit(solution)/shard_map/ppermute | solution.py:214
  76.8 0.0 collective-permute-done.3.refs_5_
  76.8 0.6 collective-permute-start.4
  77.3 0.0 collective-permute-done.14.refs_17_
  77.3 1.5 %collective-permute-start.10 = (bf16[256,512]{1,0:T(8,128)(2,1)S(1)}, bf16[256,512]{1,0:T(8,128)(2,1)S(1)}, u32[]{:S(2)}, u32[]{:S(2)}) collective-permute-start(bf16[256,512]{1,0:T(8,128)(2,1)S(1)} %collective-permute-done.1.refs_3_), channel_id=1, source_target_pairs={{0,16},{16,0},{1,17},{17,1},{2,18},{18,2},{3,19},{19,3},{4,20},{20... | collective-permute-start | bytes 786440 | tf_op jit(solution)/shard_map/ppermute | solution.py:214
  78.8 0.5 collective-permute-start.8
  79.4 3.8 %collective-permute-done.2.refs_4_ = bf16[256,512]{1,0:T(8,128)(2,1)} collective-permute-done((bf16[256,512]{1,0:T(8,128)(2,1)S(1)}, bf16[256,512]{1,0:T(8,128)(2,1)}, u32[]{:S(2)}, u32[]{:S(2)}) %collective-permute-start.2) | collective-permute-done | bytes 262176 | tf_op jit(solution)/shard_map/ppermute | solution.py:214
  83.2 0.0 collective-permute-start.16
  83.2 1.5 %collective-permute-done.5.refs_7_ = bf16[256,512]{1,0:T(8,128)(2,1)} collective-permute-done((bf16[256,512]{1,0:T(8,128)(2,1)S(1)}, bf16[256,512]{1,0:T(8,128)(2,1)}, u32[]{:S(2)}, u32[]{:S(2)}) %collective-permute-start.5) | collective-permute-done | bytes 262176 | tf_op jit(solution)/shard_map/ppermute | solution.py:214
  84.6 1.5 %collective-permute-start.7 = (bf16[256,512]{1,0:T(8,128)(2,1)S(1)}, bf16[256,512]{1,0:T(8,128)(2,1)S(1)}, u32[]{:S(2)}, u32[]{:S(2)}) collective-permute-start(bf16[256,512]{1,0:T(8,128)(2,1)S(1)} %collective-permute-done.3.refs_5_), channel_id=1, source_target_pairs={{0,16},{16,0},{1,17},{17,1},{2,18},{18,2},{3,19},{19,3},{4,20},{20... | collective-permute-start | bytes 786440 | tf_op jit(solution)/shard_map/ppermute | solution.py:214
  86.1 2.8 %collective-permute-done.4.refs_6_ = bf16[256,512]{1,0:T(8,128)(2,1)} collective-permute-done((bf16[256,512]{1,0:T(8,128)(2,1)S(1)}, bf16[256,512]{1,0:T(8,128)(2,1)}, u32[]{:S(2)}, u32[]{:S(2)}) %collective-permute-start.4) | collective-permute-done | bytes 262176 | tf_op jit(solution)/shard_map/ppermute | solution.py:214
  88.9 0.0 collective-permute-start.15
  88.9 0.0 collective-permute-done.10.refs_13_
  88.9 0.5 collective-permute-start.18
  89.4 2.8 %collective-permute-done.8.refs_11_ = bf16[256,512]{1,0:T(8,128)(2,1)S(1)} collective-permute-done((bf16[256,512]{1,0:T(8,128)(2,1)S(1)}, bf16[256,512]{1,0:T(8,128)(2,1)S(1)}, u32[]{:S(2)}, u32[]{:S(2)}) %collective-permute-start.8) | collective-permute-done | bytes 262176 | tf_op jit(solution)/shard_map/ppermute | solution.py:214
  92.2 1.5 %collective-permute-start.6 = (bf16[256,512]{1,0:T(8,128)(2,1)}, bf16[256,512]{1,0:T(8,128)(2,1)S(1)}, u32[]{:S(2)}, u32[]{:S(2)}) collective-permute-start(bf16[256,512]{1,0:T(8,128)(2,1)} %collective-permute-done.2.refs_4_), channel_id=1, source_target_pairs={{0,2},{2,0},{1,3},{3,1},{4,6},{6,4},{5,7},{7,5},{8,10},{10,8},{9,1... | collective-permute-start | bytes 786440 | tf_op jit(solution)/shard_map/ppermute | solution.py:214
  93.7 0.0 collective-permute-done.16.refs_19_
  93.7 1.5 %collective-permute-start.12 = (bf16[256,512]{1,0:T(8,128)(2,1)}, bf16[256,512]{1,0:T(8,128)(2,1)}, u32[]{:S(2)}, u32[]{:S(2)}) collective-permute-start(bf16[256,512]{1,0:T(8,128)(2,1)} %collective-permute-done.2.refs_4_), channel_id=1, source_target_pairs={{0,16},{16,0},{1,17},{17,1},{2,18},{18,2},{3,19},{19,3},{4,20},{20... | collective-permute-start | bytes 786440 | tf_op jit(solution)/shard_map/ppermute | solution.py:214
  95.2 2.7 %collective-permute-done.7.refs_10_ = bf16[256,512]{1,0:T(8,128)(2,1)S(1)} collective-permute-done((bf16[256,512]{1,0:T(8,128)(2,1)S(1)}, bf16[256,512]{1,0:T(8,128)(2,1)S(1)}, u32[]{:S(2)}, u32[]{:S(2)}) %collective-permute-start.7) | collective-permute-done | bytes 262176 | tf_op jit(solution)/shard_map/ppermute | solution.py:214
  97.8 1.5 %collective-permute-start.11 = (bf16[256,512]{1,0:T(8,128)(2,1)}, bf16[256,512]{1,0:T(8,128)(2,1)}, u32[]{:S(2)}, u32[]{:S(2)}) collective-permute-start(bf16[256,512]{1,0:T(8,128)(2,1)} %collective-permute-done.5.refs_7_), channel_id=1, source_target_pairs={{0,16},{16,0},{1,17},{17,1},{2,18},{18,2},{3,19},{19,3},{4,20},{20... | collective-permute-start | bytes 786440 | tf_op jit(solution)/shard_map/ppermute | solution.py:214
  99.3 0.0 collective-permute-start.17
  99.3 0.0 collective-permute-done.18.refs_21_
  99.4 0.6 collective-permute-start.9
  100.0 0.1 copy-done.13
  100.1 0.1 copy-done.14
  100.1 0.7 copy-done.15
  100.8 0.4 collective-permute-start.20
  101.3 0.1 copy.10
  101.4 0.1 reduce
  101.5 2.0 %collective-permute-done.12.refs_15_ = bf16[256,512]{1,0:T(8,128)(2,1)} collective-permute-done((bf16[256,512]{1,0:T(8,128)(2,1)}, bf16[256,512]{1,0:T(8,128)(2,1)}, u32[]{:S(2)}, u32[]{:S(2)}) %collective-permute-start.12) | collective-permute-done | bytes 262176 | tf_op jit(solution)/shard_map/ppermute | solution.py:214
  103.6 5.6 %collective-permute-done.11.refs_14_ = bf16[256,512]{1,0:T(8,128)(2,1)} collective-permute-done((bf16[256,512]{1,0:T(8,128)(2,1)}, bf16[256,512]{1,0:T(8,128)(2,1)}, u32[]{:S(2)}, u32[]{:S(2)}) %collective-permute-start.11) | collective-permute-done | bytes 262176 | tf_op jit(solution)/shard_map/ppermute | solution.py:214
  109.2 0.0 collective-permute-start.26
  109.2 0.5 collective-permute-start.24
  109.7 3.1 %collective-permute-done.9.refs_12_ = bf16[256,512]{1,0:T(8,128)(2,1)} collective-permute-done((bf16[256,512]{1,0:T(8,128)(2,1)}, bf16[256,512]{1,0:T(8,128)(2,1)}, u32[]{:S(2)}, u32[]{:S(2)}) %collective-permute-start.9) | collective-permute-done | bytes 262176 | tf_op jit(solution)/shard_map/ppermute | solution.py:214
  112.8 1.5 %collective-permute-start.13 = (bf16[256,512]{1,0:T(8,128)(2,1)}, bf16[256,512]{1,0:T(8,128)(2,1)S(1)}, u32[]{:S(2)}, u32[]{:S(2)}) collective-permute-start(bf16[256,512]{1,0:T(8,128)(2,1)} %copy-done.15), channel_id=1, source_target_pairs={{0,16},{16,0},{1,17},{17,1},{2,18},{18,2},{3,19},{19,3},{4,20},{20... | collective-permute-start | bytes 786440 | tf_op jit(solution)/shard_map/ppermute | solution.py:214
  114.3 0.7 fusion.1
  115.0 0.1 select_reduce_fusion
  115.1 0.0 collective-permute-done.19.refs_22_
  115.1 0.3 collective-permute-start.21
  115.4 0.3 collective-permute-start.28
  115.7 0.2 collective-permute-start.27
  115.9 0.0 collective-permute-done.23.refs_26_
  115.9 0.3 collective-permute-start.25
  116.2 5.5 %collective-permute-done.13.refs_16_ = bf16[256,512]{1,0:T(8,128)(2,1)S(1)} collective-permute-done((bf16[256,512]{1,0:T(8,128)(2,1)}, bf16[256,512]{1,0:T(8,128)(2,1)S(1)}, u32[]{:S(2)}, u32[]{:S(2)}) %collective-permute-start.13) | collective-permute-done | bytes 262176 | tf_op jit(solution)/shard_map/ppermute | solution.py:214
  121.8 0.8 compare_convert_fusion.mask
  122.6 0.0 collective-permute-done.21.refs_24_
  122.7 0.6 collective-permute-done.29.refs_32_
  123.4 0.0 copy-done.22
  123.4 0.1 copy-done.23
  123.5 0.1 copy-done.24
  123.6 0.7 copy-done.25
  124.3 8.1 %base_product.1.base = f32[512,512]{1,0:T(8,128)} custom-call(bf16[512,8192]{1,0:T(8,128)(2,1)} %tokens.1, bf16[256,512]{1,0:T(8,128)(2,1)} %copy-done.2, bf16[256,512]{1,0:T(8,128)(2,1)} %copy-done.5, bf16[256,512]{1,0:T(8,128)(2,1)} %copy-done.4, bf16[256,512]{1,0:T(8,128)(2,1)} %collective-permute-done.2.refs_4_, bf16[256,512]{1,0:T(8,128)(2,1)} %copy-done.6, ...), custom_call_target="tpu_custom_call" | custom-call | flops 4294967296 | bytes 17825792 | tf_op jit(solution)/shard_map/base_product/pallas_call | solution.py:120
  132.4 1.4 copy-done
  133.8 9.4 %adapt.1 = bf16[512,512]{1,0:T(8,128)(2,1)} custom-call(bf16[512,8192]{1,0:T(8,128)(2,1)} %tokens.1, bf16[16,272,256]{2,1,0:T(8,128)(2,1)} %copy-done, f32[512,128]{1,0:T(8,128)} %compare_convert_fusion.mask, f32[512,512]{1,0:T(8,128)} %base_product.1.base), custom_call_target="tpu_custom_call" | custom-call | flops 1073741824 | bytes 12189696 | tf_op jit(solution)/shard_map/adapt/pallas_call | solution.py:185
  (63 shorter events, 0.2 us)
Async XLA Ops:
  0.0 12.0 %copy-start.3 = (bf16[512,512]{1,0:T(8,128)(2,1)S(1)}, bf16[512,512]{1,0:T(8,128)(2,1)}, u32[]{:S(2)}) copy-start(bf16[512,512]{1,0:T(8,128)(2,1)} %param.8) | copy-start | bytes 1572868
  0.0 101.3 %copy-start.26 = (s32[1,16]{1,0:T(1,128)S(1)}, s32[1,16]{1,0:T(1,128)}, u32[]{:S(2)}) copy-start(s32[1,16]{1,0:T(1,128)} %param.11) | copy-start | bytes 196
  4.6 127.7 %all-to-all-start = ((bf16[16,272,256]{2,1,0:T(8,128)(2,1)}), bf16[16,272,256]{2,1,0:T(8,128)(2,1)S(1)}, u32[]{:S(2)}, u32[]{:S(2)}) async-start(bf16[16,272,256]{2,1,0:T(8,128)(2,1)} %make_messages.1), calls=%async_computation | async-start | bytes 4456448 | tf_op jit(solution)/shard_map/all_to_all | solution.py:251
  12.1 111.2 %copy-start.1 = (bf16[256,512]{1,0:T(8,128)(2,1)}, bf16[256,512]{1,0:T(8,128)(2,1)S(1)}, u32[]{:S(2)}) copy-start(bf16[256,512]{1,0:T(8,128)(2,1)S(1)} %get-tuple-element.5.refs_9_) | copy-start | bytes 786436
  12.1 111.2 %copy-start.2 = (bf16[256,512]{1,0:T(8,128)(2,1)}, bf16[256,512]{1,0:T(8,128)(2,1)S(1)}, u32[]{:S(2)}) copy-start(bf16[256,512]{1,0:T(8,128)(2,1)S(1)} %get-tuple-element.6.refs_1_) | copy-start | bytes 786436
  12.1 63.1 %collective-permute-start.1 = (bf16[256,512]{1,0:T(8,128)(2,1)S(1)}, bf16[256,512]{1,0:T(8,128)(2,1)S(1)}, u32[]{:S(2)}, u32[]{:S(2)}) collective-permute-start(bf16[256,512]{1,0:T(8,128)(2,1)S(1)} %get-tuple-element.6.refs_1_), channel_id=1, source_target_pairs={{0,8},{4,12},{8,0},{12,4},{1,9},{5,13},{9,1},{13,5},{2,10},{6,14},... | collective-permute-start | bytes 786440 | tf_op jit(solution)/shard_map/ppermute | solution.py:214
  15.0 60.2 %collective-permute-start = (bf16[256,512]{1,0:T(8,128)(2,1)S(1)}, bf16[256,512]{1,0:T(8,128)(2,1)S(1)}, u32[]{:S(2)}, u32[]{:S(2)}) collective-permute-start(bf16[256,512]{1,0:T(8,128)(2,1)S(1)} %get-tuple-element.6.refs_1_), channel_id=1, source_target_pairs={{0,4},{4,0},{8,12},{12,8},{1,5},{5,1},{9,13},{13,9},{2,6},{6,2},{1... | collective-permute-start | bytes 786440 | tf_op jit(solution)/shard_map/ppermute | solution.py:214
  16.5 60.3 %collective-permute-start.3 = (bf16[256,512]{1,0:T(8,128)(2,1)S(1)}, bf16[256,512]{1,0:T(8,128)(2,1)S(1)}, u32[]{:S(2)}, u32[]{:S(2)}) collective-permute-start(bf16[256,512]{1,0:T(8,128)(2,1)S(1)} %get-tuple-element.6.refs_1_), channel_id=1, source_target_pairs={{0,2},{2,0},{1,3},{3,1},{4,6},{6,4},{5,7},{7,5},{8,10},{10,8},{9,1... | collective-permute-start | bytes 786440 | tf_op jit(solution)/shard_map/ppermute | solution.py:214
  17.9 59.4 %collective-permute-start.14 = (bf16[256,512]{1,0:T(8,128)(2,1)S(1)}, bf16[256,512]{1,0:T(8,128)(2,1)S(1)}, u32[]{:S(2)}, u32[]{:S(2)}) collective-permute-start(bf16[256,512]{1,0:T(8,128)(2,1)S(1)} %get-tuple-element.6.refs_1_), channel_id=1, source_target_pairs={{0,1},{1,0},{2,3},{3,2},{4,5},{5,4},{6,7},{7,6},{8,9},{9,8},{10,11... | collective-permute-start | bytes 786440 | tf_op jit(solution)/shard_map/ppermute | solution.py:214
  17.9 60.9 %collective-permute-start.22 = (bf16[256,512]{1,0:T(8,128)(2,1)S(1)}, bf16[256,512]{1,0:T(8,128)(2,1)S(1)}, u32[]{:S(2)}, u32[]{:S(2)}) collective-permute-start(bf16[256,512]{1,0:T(8,128)(2,1)S(1)} %get-tuple-element.5.refs_9_), channel_id=1, source_target_pairs={{0,1},{1,0},{2,3},{3,2},{4,5},{5,4},{6,7},{7,6},{8,9},{9,8},{10,11... | collective-permute-start | bytes 786440 | tf_op jit(solution)/shard_map/ppermute | solution.py:214
  75.2 48.1 %copy-start.4 = (bf16[256,512]{1,0:T(8,128)(2,1)}, bf16[256,512]{1,0:T(8,128)(2,1)S(1)}, u32[]{:S(2)}) copy-start(bf16[256,512]{1,0:T(8,128)(2,1)S(1)} %collective-permute-done.1.refs_3_) | copy-start | bytes 786436
  75.2 8.0 %collective-permute-start.2 = (bf16[256,512]{1,0:T(8,128)(2,1)S(1)}, bf16[256,512]{1,0:T(8,128)(2,1)}, u32[]{:S(2)}, u32[]{:S(2)}) collective-permute-start(bf16[256,512]{1,0:T(8,128)(2,1)S(1)} %collective-permute-done.1.refs_3_), channel_id=1, source_target_pairs={{0,4},{4,0},{8,12},{12,8},{1,5},{5,1},{9,13},{13,9},{2,6},{6,2},{1... | collective-permute-start | bytes 786440 | tf_op jit(solution)/shard_map/ppermute | solution.py:214
  75.2 48.1 %copy-start.5 = (bf16[256,512]{1,0:T(8,128)(2,1)}, bf16[256,512]{1,0:T(8,128)(2,1)S(1)}, u32[]{:S(2)}) copy-start(bf16[256,512]{1,0:T(8,128)(2,1)S(1)} %collective-permute-done.refs_2_) | copy-start | bytes 786436
  75.2 9.4 %collective-permute-start.5 = (bf16[256,512]{1,0:T(8,128)(2,1)S(1)}, bf16[256,512]{1,0:T(8,128)(2,1)}, u32[]{:S(2)}, u32[]{:S(2)}) collective-permute-start(bf16[256,512]{1,0:T(8,128)(2,1)S(1)} %collective-permute-done.1.refs_3_), channel_id=1, source_target_pairs={{0,2},{2,0},{1,3},{3,1},{4,6},{6,4},{5,7},{7,5},{8,10},{10,8},{9,1... | collective-permute-start | bytes 786440 | tf_op jit(solution)/shard_map/ppermute | solution.py:214
  76.8 46.6 %copy-start.6 = (bf16[256,512]{1,0:T(8,128)(2,1)}, bf16[256,512]{1,0:T(8,128)(2,1)S(1)}, u32[]{:S(2)}) copy-start(bf16[256,512]{1,0:T(8,128)(2,1)S(1)} %collective-permute-done.3.refs_5_) | copy-start | bytes 786436
  76.8 12.1 %collective-permute-start.4 = (bf16[256,512]{1,0:T(8,128)(2,1)S(1)}, bf16[256,512]{1,0:T(8,128)(2,1)}, u32[]{:S(2)}, u32[]{:S(2)}) collective-permute-start(bf16[256,512]{1,0:T(8,128)(2,1)S(1)} %collective-permute-done.refs_2_), channel_id=1, source_target_pairs={{0,2},{2,0},{1,3},{3,1},{4,6},{6,4},{5,7},{7,5},{8,10},{10,8},{9,1... | collective-permute-start | bytes 786440 | tf_op jit(solution)/shard_map/ppermute | solution.py:214
  77.3 22.0 %copy-start.7 = (bf16[256,512]{1,0:T(8,128)(2,1)}, bf16[256,512]{1,0:T(8,128)(2,1)S(1)}, u32[]{:S(2)}) copy-start(bf16[256,512]{1,0:T(8,128)(2,1)S(1)} %collective-permute-done.14.refs_17_) | copy-start | bytes 786436
  77.3 11.5 %collective-permute-start.10 = (bf16[256,512]{1,0:T(8,128)(2,1)S(1)}, bf16[256,512]{1,0:T(8,128)(2,1)S(1)}, u32[]{:S(2)}, u32[]{:S(2)}) collective-permute-start(bf16[256,512]{1,0:T(8,128)(2,1)S(1)} %collective-permute-done.1.refs_3_), channel_id=1, source_target_pairs={{0,16},{16,0},{1,17},{17,1},{2,18},{18,2},{3,19},{19,3},{4,20},{20... | collective-permute-start | bytes 786440 | tf_op jit(solution)/shard_map/ppermute | solution.py:214
  78.8 21.1 %copy-start.8 = (bf16[256,512]{1,0:T(8,128)(2,1)}, bf16[256,512]{1,0:T(8,128)(2,1)S(1)}, u32[]{:S(2)}) copy-start(bf16[256,512]{1,0:T(8,128)(2,1)S(1)} %collective-permute-done.22.refs_25_) | copy-start | bytes 786436
  78.8 13.4 %collective-permute-start.8 = (bf16[256,512]{1,0:T(8,128)(2,1)S(1)}, bf16[256,512]{1,0:T(8,128)(2,1)S(1)}, u32[]{:S(2)}, u32[]{:S(2)}) collective-permute-start(bf16[256,512]{1,0:T(8,128)(2,1)S(1)} %collective-permute-done.refs_2_), channel_id=1, source_target_pairs={{0,16},{16,0},{1,17},{17,1},{2,18},{18,2},{3,19},{19,3},{4,20},{20... | collective-permute-start | bytes 786440 | tf_op jit(solution)/shard_map/ppermute | solution.py:214
  83.2 10.5 %collective-permute-start.16 = (bf16[256,512]{1,0:T(8,128)(2,1)S(1)}, bf16[256,512]{1,0:T(8,128)(2,1)S(1)}, u32[]{:S(2)}, u32[]{:S(2)}) collective-permute-start(bf16[256,512]{1,0:T(8,128)(2,1)S(1)} %collective-permute-done.1.refs_3_), channel_id=1, source_target_pairs={{0,1},{1,0},{2,3},{3,2},{4,5},{5,4},{6,7},{7,6},{8,9},{9,8},{10,11... | collective-permute-start | bytes 786440 | tf_op jit(solution)/shard_map/ppermute | solution.py:214
  84.6 13.2 %collective-permute-start.7 = (bf16[256,512]{1,0:T(8,128)(2,1)S(1)}, bf16[256,512]{1,0:T(8,128)(2,1)S(1)}, u32[]{:S(2)}, u32[]{:S(2)}) collective-permute-start(bf16[256,512]{1,0:T(8,128)(2,1)S(1)} %collective-permute-done.3.refs_5_), channel_id=1, source_target_pairs={{0,16},{16,0},{1,17},{17,1},{2,18},{18,2},{3,19},{19,3},{4,20},{20... | collective-permute-start | bytes 786440 | tf_op jit(solution)/shard_map/ppermute | solution.py:214
  88.9 10.4 %collective-permute-start.15 = (bf16[256,512]{1,0:T(8,128)(2,1)S(1)}, bf16[256,512]{1,0:T(8,128)(2,1)S(1)}, u32[]{:S(2)}, u32[]{:S(2)}) collective-permute-start(bf16[256,512]{1,0:T(8,128)(2,1)S(1)} %collective-permute-done.refs_2_), channel_id=1, source_target_pairs={{0,1},{1,0},{2,3},{3,2},{4,5},{5,4},{6,7},{7,6},{8,9},{9,8},{10,11... | collective-permute-start | bytes 786440 | tf_op jit(solution)/shard_map/ppermute | solution.py:214
  88.9 11.1 %copy-start.9 = (bf16[256,512]{1,0:T(8,128)(2,1)}, bf16[256,512]{1,0:T(8,128)(2,1)S(1)}, u32[]{:S(2)}) copy-start(bf16[256,512]{1,0:T(8,128)(2,1)S(1)} %collective-permute-done.10.refs_13_) | copy-start | bytes 786436
  88.9 10.4 %collective-permute-start.18 = (bf16[256,512]{1,0:T(8,128)(2,1)S(1)}, bf16[256,512]{1,0:T(8,128)(2,1)S(1)}, u32[]{:S(2)}, u32[]{:S(2)}) collective-permute-start(bf16[256,512]{1,0:T(8,128)(2,1)S(1)} %collective-permute-done.3.refs_5_), channel_id=1, source_target_pairs={{0,1},{1,0},{2,3},{3,2},{4,5},{5,4},{6,7},{7,6},{8,9},{9,8},{10,11... | collective-permute-start | bytes 786440 | tf_op jit(solution)/shard_map/ppermute | solution.py:214
  92.2 7.8 %copy-start.10 = (bf16[256,512]{1,0:T(8,128)(2,1)}, bf16[256,512]{1,0:T(8,128)(2,1)S(1)}, u32[]{:S(2)}) copy-start(bf16[256,512]{1,0:T(8,128)(2,1)S(1)} %collective-permute-done.8.refs_11_) | copy-start | bytes 786436
  92.2 7.8 %collective-permute-start.6 = (bf16[256,512]{1,0:T(8,128)(2,1)}, bf16[256,512]{1,0:T(8,128)(2,1)S(1)}, u32[]{:S(2)}, u32[]{:S(2)}) collective-permute-start(bf16[256,512]{1,0:T(8,128)(2,1)} %collective-permute-done.2.refs_4_), channel_id=1, source_target_pairs={{0,2},{2,0},{1,3},{3,1},{4,6},{6,4},{5,7},{7,5},{8,10},{10,8},{9,1... | collective-permute-start | bytes 786440 | tf_op jit(solution)/shard_map/ppermute | solution.py:214
  93.7 6.3 %copy-start.11 = (bf16[256,512]{1,0:T(8,128)(2,1)}, bf16[256,512]{1,0:T(8,128)(2,1)S(1)}, u32[]{:S(2)}) copy-start(bf16[256,512]{1,0:T(8,128)(2,1)S(1)} %collective-permute-done.16.refs_19_) | copy-start | bytes 786436
  93.7 9.9 %collective-permute-start.12 = (bf16[256,512]{1,0:T(8,128)(2,1)}, bf16[256,512]{1,0:T(8,128)(2,1)}, u32[]{:S(2)}, u32[]{:S(2)}) collective-permute-start(bf16[256,512]{1,0:T(8,128)(2,1)} %collective-permute-done.2.refs_4_), channel_id=1, source_target_pairs={{0,16},{16,0},{1,17},{17,1},{2,18},{18,2},{3,19},{19,3},{4,20},{20... | collective-permute-start | bytes 786440 | tf_op jit(solution)/shard_map/ppermute | solution.py:214
  97.8 2.2 %copy-start.12 = (bf16[256,512]{1,0:T(8,128)(2,1)}, bf16[256,512]{1,0:T(8,128)(2,1)S(1)}, u32[]{:S(2)}) copy-start(bf16[256,512]{1,0:T(8,128)(2,1)S(1)} %collective-permute-done.7.refs_10_) | copy-start | bytes 786436
  97.8 11.3 %collective-permute-start.11 = (bf16[256,512]{1,0:T(8,128)(2,1)}, bf16[256,512]{1,0:T(8,128)(2,1)}, u32[]{:S(2)}, u32[]{:S(2)}) collective-permute-start(bf16[256,512]{1,0:T(8,128)(2,1)} %collective-permute-done.5.refs_7_), channel_id=1, source_target_pairs={{0,16},{16,0},{1,17},{17,1},{2,18},{18,2},{3,19},{19,3},{4,20},{20... | collective-permute-start | bytes 786440 | tf_op jit(solution)/shard_map/ppermute | solution.py:214
  99.3 0.7 copy-start.13
  99.3 9.8 %collective-permute-start.17 = (bf16[256,512]{1,0:T(8,128)(2,1)}, bf16[256,512]{1,0:T(8,128)(2,1)}, u32[]{:S(2)}, u32[]{:S(2)}) collective-permute-start(bf16[256,512]{1,0:T(8,128)(2,1)} %collective-permute-done.2.refs_4_), channel_id=1, source_target_pairs={{0,1},{1,0},{2,3},{3,2},{4,5},{5,4},{6,7},{7,6},{8,9},{9,8},{10,11... | collective-permute-start | bytes 786440 | tf_op jit(solution)/shard_map/ppermute | solution.py:214
  99.3 0.8 copy-start.14
  99.4 13.5 %collective-permute-start.9 = (bf16[256,512]{1,0:T(8,128)(2,1)}, bf16[256,512]{1,0:T(8,128)(2,1)}, u32[]{:S(2)}, u32[]{:S(2)}) collective-permute-start(bf16[256,512]{1,0:T(8,128)(2,1)} %collective-permute-done.4.refs_6_), channel_id=1, source_target_pairs={{0,16},{16,0},{1,17},{17,1},{2,18},{18,2},{3,19},{19,3},{4,20},{20... | collective-permute-start | bytes 786440 | tf_op jit(solution)/shard_map/ppermute | solution.py:214
  100.1 0.7 copy-start.15
  100.8 12.0 %collective-permute-start.20 = (bf16[256,512]{1,0:T(8,128)(2,1)}, bf16[256,512]{1,0:T(8,128)(2,1)}, u32[]{:S(2)}, u32[]{:S(2)}) collective-permute-start(bf16[256,512]{1,0:T(8,128)(2,1)} %collective-permute-done.5.refs_7_), channel_id=1, source_target_pairs={{0,1},{1,0},{2,3},{3,2},{4,5},{5,4},{6,7},{7,6},{8,9},{9,8},{10,11... | collective-permute-start | bytes 786440 | tf_op jit(solution)/shard_map/ppermute | solution.py:214
  103.5 11.6 %collective-permute-start.19 = (bf16[256,512]{1,0:T(8,128)(2,1)}, bf16[256,512]{1,0:T(8,128)(2,1)S(1)}, u32[]{:S(2)}, u32[]{:S(2)}) collective-permute-start(bf16[256,512]{1,0:T(8,128)(2,1)} %collective-permute-done.4.refs_6_), channel_id=1, source_target_pairs={{0,1},{1,0},{2,3},{3,2},{4,5},{5,4},{6,7},{7,6},{8,9},{9,8},{10,11... | collective-permute-start | bytes 786440 | tf_op jit(solution)/shard_map/ppermute | solution.py:214
  109.2 6.3 %collective-permute-start.26 = (bf16[256,512]{1,0:T(8,128)(2,1)}, bf16[256,512]{1,0:T(8,128)(2,1)S(1)}, u32[]{:S(2)}, u32[]{:S(2)}) collective-permute-start(bf16[256,512]{1,0:T(8,128)(2,1)} %copy-done.9), channel_id=1, source_target_pairs={{0,1},{1,0},{2,3},{3,2},{4,5},{5,4},{6,7},{7,6},{8,9},{9,8},{10,11... | collective-permute-start | bytes 786440 | tf_op jit(solution)/shard_map/ppermute | solution.py:214
  109.2 6.5 %collective-permute-start.24 = (bf16[256,512]{1,0:T(8,128)(2,1)}, bf16[256,512]{1,0:T(8,128)(2,1)S(1)}, u32[]{:S(2)}, u32[]{:S(2)}) collective-permute-start(bf16[256,512]{1,0:T(8,128)(2,1)} %copy-done.10), channel_id=1, source_target_pairs={{0,1},{1,0},{2,3},{3,2},{4,5},{5,4},{6,7},{7,6},{8,9},{9,8},{10,11... | collective-permute-start | bytes 786440 | tf_op jit(solution)/shard_map/ppermute | solution.py:214
  112.8 3.1 %collective-permute-start.23 = (bf16[256,512]{1,0:T(8,128)(2,1)}, bf16[256,512]{1,0:T(8,128)(2,1)S(1)}, u32[]{:S(2)}, u32[]{:S(2)}) collective-permute-start(bf16[256,512]{1,0:T(8,128)(2,1)} %copy-done.12), channel_id=1, source_target_pairs={{0,1},{1,0},{2,3},{3,2},{4,5},{5,4},{6,7},{7,6},{8,9},{9,8},{10,11... | collective-permute-start | bytes 786440 | tf_op jit(solution)/shard_map/ppermute | solution.py:214
  112.8 8.9 %collective-permute-start.13 = (bf16[256,512]{1,0:T(8,128)(2,1)}, bf16[256,512]{1,0:T(8,128)(2,1)S(1)}, u32[]{:S(2)}, u32[]{:S(2)}) collective-permute-start(bf16[256,512]{1,0:T(8,128)(2,1)} %copy-done.15), channel_id=1, source_target_pairs={{0,16},{16,0},{1,17},{17,1},{2,18},{18,2},{3,19},{19,3},{4,20},{20... | collective-permute-start | bytes 786440 | tf_op jit(solution)/shard_map/ppermute | solution.py:214
  115.1 8.2 %copy-start.16 = (bf16[256,512]{1,0:T(8,128)(2,1)}, bf16[256,512]{1,0:T(8,128)(2,1)S(1)}, u32[]{:S(2)}) copy-start(bf16[256,512]{1,0:T(8,128)(2,1)S(1)} %collective-permute-done.19.refs_22_) | copy-start | bytes 786436
  115.1 7.5 %collective-permute-start.21 = (bf16[256,512]{1,0:T(8,128)(2,1)}, bf16[256,512]{1,0:T(8,128)(2,1)S(1)}, u32[]{:S(2)}, u32[]{:S(2)}) collective-permute-start(bf16[256,512]{1,0:T(8,128)(2,1)} %copy-done.15), channel_id=1, source_target_pairs={{0,1},{1,0},{2,3},{3,2},{4,5},{5,4},{6,7},{7,6},{8,9},{9,8},{10,11... | collective-permute-start | bytes 786440 | tf_op jit(solution)/shard_map/ppermute | solution.py:214
  115.4 7.9 %copy-start.17 = (bf16[256,512]{1,0:T(8,128)(2,1)}, bf16[256,512]{1,0:T(8,128)(2,1)S(1)}, u32[]{:S(2)}) copy-start(bf16[256,512]{1,0:T(8,128)(2,1)S(1)} %collective-permute-done.26.refs_29_) | copy-start | bytes 786436
  115.4 7.2 %collective-permute-start.28 = (bf16[256,512]{1,0:T(8,128)(2,1)}, bf16[256,512]{1,0:T(8,128)(2,1)S(1)}, u32[]{:S(2)}, u32[]{:S(2)}) collective-permute-start(bf16[256,512]{1,0:T(8,128)(2,1)} %collective-permute-done.12.refs_15_), channel_id=1, source_target_pairs={{0,1},{1,0},{2,3},{3,2},{4,5},{5,4},{6,7},{7,6},{8,9},{9,8},{10,11... | collective-permute-start | bytes 786440 | tf_op jit(solution)/shard_map/ppermute | solution.py:214
  115.7 7.6 %copy-start.18 = (bf16[256,512]{1,0:T(8,128)(2,1)}, bf16[256,512]{1,0:T(8,128)(2,1)S(1)}, u32[]{:S(2)}) copy-start(bf16[256,512]{1,0:T(8,128)(2,1)S(1)} %collective-permute-done.24.refs_27_) | copy-start | bytes 786436
  115.7 6.9 %collective-permute-start.27 = (bf16[256,512]{1,0:T(8,128)(2,1)}, bf16[256,512]{1,0:T(8,128)(2,1)S(1)}, u32[]{:S(2)}, u32[]{:S(2)}) collective-permute-start(bf16[256,512]{1,0:T(8,128)(2,1)} %collective-permute-done.11.refs_14_), channel_id=1, source_target_pairs={{0,1},{1,0},{2,3},{3,2},{4,5},{5,4},{6,7},{7,6},{8,9},{9,8},{10,11... | collective-permute-start | bytes 786440 | tf_op jit(solution)/shard_map/ppermute | solution.py:214
  115.9 7.4 %copy-start.19 = (bf16[256,512]{1,0:T(8,128)(2,1)}, bf16[256,512]{1,0:T(8,128)(2,1)S(1)}, u32[]{:S(2)}) copy-start(bf16[256,512]{1,0:T(8,128)(2,1)S(1)} %collective-permute-done.23.refs_26_) | copy-start | bytes 786436
  115.9 6.7 %collective-permute-start.25 = (bf16[256,512]{1,0:T(8,128)(2,1)}, bf16[256,512]{1,0:T(8,128)(2,1)S(1)}, u32[]{:S(2)}, u32[]{:S(2)}) collective-permute-start(bf16[256,512]{1,0:T(8,128)(2,1)} %collective-permute-done.9.refs_12_), channel_id=1, source_target_pairs={{0,1},{1,0},{2,3},{3,2},{4,5},{5,4},{6,7},{7,6},{8,9},{9,8},{10,11... | collective-permute-start | bytes 786440 | tf_op jit(solution)/shard_map/ppermute | solution.py:214
  121.8 1.6 %copy-start.20 = (bf16[256,512]{1,0:T(8,128)(2,1)}, bf16[256,512]{1,0:T(8,128)(2,1)S(1)}, u32[]{:S(2)}) copy-start(bf16[256,512]{1,0:T(8,128)(2,1)S(1)} %collective-permute-done.13.refs_16_) | copy-start | bytes 786436
  121.8 1.5 %collective-permute-start.29 = (bf16[256,512]{1,0:T(8,128)(2,1)S(1)}, bf16[256,512]{1,0:T(8,128)(2,1)S(1)}, u32[]{:S(2)}, u32[]{:S(2)}) collective-permute-start(bf16[256,512]{1,0:T(8,128)(2,1)S(1)} %collective-permute-done.13.refs_16_), channel_id=1, source_target_pairs={{0,1},{1,0},{2,3},{3,2},{4,5},{5,4},{6,7},{7,6},{8,9},{9,8},{10,11... | collective-permute-start | bytes 786440 | tf_op jit(solution)/shard_map/ppermute | solution.py:214
  122.6 0.8 copy-start.21
  122.6 0.8 copy-start.22
  122.6 0.9 copy-start.23
  122.7 0.9 copy-start.24
  123.6 0.7 copy-start.25
  132.4 1.4 copy-start

commit v3 on v2

--- a/solution.py
+++ b/solution.py
@@ -9,6 +9,7 @@
 from jax.sharding import PartitionSpec as P
 
 HALF = 256
+DEEP = 4
 MIB = 1024 * 1024
 AXES = ("parts", "line", "plane", "core")
 
@@ -97,21 +98,21 @@
         for n, mask in enumerate(masks):
             x, z, y, core = [i ^ bit for i, bit in zip(place, mask)]
             column = pl.multiple_of((((z * 2 + y) * 2 + core) * 2 + x) * HALF, HALF)
+            slot, inner = n // DEEP, pl.ds(n % DEEP * HALF, HALF)
             pair = (
                 pltpu.make_async_copy(
-                    tokens_ref.at[:, pl.ds(column, HALF)], left.at[n], left_sems.at[n]
+                    tokens_ref.at[:, pl.ds(column, HALF)], left.at[slot, :, inner], left_sems.at[n]
                 ),
-                pltpu.make_async_copy(parts[n], right.at[n], right_sems.at[n]),
+                pltpu.make_async_copy(parts[n], right.at[slot, inner, :], right_sems.at[n]),
             )
             for copy in pair:
                 copy.start()
             copies.append(pair)
-        for n in range(0, count, 2):
-            for pair in copies[n : n + 2]:
+        for n in range(count // DEEP):
+            for pair in copies[n * DEEP : (n + 1) * DEEP]:
                 for copy in pair:
                     copy.wait()
             total = jnp.dot(left[n], right[n], preferred_element_type=jnp.float32)
-            total += jnp.dot(left[n + 1], right[n + 1], preferred_element_type=jnp.float32)
             if n == 0:
                 out[...] = total
             else:
@@ -123,8 +124,8 @@
         in_specs=[pl.BlockSpec(memory_space=pl.ANY)] * (1 + count),
         out_specs=pl.BlockSpec(memory_space=pltpu.VMEM),
         scratch_shapes=[
-            pltpu.VMEM((count, rows, HALF), jnp.bfloat16),
-            pltpu.VMEM((count, HALF, width), jnp.bfloat16),
+            pltpu.VMEM((count // DEEP, rows, DEEP * HALF), jnp.bfloat16),
+            pltpu.VMEM((count // DEEP, DEEP * HALF, width), jnp.bfloat16),
             pltpu.SemaphoreType.DMA((count,)),
             pltpu.SemaphoreType.DMA((count,)),
         ],
@@ -138,45 +139,54 @@
     )(tokens, *[block for _, block in blocks])
 
 
-def adapt_kernel(halves, tokens, messages, mask, base, out, held, sems):
+def adapt_kernel(halves, tokens, messages, mask, base, out, held, got, kept, start, wide, *sems):
     groups, length = messages.shape[:2]
     pair = mask.shape[1]
-    width = out.shape[1]
     depth = halves * HALF
+    left_sems, right_sems, base_sem, mask_sem = sems
     copies = []
     for source in range(groups):
-        copy = pltpu.make_async_copy(
-            tokens.at[:, pl.ds(source * depth, depth)], held.at[source], sems.at[source]
+        two = (
+            pltpu.make_async_copy(messages.at[source], got.at[source], right_sems.at[source]),
+            pltpu.make_async_copy(
+                tokens.at[:, pl.ds(source * depth, depth)], held.at[source], left_sems.at[source]
+            ),
         )
+        for copy in two:
+            copy.start()
+        copies.append(two)
+    last = (
+        pltpu.make_async_copy(mask, kept, mask_sem),
+        pltpu.make_async_copy(base, start, base_sem),
+    )
+    for copy in last:
         copy.start()
-        copies.append(copy)
-
-    start = halves * pair
-    got = messages[:, start:, :].reshape(groups * (length - start), HALF)
-    value = lax.broadcasted_iota(jnp.int32, (width, got.shape[0]), 0)
-    row = lax.broadcasted_iota(jnp.int32, (width, got.shape[0]), 1)
-    wide = jnp.zeros((width, pair), jnp.float32)
-    for i in range(HALF // pair):
-        place = (value == row * (HALF // pair) + i).astype(jnp.float32).astype(jnp.bfloat16)
-        wide += jnp.dot(
-            place, got[:, i * pair : (i + 1) * pair], preferred_element_type=jnp.float32
-        )
-    wide = wide.astype(jnp.bfloat16)
 
     shrink = jnp.zeros(mask.shape, jnp.float32)
     for source in range(groups):
-        copies[source].wait()
+        for copy in copies[source]:
+            copy.wait()
         down = jnp.concatenate(
-            [messages[source, half * pair : (half + 1) * pair, :] for half in range(halves)], axis=1
+            [got[source, half * pair : (half + 1) * pair, :] for half in range(halves)], axis=1
         )
         shrink += lax.dot_general(
             held[source], down, (((1,), (1,)), ((), ())), preferred_element_type=jnp.float32
         )
-    picked = (shrink * mask[...]).astype(jnp.bfloat16)
+    ups = got[:, halves * pair :, :].astype(jnp.float32)
+    ups = ups.reshape(groups * (length - halves * pair), HALF)
+    step = HALF // pair
+    for i in range(step):
+        wide[pl.ds(i, ups.shape[0], stride=step), :] = ups[:, i * pair : (i + 1) * pair]
+    for copy in last:
+        copy.wait()
+    picked = (shrink * kept[...]).astype(jnp.bfloat16)
     delta = lax.dot_general(
-        picked, wide, (((1,), (1,)), ((), ())), preferred_element_type=jnp.float32
-    )
-    out[...] = (base[...] + delta).astype(out.dtype)
+        picked,
+        wide[...].astype(jnp.bfloat16),
+        (((1,), (1,)), ((), ())),
+        preferred_element_type=jnp.float32,
+    )
+    out[...] = (start[...] + delta).astype(out.dtype)
 
 
 def adapt(tokens, messages, mask, base, halves):
@@ -185,11 +195,18 @@
     return pl.pallas_call(
         functools.partial(adapt_kernel, halves),
         out_shape=jax.ShapeDtypeStruct((rows, width), jnp.bfloat16),
-        in_specs=[pl.BlockSpec(memory_space=pl.ANY)] + [pl.BlockSpec(memory_space=pltpu.VMEM)] * 3,
+        in_specs=[pl.BlockSpec(memory_space=pl.ANY)] * 4,
         out_specs=pl.BlockSpec(memory_space=pltpu.VMEM),
         scratch_shapes=[
             pltpu.VMEM((groups, rows, halves * HALF), jnp.bfloat16),
+            pltpu.VMEM(messages.shape, jnp.bfloat16),
+            pltpu.VMEM(mask.shape, jnp.float32),
+            pltpu.VMEM(base.shape, jnp.float32),
+            pltpu.VMEM((width, mask.shape[1]), jnp.float32),
             pltpu.SemaphoreType.DMA((groups,)),
+            pltpu.SemaphoreType.DMA((groups,)),
+            pltpu.SemaphoreType.DMA,
+            pltpu.SemaphoreType.DMA,
         ],
         compiler_params=pltpu.CompilerParams(vmem_limit_bytes=56 * MIB),
         cost_estimate=pl.CostEstimate(
@@ -199,6 +216,20 @@
         ),
         name="adapt",
     )(tokens, messages, mask, base)
+
+
+def after(value, *others):
+    def kernel(*refs):
+        pass
+
+    return pl.pallas_call(
+        kernel,
+        out_shape=jax.ShapeDtypeStruct(value.shape, value.dtype),
+        in_specs=[pl.BlockSpec(memory_space=pl.ANY)] * (1 + len(others)),
+        out_specs=pl.BlockSpec(memory_space=pl.ANY),
+        input_output_aliases={0: 0},
+        name="after",
+    )(value, *others)
 
 
 def row_slots(lengths, slots, rows):
@@ -230,7 +261,7 @@
             blocks[1, z, y, 0] = other if z == y == 0 else swap(source, "parts", 1)
     for (x, z, y, _), block in list(blocks.items()):
         blocks[x, z, y, 1] = swap(block, "core", 1)
-    return list(blocks.items())
+    return blocks
 
 
 def body(
@@ -248,13 +279,14 @@
         jnp.transpose(adapter_up, (1, 2, 0)).reshape(shard_width * rank, adapter_up.shape[0]),
         shard_width,
     )
+    blocks = gather_rows(base_weight)
+    messages = after(messages, blocks[0, 1, 0, 0])
     arrived = lax.all_to_all(messages, store, split_axis=0, concat_axis=0, tiled=True)
-    blocks = gather_rows(base_weight)
     slots = lax.dynamic_index_in_dim(request_slot, group, 0, keepdims=False)
     slot_of_row = row_slots(request_lengths[0], slots, tokens.shape[0])
     lane_slot = jnp.arange(choices * rank, dtype=jnp.int32)[None, :] // rank
     mask = (slot_of_row[:, None] == lane_slot).astype(jnp.float32)
-    base = base_product(tokens, blocks)
+    base = base_product(tokens, list(blocks.items()))
     return adapt(tokens, arrived, mask, base, depth // HALF)
 
 

time: 144 us -> 148 us (1.028)
  waiting for transfers between devices: 87.3 us -> 90.1 us
  local copies, waits for them, and re-layouts: 3.29 us -> 5.49 us
  Pallas kernels: 22.1 us -> 20.5 us
    ppermute x30, waiting for transfers between devices: 87.3 us -> 90.1 us  [swap(): return lax.ppermute(block, axis, [(i, i ^ bit) for i in range(size)])]
    pallas_call x1, Pallas kernels: 9.44 us -> 7.78 us  [adapt(): pl.pallas_call(functools.partial(adapt_kernel, halves), out_shape=jax.Sha...]
    ppermute x30, starting transfers between devices: 21 us -> 22.7 us  [swap(): return lax.ppermute(block, axis, [(i, i ^ bit) for i in range(size)])]
    unnamed x54 -> x56, local copies, waits for them, and re-layouts: 3.17 us -> 4.35 us
  transfers between devices with their start and end apart: 31 -> 31, of which waited for: 11 -> 11; matrix products, arithmetic and copies ran while one was open for 1% -> 1% of each run, Pallas kernels for 6% -> 9%
where the time goes in v3:
time: 148 us; the launch traced here: 147 us
  waiting for transfers between devices  90.1 us (61%)
  starting transfers between devices  28.9 us (20%)
  Pallas kernels  20.5 us (14%)
  local copies, waits for them, and re-layouts  5.49 us (4%)
  other arithmetic  1.76 us (1%)
    ppermute x30, waiting for transfers between devices, swap(): return lax.ppermute(block, axis, [(i, i ^ bit) for i in range(size)])  90.1 us
    ppermute x30, starting transfers between devices, swap(): return lax.ppermute(block, axis, [(i, i ^ bit) for i in range(size)])  22.7 us
    pallas_call x1, Pallas kernels, base_product(): pl.pallas_call(kernel, out_shape=jax.ShapeDtypeStruct((rows, width), jnp....  8.13 us
    pallas_call x1, Pallas kernels, adapt(): pl.pallas_call(functools.partial(adapt_kernel, halves), out_shape=jax.Sha...  7.78 us
    all_to_all x1, starting transfers between devices, body(): lax.all_to_all(messages, store, split_axis=0, concat_axis=0, tiled=True)  6.23 us
    pallas_call x1, Pallas kernels, make_messages(): pl.pallas_call(send_kernel, out_shape=jax.ShapeDtypeStruct((groups, rows,...  4.56 us
    unnamed x56, local copies, waits for them, and re-layouts  4.35 us
  transfers between devices with their start and end apart: 31, of which 11 were waited for; matrix products, arithmetic and copies ran while one was open for 1% of the time, Pallas kernels for 9%

profile of v3, /device:TPU:0, one launch (start us, length us, event | category | flops | bytes accessed | tf_op | source)
XLA Modules:
  0.0 147.1 jit_solution(2876592742597314136)
XLA Ops:
  0.0 1.1 constant_dynamic-slice_fusion
  1.1 3.1 %collective-permute-start = (bf16[256,512]{1,0:T(8,128)(2,1)S(1)}, bf16[256,512]{1,0:T(8,128)(2,1)S(1)}, u32[]{:S(2)}, u32[]{:S(2)}) collective-permute-start(bf16[256,512]{1,0:T(8,128)(2,1)S(1)} %get-tuple-element.6.refs_1_), channel_id=1, source_target_pairs={{0,4},{4,0},{8,12},{12,8},{1,5},{5,1},{9,13},{13,9},{2,6},{6,2},{1... | collective-permute-start | bytes 786440 | tf_op jit(solution)/shard_map/ppermute | solution.py:245
  4.2 4.6 %make_messages.1.refs_0_ = bf16[16,272,256]{2,1,0:T(8,128)(2,1)} custom-call(s32[2,16]{1,0:T(2,128)} %bitcast.17, bf16[128,64,512]{2,1,0:T(8,128)(2,1)} %bitcast.14, bf16[2048,128]{1,0:T(8,128)(2,1)} %bitcast.15), custom_call_target="tpu_custom_call" | custom-call | tf_op jit(solution)/shard_map/make_messages/pallas_call | solution.py:67
  8.7 1.7 %collective-permute-done.refs_1_.refs_2_ = bf16[256,512]{1,0:T(8,128)(2,1)S(1)} collective-permute-done((bf16[256,512]{1,0:T(8,128)(2,1)S(1)}, bf16[256,512]{1,0:T(8,128)(2,1)S(1)}, u32[]{:S(2)}, u32[]{:S(2)}) %collective-permute-start) | collective-permute-done | bytes 262176 | tf_op jit(solution)/shard_map/ppermute | solution.py:245
  10.5 0.7 copy-done.3
  11.2 6.2 %all-to-all-start = ((bf16[16,272,256]{2,1,0:T(8,128)(2,1)}), bf16[16,272,256]{2,1,0:T(8,128)(2,1)S(1)}, u32[]{:S(2)}, u32[]{:S(2)}) async-start(bf16[16,272,256]{2,1,0:T(8,128)(2,1)} %after.1), calls=%async_computation | async-start | bytes 4456448 | tf_op jit(solution)/shard_map/all_to_all | solution.py:284
  17.4 2.8 %collective-permute-start.1 = (bf16[256,512]{1,0:T(8,128)(2,1)S(1)}, bf16[256,512]{1,0:T(8,128)(2,1)S(1)}, u32[]{:S(2)}, u32[]{:S(2)}) collective-permute-start(bf16[256,512]{1,0:T(8,128)(2,1)S(1)} %get-tuple-element.6.refs_1_), channel_id=1, source_target_pairs={{0,8},{4,12},{8,0},{12,4},{1,9},{5,13},{9,1},{13,5},{2,10},{6,14},... | collective-permute-start | bytes 786440 | tf_op jit(solution)/shard_map/ppermute | solution.py:245
  20.3 1.5 collective-permute-start.3
  21.7 0.5 collective-permute-start.22
  22.2 58.4 %collective-permute-done.1.refs_3_ = bf16[256,512]{1,0:T(8,128)(2,1)S(1)} collective-permute-done((bf16[256,512]{1,0:T(8,128)(2,1)S(1)}, bf16[256,512]{1,0:T(8,128)(2,1)S(1)}, u32[]{:S(2)}, u32[]{:S(2)}) %collective-permute-start.1) | collective-permute-done | bytes 262176 | tf_op jit(solution)/shard_map/ppermute | solution.py:245
  80.6 0.0 collective-permute-start.2
  80.6 1.5 %collective-permute-start.4 = (bf16[256,512]{1,0:T(8,128)(2,1)S(1)}, bf16[256,512]{1,0:T(8,128)(2,1)}, u32[]{:S(2)}, u32[]{:S(2)}) collective-permute-start(bf16[256,512]{1,0:T(8,128)(2,1)S(1)} %copy-done.4), channel_id=1, source_target_pairs={{0,2},{2,0},{1,3},{3,1},{4,6},{6,4},{5,7},{7,5},{8,10},{10,8},{9,1... | collective-permute-start | bytes 786440 | tf_op jit(solution)/shard_map/ppermute | solution.py:245
  82.2 0.0 collective-permute-done.3.refs_5_
  82.2 0.6 collective-permute-start.5
  82.7 1.5 %collective-permute-start.8 = (bf16[256,512]{1,0:T(8,128)(2,1)S(1)}, bf16[256,512]{1,0:T(8,128)(2,1)S(1)}, u32[]{:S(2)}, u32[]{:S(2)}) collective-permute-start(bf16[256,512]{1,0:T(8,128)(2,1)S(1)} %copy-done.4), channel_id=1, source_target_pairs={{0,16},{16,0},{1,17},{17,1},{2,18},{18,2},{3,19},{19,3},{4,20},{20... | collective-permute-start | bytes 786440 | tf_op jit(solution)/shard_map/ppermute | solution.py:245
  84.2 0.0 collective-permute-done.22.refs_25_
  84.2 0.5 collective-permute-start.10
  84.8 3.8 %collective-permute-done.2.refs_4_ = bf16[256,512]{1,0:T(8,128)(2,1)} collective-permute-done((bf16[256,512]{1,0:T(8,128)(2,1)S(1)}, bf16[256,512]{1,0:T(8,128)(2,1)}, u32[]{:S(2)}, u32[]{:S(2)}) %collective-permute-start.2) | collective-permute-done | bytes 262176 | tf_op jit(solution)/shard_map/ppermute | solution.py:245
  88.6 1.4 collective-permute-done.4.refs_6_
  90.0 0.0 collective-permute-start.16
  90.0 4.2 %collective-permute-done.5.refs_7_ = bf16[256,512]{1,0:T(8,128)(2,1)} collective-permute-done((bf16[256,512]{1,0:T(8,128)(2,1)S(1)}, bf16[256,512]{1,0:T(8,128)(2,1)}, u32[]{:S(2)}, u32[]{:S(2)}) %collective-permute-start.5) | collective-permute-done | bytes 262176 | tf_op jit(solution)/shard_map/ppermute | solution.py:245
  94.3 1.5 %collective-permute-start.7 = (bf16[256,512]{1,0:T(8,128)(2,1)S(1)}, bf16[256,512]{1,0:T(8,128)(2,1)S(1)}, u32[]{:S(2)}, u32[]{:S(2)}) collective-permute-start(bf16[256,512]{1,0:T(8,128)(2,1)S(1)} %collective-permute-done.3.refs_5_), channel_id=1, source_target_pairs={{0,16},{16,0},{1,17},{17,1},{2,18},{18,2},{3,19},{19,3},{4,20},{20... | collective-permute-start | bytes 786440 | tf_op jit(solution)/shard_map/ppermute | solution.py:245
  95.8 0.0 collective-permute-done.10.refs_13_
  95.8 1.5 %collective-permute-start.6 = (bf16[256,512]{1,0:T(8,128)(2,1)}, bf16[256,512]{1,0:T(8,128)(2,1)S(1)}, u32[]{:S(2)}, u32[]{:S(2)}) collective-permute-start(bf16[256,512]{1,0:T(8,128)(2,1)} %collective-permute-done.2.refs_4_), channel_id=1, source_target_pairs={{0,2},{2,0},{1,3},{3,1},{4,6},{6,4},{5,7},{7,5},{8,10},{10,8},{9,1... | collective-permute-start | bytes 786440 | tf_op jit(solution)/shard_map/ppermute | solution.py:245
  97.3 0.0 collective-permute-done.15.refs_18_
  97.3 1.3 collective-permute-start.12
  98.6 0.7 collective-permute-start.9
  99.4 2.8 %collective-permute-done.7.refs_10_ = bf16[256,512]{1,0:T(8,128)(2,1)S(1)} collective-permute-done((bf16[256,512]{1,0:T(8,128)(2,1)S(1)}, bf16[256,512]{1,0:T(8,128)(2,1)S(1)}, u32[]{:S(2)}, u32[]{:S(2)}) %collective-permute-start.7) | collective-permute-done | bytes 262176 | tf_op jit(solution)/shard_map/ppermute | solution.py:245
  102.2 2.5 %collective-permute-start.11 = (bf16[256,512]{1,0:T(8,128)(2,1)}, bf16[256,512]{1,0:T(8,128)(2,1)}, u32[]{:S(2)}, u32[]{:S(2)}) collective-permute-start(bf16[256,512]{1,0:T(8,128)(2,1)} %collective-permute-done.5.refs_7_), channel_id=1, source_target_pairs={{0,16},{16,0},{1,17},{17,1},{2,18},{18,2},{3,19},{19,3},{4,20},{20... | collective-permute-start | bytes 786440 | tf_op jit(solution)/shard_map/ppermute | solution.py:245
  104.6 0.0 collective-permute-done.18.refs_21_
  104.6 0.1 collective-permute-start.17
  104.8 0.6 copy-done.14
  105.4 0.7 copy-done.15
  106.1 0.1 copy.11
  106.2 0.1 reduce
  106.3 1.6 %collective-permute-done.12.refs_15_ = bf16[256,512]{1,0:T(8,128)(2,1)S(1)} collective-permute-done((bf16[256,512]{1,0:T(8,128)(2,1)}, bf16[256,512]{1,0:T(8,128)(2,1)S(1)}, u32[]{:S(2)}, u32[]{:S(2)}) %collective-permute-start.12) | collective-permute-done | bytes 262176 | tf_op jit(solution)/shard_map/ppermute | solution.py:245
  107.9 5.6 %collective-permute-done.9.refs_12_ = bf16[256,512]{1,0:T(8,128)(2,1)} collective-permute-done((bf16[256,512]{1,0:T(8,128)(2,1)}, bf16[256,512]{1,0:T(8,128)(2,1)}, u32[]{:S(2)}, u32[]{:S(2)}) %collective-permute-start.9) | collective-permute-done | bytes 262176 | tf_op jit(solution)/shard_map/ppermute | solution.py:245
  113.5 0.0 collective-permute-start.24
  113.5 4.7 %collective-permute-done.11.refs_14_ = bf16[256,512]{1,0:T(8,128)(2,1)} collective-permute-done((bf16[256,512]{1,0:T(8,128)(2,1)}, bf16[256,512]{1,0:T(8,128)(2,1)}, u32[]{:S(2)}, u32[]{:S(2)}) %collective-permute-start.11) | collective-permute-done | bytes 262176 | tf_op jit(solution)/shard_map/ppermute | solution.py:245
  118.2 0.0 collective-permute-start.26
  118.2 0.0 collective-permute-done.17.refs_20_
  118.2 0.5 collective-permute-start.23
  118.7 0.0 collective-permute-done.19.refs_22_
  118.7 1.5 %collective-permute-start.13 = (bf16[256,512]{1,0:T(8,128)(2,1)}, bf16[256,512]{1,0:T(8,128)(2,1)S(1)}, u32[]{:S(2)}, u32[]{:S(2)}) collective-permute-start(bf16[256,512]{1,0:T(8,128)(2,1)} %copy-done.15), channel_id=1, source_target_pairs={{0,16},{16,0},{1,17},{17,1},{2,18},{18,2},{3,19},{19,3},{4,20},{20... | collective-permute-start | bytes 786440 | tf_op jit(solution)/shard_map/ppermute | solution.py:245
  120.2 0.7 fusion.1
  120.9 0.1 select_reduce_fusion
  121.0 0.1 collective-permute-start.21
  121.1 0.0 collective-permute-done.24.refs_27_
  121.1 0.5 collective-permute-start.28
  121.6 0.0 collective-permute-done.26.refs_29_
  121.6 0.1 collective-permute-start.25
  121.7 0.4 collective-permute-start.27
  122.1 5.1 %collective-permute-done.13.refs_16_ = bf16[256,512]{1,0:T(8,128)(2,1)S(1)} collective-permute-done((bf16[256,512]{1,0:T(8,128)(2,1)}, bf16[256,512]{1,0:T(8,128)(2,1)S(1)}, u32[]{:S(2)}, u32[]{:S(2)}) %collective-permute-start.13) | collective-permute-done | bytes 262176 | tf_op jit(solution)/shard_map/ppermute | solution.py:245
  127.2 0.0 collective-permute-start.29
  127.3 0.8 compare_convert_fusion.mask
  128.1 0.0 collective-permute-done.28.refs_31_
  128.1 0.6 collective-permute-done.29.refs_32_
  128.9 0.0 copy-done.23
  128.9 0.1 copy-done.24
  129.0 0.1 copy-done.25
  129.0 0.7 copy-done.26
  129.7 8.1 %base_product.1.base = f32[512,512]{1,0:T(8,128)} custom-call(bf16[512,8192]{1,0:T(8,128)(2,1)} %tokens.1, bf16[256,512]{1,0:T(8,128)(2,1)} %copy-done.2, bf16[256,512]{1,0:T(8,128)(2,1)} %copy-done.3, bf16[256,512]{1,0:T(8,128)(2,1)} %copy-done.5, bf16[256,512]{1,0:T(8,128)(2,1)} %collective-permute-done.2.refs_4_, bf16[256,512]{1,0:T(8,128)(2,1)} %copy-done.6, ...), custom_call_target="tpu_custom_call" | custom-call | flops 4294967296 | bytes 17825792 | tf_op jit(solution)/shard_map/base_product/pallas_call | solution.py:121
  137.9 1.4 copy-done
  139.3 7.8 %adapt.1 = bf16[512,512]{1,0:T(8,128)(2,1)} custom-call(bf16[512,8192]{1,0:T(8,128)(2,1)} %tokens.1, bf16[16,272,256]{2,1,0:T(8,128)(2,1)} %copy-done, f32[512,128]{1,0:T(8,128)} %compare_convert_fusion.mask, f32[512,512]{1,0:T(8,128)} %base_product.1.base), custom_call_target="tpu_custom_call" | custom-call | flops 1073741824 | bytes 12189696 | tf_op jit(solution)/shard_map/adapt/pallas_call | solution.py:195
  (66 shorter events, 0.2 us)
Async XLA Ops:
  1.1 20.7 %copy-start.2 = (bf16[256,512]{1,0:T(8,128)(2,1)}, bf16[256,512]{1,0:T(8,128)(2,1)S(1)}, u32[]{:S(2)}) copy-start(bf16[256,512]{1,0:T(8,128)(2,1)S(1)} %get-tuple-element.6.refs_1_) | copy-start | bytes 786436
  1.1 20.7 %copy-start.1 = (bf16[256,512]{1,0:T(8,128)(2,1)}, bf16[256,512]{1,0:T(8,128)(2,1)S(1)}, u32[]{:S(2)}) copy-start(bf16[256,512]{1,0:T(8,128)(2,1)S(1)} %get-tuple-element.5.refs_9_) | copy-start | bytes 786436
  1.1 9.4 %collective-permute-start = (bf16[256,512]{1,0:T(8,128)(2,1)S(1)}, bf16[256,512]{1,0:T(8,128)(2,1)S(1)}, u32[]{:S(2)}, u32[]{:S(2)}) collective-permute-start(bf16[256,512]{1,0:T(8,128)(2,1)S(1)} %get-tuple-element.6.refs_1_), channel_id=1, source_target_pairs={{0,4},{4,0},{8,12},{12,8},{1,5},{5,1},{9,13},{13,9},{2,6},{6,2},{1... | collective-permute-start | bytes 786440 | tf_op jit(solution)/shard_map/ppermute | solution.py:245
  10.5 0.7 copy-start.3
  11.2 69.5 %copy-start.4 = (bf16[256,512]{1,0:T(8,128)(2,1)S(1)}, bf16[256,512]{1,0:T(8,128)(2,1)}, u32[]{:S(2)}) copy-start(bf16[256,512]{1,0:T(8,128)(2,1)} %copy-done.3) | copy-start | bytes 786436
  11.2 94.9 %copy-start.27 = (s32[1,16]{1,0:T(1,128)S(1)}, s32[1,16]{1,0:T(1,128)}, u32[]{:S(2)}) copy-start(s32[1,16]{1,0:T(1,128)} %param.11) | copy-start | bytes 196
  11.2 126.7 %all-to-all-start = ((bf16[16,272,256]{2,1,0:T(8,128)(2,1)}), bf16[16,272,256]{2,1,0:T(8,128)(2,1)S(1)}, u32[]{:S(2)}, u32[]{:S(2)}) async-start(bf16[16,272,256]{2,1,0:T(8,128)(2,1)} %after.1), calls=%async_computation | async-start | bytes 4456448 | tf_op jit(solution)/shard_map/all_to_all | solution.py:284
  17.4 63.2 %collective-permute-start.1 = (bf16[256,512]{1,0:T(8,128)(2,1)S(1)}, bf16[256,512]{1,0:T(8,128)(2,1)S(1)}, u32[]{:S(2)}, u32[]{:S(2)}) collective-permute-start(bf16[256,512]{1,0:T(8,128)(2,1)S(1)} %get-tuple-element.6.refs_1_), channel_id=1, source_target_pairs={{0,8},{4,12},{8,0},{12,4},{1,9},{5,13},{9,1},{13,5},{2,10},{6,14},... | collective-permute-start | bytes 786440 | tf_op jit(solution)/shard_map/ppermute | solution.py:245
  20.3 61.9 %collective-permute-start.3 = (bf16[256,512]{1,0:T(8,128)(2,1)S(1)}, bf16[256,512]{1,0:T(8,128)(2,1)S(1)}, u32[]{:S(2)}, u32[]{:S(2)}) collective-permute-start(bf16[256,512]{1,0:T(8,128)(2,1)S(1)} %get-tuple-element.6.refs_1_), channel_id=1, source_target_pairs={{0,2},{2,0},{1,3},{3,1},{4,6},{6,4},{5,7},{7,5},{8,10},{10,8},{9,1... | collective-permute-start | bytes 786440 | tf_op jit(solution)/shard_map/ppermute | solution.py:245
  21.7 61.0 %collective-permute-start.14 = (bf16[256,512]{1,0:T(8,128)(2,1)S(1)}, bf16[256,512]{1,0:T(8,128)(2,1)S(1)}, u32[]{:S(2)}, u32[]{:S(2)}) collective-permute-start(bf16[256,512]{1,0:T(8,128)(2,1)S(1)} %get-tuple-element.6.refs_1_), channel_id=1, source_target_pairs={{0,1},{1,0},{2,3},{3,2},{4,5},{5,4},{6,7},{7,6},{8,9},{9,8},{10,11... | collective-permute-start | bytes 786440 | tf_op jit(solution)/shard_map/ppermute | solution.py:245
  21.7 62.5 %collective-permute-start.22 = (bf16[256,512]{1,0:T(8,128)(2,1)S(1)}, bf16[256,512]{1,0:T(8,128)(2,1)S(1)}, u32[]{:S(2)}, u32[]{:S(2)}) collective-permute-start(bf16[256,512]{1,0:T(8,128)(2,1)S(1)} %get-tuple-element.5.refs_9_), channel_id=1, source_target_pairs={{0,1},{1,0},{2,3},{3,2},{4,5},{5,4},{6,7},{7,6},{8,9},{9,8},{10,11... | collective-permute-start | bytes 786440 | tf_op jit(solution)/shard_map/ppermute | solution.py:245
  80.6 48.1 %copy-start.5 = (bf16[256,512]{1,0:T(8,128)(2,1)}, bf16[256,512]{1,0:T(8,128)(2,1)S(1)}, u32[]{:S(2)}) copy-start(bf16[256,512]{1,0:T(8,128)(2,1)S(1)} %collective-permute-done.1.refs_3_) | copy-start | bytes 786436
  80.6 8.0 %collective-permute-start.2 = (bf16[256,512]{1,0:T(8,128)(2,1)S(1)}, bf16[256,512]{1,0:T(8,128)(2,1)}, u32[]{:S(2)}, u32[]{:S(2)}) collective-permute-start(bf16[256,512]{1,0:T(8,128)(2,1)S(1)} %collective-permute-done.1.refs_3_), channel_id=1, source_target_pairs={{0,4},{4,0},{8,12},{12,8},{1,5},{5,1},{9,13},{13,9},{2,6},{6,2},{1... | collective-permute-start | bytes 786440 | tf_op jit(solution)/shard_map/ppermute | solution.py:245
  80.6 9.4 %collective-permute-start.4 = (bf16[256,512]{1,0:T(8,128)(2,1)S(1)}, bf16[256,512]{1,0:T(8,128)(2,1)}, u32[]{:S(2)}, u32[]{:S(2)}) collective-permute-start(bf16[256,512]{1,0:T(8,128)(2,1)S(1)} %copy-done.4), channel_id=1, source_target_pairs={{0,2},{2,0},{1,3},{3,1},{4,6},{6,4},{5,7},{7,5},{8,10},{10,8},{9,1... | collective-permute-start | bytes 786440 | tf_op jit(solution)/shard_map/ppermute | solution.py:245
  82.2 46.6 %copy-start.6 = (bf16[256,512]{1,0:T(8,128)(2,1)}, bf16[256,512]{1,0:T(8,128)(2,1)S(1)}, u32[]{:S(2)}) copy-start(bf16[256,512]{1,0:T(8,128)(2,1)S(1)} %collective-permute-done.3.refs_5_) | copy-start | bytes 786436
  82.2 12.1 %collective-permute-start.5 = (bf16[256,512]{1,0:T(8,128)(2,1)S(1)}, bf16[256,512]{1,0:T(8,128)(2,1)}, u32[]{:S(2)}, u32[]{:S(2)}) collective-permute-start(bf16[256,512]{1,0:T(8,128)(2,1)S(1)} %collective-permute-done.1.refs_3_), channel_id=1, source_target_pairs={{0,2},{2,0},{1,3},{3,1},{4,6},{6,4},{5,7},{7,5},{8,10},{10,8},{9,1... | collective-permute-start | bytes 786440 | tf_op jit(solution)/shard_map/ppermute | solution.py:245
  82.7 21.9 %copy-start.7 = (bf16[256,512]{1,0:T(8,128)(2,1)}, bf16[256,512]{1,0:T(8,128)(2,1)S(1)}, u32[]{:S(2)}) copy-start(bf16[256,512]{1,0:T(8,128)(2,1)S(1)} %collective-permute-done.14.refs_17_) | copy-start | bytes 786436
  82.7 13.0 %collective-permute-start.8 = (bf16[256,512]{1,0:T(8,128)(2,1)S(1)}, bf16[256,512]{1,0:T(8,128)(2,1)S(1)}, u32[]{:S(2)}, u32[]{:S(2)}) collective-permute-start(bf16[256,512]{1,0:T(8,128)(2,1)S(1)} %copy-done.4), channel_id=1, source_target_pairs={{0,16},{16,0},{1,17},{17,1},{2,18},{18,2},{3,19},{19,3},{4,20},{20... | collective-permute-start | bytes 786440 | tf_op jit(solution)/shard_map/ppermute | solution.py:245
  84.2 20.5 %copy-start.8 = (bf16[256,512]{1,0:T(8,128)(2,1)}, bf16[256,512]{1,0:T(8,128)(2,1)S(1)}, u32[]{:S(2)}) copy-start(bf16[256,512]{1,0:T(8,128)(2,1)S(1)} %collective-permute-done.22.refs_25_) | copy-start | bytes 786436
  84.2 11.5 %collective-permute-start.10 = (bf16[256,512]{1,0:T(8,128)(2,1)S(1)}, bf16[256,512]{1,0:T(8,128)(2,1)S(1)}, u32[]{:S(2)}, u32[]{:S(2)}) collective-permute-start(bf16[256,512]{1,0:T(8,128)(2,1)S(1)} %collective-permute-done.1.refs_3_), channel_id=1, source_target_pairs={{0,16},{16,0},{1,17},{17,1},{2,18},{18,2},{3,19},{19,3},{4,20},{20... | collective-permute-start | bytes 786440 | tf_op jit(solution)/shard_map/ppermute | solution.py:245
  88.6 8.7 %collective-permute-start.15 = (bf16[256,512]{1,0:T(8,128)(2,1)S(1)}, bf16[256,512]{1,0:T(8,128)(2,1)S(1)}, u32[]{:S(2)}, u32[]{:S(2)}) collective-permute-start(bf16[256,512]{1,0:T(8,128)(2,1)S(1)} %copy-done.4), channel_id=1, source_target_pairs={{0,1},{1,0},{2,3},{3,2},{4,5},{5,4},{6,7},{7,6},{8,9},{9,8},{10,11... | collective-permute-start | bytes 786440 | tf_op jit(solution)/shard_map/ppermute | solution.py:245
  90.0 8.6 %collective-permute-start.16 = (bf16[256,512]{1,0:T(8,128)(2,1)S(1)}, bf16[256,512]{1,0:T(8,128)(2,1)S(1)}, u32[]{:S(2)}, u32[]{:S(2)}) collective-permute-start(bf16[256,512]{1,0:T(8,128)(2,1)S(1)} %collective-permute-done.1.refs_3_), channel_id=1, source_target_pairs={{0,1},{1,0},{2,3},{3,2},{4,5},{5,4},{6,7},{7,6},{8,9},{9,8},{10,11... | collective-permute-start | bytes 786440 | tf_op jit(solution)/shard_map/ppermute | solution.py:245
  94.3 7.9 %collective-permute-start.7 = (bf16[256,512]{1,0:T(8,128)(2,1)S(1)}, bf16[256,512]{1,0:T(8,128)(2,1)S(1)}, u32[]{:S(2)}, u32[]{:S(2)}) collective-permute-start(bf16[256,512]{1,0:T(8,128)(2,1)S(1)} %collective-permute-done.3.refs_5_), channel_id=1, source_target_pairs={{0,16},{16,0},{1,17},{17,1},{2,18},{18,2},{3,19},{19,3},{4,20},{20... | collective-permute-start | bytes 786440 | tf_op jit(solution)/shard_map/ppermute | solution.py:245
  95.8 33.0 %copy-start.9 = (bf16[256,512]{1,0:T(8,128)(2,1)}, bf16[256,512]{1,0:T(8,128)(2,1)S(1)}, u32[]{:S(2)}) copy-start(bf16[256,512]{1,0:T(8,128)(2,1)S(1)} %collective-permute-done.8.refs_11_) | copy-start | bytes 786436
  95.8 8.9 %collective-permute-start.18 = (bf16[256,512]{1,0:T(8,128)(2,1)S(1)}, bf16[256,512]{1,0:T(8,128)(2,1)S(1)}, u32[]{:S(2)}, u32[]{:S(2)}) collective-permute-start(bf16[256,512]{1,0:T(8,128)(2,1)S(1)} %collective-permute-done.3.refs_5_), channel_id=1, source_target_pairs={{0,1},{1,0},{2,3},{3,2},{4,5},{5,4},{6,7},{7,6},{8,9},{9,8},{10,11... | collective-permute-start | bytes 786440 | tf_op jit(solution)/shard_map/ppermute | solution.py:245
  95.8 33.0 %copy-start.10 = (bf16[256,512]{1,0:T(8,128)(2,1)}, bf16[256,512]{1,0:T(8,128)(2,1)S(1)}, u32[]{:S(2)}) copy-start(bf16[256,512]{1,0:T(8,128)(2,1)S(1)} %collective-permute-done.10.refs_13_) | copy-start | bytes 786436
  95.8 8.9 %collective-permute-start.6 = (bf16[256,512]{1,0:T(8,128)(2,1)}, bf16[256,512]{1,0:T(8,128)(2,1)S(1)}, u32[]{:S(2)}, u32[]{:S(2)}) collective-permute-start(bf16[256,512]{1,0:T(8,128)(2,1)} %collective-permute-done.2.refs_4_), channel_id=1, source_target_pairs={{0,2},{2,0},{1,3},{3,1},{4,6},{6,4},{5,7},{7,5},{8,10},{10,8},{9,1... | collective-permute-start | bytes 786440 | tf_op jit(solution)/shard_map/ppermute | solution.py:245
  97.3 7.4 %copy-start.11 = (bf16[256,512]{1,0:T(8,128)(2,1)}, bf16[256,512]{1,0:T(8,128)(2,1)S(1)}, u32[]{:S(2)}) copy-start(bf16[256,512]{1,0:T(8,128)(2,1)S(1)} %collective-permute-done.15.refs_18_) | copy-start | bytes 786436
  97.3 10.5 %collective-permute-start.12 = (bf16[256,512]{1,0:T(8,128)(2,1)}, bf16[256,512]{1,0:T(8,128)(2,1)S(1)}, u32[]{:S(2)}, u32[]{:S(2)}) collective-permute-start(bf16[256,512]{1,0:T(8,128)(2,1)} %collective-permute-done.2.refs_4_), channel_id=1, source_target_pairs={{0,16},{16,0},{1,17},{17,1},{2,18},{18,2},{3,19},{19,3},{4,20},{20... | collective-permute-start | bytes 786440 | tf_op jit(solution)/shard_map/ppermute | solution.py:245
  98.6 6.1 %copy-start.12 = (bf16[256,512]{1,0:T(8,128)(2,1)}, bf16[256,512]{1,0:T(8,128)(2,1)S(1)}, u32[]{:S(2)}) copy-start(bf16[256,512]{1,0:T(8,128)(2,1)S(1)} %collective-permute-done.16.refs_19_) | copy-start | bytes 786436
  98.6 14.9 %collective-permute-start.9 = (bf16[256,512]{1,0:T(8,128)(2,1)}, bf16[256,512]{1,0:T(8,128)(2,1)}, u32[]{:S(2)}, u32[]{:S(2)}) collective-permute-start(bf16[256,512]{1,0:T(8,128)(2,1)} %collective-permute-done.4.refs_6_), channel_id=1, source_target_pairs={{0,16},{16,0},{1,17},{17,1},{2,18},{18,2},{3,19},{19,3},{4,20},{20... | collective-permute-start | bytes 786440 | tf_op jit(solution)/shard_map/ppermute | solution.py:245
  102.2 2.6 %copy-start.13 = (bf16[256,512]{1,0:T(8,128)(2,1)}, bf16[256,512]{1,0:T(8,128)(2,1)S(1)}, u32[]{:S(2)}) copy-start(bf16[256,512]{1,0:T(8,128)(2,1)S(1)} %collective-permute-done.7.refs_10_) | copy-start | bytes 786436
  102.2 16.1 %collective-permute-start.11 = (bf16[256,512]{1,0:T(8,128)(2,1)}, bf16[256,512]{1,0:T(8,128)(2,1)}, u32[]{:S(2)}, u32[]{:S(2)}) collective-permute-start(bf16[256,512]{1,0:T(8,128)(2,1)} %collective-permute-done.5.refs_7_), channel_id=1, source_target_pairs={{0,16},{16,0},{1,17},{17,1},{2,18},{18,2},{3,19},{19,3},{4,20},{20... | collective-permute-start | bytes 786440 | tf_op jit(solution)/shard_map/ppermute | solution.py:245
  104.6 0.7 copy-start.14
  104.6 13.6 %collective-permute-start.17 = (bf16[256,512]{1,0:T(8,128)(2,1)}, bf16[256,512]{1,0:T(8,128)(2,1)}, u32[]{:S(2)}, u32[]{:S(2)}) collective-permute-start(bf16[256,512]{1,0:T(8,128)(2,1)} %collective-permute-done.2.refs_4_), channel_id=1, source_target_pairs={{0,1},{1,0},{2,3},{3,2},{4,5},{5,4},{6,7},{7,6},{8,9},{9,8},{10,11... | collective-permute-start | bytes 786440 | tf_op jit(solution)/shard_map/ppermute | solution.py:245
  105.4 0.7 copy-start.15
  106.1 12.7 %collective-permute-start.19 = (bf16[256,512]{1,0:T(8,128)(2,1)}, bf16[256,512]{1,0:T(8,128)(2,1)}, u32[]{:S(2)}, u32[]{:S(2)}) collective-permute-start(bf16[256,512]{1,0:T(8,128)(2,1)} %collective-permute-done.4.refs_6_), channel_id=1, source_target_pairs={{0,1},{1,0},{2,3},{3,2},{4,5},{5,4},{6,7},{7,6},{8,9},{9,8},{10,11... | collective-permute-start | bytes 786440 | tf_op jit(solution)/shard_map/ppermute | solution.py:245
  107.9 20.9 %copy-start.16 = (bf16[256,512]{1,0:T(8,128)(2,1)}, bf16[256,512]{1,0:T(8,128)(2,1)S(1)}, u32[]{:S(2)}) copy-start(bf16[256,512]{1,0:T(8,128)(2,1)S(1)} %collective-permute-done.12.refs_15_) | copy-start | bytes 786436
  107.9 13.2 %collective-permute-start.20 = (bf16[256,512]{1,0:T(8,128)(2,1)}, bf16[256,512]{1,0:T(8,128)(2,1)S(1)}, u32[]{:S(2)}, u32[]{:S(2)}) collective-permute-start(bf16[256,512]{1,0:T(8,128)(2,1)} %collective-permute-done.5.refs_7_), channel_id=1, source_target_pairs={{0,1},{1,0},{2,3},{3,2},{4,5},{5,4},{6,7},{7,6},{8,9},{9,8},{10,11... | collective-permute-start | bytes 786440 | tf_op jit(solution)/shard_map/ppermute | solution.py:245
  113.5 7.6 %collective-permute-start.24 = (bf16[256,512]{1,0:T(8,128)(2,1)S(1)}, bf16[256,512]{1,0:T(8,128)(2,1)S(1)}, u32[]{:S(2)}, u32[]{:S(2)}) collective-permute-start(bf16[256,512]{1,0:T(8,128)(2,1)S(1)} %collective-permute-done.8.refs_11_), channel_id=1, source_target_pairs={{0,1},{1,0},{2,3},{3,2},{4,5},{5,4},{6,7},{7,6},{8,9},{9,8},{10,11... | collective-permute-start | bytes 786440 | tf_op jit(solution)/shard_map/ppermute | solution.py:245
  118.2 3.4 %collective-permute-start.26 = (bf16[256,512]{1,0:T(8,128)(2,1)S(1)}, bf16[256,512]{1,0:T(8,128)(2,1)S(1)}, u32[]{:S(2)}, u32[]{:S(2)}) collective-permute-start(bf16[256,512]{1,0:T(8,128)(2,1)S(1)} %collective-permute-done.10.refs_13_), channel_id=1, source_target_pairs={{0,1},{1,0},{2,3},{3,2},{4,5},{5,4},{6,7},{7,6},{8,9},{9,8},{10,11... | collective-permute-start | bytes 786440 | tf_op jit(solution)/shard_map/ppermute | solution.py:245
  118.2 3.5 %collective-permute-start.23 = (bf16[256,512]{1,0:T(8,128)(2,1)}, bf16[256,512]{1,0:T(8,128)(2,1)S(1)}, u32[]{:S(2)}, u32[]{:S(2)}) collective-permute-start(bf16[256,512]{1,0:T(8,128)(2,1)} %copy-done.13), channel_id=1, source_target_pairs={{0,1},{1,0},{2,3},{3,2},{4,5},{5,4},{6,7},{7,6},{8,9},{9,8},{10,11... | collective-permute-start | bytes 786440 | tf_op jit(solution)/shard_map/ppermute | solution.py:245
  118.7 8.5 %collective-permute-start.13 = (bf16[256,512]{1,0:T(8,128)(2,1)}, bf16[256,512]{1,0:T(8,128)(2,1)S(1)}, u32[]{:S(2)}, u32[]{:S(2)}) collective-permute-start(bf16[256,512]{1,0:T(8,128)(2,1)} %copy-done.15), channel_id=1, source_target_pairs={{0,16},{16,0},{1,17},{17,1},{2,18},{18,2},{3,19},{19,3},{4,20},{20... | collective-permute-start | bytes 786440 | tf_op jit(solution)/shard_map/ppermute | solution.py:245
  121.0 7.8 %copy-start.17 = (bf16[256,512]{1,0:T(8,128)(2,1)}, bf16[256,512]{1,0:T(8,128)(2,1)S(1)}, u32[]{:S(2)}) copy-start(bf16[256,512]{1,0:T(8,128)(2,1)S(1)} %collective-permute-done.20.refs_23_) | copy-start | bytes 786436
  121.0 7.0 %collective-permute-start.21 = (bf16[256,512]{1,0:T(8,128)(2,1)}, bf16[256,512]{1,0:T(8,128)(2,1)S(1)}, u32[]{:S(2)}, u32[]{:S(2)}) collective-permute-start(bf16[256,512]{1,0:T(8,128)(2,1)} %copy-done.15), channel_id=1, source_target_pairs={{0,1},{1,0},{2,3},{3,2},{4,5},{5,4},{6,7},{7,6},{8,9},{9,8},{10,11... | collective-permute-start | bytes 786440 | tf_op jit(solution)/shard_map/ppermute | solution.py:245
  121.1 7.7 %copy-start.18 = (bf16[256,512]{1,0:T(8,128)(2,1)}, bf16[256,512]{1,0:T(8,128)(2,1)S(1)}, u32[]{:S(2)}) copy-start(bf16[256,512]{1,0:T(8,128)(2,1)S(1)} %collective-permute-done.24.refs_27_) | copy-start | bytes 786436
  121.1 6.9 %collective-permute-start.28 = (bf16[256,512]{1,0:T(8,128)(2,1)S(1)}, bf16[256,512]{1,0:T(8,128)(2,1)S(1)}, u32[]{:S(2)}, u32[]{:S(2)}) collective-permute-start(bf16[256,512]{1,0:T(8,128)(2,1)S(1)} %collective-permute-done.12.refs_15_), channel_id=1, source_target_pairs={{0,1},{1,0},{2,3},{3,2},{4,5},{5,4},{6,7},{7,6},{8,9},{9,8},{10,11... | collective-permute-start | bytes 786440 | tf_op jit(solution)/shard_map/ppermute | solution.py:245
  121.6 7.2 %copy-start.19 = (bf16[256,512]{1,0:T(8,128)(2,1)}, bf16[256,512]{1,0:T(8,128)(2,1)S(1)}, u32[]{:S(2)}) copy-start(bf16[256,512]{1,0:T(8,128)(2,1)S(1)} %collective-permute-done.26.refs_29_) | copy-start | bytes 786436
  121.6 6.5 %collective-permute-start.25 = (bf16[256,512]{1,0:T(8,128)(2,1)}, bf16[256,512]{1,0:T(8,128)(2,1)S(1)}, u32[]{:S(2)}, u32[]{:S(2)}) collective-permute-start(bf16[256,512]{1,0:T(8,128)(2,1)} %collective-permute-done.9.refs_12_), channel_id=1, source_target_pairs={{0,1},{1,0},{2,3},{3,2},{4,5},{5,4},{6,7},{7,6},{8,9},{9,8},{10,11... | collective-permute-start | bytes 786440 | tf_op jit(solution)/shard_map/ppermute | solution.py:245
  121.7 7.1 %copy-start.20 = (bf16[256,512]{1,0:T(8,128)(2,1)}, bf16[256,512]{1,0:T(8,128)(2,1)S(1)}, u32[]{:S(2)}) copy-start(bf16[256,512]{1,0:T(8,128)(2,1)S(1)} %collective-permute-done.23.refs_26_) | copy-start | bytes 786436
  121.7 6.4 %collective-permute-start.27 = (bf16[256,512]{1,0:T(8,128)(2,1)}, bf16[256,512]{1,0:T(8,128)(2,1)S(1)}, u32[]{:S(2)}, u32[]{:S(2)}) collective-permute-start(bf16[256,512]{1,0:T(8,128)(2,1)} %collective-permute-done.11.refs_14_), channel_id=1, source_target_pairs={{0,1},{1,0},{2,3},{3,2},{4,5},{5,4},{6,7},{7,6},{8,9},{9,8},{10,11... | collective-permute-start | bytes 786440 | tf_op jit(solution)/shard_map/ppermute | solution.py:245
  127.2 1.6 %copy-start.21 = (bf16[256,512]{1,0:T(8,128)(2,1)}, bf16[256,512]{1,0:T(8,128)(2,1)S(1)}, u32[]{:S(2)}) copy-start(bf16[256,512]{1,0:T(8,128)(2,1)S(1)} %collective-permute-done.13.refs_16_) | copy-start | bytes 786436
  127.2 1.5 %collective-permute-start.29 = (bf16[256,512]{1,0:T(8,128)(2,1)S(1)}, bf16[256,512]{1,0:T(8,128)(2,1)S(1)}, u32[]{:S(2)}, u32[]{:S(2)}) collective-permute-start(bf16[256,512]{1,0:T(8,128)(2,1)S(1)} %collective-permute-done.13.refs_16_), channel_id=1, source_target_pairs={{0,1},{1,0},{2,3},{3,2},{4,5},{5,4},{6,7},{7,6},{8,9},{9,8},{10,11... | collective-permute-start | bytes 786440 | tf_op jit(solution)/shard_map/ppermute | solution.py:245
  128.1 0.8 copy-start.22
  128.1 0.8 copy-start.23
  128.1 0.9 copy-start.24
  128.1 0.9 copy-start.25
  129.0 0.7 copy-start.26
  137.9 1.4 copy-start

commit v4 on v2

v4 whole, which is shorter than its diff:
```python
import functools

import jax
import jax.numpy as jnp
from jax import lax
from jax.experimental import pallas as pl
from jax.experimental.pallas import tpu as pltpu
from jax.sharding import Mesh
from jax.sharding import PartitionSpec as P

HALF = 256
DEEP = 4
MIB = 1024 * 1024
AXES = ("parts", "line", "plane", "core")


def in_vmem(value):
    return pltpu.with_memory_space_constraint(value, pltpu.VMEM)


def store_index():
    return (lax.axis_index("line") * 2 + lax.axis_index("plane")) * 2 + lax.axis_index("core")


def send_kernel(groups, wanted, down, up, *refs):
    outs, (pick, even_rows, odd_rows, sems) = refs[:groups], refs[groups:]
    choices = wanted.shape[0]
    rank = down.shape[1]
    halves = down.shape[2] // HALF
    me = store_index()
    copies = []
    for k in range(groups):
        for choice in range(choices):
            for half in range(halves):
                copy = pltpu.make_async_copy(
                    down.at[wanted[choice, me ^ k], :, pl.ds(half * HALF, HALF)],
                    outs[k].at[pl.ds((half * choices + choice) * rank, rank), :],
                    sems.at[len(copies)],
                )
                copy.start()
                copies.append(copy)

    ids = lax.broadcasted_iota(jnp.int32, (1, up.shape[1]), 1)
    for choice in range(choices):
        for k in range(groups):
            here = (ids == wanted[choice, me ^ k]).astype(jnp.float32)
            pick[pl.ds(choice * groups + k, 1), :] = here
    rows = lax.dot_general(
        pick[...].astype(jnp.bfloat16),
        up[...],
        (((1,), (1,)), ((), ())),
        preferred_element_type=jnp.float32,
    )
    first, second = rows[:groups], rows[groups:]
    low = lax.broadcasted_iota(jnp.int32, (groups, 2 * rank), 1) < rank
    count = even_rows.shape[0] // groups
    for i in range(count):
        a = first[:, 2 * rank * i : 2 * rank * (i + 1)]
        b = second[:, 2 * rank * i : 2 * rank * (i + 1)]
        even_rows[pl.ds(i, groups, stride=count), :] = jnp.where(low, a, pltpu.roll(b, rank, 1))
        odd_rows[pl.ds(i, groups, stride=count), :] = jnp.where(low, pltpu.roll(a, rank, 1), b)
    start = choices * halves * rank
    for k in range(groups):
        own = pl.ds(k * count, count)
        outs[k][start:, : 2 * rank] = even_rows[own, :].astype(jnp.bfloat16)
        outs[k][start:, 2 * rank :] = odd_rows[own, :].astype(jnp.bfloat16)
    for copy in copies:
        copy.wait()


def make_messages(wanted, down, up, shard_width):
    choices, groups = wanted.shape
    rank, depth = down.shape[1:]
    halves = depth // HALF
    count = shard_width * choices * rank // HALF
    rows = choices * rank * halves + count
    return pl.pallas_call(
        functools.partial(send_kernel, groups),
        out_shape=[pltpu.VMEM((rows, HALF), jnp.bfloat16)] * groups,
        in_specs=[
            pl.BlockSpec(memory_space=pltpu.SMEM),
            pl.BlockSpec(memory_space=pl.ANY),
            pl.BlockSpec(memory_space=pltpu.VMEM),
        ],
        out_specs=[pl.BlockSpec(memory_space=pltpu.VMEM)] * groups,
        scratch_shapes=[
            pltpu.VMEM((choices * groups, up.shape[1]), jnp.float32),
            pltpu.VMEM((groups * count, 2 * rank), jnp.float32),
            pltpu.VMEM((groups * count, 2 * rank), jnp.float32),
            pltpu.SemaphoreType.DMA((groups * choices * halves,)),
        ],
        compiler_params=pltpu.CompilerParams(vmem_limit_bytes=16 * MIB),
        name="make_messages",
    )(wanted, down, up)


def base_product(tokens, blocks):
    rows, depth = tokens.shape
    width = blocks[0][1].shape[1]
    count = len(blocks)
    masks = [mask for mask, _ in blocks]

    def kernel(tokens_ref, *refs):
        parts, out = refs[:count], refs[count]
        place = [lax.axis_index(name) for name in AXES]
        for n in range(0, count, DEEP):
            left, right = [], []
            for mask, part in zip(masks[n : n + DEEP], parts[n : n + DEEP]):
                x, z, y, core = [i ^ bit for i, bit in zip(place, mask)]
                column = pl.multiple_of((((z * 2 + y) * 2 + core) * 2 + x) * HALF, HALF)
                left.append(tokens_ref[:, pl.ds(column, HALF)])
                right.append(part[...])
            total = jnp.dot(
                jnp.concatenate(left, axis=1),
                jnp.concatenate(right, axis=0),
                preferred_element_type=jnp.float32,
            )
            if n == 0:
                out[...] = total
            else:
                out[...] += total

    return pl.pallas_call(
        kernel,
        out_shape=pltpu.VMEM((rows, width), jnp.float32),
        in_specs=[pl.BlockSpec(memory_space=pltpu.VMEM)] * (1 + count),
        out_specs=pl.BlockSpec(memory_space=pltpu.VMEM),
        compiler_params=pltpu.CompilerParams(vmem_limit_bytes=16 * MIB),
        cost_estimate=pl.CostEstimate(
            flops=2 * rows * depth * width,
            bytes_accessed=2 * rows * depth + 2 * depth * width + 4 * rows * width,
            transcendentals=0,
        ),
        name="base_product",
    )(in_vmem(tokens), *[in_vmem(block) for _, block in blocks])


def adapt_kernel(tokens, mask, base, *refs):
    *messages, out, ups, wide = refs
    pair = mask.shape[1]
    depth = tokens.shape[1] // len(messages)
    halves = depth // HALF
    step = HALF // pair
    me = store_index()
    shrink = jnp.zeros(mask.shape, jnp.float32)
    for k, message in enumerate(messages):
        source = me ^ k
        column = pl.multiple_of(source * depth, depth)
        down = jnp.concatenate(
            [message[half * pair : (half + 1) * pair, :] for half in range(halves)], axis=1
        )
        shrink += lax.dot_general(
            tokens[:, pl.ds(column, depth)],
            down,
            (((1,), (1,)), ((), ())),
            preferred_element_type=jnp.float32,
        )
        up = message[halves * pair :, :].astype(jnp.float32)
        count = up.shape[0]
        for i in range(step):
            ups[k, pl.ds(i, count, stride=step), :] = up[:, i * pair : (i + 1) * pair]
        own = pl.ds(pl.multiple_of(source * count * step, count * step), count * step)
        wide[own, :] = ups[k].astype(jnp.bfloat16)
    picked = (shrink * mask[...]).astype(jnp.bfloat16)
    delta = lax.dot_general(
        picked, wide[...], (((1,), (1,)), ((), ())), preferred_element_type=jnp.float32
    )
    out[...] = (base[...] + delta).astype(out.dtype)


def adapt(tokens, messages, mask, base):
    rows, width = base.shape
    groups = len(messages)
    pair = mask.shape[1]
    return pl.pallas_call(
        adapt_kernel,
        out_shape=jax.ShapeDtypeStruct((rows, width), jnp.bfloat16),
        in_specs=[pl.BlockSpec(memory_space=pltpu.VMEM)] * (3 + groups),
        out_specs=pl.BlockSpec(memory_space=pltpu.VMEM),
        scratch_shapes=[
            pltpu.VMEM((groups, width // groups, pair), jnp.float32),
            pltpu.VMEM((width, pair), jnp.bfloat16),
        ],
        compiler_params=pltpu.CompilerParams(vmem_limit_bytes=16 * MIB),
        cost_estimate=pl.CostEstimate(
            flops=2 * rows * tokens.shape[1] * pair,
            bytes_accessed=2 * tokens.size + 2 * groups * messages[0].size + 6 * rows * width,
            transcendentals=0,
        ),
        name="adapt",
    )(*[in_vmem(value) for value in (tokens, mask, base, *messages)])


def after(value, *others):
    def kernel(*refs):
        pass

    return pl.pallas_call(
        kernel,
        out_shape=pltpu.VMEM(value.shape, value.dtype),
        in_specs=[pl.BlockSpec(memory_space=pl.ANY)] * (1 + len(others)),
        out_specs=pl.BlockSpec(memory_space=pl.ANY),
        input_output_aliases={0: 0},
        compiler_params=pltpu.CompilerParams(vmem_limit_bytes=MIB),
        name="after",
    )(*[in_vmem(other) for other in (value, *others)])


def row_slots(lengths, slots, rows):
    ends = jnp.cumsum(lengths)
    starts = ends - lengths
    position = jnp.arange(rows, dtype=jnp.int32)[:, None]
    member = (position >= starts[None, :]) & (position < ends[None, :])
    return jnp.sum(jnp.where(member, slots[None, :], 0), axis=1)


def swap(block, axis, bit):
    size = lax.axis_size(axis)
    return lax.ppermute(block, axis, [(i, i ^ bit) for i in range(size)])


def gather_rows(base_weight):
    x = lax.axis_index("parts")
    own = lax.dynamic_slice_in_dim(base_weight, x * HALF, HALF, 0)
    other = lax.dynamic_slice_in_dim(base_weight, (1 - x) * HALF, HALF, 0)
    blocks = {(0, 0, 0, 0): own}
    blocks[0, 1, 0, 0] = swap(own, "line", 1)
    blocks[0, 2, 0, 0] = swap(own, "line", 2)
    blocks[0, 3, 0, 0] = swap(blocks[0, 2, 0, 0], "line", 1)
    for z in range(4):
        blocks[0, z, 1, 0] = swap(blocks[0, z, 0, 0], "plane", 1)
    for z in range(4):
        for y in range(2):
            source = blocks[0, z, y, 0]
            blocks[1, z, y, 0] = other if z == y == 0 else swap(source, "parts", 1)
    for (x, z, y, _), block in list(blocks.items()):
        blocks[x, z, y, 1] = swap(block, "core", 1)
    return blocks


def exchange(messages, first):
    store = AXES[1:]
    groups = len(messages)

    def send(k, *others):
        pairs = [(i, i ^ k) for i in range(groups)]
        return lax.ppermute(after(messages[k], *others), store, pairs)

    arrived = {0: messages[0]}
    across = [k for k in range(1, groups) if k >= groups // 2]
    near = [k for k in range(1, groups) if k < groups // 2]
    for n, k in enumerate(across):
        arrived[k] = send(k, arrived[across[n - 2]] if n >= 2 else first)
    for n, k in enumerate(near):
        arrived[k] = send(k, arrived[across[n]])
    return [arrived[k] for k in range(groups)]


def body(
    tokens, base_weight, adapter_down, adapter_up, request_lengths, group_adapters, request_slot
):
    rank = adapter_down.shape[2]
    choices = group_adapters.shape[1]
    group = store_index()
    shard_width = adapter_up.shape[1]
    messages = make_messages(
        jnp.transpose(group_adapters),
        jnp.swapaxes(adapter_down, 1, 2),
        jnp.transpose(adapter_up, (1, 2, 0)).reshape(shard_width * rank, adapter_up.shape[0]),
        shard_width,
    )
    blocks = gather_rows(base_weight)
    arrived = exchange(messages, blocks[0, 1, 0, 0])
    slots = lax.dynamic_index_in_dim(request_slot, group, 0, keepdims=False)
    slot_of_row = row_slots(request_lengths[0], slots, tokens.shape[0])
    lane_slot = jnp.arange(choices * rank, dtype=jnp.int32)[None, :] // rank
    mask = (slot_of_row[:, None] == lane_slot).astype(jnp.float32)
    base = base_product(tokens, list(blocks.items()))
    return adapt(tokens, arrived, mask, base)


def plain_body(
    tokens, base_weight, adapter_down, adapter_up, request_lengths, group_adapters, request_slot
):
    store = AXES[1:]
    rank = adapter_down.shape[2]
    choices = group_adapters.shape[1]
    group = lax.axis_index(store)
    wanted = jnp.transpose(group_adapters)
    slots = lax.dynamic_index_in_dim(request_slot, group, 0, keepdims=False)
    slot_of_row = row_slots(request_lengths[0], slots, tokens.shape[0])
    lane_slot = jnp.arange(choices * rank, dtype=jnp.int32)[None, :] // rank
    mask = (slot_of_row[:, None] == lane_slot).astype(jnp.float32)
    exchange = functools.partial(
        lax.all_to_all, axis_name=store, split_axis=1, concat_axis=1, tiled=True
    )
    down = exchange(jnp.take(adapter_down, wanted, axis=0))
    up = exchange(jnp.take(adapter_up, wanted, axis=0))
    weight = lax.all_gather(base_weight, store, axis=0, tiled=True)
    down = down.reshape(choices, tokens.shape[1], rank)
    up = up.reshape(choices, base_weight.shape[1], rank)
    base = jnp.dot(tokens, weight, preferred_element_type=jnp.float32)
    shrink = jnp.einsum("td,kdr->tkr", tokens, down, preferred_element_type=jnp.float32)
    picked = (shrink.reshape(mask.shape) * mask).astype(jnp.bfloat16)
    picked = picked.reshape(shrink.shape)
    delta = jnp.einsum("tkr,kvr->tv", picked, up, preferred_element_type=jnp.float32)
    return (base + delta).astype(jnp.bfloat16)


def solution(mesh):
    parts, size = mesh.shape["parts"], mesh.shape["store"]
    chips = size // 2
    plane = 1
    while 4 * plane * plane <= chips:
        plane *= 2
    lines = chips // plane
    split = Mesh(mesh.devices.reshape(parts, lines, plane, 2), AXES)
    store = AXES[1:]

    def run(tokens, base_weight, *rest):
        small = (parts, lines, plane) == (2, 4, 2) and base_weight.shape[0] // size == 2 * HALF
        return jax.shard_map(
            body if small else plain_body,
            mesh=split,
            in_specs=(
                P(AXES, None),
                P(store, None),
                P(None, store, None),
                P(None, store, None),
                P(AXES, None),
                P("parts", None),
                P("parts", None),
            ),
            out_specs=P(AXES, None),
            check_vma=False,
        )(tokens, base_weight, *rest)

    return run
```

time: 144 us -> 130 us (0.903)
  waiting for transfers between devices: 87.3 us -> 48.9 us
  local copies, waits for them, and re-layouts: 3.29 us -> 24.1 us
  starting transfers between devices: 28.4 us -> 42.7 us
  Pallas kernels: 22.1 us -> 12.4 us
    ppermute x30, waiting for transfers between devices: 87.3 us -> 25.4 us  [swap(): return lax.ppermute(block, axis, [(i, i ^ bit) for i in range(size)])]
    ppermute x0 -> x15, waiting for transfers between devices: none -> 23.5 us  [send(): return lax.ppermute(after(messages[k], *others), store, pairs)]
    ppermute x0 -> x15, starting transfers between devices: none -> 21.7 us  [send(): return lax.ppermute(after(messages[k], *others), store, pairs)]
    unnamed x54 -> x70, local copies, waits for them, and re-layouts: 3.17 us -> 22.9 us
    pallas_call x3 -> x18, Pallas kernels: 22.1 us -> 12.4 us  [the longest x1 5.77 us: base_product(): pl.pallas_call(kernel, out_shape=pltpu.VMEM((rows, width), jnp.float32),...]
    all_to_all x1 -> x0, starting transfers between devices: 7.4 us -> none  [body(): lax.all_to_all(messages, store, split_axis=0, concat_axis=0, tiled=True)]
  transfers between devices with their start and end apart: 31 -> 45, of which waited for: 11 -> 13; matrix products, arithmetic and copies ran while one was open for 1% -> 1% of each run, Pallas kernels for 6% -> 7%
where the time goes in v4:
time: 130 us; the launch traced here: 129 us
  waiting for transfers between devices  48.9 us (38%)
  starting transfers between devices  42.7 us (33%)
  local copies, waits for them, and re-layouts  24.1 us (19%)
  Pallas kernels  12.4 us (10%)
    ppermute x30, waiting for transfers between devices, swap(): return lax.ppermute(block, axis, [(i, i ^ bit) for i in range(size)])  25.4 us
    ppermute x15, waiting for transfers between devices, send(): return lax.ppermute(after(messages[k], *others), store, pairs)  23.5 us
    unnamed x70, local copies, waits for them, and re-layouts  22.9 us
    ppermute x15, starting transfers between devices, send(): return lax.ppermute(after(messages[k], *others), store, pairs)  21.7 us
    ppermute x30, starting transfers between devices, swap(): return lax.ppermute(block, axis, [(i, i ^ bit) for i in range(size)])  20.9 us
    pallas_call x1, Pallas kernels, base_product(): pl.pallas_call(kernel, out_shape=pltpu.VMEM((rows, width), jnp.float32),...  5.77 us
    pallas_call x1, Pallas kernels, adapt(): pl.pallas_call(adapt_kernel, out_shape=jax.ShapeDtypeStruct((rows, width)...  3.54 us
    pallas_call x1, Pallas kernels, make_messages(): pl.pallas_call(functools.partial(send_kernel, groups), out_shape=[pltpu.V...  3.05 us
  transfers between devices with their start and end apart: 45, of which 13 were waited for; matrix products, arithmetic and copies ran while one was open for 1% of the time, Pallas kernels for 7%

profile of v4, /device:TPU:0, one launch (start us, length us, event | category | flops | bytes accessed | tf_op | source)
XLA Modules:
  0.0 129.4 jit_solution(9431266406780433360)
XLA Ops:
  0.0 1.1 constant_dynamic-slice_fusion
  1.1 4.1 %collective-permute-start.1 = (bf16[256,512]{1,0:T(8,128)(2,1)S(1)}, bf16[256,512]{1,0:T(8,128)(2,1)S(1)}, u32[]{:S(2)}, u32[]{:S(2)}) collective-permute-start(bf16[256,512]{1,0:T(8,128)(2,1)S(1)} %get-tuple-element.38.refs_0_), channel_id=1, source_target_pairs={{0,8},{4,12},{8,0},{12,4},{1,9},{5,13},{9,1},{13,5},{2,10},{6,14},... | collective-permute-start | bytes 786440 | tf_op jit(solution)/shard_map/ppermute | solution.py:219
  5.2 1.6 %collective-permute-start = (bf16[256,512]{1,0:T(8,128)(2,1)S(1)}, bf16[256,512]{1,0:T(8,128)(2,1)S(1)}, u32[]{:S(2)}, u32[]{:S(2)}) collective-permute-start(bf16[256,512]{1,0:T(8,128)(2,1)S(1)} %get-tuple-element.38.refs_0_), channel_id=1, source_target_pairs={{0,4},{4,0},{8,12},{12,8},{1,5},{5,1},{9,13},{13,9},{2,6},{6,2},{1... | collective-permute-start | bytes 786440 | tf_op jit(solution)/shard_map/ppermute | solution.py:219
  6.8 1.5 %collective-permute-start.3 = (bf16[256,512]{1,0:T(8,128)(2,1)S(1)}, bf16[256,512]{1,0:T(8,128)(2,1)S(1)}, u32[]{:S(2)}, u32[]{:S(2)}) collective-permute-start(bf16[256,512]{1,0:T(8,128)(2,1)S(1)} %get-tuple-element.38.refs_0_), channel_id=1, source_target_pairs={{0,2},{2,0},{1,3},{3,1},{4,6},{6,4},{5,7},{7,5},{8,10},{10,8},{9,1... | collective-permute-start | bytes 786440 | tf_op jit(solution)/shard_map/ppermute | solution.py:219
  8.8 8.4 %collective-permute-done.1.refs_2_ = bf16[256,512]{1,0:T(8,128)(2,1)S(1)} collective-permute-done((bf16[256,512]{1,0:T(8,128)(2,1)S(1)}, bf16[256,512]{1,0:T(8,128)(2,1)S(1)}, u32[]{:S(2)}, u32[]{:S(2)}) %collective-permute-start.1) | collective-permute-done | bytes 262176 | tf_op jit(solution)/shard_map/ppermute | solution.py:219
  17.2 0.6 collective-permute-start.2
  17.8 3.4 %copy-done.1 = bf16[128,512,64]{1,2,0:T(8,128)(2,1)S(1)} copy-done((bf16[128,512,64]{1,2,0:T(8,128)(2,1)S(1)}, bf16[128,512,64]{1,2,0:T(8,128)(2,1)}, u32[]{:S(2)}) %copy-start.1) | copy-done | bytes 8388632
  21.2 1.0 copy-done.2
  22.3 0.7 copy-done.33
  22.9 3.1 %make_messages.1 = (bf16[272,256]{1,0:T(8,128)(2,1)S(1)}, bf16[272,256]{1,0:T(8,128)(2,1)S(1)}, bf16[272,256]{1,0:T(8,128)(2,1)S(1)}, bf16[272,256]{1,0:T(8,128)...) custom-call(s32[2,16]{1,0:T(2,128)S(1)} %bitcast.16, ...), custom_call_target="tpu_custom_call" | custom-call | tf_op jit(solution)/shard_map/make_messages/pallas_call | solution.py:77
  26.0 3.4 %collective-permute-start.30 = (bf16[272,256]{1,0:T(8,128)(2,1)S(1)}, bf16[272,256]{1,0:T(8,128)(2,1)S(1)}, u32[]{:S(2)}, u32[]{:S(2)}) collective-permute-start(bf16[272,256]{1,0:T(8,128)(2,1)S(1)} %after.15), channel_id=1, source_target_pairs={{0,8},{1,9},{2,10},{3,11},{4,12},{5,13},{6,14},{7,15},{8,0},{9,1},... | collective-permute-start | bytes 417800 | tf_op jit(solution)/shard_map/ppermute | solution.py:247
  29.5 1.5 %collective-permute-start.4 = (bf16[256,512]{1,0:T(8,128)(2,1)S(1)}, bf16[256,512]{1,0:T(8,128)(2,1)S(1)}, u32[]{:S(2)}, u32[]{:S(2)}) collective-permute-start(bf16[256,512]{1,0:T(8,128)(2,1)S(1)} %collective-permute-done.refs_1_), channel_id=1, source_target_pairs={{0,2},{2,0},{1,3},{3,1},{4,6},{6,4},{5,7},{7,5},{8,10},{10,8},{9,1... | collective-permute-start | bytes 786440 | tf_op jit(solution)/shard_map/ppermute | solution.py:219
  31.5 7.3 %collective-permute-done.30.refs_1_.refs_8_ = bf16[272,256]{1,0:T(8,128)(2,1)S(1)} collective-permute-done((bf16[272,256]{1,0:T(8,128)(2,1)S(1)}, bf16[272,256]{1,0:T(8,128)(2,1)S(1)}, u32[]{:S(2)}, u32[]{:S(2)}) %collective-permute-start.30) | collective-permute-done | bytes 139296 | tf_op jit(solution)/shard_map/ppermute | solution.py:247
  38.8 1.5 %collective-permute-start.8 = (bf16[256,512]{1,0:T(8,128)(2,1)S(1)}, bf16[256,512]{1,0:T(8,128)(2,1)S(1)}, u32[]{:S(2)}, u32[]{:S(2)}) collective-permute-start(bf16[256,512]{1,0:T(8,128)(2,1)S(1)} %collective-permute-done.refs_1_), channel_id=1, source_target_pairs={{0,16},{16,0},{1,17},{17,1},{2,18},{18,2},{3,19},{19,3},{4,20},{20... | collective-permute-start | bytes 786440 | tf_op jit(solution)/shard_map/ppermute | solution.py:219
  40.3 1.3 %collective-permute-done.32.refs_1_.refs_9_ = bf16[272,256]{1,0:T(8,128)(2,1)S(1)} collective-permute-done((bf16[272,256]{1,0:T(8,128)(2,1)S(1)}, bf16[272,256]{1,0:T(8,128)(2,1)S(1)}, u32[]{:S(2)}, u32[]{:S(2)}) %collective-permute-start.32) | collective-permute-done | bytes 139296 | tf_op jit(solution)/shard_map/ppermute | solution.py:247
  41.6 1.5 %collective-permute-start.10 = (bf16[256,512]{1,0:T(8,128)(2,1)S(1)}, bf16[256,512]{1,0:T(8,128)(2,1)S(1)}, u32[]{:S(2)}, u32[]{:S(2)}) collective-permute-start(bf16[256,512]{1,0:T(8,128)(2,1)S(1)} %collective-permute-done.1.refs_2_), channel_id=1, source_target_pairs={{0,16},{16,0},{1,17},{17,1},{2,18},{18,2},{3,19},{19,3},{4,20},{20... | collective-permute-start | bytes 786440 | tf_op jit(solution)/shard_map/ppermute | solution.py:219
  43.7 0.6 collective-permute-start.7
  44.3 3.7 %collective-permute-done.8.refs_10_ = bf16[256,512]{1,0:T(8,128)(2,1)S(1)} collective-permute-done((bf16[256,512]{1,0:T(8,128)(2,1)S(1)}, bf16[256,512]{1,0:T(8,128)(2,1)S(1)}, u32[]{:S(2)}, u32[]{:S(2)}) %collective-permute-start.8) | collective-permute-done | bytes 262176 | tf_op jit(solution)/shard_map/ppermute | solution.py:219
  48.0 5.6 %collective-permute-done.10.refs_12_ = bf16[256,512]{1,0:T(8,128)(2,1)S(1)} collective-permute-done((bf16[256,512]{1,0:T(8,128)(2,1)S(1)}, bf16[256,512]{1,0:T(8,128)(2,1)S(1)}, u32[]{:S(2)}, u32[]{:S(2)}) %collective-permute-start.10) | collective-permute-done | bytes 262176 | tf_op jit(solution)/shard_map/ppermute | solution.py:219
  54.1 0.7 collective-permute-start.36
  54.8 2.7 %collective-permute-start.31 = (bf16[272,256]{1,0:T(8,128)(2,1)S(1)}, bf16[272,256]{1,0:T(8,128)(2,1)S(1)}, u32[]{:S(2)}, u32[]{:S(2)}) collective-permute-start(bf16[272,256]{1,0:T(8,128)(2,1)S(1)} %after.16), channel_id=1, source_target_pairs={{0,1},{1,0},{2,3},{3,2},{4,5},{5,4},{6,7},{7,6},{8,9},{9,8},{10,11... | collective-permute-start | bytes 417800 | tf_op jit(solution)/shard_map/ppermute | solution.py:247
  57.6 0.6 collective-permute-done.7.refs_9_
  58.2 1.5 %collective-permute-start.33 = (bf16[272,256]{1,0:T(8,128)(2,1)S(1)}, bf16[272,256]{1,0:T(8,128)(2,1)S(1)}, u32[]{:S(2)}, u32[]{:S(2)}) collective-permute-start(bf16[272,256]{1,0:T(8,128)(2,1)S(1)} %after.18), channel_id=1, source_target_pairs={{0,2},{1,3},{2,0},{3,1},{4,6},{5,7},{6,4},{7,5},{8,10},{9,11},{10,... | collective-permute-start | bytes 417800 | tf_op jit(solution)/shard_map/ppermute | solution.py:247
  59.7 6.7 %collective-permute-done.34.refs_1_.refs_10_ = bf16[272,256]{1,0:T(8,128)(2,1)S(1)} collective-permute-done((bf16[272,256]{1,0:T(8,128)(2,1)S(1)}, bf16[272,256]{1,0:T(8,128)(2,1)S(1)}, u32[]{:S(2)}, u32[]{:S(2)}) %collective-permute-start.34) | collective-permute-done | bytes 139296 | tf_op jit(solution)/shard_map/ppermute | solution.py:247
  66.5 1.1 collective-permute-start.6
  67.6 1.5 %collective-permute-start.9 = (bf16[256,512]{1,0:T(8,128)(2,1)S(1)}, bf16[256,512]{1,0:T(8,128)(2,1)S(1)}, u32[]{:S(2)}, u32[]{:S(2)}) collective-permute-start(bf16[256,512]{1,0:T(8,128)(2,1)S(1)} %collective-permute-done.4.refs_5_), channel_id=1, source_target_pairs={{0,16},{16,0},{1,17},{17,1},{2,18},{18,2},{3,19},{19,3},{4,20},{20... | collective-permute-start | bytes 786440 | tf_op jit(solution)/shard_map/ppermute | solution.py:219
  69.1 0.7 copy-done.13
  69.8 1.0 collective-permute-start.38
  70.8 0.7 copy-done.21
  71.5 2.0 %collective-permute-start.40 = (bf16[272,256]{1,0:T(8,128)(2,1)S(1)}, bf16[272,256]{1,0:T(8,128)(2,1)S(1)}, u32[]{:S(2)}, u32[]{:S(2)}) collective-permute-start(bf16[272,256]{1,0:T(8,128)(2,1)S(1)} %after.25), channel_id=1, source_target_pairs={{0,13},{1,12},{2,15},{3,14},{4,9},{5,8},{6,11},{7,10},{8,5},{9,4},... | collective-permute-start | bytes 417800 | tf_op jit(solution)/shard_map/ppermute | solution.py:247
  73.5 0.7 copy-done.23
  74.2 1.4 %collective-permute-start.35 = (bf16[272,256]{1,0:T(8,128)(2,1)S(1)}, bf16[272,256]{1,0:T(8,128)(2,1)S(1)}, u32[]{:S(2)}, u32[]{:S(2)}) collective-permute-start(bf16[272,256]{1,0:T(8,128)(2,1)S(1)} %after.20), channel_id=1, source_target_pairs={{0,3},{1,2},{2,1},{3,0},{4,7},{5,6},{6,5},{7,4},{8,11},{9,10},{10,... | collective-permute-start | bytes 417800 | tf_op jit(solution)/shard_map/ppermute | solution.py:247
  75.5 2.5 %collective-permute-done.38.refs_1_.refs_12_ = bf16[272,256]{1,0:T(8,128)(2,1)S(1)} collective-permute-done((bf16[272,256]{1,0:T(8,128)(2,1)S(1)}, bf16[272,256]{1,0:T(8,128)(2,1)S(1)}, u32[]{:S(2)}, u32[]{:S(2)}) %collective-permute-start.38) | collective-permute-done | bytes 139296 | tf_op jit(solution)/shard_map/ppermute | solution.py:247
  78.0 0.5 collective-permute-start.12
  78.6 0.7 collective-permute-done.40.refs_1_.refs_13_
  79.3 0.8 collective-permute-start.11
  80.1 0.6 copy-done.25
  81.6 0.7 copy-done.17
  82.9 0.9 copy-done.31
  83.8 0.7 copy-done.32
  84.4 1.9 %collective-permute-done.12.refs_14_ = bf16[256,512]{1,0:T(8,128)(2,1)} collective-permute-done((bf16[256,512]{1,0:T(8,128)(2,1)S(1)}, bf16[256,512]{1,0:T(8,128)(2,1)}, u32[]{:S(2)}, u32[]{:S(2)}) %collective-permute-start.12) | collective-permute-done | bytes 262176 | tf_op jit(solution)/shard_map/ppermute | solution.py:219
  86.3 3.8 %collective-permute-done.11.refs_13_ = bf16[256,512]{1,0:T(8,128)(2,1)} collective-permute-done((bf16[256,512]{1,0:T(8,128)(2,1)S(1)}, bf16[256,512]{1,0:T(8,128)(2,1)}, u32[]{:S(2)}, u32[]{:S(2)}) %collective-permute-start.11) | collective-permute-done | bytes 262176 | tf_op jit(solution)/shard_map/ppermute | solution.py:219
  90.1 0.5 collective-permute-start.23
  90.7 1.7 %collective-permute-start.42 = (bf16[272,256]{1,0:T(8,128)(2,1)}, bf16[272,256]{1,0:T(8,128)(2,1)S(1)}, u32[]{:S(2)}, u32[]{:S(2)}) collective-permute-start(bf16[272,256]{1,0:T(8,128)(2,1)} %copy-done.32), channel_id=1, source_target_pairs={{0,14},{1,15},{2,12},{3,13},{4,10},{5,11},{6,8},{7,9},{8,6},{9,7},... | collective-permute-start | bytes 417800 | tf_op jit(solution)/shard_map/ppermute | solution.py:247
  92.4 0.5 collective-permute-start.13
  92.9 0.7 fusion.1
  94.4 4.9 %collective-permute-done.42.refs_1_.refs_14_ = bf16[272,256]{1,0:T(8,128)(2,1)S(1)} collective-permute-done((bf16[272,256]{1,0:T(8,128)(2,1)}, bf16[272,256]{1,0:T(8,128)(2,1)S(1)}, u32[]{:S(2)}, u32[]{:S(2)}) %collective-permute-start.42) | collective-permute-done | bytes 139296 | tf_op jit(solution)/shard_map/ppermute | solution.py:247
  99.3 1.3 collective-permute-done.13.refs_15_
  100.8 0.9 copy-done.28
  101.7 0.7 copy-done.29
  102.4 2.7 %collective-permute-start.37 = (bf16[272,256]{1,0:T(8,128)(2,1)}, bf16[272,256]{1,0:T(8,128)(2,1)S(1)}, u32[]{:S(2)}, u32[]{:S(2)}) collective-permute-start(bf16[272,256]{1,0:T(8,128)(2,1)} %after.22), channel_id=1, source_target_pairs={{0,4},{1,5},{2,6},{3,7},{4,0},{5,1},{6,2},{7,3},{8,12},{9,13},{10,... | collective-permute-start | bytes 417800 | tf_op jit(solution)/shard_map/ppermute | solution.py:247
  105.3 2.6 %collective-permute-start.41 = (bf16[272,256]{1,0:T(8,128)(2,1)}, bf16[272,256]{1,0:T(8,128)(2,1)S(1)}, u32[]{:S(2)}, u32[]{:S(2)}) collective-permute-start(bf16[272,256]{1,0:T(8,128)(2,1)} %after.26), channel_id=1, source_target_pairs={{0,6},{1,7},{2,4},{3,5},{4,2},{5,3},{6,0},{7,1},{8,14},{9,15},{10,... | collective-permute-start | bytes 417800 | tf_op jit(solution)/shard_map/ppermute | solution.py:247
  107.9 0.9 collective-permute-start.44
  109.1 3.4 %copy-done = bf16[512,8192]{1,0:T(8,128)(2,1)S(1)} copy-done((bf16[512,8192]{1,0:T(8,128)(2,1)S(1)}, bf16[512,8192]{1,0:T(8,128)(2,1)}, u32[]{:S(2)}) %copy-start) | copy-done | bytes 8388632
  112.4 0.9 copy-done.4
  113.4 0.9 copy-done.6
  114.3 0.9 copy-done.8
  115.3 0.9 copy-done.10
  116.2 0.9 copy-done.12
  117.2 0.9 copy-done.14
  118.1 0.9 copy-done.16
  119.1 0.9 copy-done.18
  120.0 5.8 %base_product.1.base = f32[512,512]{1,0:T(8,128)S(1)} custom-call(bf16[512,8192]{1,0:T(8,128)(2,1)S(1)} %copy-done, bf16[256,512]{1,0:T(8,128)(2,1)S(1)} %get-tuple-element.38.refs_0_, bf16[256,512]{1,0:T(8,128)(2,1)S(1)} %collective-permute-done.refs_1_, bf16[256,512]{1,0:T(8,128)(2,1)S(1)} %collective-permute-done.1.refs_2_, ...), custom_call_target="tpu_custom_call" | custom-call | flops 4294967296 | bytes 17825792 | tf_op jit(solution)/shard_map/base_product/pallas_call | solution.py:123
  125.9 3.5 %adapt.1 = bf16[512,512]{1,0:T(8,128)(2,1)} custom-call(bf16[512,8192]{1,0:T(8,128)(2,1)S(1)} %copy-done, f32[512,128]{1,0:T(8,128)S(1)} %compare_convert_fusion.mask, f32[512,512]{1,0:T(8,128)S(1)} %base_product.1.base, bf16[272,256]{1,0:T(8,128)(2,1)S(1)} %copy-done.20, bf16[272,256]{1,0:T(8,128)(2,1)S(1)} %copy-done.22, bf16[272,256]{1,0:T(8,128)(2,1)S(1)} %copy-done.24, ...), custom_call_target="tpu_custom_call" | custom-call | flops 1073741824 | bytes 12189696 | tf_op jit(solution)/shard_map/adapt/pallas_call | solution.py:175
  (122 shorter events, 5.0 us)
Async XLA Ops:
  0.0 82.6 %copy-start.34 = (s32[1,16]{1,0:T(1,128)S(1)}, s32[1,16]{1,0:T(1,128)}, u32[]{:S(2)}) copy-start(s32[1,16]{1,0:T(1,128)} %param.11) | copy-start | bytes 196
  1.1 16.1 %collective-permute-start.1 = (bf16[256,512]{1,0:T(8,128)(2,1)S(1)}, bf16[256,512]{1,0:T(8,128)(2,1)S(1)}, u32[]{:S(2)}, u32[]{:S(2)}) collective-permute-start(bf16[256,512]{1,0:T(8,128)(2,1)S(1)} %get-tuple-element.38.refs_0_), channel_id=1, source_target_pairs={{0,8},{4,12},{8,0},{12,4},{1,9},{5,13},{9,1},{13,5},{2,10},{6,14},... | collective-permute-start | bytes 786440 | tf_op jit(solution)/shard_map/ppermute | solution.py:219
  5.2 20.8 %collective-permute-start = (bf16[256,512]{1,0:T(8,128)(2,1)S(1)}, bf16[256,512]{1,0:T(8,128)(2,1)S(1)}, u32[]{:S(2)}, u32[]{:S(2)}) collective-permute-start(bf16[256,512]{1,0:T(8,128)(2,1)S(1)} %get-tuple-element.38.refs_0_), channel_id=1, source_target_pairs={{0,4},{4,0},{8,12},{12,8},{1,5},{5,1},{9,13},{13,9},{2,6},{6,2},{1... | collective-permute-start | bytes 786440 | tf_op jit(solution)/shard_map/ppermute | solution.py:219
  6.8 22.7 %collective-permute-start.3 = (bf16[256,512]{1,0:T(8,128)(2,1)S(1)}, bf16[256,512]{1,0:T(8,128)(2,1)S(1)}, u32[]{:S(2)}, u32[]{:S(2)}) collective-permute-start(bf16[256,512]{1,0:T(8,128)(2,1)S(1)} %get-tuple-element.38.refs_0_), channel_id=1, source_target_pairs={{0,2},{2,0},{1,3},{3,1},{4,6},{6,4},{5,7},{7,5},{8,10},{10,8},{9,1... | collective-permute-start | bytes 786440 | tf_op jit(solution)/shard_map/ppermute | solution.py:219
  8.3 22.7 %collective-permute-start.14 = (bf16[256,512]{1,0:T(8,128)(2,1)S(1)}, bf16[256,512]{1,0:T(8,128)(2,1)S(1)}, u32[]{:S(2)}, u32[]{:S(2)}) collective-permute-start(bf16[256,512]{1,0:T(8,128)(2,1)S(1)} %get-tuple-element.38.refs_0_), channel_id=1, source_target_pairs={{0,1},{1,0},{2,3},{3,2},{4,5},{5,4},{6,7},{7,6},{8,9},{9,8},{10,11... | collective-permute-start | bytes 786440 | tf_op jit(solution)/shard_map/ppermute | solution.py:219
  8.3 23.2 %collective-permute-start.22 = (bf16[256,512]{1,0:T(8,128)(2,1)S(1)}, bf16[256,512]{1,0:T(8,128)(2,1)S(1)}, u32[]{:S(2)}, u32[]{:S(2)}) collective-permute-start(bf16[256,512]{1,0:T(8,128)(2,1)S(1)} %get-tuple-element.37.refs_8_), channel_id=1, source_target_pairs={{0,1},{1,0},{2,3},{3,2},{4,5},{5,4},{6,7},{7,6},{8,9},{9,8},{10,11... | collective-permute-start | bytes 786440 | tf_op jit(solution)/shard_map/ppermute | solution.py:219
  17.2 25.9 %collective-permute-start.2 = (bf16[256,512]{1,0:T(8,128)(2,1)S(1)}, bf16[256,512]{1,0:T(8,128)(2,1)S(1)}, u32[]{:S(2)}, u32[]{:S(2)}) collective-permute-start(bf16[256,512]{1,0:T(8,128)(2,1)S(1)} %collective-permute-done.1.refs_2_), channel_id=1, source_target_pairs={{0,4},{4,0},{8,12},{12,8},{1,5},{5,1},{9,13},{13,9},{2,6},{6,2},{1... | collective-permute-start | bytes 786440 | tf_op jit(solution)/shard_map/ppermute | solution.py:219
  17.8 3.4 %copy-start.1 = (bf16[128,512,64]{1,2,0:T(8,128)(2,1)S(1)}, bf16[128,512,64]{1,2,0:T(8,128)(2,1)}, u32[]{:S(2)}) copy-start(bf16[128,512,64]{1,2,0:T(8,128)(2,1)} %param.9) | copy-start | bytes 25165828
  21.2 1.0 copy-start.2
  26.0 55.2 %copy-start.19 = (bf16[272,256]{1,0:T(8,128)(2,1)}, bf16[272,256]{1,0:T(8,128)(2,1)S(1)}, u32[]{:S(2)}) copy-start(bf16[272,256]{1,0:T(8,128)(2,1)S(1)} %get-tuple-element.21.refs_0_) | copy-start | bytes 417796
  26.0 55.2 %copy-start.27 = (bf16[272,256]{1,0:T(8,128)(2,1)}, bf16[272,256]{1,0:T(8,128)(2,1)S(1)}, u32[]{:S(2)}) copy-start(bf16[272,256]{1,0:T(8,128)(2,1)S(1)} %get-tuple-element.36.refs_0_) | copy-start | bytes 417796
  26.0 55.2 %copy-start.30 = (bf16[272,256]{1,0:T(8,128)(2,1)}, bf16[272,256]{1,0:T(8,128)(2,1)S(1)}, u32[]{:S(2)}) copy-start(bf16[272,256]{1,0:T(8,128)(2,1)S(1)} %get-tuple-element.35.refs_0_) | copy-start | bytes 417796
  26.0 12.8 %collective-permute-start.30 = (bf16[272,256]{1,0:T(8,128)(2,1)S(1)}, bf16[272,256]{1,0:T(8,128)(2,1)S(1)}, u32[]{:S(2)}, u32[]{:S(2)}) collective-permute-start(bf16[272,256]{1,0:T(8,128)(2,1)S(1)} %after.15), channel_id=1, source_target_pairs={{0,8},{1,9},{2,10},{3,11},{4,12},{5,13},{6,14},{7,15},{8,0},{9,1},... | collective-permute-start | bytes 417800 | tf_op jit(solution)/shard_map/ppermute | solution.py:247
  29.5 13.7 %collective-permute-start.4 = (bf16[256,512]{1,0:T(8,128)(2,1)S(1)}, bf16[256,512]{1,0:T(8,128)(2,1)S(1)}, u32[]{:S(2)}, u32[]{:S(2)}) collective-permute-start(bf16[256,512]{1,0:T(8,128)(2,1)S(1)} %collective-permute-done.refs_1_), channel_id=1, source_target_pairs={{0,2},{2,0},{1,3},{3,1},{4,6},{6,4},{5,7},{7,5},{8,10},{10,8},{9,1... | collective-permute-start | bytes 786440 | tf_op jit(solution)/shard_map/ppermute | solution.py:219
  31.0 12.6 %collective-permute-start.5 = (bf16[256,512]{1,0:T(8,128)(2,1)S(1)}, bf16[256,512]{1,0:T(8,128)(2,1)S(1)}, u32[]{:S(2)}, u32[]{:S(2)}) collective-permute-start(bf16[256,512]{1,0:T(8,128)(2,1)S(1)} %collective-permute-done.1.refs_2_), channel_id=1, source_target_pairs={{0,2},{2,0},{1,3},{3,1},{4,6},{6,4},{5,7},{7,5},{8,10},{10,8},{9,1... | collective-permute-start | bytes 786440 | tf_op jit(solution)/shard_map/ppermute | solution.py:219
  31.5 10.1 %collective-permute-start.32 = (bf16[272,256]{1,0:T(8,128)(2,1)S(1)}, bf16[272,256]{1,0:T(8,128)(2,1)S(1)}, u32[]{:S(2)}, u32[]{:S(2)}) collective-permute-start(bf16[272,256]{1,0:T(8,128)(2,1)S(1)} %after.17), channel_id=1, source_target_pairs={{0,9},{1,8},{2,11},{3,10},{4,13},{5,12},{6,15},{7,14},{8,1},{9,0},... | collective-permute-start | bytes 417800 | tf_op jit(solution)/shard_map/ppermute | solution.py:247
  38.8 9.2 %collective-permute-start.8 = (bf16[256,512]{1,0:T(8,128)(2,1)S(1)}, bf16[256,512]{1,0:T(8,128)(2,1)S(1)}, u32[]{:S(2)}, u32[]{:S(2)}) collective-permute-start(bf16[256,512]{1,0:T(8,128)(2,1)S(1)} %collective-permute-done.refs_1_), channel_id=1, source_target_pairs={{0,16},{16,0},{1,17},{17,1},{2,18},{18,2},{3,19},{19,3},{4,20},{20... | collective-permute-start | bytes 786440 | tf_op jit(solution)/shard_map/ppermute | solution.py:219
  41.6 12.0 %collective-permute-start.10 = (bf16[256,512]{1,0:T(8,128)(2,1)S(1)}, bf16[256,512]{1,0:T(8,128)(2,1)S(1)}, u32[]{:S(2)}, u32[]{:S(2)}) collective-permute-start(bf16[256,512]{1,0:T(8,128)(2,1)S(1)} %collective-permute-done.1.refs_2_), channel_id=1, source_target_pairs={{0,16},{16,0},{1,17},{17,1},{2,18},{18,2},{3,19},{19,3},{4,20},{20... | collective-permute-start | bytes 786440 | tf_op jit(solution)/shard_map/ppermute | solution.py:219
  43.1 11.0 %collective-permute-start.15 = (bf16[256,512]{1,0:T(8,128)(2,1)S(1)}, bf16[256,512]{1,0:T(8,128)(2,1)S(1)}, u32[]{:S(2)}, u32[]{:S(2)}) collective-permute-start(bf16[256,512]{1,0:T(8,128)(2,1)S(1)} %collective-permute-done.refs_1_), channel_id=1, source_target_pairs={{0,1},{1,0},{2,3},{3,2},{4,5},{5,4},{6,7},{7,6},{8,9},{9,8},{10,11... | collective-permute-start | bytes 786440 | tf_op jit(solution)/shard_map/ppermute | solution.py:219
  43.1 11.7 %collective-permute-start.16 = (bf16[256,512]{1,0:T(8,128)(2,1)S(1)}, bf16[256,512]{1,0:T(8,128)(2,1)S(1)}, u32[]{:S(2)}, u32[]{:S(2)}) collective-permute-start(bf16[256,512]{1,0:T(8,128)(2,1)S(1)} %collective-permute-done.1.refs_2_), channel_id=1, source_target_pairs={{0,1},{1,0},{2,3},{3,2},{4,5},{5,4},{6,7},{7,6},{8,9},{9,8},{10,11... | collective-permute-start | bytes 786440 | tf_op jit(solution)/shard_map/ppermute | solution.py:219
  43.7 14.6 %collective-permute-start.7 = (bf16[256,512]{1,0:T(8,128)(2,1)S(1)}, bf16[256,512]{1,0:T(8,128)(2,1)S(1)}, u32[]{:S(2)}, u32[]{:S(2)}) collective-permute-start(bf16[256,512]{1,0:T(8,128)(2,1)S(1)} %collective-permute-done.3.refs_4_), channel_id=1, source_target_pairs={{0,16},{16,0},{1,17},{17,1},{2,18},{18,2},{3,19},{19,3},{4,20},{20... | collective-permute-start | bytes 786440 | tf_op jit(solution)/shard_map/ppermute | solution.py:219
  48.0 33.2 %copy-start.3 = (bf16[256,512]{1,0:T(8,128)(2,1)}, bf16[256,512]{1,0:T(8,128)(2,1)S(1)}, u32[]{:S(2)}) copy-start(bf16[256,512]{1,0:T(8,128)(2,1)S(1)} %collective-permute-done.8.refs_10_) | copy-start | bytes 786436
  48.0 21.1 %collective-permute-start.18 = (bf16[256,512]{1,0:T(8,128)(2,1)S(1)}, bf16[256,512]{1,0:T(8,128)(2,1)S(1)}, u32[]{:S(2)}, u32[]{:S(2)}) collective-permute-start(bf16[256,512]{1,0:T(8,128)(2,1)S(1)} %collective-permute-done.3.refs_4_), channel_id=1, source_target_pairs={{0,1},{1,0},{2,3},{3,2},{4,5},{5,4},{6,7},{7,6},{8,9},{9,8},{10,11... | collective-permute-start | bytes 786440 | tf_op jit(solution)/shard_map/ppermute | solution.py:219
  53.6 27.6 %copy-start.5 = (bf16[256,512]{1,0:T(8,128)(2,1)}, bf16[256,512]{1,0:T(8,128)(2,1)S(1)}, u32[]{:S(2)}) copy-start(bf16[256,512]{1,0:T(8,128)(2,1)S(1)} %collective-permute-done.10.refs_12_) | copy-start | bytes 786436
  53.6 12.8 %collective-permute-start.34 = (bf16[272,256]{1,0:T(8,128)(2,1)S(1)}, bf16[272,256]{1,0:T(8,128)(2,1)S(1)}, u32[]{:S(2)}, u32[]{:S(2)}) collective-permute-start(bf16[272,256]{1,0:T(8,128)(2,1)S(1)} %after.19), channel_id=1, source_target_pairs={{0,10},{1,11},{2,8},{3,9},{4,14},{5,15},{6,12},{7,13},{8,2},{9,3},... | collective-permute-start | bytes 417800 | tf_op jit(solution)/shard_map/ppermute | solution.py:247
  54.1 27.1 %copy-start.7 = (bf16[256,512]{1,0:T(8,128)(2,1)}, bf16[256,512]{1,0:T(8,128)(2,1)S(1)}, u32[]{:S(2)}) copy-start(bf16[256,512]{1,0:T(8,128)(2,1)S(1)} %collective-permute-done.15.refs_17_) | copy-start | bytes 786436
  54.1 13.5 %collective-permute-start.36 = (bf16[272,256]{1,0:T(8,128)(2,1)S(1)}, bf16[272,256]{1,0:T(8,128)(2,1)S(1)}, u32[]{:S(2)}, u32[]{:S(2)}) collective-permute-start(bf16[272,256]{1,0:T(8,128)(2,1)S(1)} %after.21), channel_id=1, source_target_pairs={{0,11},{1,10},{2,9},{3,8},{4,15},{5,14},{6,13},{7,12},{8,3},{9,2},... | collective-permute-start | bytes 417800 | tf_op jit(solution)/shard_map/ppermute | solution.py:247
  54.8 26.4 %copy-start.9 = (bf16[256,512]{1,0:T(8,128)(2,1)}, bf16[256,512]{1,0:T(8,128)(2,1)S(1)}, u32[]{:S(2)}) copy-start(bf16[256,512]{1,0:T(8,128)(2,1)S(1)} %collective-permute-done.16.refs_18_) | copy-start | bytes 786436
  54.8 16.0 %collective-permute-start.31 = (bf16[272,256]{1,0:T(8,128)(2,1)S(1)}, bf16[272,256]{1,0:T(8,128)(2,1)S(1)}, u32[]{:S(2)}, u32[]{:S(2)}) collective-permute-start(bf16[272,256]{1,0:T(8,128)(2,1)S(1)} %after.16), channel_id=1, source_target_pairs={{0,1},{1,0},{2,3},{3,2},{4,5},{5,4},{6,7},{7,6},{8,9},{9,8},{10,11... | collective-permute-start | bytes 417800 | tf_op jit(solution)/shard_map/ppermute | solution.py:247
  58.2 23.1 %copy-start.11 = (bf16[256,512]{1,0:T(8,128)(2,1)}, bf16[256,512]{1,0:T(8,128)(2,1)S(1)}, u32[]{:S(2)}) copy-start(bf16[256,512]{1,0:T(8,128)(2,1)S(1)} %collective-permute-done.7.refs_9_) | copy-start | bytes 786436
  58.2 15.3 %collective-permute-start.33 = (bf16[272,256]{1,0:T(8,128)(2,1)S(1)}, bf16[272,256]{1,0:T(8,128)(2,1)S(1)}, u32[]{:S(2)}, u32[]{:S(2)}) collective-permute-start(bf16[272,256]{1,0:T(8,128)(2,1)S(1)} %after.18), channel_id=1, source_target_pairs={{0,2},{1,3},{2,0},{3,1},{4,6},{5,7},{6,4},{7,5},{8,10},{9,11},{10,... | collective-permute-start | bytes 417800 | tf_op jit(solution)/shard_map/ppermute | solution.py:247
  66.5 14.4 %collective-permute-start.6 = (bf16[256,512]{1,0:T(8,128)(2,1)S(1)}, bf16[256,512]{1,0:T(8,128)(2,1)S(1)}, u32[]{:S(2)}, u32[]{:S(2)}) collective-permute-start(bf16[256,512]{1,0:T(8,128)(2,1)S(1)} %collective-permute-done.2.refs_3_), channel_id=1, source_target_pairs={{0,2},{2,0},{1,3},{3,1},{4,6},{6,4},{5,7},{7,5},{8,10},{10,8},{9,1... | collective-permute-start | bytes 786440 | tf_op jit(solution)/shard_map/ppermute | solution.py:219
  67.6 13.6 %collective-permute-start.9 = (bf16[256,512]{1,0:T(8,128)(2,1)S(1)}, bf16[256,512]{1,0:T(8,128)(2,1)S(1)}, u32[]{:S(2)}, u32[]{:S(2)}) collective-permute-start(bf16[256,512]{1,0:T(8,128)(2,1)S(1)} %collective-permute-done.4.refs_5_), channel_id=1, source_target_pairs={{0,16},{16,0},{1,17},{17,1},{2,18},{18,2},{3,19},{19,3},{4,20},{20... | collective-permute-start | bytes 786440 | tf_op jit(solution)/shard_map/ppermute | solution.py:219
  69.8 8.2 %collective-permute-start.38 = (bf16[272,256]{1,0:T(8,128)(2,1)S(1)}, bf16[272,256]{1,0:T(8,128)(2,1)S(1)}, u32[]{:S(2)}, u32[]{:S(2)}) collective-permute-start(bf16[272,256]{1,0:T(8,128)(2,1)S(1)} %after.23), channel_id=1, source_target_pairs={{0,12},{1,13},{2,14},{3,15},{4,8},{5,9},{6,10},{7,11},{8,4},{9,5},... | collective-permute-start | bytes 417800 | tf_op jit(solution)/shard_map/ppermute | solution.py:247
  71.5 7.8 %collective-permute-start.40 = (bf16[272,256]{1,0:T(8,128)(2,1)S(1)}, bf16[272,256]{1,0:T(8,128)(2,1)S(1)}, u32[]{:S(2)}, u32[]{:S(2)}) collective-permute-start(bf16[272,256]{1,0:T(8,128)(2,1)S(1)} %after.25), channel_id=1, source_target_pairs={{0,13},{1,12},{2,15},{3,14},{4,9},{5,8},{6,11},{7,10},{8,5},{9,4},... | collective-permute-start | bytes 417800 | tf_op jit(solution)/shard_map/ppermute | solution.py:247
  74.2 5.9 %collective-permute-start.35 = (bf16[272,256]{1,0:T(8,128)(2,1)S(1)}, bf16[272,256]{1,0:T(8,128)(2,1)S(1)}, u32[]{:S(2)}, u32[]{:S(2)}) collective-permute-start(bf16[272,256]{1,0:T(8,128)(2,1)S(1)} %after.20), channel_id=1, source_target_pairs={{0,3},{1,2},{2,1},{3,0},{4,7},{5,6},{6,5},{7,4},{8,11},{9,10},{10,... | collective-permute-start | bytes 417800 | tf_op jit(solution)/shard_map/ppermute | solution.py:247
  78.0 8.3 %collective-permute-start.12 = (bf16[256,512]{1,0:T(8,128)(2,1)S(1)}, bf16[256,512]{1,0:T(8,128)(2,1)}, u32[]{:S(2)}, u32[]{:S(2)}) collective-permute-start(bf16[256,512]{1,0:T(8,128)(2,1)S(1)} %collective-permute-done.2.refs_3_), channel_id=1, source_target_pairs={{0,16},{16,0},{1,17},{17,1},{2,18},{18,2},{3,19},{19,3},{4,20},{20... | collective-permute-start | bytes 786440 | tf_op jit(solution)/shard_map/ppermute | solution.py:219
  79.3 10.8 %collective-permute-start.11 = (bf16[256,512]{1,0:T(8,128)(2,1)S(1)}, bf16[256,512]{1,0:T(8,128)(2,1)}, u32[]{:S(2)}, u32[]{:S(2)}) collective-permute-start(bf16[256,512]{1,0:T(8,128)(2,1)S(1)} %collective-permute-done.5.refs_6_), channel_id=1, source_target_pairs={{0,16},{16,0},{1,17},{17,1},{2,18},{18,2},{3,19},{19,3},{4,20},{20... | collective-permute-start | bytes 786440 | tf_op jit(solution)/shard_map/ppermute | solution.py:219
  80.7 9.4 %collective-permute-start.17 = (bf16[256,512]{1,0:T(8,128)(2,1)S(1)}, bf16[256,512]{1,0:T(8,128)(2,1)}, u32[]{:S(2)}, u32[]{:S(2)}) collective-permute-start(bf16[256,512]{1,0:T(8,128)(2,1)S(1)} %collective-permute-done.2.refs_3_), channel_id=1, source_target_pairs={{0,1},{1,0},{2,3},{3,2},{4,5},{5,4},{6,7},{7,6},{8,9},{9,8},{10,11... | collective-permute-start | bytes 786440 | tf_op jit(solution)/shard_map/ppermute | solution.py:219
  80.9 9.8 %collective-permute-start.19 = (bf16[256,512]{1,0:T(8,128)(2,1)S(1)}, bf16[256,512]{1,0:T(8,128)(2,1)}, u32[]{:S(2)}, u32[]{:S(2)}) collective-permute-start(bf16[256,512]{1,0:T(8,128)(2,1)S(1)} %collective-permute-done.4.refs_5_), channel_id=1, source_target_pairs={{0,1},{1,0},{2,3},{3,2},{4,5},{5,4},{6,7},{7,6},{8,9},{9,8},{10,11... | collective-permute-start | bytes 786440 | tf_op jit(solution)/shard_map/ppermute | solution.py:219
  82.3 10.1 %collective-permute-start.20 = (bf16[256,512]{1,0:T(8,128)(2,1)S(1)}, bf16[256,512]{1,0:T(8,128)(2,1)}, u32[]{:S(2)}, u32[]{:S(2)}) collective-permute-start(bf16[256,512]{1,0:T(8,128)(2,1)S(1)} %collective-permute-done.5.refs_6_), channel_id=1, source_target_pairs={{0,1},{1,0},{2,3},{3,2},{4,5},{5,4},{6,7},{7,6},{8,9},{9,8},{10,11... | collective-permute-start | bytes 786440 | tf_op jit(solution)/shard_map/ppermute | solution.py:219
  86.3 7.4 %collective-permute-start.24 = (bf16[256,512]{1,0:T(8,128)(2,1)}, bf16[256,512]{1,0:T(8,128)(2,1)S(1)}, u32[]{:S(2)}, u32[]{:S(2)}) collective-permute-start(bf16[256,512]{1,0:T(8,128)(2,1)} %copy-done.3), channel_id=1, source_target_pairs={{0,1},{1,0},{2,3},{3,2},{4,5},{5,4},{6,7},{7,6},{8,9},{9,8},{10,11... | collective-permute-start | bytes 786440 | tf_op jit(solution)/shard_map/ppermute | solution.py:219
  90.1 3.7 %collective-permute-start.26 = (bf16[256,512]{1,0:T(8,128)(2,1)}, bf16[256,512]{1,0:T(8,128)(2,1)S(1)}, u32[]{:S(2)}, u32[]{:S(2)}) collective-permute-start(bf16[256,512]{1,0:T(8,128)(2,1)} %copy-done.5), channel_id=1, source_target_pairs={{0,1},{1,0},{2,3},{3,2},{4,5},{5,4},{6,7},{7,6},{8,9},{9,8},{10,11... | collective-permute-start | bytes 786440 | tf_op jit(solution)/shard_map/ppermute | solution.py:219
  90.1 4.2 %collective-permute-start.23 = (bf16[256,512]{1,0:T(8,128)(2,1)}, bf16[256,512]{1,0:T(8,128)(2,1)S(1)}, u32[]{:S(2)}, u32[]{:S(2)}) collective-permute-start(bf16[256,512]{1,0:T(8,128)(2,1)} %copy-done.11), channel_id=1, source_target_pairs={{0,1},{1,0},{2,3},{3,2},{4,5},{5,4},{6,7},{7,6},{8,9},{9,8},{10,11... | collective-permute-start | bytes 786440 | tf_op jit(solution)/shard_map/ppermute | solution.py:219
  90.7 8.7 %collective-permute-start.42 = (bf16[272,256]{1,0:T(8,128)(2,1)}, bf16[272,256]{1,0:T(8,128)(2,1)S(1)}, u32[]{:S(2)}, u32[]{:S(2)}) collective-permute-start(bf16[272,256]{1,0:T(8,128)(2,1)} %copy-done.32), channel_id=1, source_target_pairs={{0,14},{1,15},{2,12},{3,13},{4,10},{5,11},{6,8},{7,9},{8,6},{9,7},... | collective-permute-start | bytes 417800 | tf_op jit(solution)/shard_map/ppermute | solution.py:247
  92.4 8.2 %collective-permute-start.13 = (bf16[256,512]{1,0:T(8,128)(2,1)}, bf16[256,512]{1,0:T(8,128)(2,1)S(1)}, u32[]{:S(2)}, u32[]{:S(2)}) collective-permute-start(bf16[256,512]{1,0:T(8,128)(2,1)} %copy-done.15), channel_id=1, source_target_pairs={{0,16},{16,0},{1,17},{17,1},{2,18},{18,2},{3,19},{19,3},{4,20},{20... | collective-permute-start | bytes 786440 | tf_op jit(solution)/shard_map/ppermute | solution.py:219
  93.7 8.7 %collective-permute-start.21 = (bf16[256,512]{1,0:T(8,128)(2,1)}, bf16[256,512]{1,0:T(8,128)(2,1)S(1)}, u32[]{:S(2)}, u32[]{:S(2)}) collective-permute-start(bf16[256,512]{1,0:T(8,128)(2,1)} %copy-done.15), channel_id=1, source_target_pairs={{0,1},{1,0},{2,3},{3,2},{4,5},{5,4},{6,7},{7,6},{8,9},{9,8},{10,11... | collective-permute-start | bytes 786440 | tf_op jit(solution)/shard_map/ppermute | solution.py:219
  93.8 11.3 %collective-permute-start.25 = (bf16[256,512]{1,0:T(8,128)(2,1)}, bf16[256,512]{1,0:T(8,128)(2,1)S(1)}, u32[]{:S(2)}, u32[]{:S(2)}) collective-permute-start(bf16[256,512]{1,0:T(8,128)(2,1)} %copy-done.17), channel_id=1, source_target_pairs={{0,1},{1,0},{2,3},{3,2},{4,5},{5,4},{6,7},{7,6},{8,9},{9,8},{10,11... | collective-permute-start | bytes 786440 | tf_op jit(solution)/shard_map/ppermute | solution.py:219
  94.3 11.0 %collective-permute-start.28 = (bf16[256,512]{1,0:T(8,128)(2,1)}, bf16[256,512]{1,0:T(8,128)(2,1)S(1)}, u32[]{:S(2)}, u32[]{:S(2)}) collective-permute-start(bf16[256,512]{1,0:T(8,128)(2,1)} %collective-permute-done.12.refs_14_), channel_id=1, source_target_pairs={{0,1},{1,0},{2,3},{3,2},{4,5},{5,4},{6,7},{7,6},{8,9},{9,8},{10,11... | collective-permute-start | bytes 786440 | tf_op jit(solution)/shard_map/ppermute | solution.py:219
  99.3 8.6 %collective-permute-start.27 = (bf16[256,512]{1,0:T(8,128)(2,1)}, bf16[256,512]{1,0:T(8,128)(2,1)S(1)}, u32[]{:S(2)}, u32[]{:S(2)}) collective-permute-start(bf16[256,512]{1,0:T(8,128)(2,1)} %collective-permute-done.11.refs_13_), channel_id=1, source_target_pairs={{0,1},{1,0},{2,3},{3,2},{4,5},{5,4},{6,7},{7,6},{8,9},{9,8},{10,11... | collective-permute-start | bytes 786440 | tf_op jit(solution)/shard_map/ppermute | solution.py:219
  100.6 8.1 %collective-permute-start.29 = (bf16[256,512]{1,0:T(8,128)(2,1)S(1)}, bf16[256,512]{1,0:T(8,128)(2,1)S(1)}, u32[]{:S(2)}, u32[]{:S(2)}) collective-permute-start(bf16[256,512]{1,0:T(8,128)(2,1)S(1)} %collective-permute-done.13.refs_15_), channel_id=1, source_target_pairs={{0,1},{1,0},{2,3},{3,2},{4,5},{5,4},{6,7},{7,6},{8,9},{9,8},{10,11... | collective-permute-start | bytes 786440 | tf_op jit(solution)/shard_map/ppermute | solution.py:219
  101.7 24.2 %copy-start.26 = (bf16[272,256]{1,0:T(8,128)(2,1)S(1)}, bf16[272,256]{1,0:T(8,128)(2,1)}, u32[]{:S(2)}) copy-start(bf16[272,256]{1,0:T(8,128)(2,1)} %copy-done.25) | copy-start | bytes 417796
  102.4 23.5 %copy-start.20 = (bf16[272,256]{1,0:T(8,128)(2,1)S(1)}, bf16[272,256]{1,0:T(8,128)(2,1)}, u32[]{:S(2)}) copy-start(bf16[272,256]{1,0:T(8,128)(2,1)} %copy-done.19) | copy-start | bytes 417796
  102.4 23.5 %copy-start.22 = (bf16[272,256]{1,0:T(8,128)(2,1)S(1)}, bf16[272,256]{1,0:T(8,128)(2,1)}, u32[]{:S(2)}) copy-start(bf16[272,256]{1,0:T(8,128)(2,1)} %copy-done.21) | copy-start | bytes 417796
  102.4 23.5 %copy-start.24 = (bf16[272,256]{1,0:T(8,128)(2,1)S(1)}, bf16[272,256]{1,0:T(8,128)(2,1)}, u32[]{:S(2)}) copy-start(bf16[272,256]{1,0:T(8,128)(2,1)} %copy-done.23) | copy-start | bytes 417796
  102.4 23.4 %collective-permute-start.37 = (bf16[272,256]{1,0:T(8,128)(2,1)}, bf16[272,256]{1,0:T(8,128)(2,1)S(1)}, u32[]{:S(2)}, u32[]{:S(2)}) collective-permute-start(bf16[272,256]{1,0:T(8,128)(2,1)} %after.22), channel_id=1, source_target_pairs={{0,4},{1,5},{2,6},{3,7},{4,0},{5,1},{6,2},{7,3},{8,12},{9,13},{10,... | collective-permute-start | bytes 417800 | tf_op jit(solution)/shard_map/ppermute | solution.py:247
  105.1 20.7 %collective-permute-start.39 = (bf16[272,256]{1,0:T(8,128)(2,1)}, bf16[272,256]{1,0:T(8,128)(2,1)S(1)}, u32[]{:S(2)}, u32[]{:S(2)}) collective-permute-start(bf16[272,256]{1,0:T(8,128)(2,1)} %after.24), channel_id=1, source_target_pairs={{0,5},{1,4},{2,7},{3,6},{4,1},{5,0},{6,3},{7,2},{8,13},{9,12},{10,... | collective-permute-start | bytes 417800 | tf_op jit(solution)/shard_map/ppermute | solution.py:247
  105.3 20.5 %collective-permute-start.41 = (bf16[272,256]{1,0:T(8,128)(2,1)}, bf16[272,256]{1,0:T(8,128)(2,1)S(1)}, u32[]{:S(2)}, u32[]{:S(2)}) collective-permute-start(bf16[272,256]{1,0:T(8,128)(2,1)} %after.26), channel_id=1, source_target_pairs={{0,6},{1,7},{2,4},{3,5},{4,2},{5,3},{6,0},{7,1},{8,14},{9,15},{10,... | collective-permute-start | bytes 417800 | tf_op jit(solution)/shard_map/ppermute | solution.py:247
  107.9 18.0 %collective-permute-start.44 = (bf16[272,256]{1,0:T(8,128)(2,1)}, bf16[272,256]{1,0:T(8,128)(2,1)S(1)}, u32[]{:S(2)}, u32[]{:S(2)}) collective-permute-start(bf16[272,256]{1,0:T(8,128)(2,1)} %copy-done.29), channel_id=1, source_target_pairs={{0,15},{1,14},{2,13},{3,12},{4,11},{5,10},{6,9},{7,8},{8,7},{9,6},... | collective-permute-start | bytes 417800 | tf_op jit(solution)/shard_map/ppermute | solution.py:247
  108.7 17.1 %collective-permute-start.43 = (bf16[272,256]{1,0:T(8,128)(2,1)}, bf16[272,256]{1,0:T(8,128)(2,1)S(1)}, u32[]{:S(2)}, u32[]{:S(2)}) collective-permute-start(bf16[272,256]{1,0:T(8,128)(2,1)} %after.28), channel_id=1, source_target_pairs={{0,7},{1,6},{2,5},{3,4},{4,3},{5,2},{6,1},{7,0},{8,15},{9,14},{10,... | collective-permute-start | bytes 417800 | tf_op jit(solution)/shard_map/ppermute | solution.py:247
  109.0 3.4 %copy-start = (bf16[512,8192]{1,0:T(8,128)(2,1)S(1)}, bf16[512,8192]{1,0:T(8,128)(2,1)}, u32[]{:S(2)}) copy-start(bf16[512,8192]{1,0:T(8,128)(2,1)} %tokens.1) | copy-start | bytes 25165828
  112.4 0.9 copy-start.4
  113.4 0.9 copy-start.6
  114.3 0.9 copy-start.8
  (16 other events, 12.6 us)

commit v5 on v4

--- a/solution.py
+++ b/solution.py
@@ -9,7 +9,6 @@
 from jax.sharding import PartitionSpec as P
 
 HALF = 256
-DEEP = 4
 MIB = 1024 * 1024
 AXES = ("parts", "line", "plane", "core")
 
@@ -18,12 +17,16 @@
     return pltpu.with_memory_space_constraint(value, pltpu.VMEM)
 
 
+def in_hbm(value):
+    return pltpu.with_memory_space_constraint(value, pltpu.HBM)
+
+
 def store_index():
     return (lax.axis_index("line") * 2 + lax.axis_index("plane")) * 2 + lax.axis_index("core")
 
 
 def send_kernel(groups, wanted, down, up, *refs):
-    outs, (pick, even_rows, odd_rows, sems) = refs[:groups], refs[groups:]
+    outs, (table, pick, even_rows, odd_rows, table_sem, sems) = refs[:groups], refs[groups:]
     choices = wanted.shape[0]
     rank = down.shape[1]
     halves = down.shape[2] // HALF
@@ -39,15 +42,18 @@
                 )
                 copy.start()
                 copies.append(copy)
+    table_copy = pltpu.make_async_copy(up, table, table_sem)
+    table_copy.start()
 
     ids = lax.broadcasted_iota(jnp.int32, (1, up.shape[1]), 1)
     for choice in range(choices):
         for k in range(groups):
             here = (ids == wanted[choice, me ^ k]).astype(jnp.float32)
             pick[pl.ds(choice * groups + k, 1), :] = here
+    table_copy.wait()
     rows = lax.dot_general(
         pick[...].astype(jnp.bfloat16),
-        up[...],
+        table[...],
         (((1,), (1,)), ((), ())),
         preferred_element_type=jnp.float32,
     )
@@ -79,60 +85,71 @@
         out_shape=[pltpu.VMEM((rows, HALF), jnp.bfloat16)] * groups,
         in_specs=[
             pl.BlockSpec(memory_space=pltpu.SMEM),
-            pl.BlockSpec(memory_space=pl.ANY),
-            pl.BlockSpec(memory_space=pltpu.VMEM),
+            pl.BlockSpec(memory_space=pltpu.HBM),
+            pl.BlockSpec(memory_space=pltpu.HBM),
         ],
         out_specs=[pl.BlockSpec(memory_space=pltpu.VMEM)] * groups,
         scratch_shapes=[
+            pltpu.VMEM(up.shape, up.dtype),
             pltpu.VMEM((choices * groups, up.shape[1]), jnp.float32),
             pltpu.VMEM((groups * count, 2 * rank), jnp.float32),
             pltpu.VMEM((groups * count, 2 * rank), jnp.float32),
+            pltpu.SemaphoreType.DMA,
             pltpu.SemaphoreType.DMA((groups * choices * halves,)),
         ],
         compiler_params=pltpu.CompilerParams(vmem_limit_bytes=16 * MIB),
         name="make_messages",
-    )(wanted, down, up)
-
-
-def base_product(tokens, blocks):
+    )(wanted, in_hbm(down), in_hbm(up))
+
+
+def base_product(tokens, bundles, start=None):
     rows, depth = tokens.shape
-    width = blocks[0][1].shape[1]
-    count = len(blocks)
-    masks = [mask for mask, _ in blocks]
+    width = bundles[0][1].shape[1]
+    count = len(bundles)
+    total_rows = sum(bundle.shape[0] for _, bundle in bundles)
 
     def kernel(tokens_ref, *refs):
-        parts, out = refs[:count], refs[count]
-        place = [lax.axis_index(name) for name in AXES]
-        for n in range(0, count, DEEP):
-            left, right = [], []
-            for mask, part in zip(masks[n : n + DEEP], parts[n : n + DEEP]):
-                x, z, y, core = [i ^ bit for i, bit in zip(place, mask)]
-                column = pl.multiple_of((((z * 2 + y) * 2 + core) * 2 + x) * HALF, HALF)
-                left.append(tokens_ref[:, pl.ds(column, HALF)])
-                right.append(part[...])
+        parts, out = refs[:count], refs[-1]
+        place = dict(zip(AXES, [lax.axis_index(name) for name in AXES]))
+        first = start is None
+        for (masks, _), part in zip(bundles, parts):
+            left = []
+            for x, z, y, core in masks:
+                z, y, core = place["line"] ^ z, place["plane"] ^ y, place["core"] ^ core
+                owner = (z * 2 + y) * 2 + core
+                if x is None:
+                    column, size = pl.multiple_of(owner * 2 * HALF, 2 * HALF), 2 * HALF
+                else:
+                    column = pl.multiple_of((owner * 2 + (place["parts"] ^ x)) * HALF, HALF)
+                    size = HALF
+                left.append(tokens_ref[:, pl.ds(column, size)])
             total = jnp.dot(
-                jnp.concatenate(left, axis=1),
-                jnp.concatenate(right, axis=0),
-                preferred_element_type=jnp.float32,
+                jnp.concatenate(left, axis=1), part[...], preferred_element_type=jnp.float32
             )
-            if n == 0:
-                out[...] = total
+            if first:
+                out[...] = total if start is None else refs[count][...] + total
             else:
                 out[...] += total
-
-    return pl.pallas_call(
-        kernel,
+            first = False
+
+    def kernel_with_start(tokens_ref, *refs):
+        refs[-1][...] = refs[count][...]
+        kernel(tokens_ref, *refs)
+
+    extra = [] if start is None else [start]
+    return pl.pallas_call(
+        kernel if start is None else kernel_with_start,
         out_shape=pltpu.VMEM((rows, width), jnp.float32),
-        in_specs=[pl.BlockSpec(memory_space=pltpu.VMEM)] * (1 + count),
+        in_specs=[pl.BlockSpec(memory_space=pltpu.VMEM)] * (1 + count + len(extra)),
         out_specs=pl.BlockSpec(memory_space=pltpu.VMEM),
         compiler_params=pltpu.CompilerParams(vmem_limit_bytes=16 * MIB),
         cost_estimate=pl.CostEstimate(
-            flops=2 * rows * depth * width,
-            bytes_accessed=2 * rows * depth + 2 * depth * width + 4 * rows * width,
+            flops=2 * rows * total_rows * width,
+            bytes_accessed=2 * rows * total_rows + 2 * total_rows * width + 4 * rows * width,
             transcendentals=0,
         ),
         name="base_product",
-    )(in_vmem(tokens), *[in_vmem(block) for _, block in blocks])
+    )(*[in_vmem(value) for value in (tokens, *[bundle for _, bundle in bundles], *extra)])
 
 
 def adapt_kernel(tokens, mask, base, *refs):
@@ -206,6 +223,72 @@
     )(*[in_vmem(other) for other in (value, *others)])
 
 
+def bundle(blocks):
+    size, width = blocks[0].shape
+
+    def kernel(*refs):
+        for n, ref in enumerate(refs[:-1]):
+            refs[-1][n * size : (n + 1) * size, :] = ref[...]
+
+    return pl.pallas_call(
+        kernel,
+        out_shape=pltpu.VMEM((size * len(blocks), width), blocks[0].dtype),
+        in_specs=[pl.BlockSpec(memory_space=pltpu.VMEM)] * len(blocks),
+        out_specs=pl.BlockSpec(memory_space=pltpu.VMEM),
+        compiler_params=pltpu.CompilerParams(vmem_limit_bytes=2 * MIB),
+        name="bundle",
+    )(*[in_vmem(block) for block in blocks])
+
+
+def load_rows(base_weight):
+    def kernel(weight, whole, half, sems):
+        x = lax.axis_index("parts")
+        own = pltpu.make_async_copy(weight.at[pl.ds(x * HALF, HALF), :], half, sems.at[0])
+        rest = pltpu.make_async_copy(weight, whole, sems.at[1])
+        own.start()
+        rest.start()
+        own.wait()
+        rest.wait()
+
+    return pl.pallas_call(
+        kernel,
+        out_shape=[
+            pltpu.VMEM(base_weight.shape, base_weight.dtype),
+            pltpu.VMEM((HALF, base_weight.shape[1]), base_weight.dtype),
+        ],
+        in_specs=[pl.BlockSpec(memory_space=pltpu.HBM)],
+        out_specs=[pl.BlockSpec(memory_space=pltpu.VMEM)] * 2,
+        scratch_shapes=[pltpu.SemaphoreType.DMA((2,))],
+        compiler_params=pltpu.CompilerParams(vmem_limit_bytes=2 * MIB),
+        name="load_rows",
+    )(in_hbm(base_weight))
+
+
+def row_mask(lengths, slots, rows, choices, rank):
+    requests = lengths.shape[1]
+
+    def kernel(lengths_ref, slots_ref, out):
+        group = store_index()
+        position = lax.broadcasted_iota(jnp.int32, out.shape, 0)
+        lane_slot = lax.broadcasted_iota(jnp.int32, out.shape, 1) // rank
+        chosen = jnp.full(out.shape, slots_ref[group, 0], jnp.int32)
+        begin = lengths_ref[0, 0]
+        for request in range(1, requests):
+            change = slots_ref[group, request] - slots_ref[group, request - 1]
+            chosen += jnp.where(position >= begin, change, 0)
+            begin += lengths_ref[0, request]
+        out[...] = (chosen == lane_slot).astype(jnp.float32)
+
+    return pl.pallas_call(
+        kernel,
+        out_shape=pltpu.VMEM((rows, choices * rank), jnp.float32),
+        in_specs=[pl.BlockSpec(memory_space=pltpu.SMEM)] * 2,
+        out_specs=pl.BlockSpec(memory_space=pltpu.VMEM),
+        compiler_params=pltpu.CompilerParams(vmem_limit_bytes=2 * MIB),
+        name="row_mask",
+    )(lengths, slots)
+
+
 def row_slots(lengths, slots, rows):
     ends = jnp.cumsum(lengths)
     starts = ends - lengths
@@ -220,22 +303,25 @@
 
 
 def gather_rows(base_weight):
-    x = lax.axis_index("parts")
-    own = lax.dynamic_slice_in_dim(base_weight, x * HALF, HALF, 0)
-    other = lax.dynamic_slice_in_dim(base_weight, (1 - x) * HALF, HALF, 0)
-    blocks = {(0, 0, 0, 0): own}
-    blocks[0, 1, 0, 0] = swap(own, "line", 1)
-    blocks[0, 2, 0, 0] = swap(own, "line", 2)
-    blocks[0, 3, 0, 0] = swap(blocks[0, 2, 0, 0], "line", 1)
-    for z in range(4):
-        blocks[0, z, 1, 0] = swap(blocks[0, z, 0, 0], "plane", 1)
-    for z in range(4):
-        for y in range(2):
-            source = blocks[0, z, y, 0]
-            blocks[1, z, y, 0] = other if z == y == 0 else swap(source, "parts", 1)
-    for (x, z, y, _), block in list(blocks.items()):
-        blocks[x, z, y, 1] = swap(block, "core", 1)
-    return blocks
+    whole, own = load_rows(base_weight)
+    z1 = swap(own, "line", 1)
+    z2 = swap(own, "line", 2)
+    y0 = swap(own, "plane", 1)
+    z3 = swap(z2, "line", 1)
+    y1 = swap(z1, "plane", 1)
+    y23 = swap(bundle([z2, z3]), "plane", 1)
+    sent = [
+        ([(1, 0), (0, 1)], bundle([z1, y0])),
+        ([(2, 0), (1, 1)], bundle([z2, y1])),
+        ([(3, 0)], z3),
+        ([(2, 1), (3, 1)], y23),
+    ]
+    bundles = [([(None, 0, 0, 0)], whole), ([(None, 0, 0, 1)], swap(whole, "core", 1))]
+    for places, block in sent:
+        for x, held in enumerate([block, swap(block, "parts", 1)]):
+            for core, got in enumerate([held, swap(held, "core", 1)]):
+                bundles.append(([(x, z, y, core) for z, y in places], got))
+    return bundles, z1
 
 
 def exchange(messages, first):
@@ -261,7 +347,6 @@
 ):
     rank = adapter_down.shape[2]
     choices = group_adapters.shape[1]
-    group = store_index()
     shard_width = adapter_up.shape[1]
     messages = make_messages(
         jnp.transpose(group_adapters),
@@ -269,13 +354,10 @@
         jnp.transpose(adapter_up, (1, 2, 0)).reshape(shard_width * rank, adapter_up.shape[0]),
         shard_width,
     )
-    blocks = gather_rows(base_weight)
-    arrived = exchange(messages, blocks[0, 1, 0, 0])
-    slots = lax.dynamic_index_in_dim(request_slot, group, 0, keepdims=False)
-    slot_of_row = row_slots(request_lengths[0], slots, tokens.shape[0])
-    lane_slot = jnp.arange(choices * rank, dtype=jnp.int32)[None, :] // rank
-    mask = (slot_of_row[:, None] == lane_slot).astype(jnp.float32)
-    base = base_product(tokens, list(blocks.items()))
+    bundles, first = gather_rows(base_weight)
+    arrived = exchange(messages, first)
+    mask = row_mask(request_lengths, request_slot, tokens.shape[0], choices, rank)
+    base = base_product(tokens, bundles)
     return adapt(tokens, arrived, mask, base)
 
 

time: 130 us -> 131 us (level)
  waiting for transfers between devices: 48.9 us -> 79.8 us
  local copies, waits for them, and re-layouts: 24.1 us -> 0.7 us
  starting transfers between devices: 42.7 us -> 35.9 us
  Pallas kernels: 12.4 us -> 14.1 us
    unnamed x70 -> x10, local copies, waits for them, and re-layouts: 22.9 us -> 0.7 us
    ppermute x15, waiting for transfers between devices: 23.5 us -> 42.4 us  [send(): return lax.ppermute(after(messages[k], *others), store, pairs)]
    ppermute x30 -> x19, waiting for transfers between devices: 25.4 us -> 37.5 us  [swap(): return lax.ppermute(block, axis, [(i, i ^ bit) for i in range(size)])]
    ppermute x30 -> x19, starting transfers between devices: 20.9 us -> 15.3 us  [swap(): return lax.ppermute(block, axis, [(i, i ^ bit) for i in range(size)])]
    pallas_call x1 -> x6, Pallas kernels: 5.77 us -> 6.9 us  [the longest x1 4.51 us: base_product(): pl.pallas_call(kernel if start is None else kernel_with_start, out_shape=...]
  transfers between devices with their start and end apart: 45 -> 34, of which waited for: 13 -> 15; matrix products, arithmetic and copies ran while one was open for 1% -> 0% of each run, Pallas kernels for 7% -> 7%
where the time goes in v5:
time: 131 us
  waiting for transfers between devices  79.8 us (61%)
  starting transfers between devices  35.9 us (27%)
  Pallas kernels  14.1 us (11%)
    ppermute x15, waiting for transfers between devices, send(): return lax.ppermute(after(messages[k], *others), store, pairs)  42.4 us
    ppermute x19, waiting for transfers between devices, swap(): return lax.ppermute(block, axis, [(i, i ^ bit) for i in range(size)])  37.5 us
    ppermute x15, starting transfers between devices, send(): return lax.ppermute(after(messages[k], *others), store, pairs)  20.5 us
    ppermute x19, starting transfers between devices, swap(): return lax.ppermute(block, axis, [(i, i ^ bit) for i in range(size)])  15.3 us
    pallas_call x1, Pallas kernels, base_product(): pl.pallas_call(kernel if start is None else kernel_with_start, out_shape=...  4.51 us
    pallas_call x1, Pallas kernels, make_messages(): pl.pallas_call(functools.partial(send_kernel, groups), out_shape=[pltpu.V...  3.65 us
    pallas_call x1, Pallas kernels, adapt(): pl.pallas_call(adapt_kernel, out_shape=jax.ShapeDtypeStruct((rows, width)...  3.52 us
  transfers between devices with their start and end apart: 34, of which 15 were waited for; matrix products, arithmetic and copies ran while one was open for 0% of the time, Pallas kernels for 7%

profile of v5, /device:TPU:0, one launch (start us, length us, event | category | flops | bytes accessed | tf_op | source)
XLA Modules:
  0.0 130.7 jit_solution(6834442479562830137)
XLA Ops:
  0.0 1.2 load_rows.1
  1.2 4.1 %collective-permute-start.6 = (bf16[256,512]{1,0:T(8,128)(2,1)S(1)}, bf16[256,512]{1,0:T(8,128)(2,1)S(1)}, u32[]{:S(2)}, u32[]{:S(2)}) collective-permute-start(bf16[256,512]{1,0:T(8,128)(2,1)S(1)} %get-tuple-element.24), channel_id=1, source_target_pairs={{0,8},{4,12},{8,0},{12,4},{1,9},{5,13},{9,1},{13,5},{2,10},{6,14},... | collective-permute-start | bytes 786440 | tf_op jit(solution)/shard_map/ppermute | solution.py:302
  5.3 1.6 %collective-permute-start.1 = (bf16[256,512]{1,0:T(8,128)(2,1)S(1)}, bf16[256,512]{1,0:T(8,128)(2,1)S(1)}, u32[]{:S(2)}, u32[]{:S(2)}) collective-permute-start(bf16[256,512]{1,0:T(8,128)(2,1)S(1)} %get-tuple-element.24), channel_id=1, source_target_pairs={{0,4},{4,0},{8,12},{12,8},{1,5},{5,1},{9,13},{13,9},{2,6},{6,2},{1... | collective-permute-start | bytes 786440 | tf_op jit(solution)/shard_map/ppermute | solution.py:302
  6.9 10.5 %collective-permute-done.6.refs_0_ = bf16[256,512]{1,0:T(8,128)(2,1)S(1)} collective-permute-done((bf16[256,512]{1,0:T(8,128)(2,1)S(1)}, bf16[256,512]{1,0:T(8,128)(2,1)S(1)}, u32[]{:S(2)}, u32[]{:S(2)}) %collective-permute-start.6) | collective-permute-done | bytes 262176 | tf_op jit(solution)/shard_map/ppermute | solution.py:302
  17.3 0.6 collective-permute-start.11
  17.9 1.5 %collective-permute-start.2 = (bf16[256,512]{1,0:T(8,128)(2,1)S(1)}, bf16[256,512]{1,0:T(8,128)(2,1)S(1)}, u32[]{:S(2)}, u32[]{:S(2)}) collective-permute-start(bf16[256,512]{1,0:T(8,128)(2,1)S(1)} %get-tuple-element.24), channel_id=1, source_target_pairs={{0,2},{2,0},{1,3},{3,1},{4,6},{6,4},{5,7},{7,5},{8,10},{10,8},{9,1... | collective-permute-start | bytes 786440 | tf_op jit(solution)/shard_map/ppermute | solution.py:302
  19.4 0.7 copy-done.1
  20.1 3.6 %make_messages.1 = (bf16[272,256]{1,0:T(8,128)(2,1)S(1)}, bf16[272,256]{1,0:T(8,128)(2,1)S(1)}, bf16[272,256]{1,0:T(8,128)(2,1)S(1)}, bf16[272,256]{1,0:T(8,128)...) custom-call(s32[2,16]{1,0:T(2,128)S(1)} %bitcast.7, ...), custom_call_target="tpu_custom_call" | custom-call | tf_op jit(solution)/shard_map/make_messages/pallas_call | solution.py:83
  23.8 0.0 collective-permute-done.1.refs_0_.refs_1_
  23.8 0.0 slice-start.1
  23.8 3.4 %collective-permute-start.19 = (bf16[272,256]{1,0:T(8,128)(2,1)S(1)}, bf16[272,256]{1,0:T(8,128)(2,1)S(1)}, u32[]{:S(2)}, u32[]{:S(2)}) collective-permute-start(bf16[272,256]{1,0:T(8,128)(2,1)S(1)} %after.15), channel_id=1, source_target_pairs={{0,8},{1,9},{2,10},{3,11},{4,12},{5,13},{6,14},{7,15},{8,0},{9,1},... | collective-permute-start | bytes 417800 | tf_op jit(solution)/shard_map/ppermute | solution.py:333
  27.3 0.5 collective-permute-start.7
  27.8 0.0 collective-permute-done.11.refs_1_.refs_10_
  27.8 0.0 collective-permute-start.21
  27.8 9.7 %collective-permute-done.19.refs_1_.refs_8_ = bf16[272,256]{1,0:T(8,128)(2,1)S(1)} collective-permute-done((bf16[272,256]{1,0:T(8,128)(2,1)S(1)}, bf16[272,256]{1,0:T(8,128)(2,1)S(1)}, u32[]{:S(2)}, u32[]{:S(2)}) %collective-permute-start.19) | collective-permute-done | bytes 139296 | tf_op jit(solution)/shard_map/ppermute | solution.py:333
  37.5 0.5 collective-permute-start.15
  38.0 2.0 %collective-permute-done.21.refs_1_.refs_9_ = bf16[272,256]{1,0:T(8,128)(2,1)S(1)} collective-permute-done((bf16[272,256]{1,0:T(8,128)(2,1)S(1)}, bf16[272,256]{1,0:T(8,128)(2,1)S(1)}, u32[]{:S(2)}, u32[]{:S(2)}) %collective-permute-start.21) | collective-permute-done | bytes 139296 | tf_op jit(solution)/shard_map/ppermute | solution.py:333
  40.0 0.0 collective-permute-done.2.refs_1_
  40.0 3.3 %collective-permute-start.25 = (bf16[272,256]{1,0:T(8,128)(2,1)S(1)}, bf16[272,256]{1,0:T(8,128)(2,1)S(1)}, u32[]{:S(2)}, u32[]{:S(2)}) collective-permute-start(bf16[272,256]{1,0:T(8,128)(2,1)S(1)} %after.21), channel_id=1, source_target_pairs={{0,11},{1,10},{2,9},{3,8},{4,15},{5,14},{6,13},{7,12},{8,3},{9,2},... | collective-permute-start | bytes 417800 | tf_op jit(solution)/shard_map/ppermute | solution.py:333
  43.3 0.0 collective-permute-done.7.refs_1_
  43.3 0.7 collective-permute-start.20
  44.0 0.0 collective-permute-done.refs_1_
  44.0 0.6 collective-permute-start.22
  44.6 7.6 %collective-permute-done.23.refs_1_.refs_10_ = bf16[272,256]{1,0:T(8,128)(2,1)S(1)} collective-permute-done((bf16[272,256]{1,0:T(8,128)(2,1)S(1)}, bf16[272,256]{1,0:T(8,128)(2,1)S(1)}, u32[]{:S(2)}, u32[]{:S(2)}) %collective-permute-start.23) | collective-permute-done | bytes 139296 | tf_op jit(solution)/shard_map/ppermute | solution.py:333
  52.2 1.5 %collective-permute-start.4 = (bf16[512,512]{1,0:T(8,128)(2,1)S(1)}, bf16[512,512]{1,0:T(8,128)(2,1)S(1)}, u32[]{:S(2)}, u32[]{:S(2)}) collective-permute-start(bf16[512,512]{1,0:T(8,128)(2,1)S(1)} %bundle.3.refs_2_), channel_id=1, source_target_pairs={{0,16},{16,0},{1,17},{17,1},{2,18},{18,2},{3,19},{19,3},{4,20},{20... | collective-permute-start | bytes 1572872 | tf_op jit(solution)/shard_map/ppermute | solution.py:302
  53.6 1.3 %collective-permute-done.25.refs_1_.refs_11_ = bf16[272,256]{1,0:T(8,128)(2,1)S(1)} collective-permute-done((bf16[272,256]{1,0:T(8,128)(2,1)S(1)}, bf16[272,256]{1,0:T(8,128)(2,1)S(1)}, u32[]{:S(2)}, u32[]{:S(2)}) %collective-permute-start.25) | collective-permute-done | bytes 139296 | tf_op jit(solution)/shard_map/ppermute | solution.py:333
  55.0 0.0 collective-permute-start.3
  55.0 0.0 collective-permute-done.20.refs_1_
  55.0 2.1 %collective-permute-start.27 = (bf16[272,256]{1,0:T(8,128)(2,1)S(1)}, bf16[272,256]{1,0:T(8,128)(2,1)S(1)}, u32[]{:S(2)}, u32[]{:S(2)}) collective-permute-start(bf16[272,256]{1,0:T(8,128)(2,1)S(1)} %after.23), channel_id=1, source_target_pairs={{0,12},{1,13},{2,14},{3,15},{4,8},{5,9},{6,10},{7,11},{8,4},{9,5},... | collective-permute-start | bytes 417800 | tf_op jit(solution)/shard_map/ppermute | solution.py:333
  57.1 2.8 %collective-permute-done.22.refs_2_ = bf16[272,256]{1,0:T(8,128)(2,1)S(1)} collective-permute-done((bf16[272,256]{1,0:T(8,128)(2,1)S(1)}, bf16[272,256]{1,0:T(8,128)(2,1)S(1)}, u32[]{:S(2)}, u32[]{:S(2)}) %collective-permute-start.22) | collective-permute-done | bytes 139296 | tf_op jit(solution)/shard_map/ppermute | solution.py:333
  59.9 0.0 collective-permute-start.29
  59.9 3.0 %collective-permute-done.27.refs_1_.refs_12_ = bf16[272,256]{1,0:T(8,128)(2,1)S(1)} collective-permute-done((bf16[272,256]{1,0:T(8,128)(2,1)S(1)}, bf16[272,256]{1,0:T(8,128)(2,1)S(1)}, u32[]{:S(2)}, u32[]{:S(2)}) %collective-permute-start.27) | collective-permute-done | bytes 139296 | tf_op jit(solution)/shard_map/ppermute | solution.py:333
  63.0 0.7 collective-permute-start.24
  63.7 3.0 %collective-permute-done.29.refs_1_.refs_13_ = bf16[272,256]{1,0:T(8,128)(2,1)S(1)} collective-permute-done((bf16[272,256]{1,0:T(8,128)(2,1)S(1)}, bf16[272,256]{1,0:T(8,128)(2,1)S(1)}, u32[]{:S(2)}, u32[]{:S(2)}) %collective-permute-start.29) | collective-permute-done | bytes 139296 | tf_op jit(solution)/shard_map/ppermute | solution.py:333
  66.7 1.5 %collective-permute-start.9 = (bf16[512,512]{1,0:T(8,128)(2,1)S(1)}, bf16[512,512]{1,0:T(8,128)(2,1)S(1)}, u32[]{:S(2)}, u32[]{:S(2)}) collective-permute-start(bf16[512,512]{1,0:T(8,128)(2,1)S(1)} %bundle.4.refs_6_), channel_id=1, source_target_pairs={{0,16},{16,0},{1,17},{17,1},{2,18},{18,2},{3,19},{19,3},{4,20},{20... | collective-permute-start | bytes 1572872 | tf_op jit(solution)/shard_map/ppermute | solution.py:302
  68.2 0.0 collective-permute-done.15.refs_14_
  68.2 0.5 collective-permute-start.17
  68.7 0.2 collective-permute-done.24.refs_3_
  68.9 1.5 %collective-permute-start.13 = (bf16[256,512]{1,0:T(8,128)(2,1)S(1)}, bf16[256,512]{1,0:T(8,128)(2,1)S(1)}, u32[]{:S(2)}, u32[]{:S(2)}) collective-permute-start(bf16[256,512]{1,0:T(8,128)(2,1)S(1)} %collective-permute-done.11.refs_1_.refs_10_), channel_id=1, source_target_pairs={{0,16},{16,0},{1,17},{17,1},{2,18},{18,2},{3,19},{19,3},{4,20},{20... | collective-permute-start | bytes 786440 | tf_op jit(solution)/shard_map/ppermute | solution.py:302
  70.4 0.0 collective-permute-done.4.refs_4_
  70.4 0.0 collective-permute-start.8
  70.4 0.0 collective-permute-done.3.refs_3_
  70.4 0.5 collective-permute-start.12
  70.9 25.4 %collective-permute-done.13.refs_12_ = bf16[256,512]{1,0:T(8,128)(2,1)S(1)} collective-permute-done((bf16[256,512]{1,0:T(8,128)(2,1)S(1)}, bf16[256,512]{1,0:T(8,128)(2,1)S(1)}, u32[]{:S(2)}, u32[]{:S(2)}) %collective-permute-start.13) | collective-permute-done | bytes 262176 | tf_op jit(solution)/shard_map/ppermute | solution.py:302
  96.3 2.3 %collective-permute-start.31 = (bf16[272,256]{1,0:T(8,128)(2,1)S(1)}, bf16[272,256]{1,0:T(8,128)(2,1)S(1)}, u32[]{:S(2)}, u32[]{:S(2)}) collective-permute-start(bf16[272,256]{1,0:T(8,128)(2,1)S(1)} %after.27), channel_id=1, source_target_pairs={{0,14},{1,15},{2,12},{3,13},{4,10},{5,11},{6,8},{7,9},{8,6},{9,7},... | collective-permute-start | bytes 417800 | tf_op jit(solution)/shard_map/ppermute | solution.py:333
  98.7 5.5 %collective-permute-done.31.refs_1_.refs_14_ = bf16[272,256]{1,0:T(8,128)(2,1)S(1)} collective-permute-done((bf16[272,256]{1,0:T(8,128)(2,1)S(1)}, bf16[272,256]{1,0:T(8,128)(2,1)S(1)}, u32[]{:S(2)}, u32[]{:S(2)}) %collective-permute-start.31) | collective-permute-done | bytes 139296 | tf_op jit(solution)/shard_map/ppermute | solution.py:333
  104.2 0.0 collective-permute-start.16
  104.2 0.0 collective-permute-done.9.refs_8_
  104.2 0.5 collective-permute-start.10
  104.7 0.0 collective-permute-done.17.refs_16_
  104.7 0.1 collective-permute-start.18
  104.8 0.0 collective-permute-done.8.refs_7_
  104.8 0.4 collective-permute-start.14
  105.2 1.1 row_mask.1.mask
  106.4 1.6 %collective-permute-done.14.refs_13_ = bf16[256,512]{1,0:T(8,128)(2,1)S(1)} collective-permute-done((bf16[256,512]{1,0:T(8,128)(2,1)S(1)}, bf16[256,512]{1,0:T(8,128)(2,1)S(1)}, u32[]{:S(2)}, u32[]{:S(2)}) %collective-permute-start.14) | collective-permute-done | bytes 262176 | tf_op jit(solution)/shard_map/ppermute | solution.py:302
  108.0 3.3 %collective-permute-start.26 = (bf16[272,256]{1,0:T(8,128)(2,1)S(1)}, bf16[272,256]{1,0:T(8,128)(2,1)S(1)}, u32[]{:S(2)}, u32[]{:S(2)}) collective-permute-start(bf16[272,256]{1,0:T(8,128)(2,1)S(1)} %after.22), channel_id=1, source_target_pairs={{0,4},{1,5},{2,6},{3,7},{4,0},{5,1},{6,2},{7,3},{8,12},{9,13},{10,... | collective-permute-start | bytes 417800 | tf_op jit(solution)/shard_map/ppermute | solution.py:333
  111.2 0.0 collective-permute-done.5.refs_5_
  111.2 2.0 %collective-permute-start.30 = (bf16[272,256]{1,0:T(8,128)(2,1)S(1)}, bf16[272,256]{1,0:T(8,128)(2,1)S(1)}, u32[]{:S(2)}, u32[]{:S(2)}) collective-permute-start(bf16[272,256]{1,0:T(8,128)(2,1)S(1)} %after.26), channel_id=1, source_target_pairs={{0,6},{1,7},{2,4},{3,5},{4,2},{5,3},{6,0},{7,1},{8,14},{9,15},{10,... | collective-permute-start | bytes 417800 | tf_op jit(solution)/shard_map/ppermute | solution.py:333
  113.2 2.3 %collective-permute-start.33 = (bf16[272,256]{1,0:T(8,128)(2,1)S(1)}, bf16[272,256]{1,0:T(8,128)(2,1)S(1)}, u32[]{:S(2)}, u32[]{:S(2)}) collective-permute-start(bf16[272,256]{1,0:T(8,128)(2,1)S(1)} %after.29), channel_id=1, source_target_pairs={{0,15},{1,14},{2,13},{3,12},{4,11},{5,10},{6,9},{7,8},{8,7},{9,6},... | collective-permute-start | bytes 417800 | tf_op jit(solution)/shard_map/ppermute | solution.py:333
  115.5 4.5 %base_product.1.base = f32[512,512]{1,0:T(8,128)S(1)} custom-call(bf16[512,8192]{1,0:T(8,128)(2,1)S(1)} %bitcast.6, bf16[512,512]{1,0:T(8,128)(2,1)S(1)} %get-tuple-element.23.refs_0_, bf16[512,512]{1,0:T(8,128)(2,1)S(1)} %collective-permute-done.refs_1_, bf16[512,512]{1,0:T(8,128)(2,1)S(1)} %bundle.3.refs_2_, ...), custom_call_target="tpu_custom_call" | custom-call | flops 4294967296 | bytes 17825792 | tf_op jit(solution)/shard_map/base_product/pallas_call | solution.py:140
  120.0 2.1 %collective-permute-done.30.refs_6_ = bf16[272,256]{1,0:T(8,128)(2,1)S(1)} collective-permute-done((bf16[272,256]{1,0:T(8,128)(2,1)S(1)}, bf16[272,256]{1,0:T(8,128)(2,1)S(1)}, u32[]{:S(2)}, u32[]{:S(2)}) %collective-permute-start.30) | collective-permute-done | bytes 139296 | tf_op jit(solution)/shard_map/ppermute | solution.py:333
  122.1 3.3 %collective-permute-done.33.refs_15_ = bf16[272,256]{1,0:T(8,128)(2,1)S(1)} collective-permute-done((bf16[272,256]{1,0:T(8,128)(2,1)S(1)}, bf16[272,256]{1,0:T(8,128)(2,1)S(1)}, u32[]{:S(2)}, u32[]{:S(2)}) %collective-permute-start.33) | collective-permute-done | bytes 139296 | tf_op jit(solution)/shard_map/ppermute | solution.py:333
  125.4 1.7 %collective-permute-done.32.refs_7_ = bf16[272,256]{1,0:T(8,128)(2,1)S(1)} collective-permute-done((bf16[272,256]{1,0:T(8,128)(2,1)S(1)}, bf16[272,256]{1,0:T(8,128)(2,1)S(1)}, u32[]{:S(2)}, u32[]{:S(2)}) %collective-permute-start.32) | collective-permute-done | bytes 139296 | tf_op jit(solution)/shard_map/ppermute | solution.py:333
  127.1 3.5 %adapt.1 = bf16[512,512]{1,0:T(8,128)(2,1)} custom-call(bf16[512,8192]{1,0:T(8,128)(2,1)S(1)} %bitcast.6, f32[512,128]{1,0:T(8,128)S(1)} %row_mask.1.mask, f32[512,512]{1,0:T(8,128)S(1)} %base_product.1.base, bf16[272,256]{1,0:T(8,128)(2,1)S(1)} %get-tuple-element.25.refs_0_, bf16[272,256]{1,0:T(8,128)(2,1)S(1)} %collective-permute-done.20.refs_1_, ...), custom_call_target="tpu_custom_call" | custom-call | flops 1073741824 | bytes 12189696 | tf_op jit(solution)/shard_map/adapt/pallas_call | solution.py:192
  (38 shorter events, 0.2 us)
Async XLA Ops:
  0.0 105.2 %copy-start.2 = (s32[1,16]{1,0:T(1,128)S(1)}, s32[1,16]{1,0:T(1,128)}, u32[]{:S(2)}) copy-start(s32[1,16]{1,0:T(1,128)} %lengths_ref.1) | copy-start | bytes 196
  0.0 105.2 %copy-start = (s32[16,16]{1,0:T(8,128)S(1)}, s32[16,16]{1,0:T(8,128)}, u32[]{:S(2)}) copy-start(s32[16,16]{1,0:T(8,128)} %slots_ref.1) | copy-start | bytes 3076
  1.2 16.1 %collective-permute-start.6 = (bf16[256,512]{1,0:T(8,128)(2,1)S(1)}, bf16[256,512]{1,0:T(8,128)(2,1)S(1)}, u32[]{:S(2)}, u32[]{:S(2)}) collective-permute-start(bf16[256,512]{1,0:T(8,128)(2,1)S(1)} %get-tuple-element.24), channel_id=1, source_target_pairs={{0,8},{4,12},{8,0},{12,4},{1,9},{5,13},{9,1},{13,5},{2,10},{6,14},... | collective-permute-start | bytes 786440 | tf_op jit(solution)/shard_map/ppermute | solution.py:302
  5.3 18.5 %collective-permute-start.1 = (bf16[256,512]{1,0:T(8,128)(2,1)S(1)}, bf16[256,512]{1,0:T(8,128)(2,1)S(1)}, u32[]{:S(2)}, u32[]{:S(2)}) collective-permute-start(bf16[256,512]{1,0:T(8,128)(2,1)S(1)} %get-tuple-element.24), channel_id=1, source_target_pairs={{0,4},{4,0},{8,12},{12,8},{1,5},{5,1},{9,13},{13,9},{2,6},{6,2},{1... | collective-permute-start | bytes 786440 | tf_op jit(solution)/shard_map/ppermute | solution.py:302
  17.3 10.5 %collective-permute-start.11 = (bf16[256,512]{1,0:T(8,128)(2,1)S(1)}, bf16[256,512]{1,0:T(8,128)(2,1)S(1)}, u32[]{:S(2)}, u32[]{:S(2)}) collective-permute-start(bf16[256,512]{1,0:T(8,128)(2,1)S(1)} %collective-permute-done.6.refs_0_), channel_id=1, source_target_pairs={{0,4},{4,0},{8,12},{12,8},{1,5},{5,1},{9,13},{13,9},{2,6},{6,2},{1... | collective-permute-start | bytes 786440 | tf_op jit(solution)/shard_map/ppermute | solution.py:302
  17.9 26.1 %collective-permute-start = (bf16[512,512]{1,0:T(8,128)(2,1)S(1)}, bf16[512,512]{1,0:T(8,128)(2,1)S(1)}, u32[]{:S(2)}, u32[]{:S(2)}) collective-permute-start(bf16[512,512]{1,0:T(8,128)(2,1)S(1)} %get-tuple-element.23.refs_0_), channel_id=1, source_target_pairs={{0,1},{1,0},{2,3},{3,2},{4,5},{5,4},{6,7},{7,6},{8,9},{9,8},{10,11... | collective-permute-start | bytes 1572872 | tf_op jit(solution)/shard_map/ppermute | solution.py:302
  17.9 22.1 %collective-permute-start.2 = (bf16[256,512]{1,0:T(8,128)(2,1)S(1)}, bf16[256,512]{1,0:T(8,128)(2,1)S(1)}, u32[]{:S(2)}, u32[]{:S(2)}) collective-permute-start(bf16[256,512]{1,0:T(8,128)(2,1)S(1)} %get-tuple-element.24), channel_id=1, source_target_pairs={{0,2},{2,0},{1,3},{3,1},{4,6},{6,4},{5,7},{7,5},{8,10},{10,8},{9,1... | collective-permute-start | bytes 786440 | tf_op jit(solution)/shard_map/ppermute | solution.py:302
  19.4 0.7 copy-start.1
  20.1 95.4 %slice-start = ((s8[8388608]{0:T(1024)(128)(4,1)}), s8[4194304]{0:T(1024)(128)(4,1)S(1)}, s32[]{:S(2)}) async-start(s8[8388608]{0:T(1024)(128)(4,1)} %bitcast.5), calls=%async_computation | async-start | bytes 8388608
  23.8 91.7 %slice-start.1 = ((s8[8388608]{0:T(1024)(128)(4,1)}), s8[4194304]{0:T(1024)(128)(4,1)S(1)}, s32[]{:S(2)}) async-start(s8[8388608]{0:T(1024)(128)(4,1)} %bitcast.5), calls=%async_computation.1 | async-start | bytes 8388608
  23.8 13.7 %collective-permute-start.19 = (bf16[272,256]{1,0:T(8,128)(2,1)S(1)}, bf16[272,256]{1,0:T(8,128)(2,1)S(1)}, u32[]{:S(2)}, u32[]{:S(2)}) collective-permute-start(bf16[272,256]{1,0:T(8,128)(2,1)S(1)} %after.15), channel_id=1, source_target_pairs={{0,8},{1,9},{2,10},{3,11},{4,12},{5,13},{6,14},{7,15},{8,0},{9,1},... | collective-permute-start | bytes 417800 | tf_op jit(solution)/shard_map/ppermute | solution.py:333
  27.3 16.0 %collective-permute-start.7 = (bf16[256,512]{1,0:T(8,128)(2,1)S(1)}, bf16[256,512]{1,0:T(8,128)(2,1)S(1)}, u32[]{:S(2)}, u32[]{:S(2)}) collective-permute-start(bf16[256,512]{1,0:T(8,128)(2,1)S(1)} %collective-permute-done.1.refs_0_.refs_1_), channel_id=1, source_target_pairs={{0,2},{2,0},{1,3},{3,1},{4,6},{6,4},{5,7},{7,5},{8,10},{10,8},{9,1... | collective-permute-start | bytes 786440 | tf_op jit(solution)/shard_map/ppermute | solution.py:302
  27.8 12.2 %collective-permute-start.21 = (bf16[272,256]{1,0:T(8,128)(2,1)S(1)}, bf16[272,256]{1,0:T(8,128)(2,1)S(1)}, u32[]{:S(2)}, u32[]{:S(2)}) collective-permute-start(bf16[272,256]{1,0:T(8,128)(2,1)S(1)} %after.17), channel_id=1, source_target_pairs={{0,9},{1,8},{2,11},{3,10},{4,13},{5,12},{6,15},{7,14},{8,1},{9,0},... | collective-permute-start | bytes 417800 | tf_op jit(solution)/shard_map/ppermute | solution.py:333
  37.5 30.7 %collective-permute-start.15 = (bf16[512,512]{1,0:T(8,128)(2,1)S(1)}, bf16[512,512]{1,0:T(8,128)(2,1)S(1)}, u32[]{:S(2)}, u32[]{:S(2)}) collective-permute-start(bf16[512,512]{1,0:T(8,128)(2,1)S(1)} %bundle.5), channel_id=1, source_target_pairs={{0,2},{2,0},{1,3},{3,1},{4,6},{6,4},{5,7},{7,5},{8,10},{10,8},{9,1... | collective-permute-start | bytes 1572872 | tf_op jit(solution)/shard_map/ppermute | solution.py:302
  40.0 12.1 %collective-permute-start.23 = (bf16[272,256]{1,0:T(8,128)(2,1)S(1)}, bf16[272,256]{1,0:T(8,128)(2,1)S(1)}, u32[]{:S(2)}, u32[]{:S(2)}) collective-permute-start(bf16[272,256]{1,0:T(8,128)(2,1)S(1)} %after.19), channel_id=1, source_target_pairs={{0,10},{1,11},{2,8},{3,9},{4,14},{5,15},{6,12},{7,13},{8,2},{9,3},... | collective-permute-start | bytes 417800 | tf_op jit(solution)/shard_map/ppermute | solution.py:333
  40.0 14.9 %collective-permute-start.25 = (bf16[272,256]{1,0:T(8,128)(2,1)S(1)}, bf16[272,256]{1,0:T(8,128)(2,1)S(1)}, u32[]{:S(2)}, u32[]{:S(2)}) collective-permute-start(bf16[272,256]{1,0:T(8,128)(2,1)S(1)} %after.21), channel_id=1, source_target_pairs={{0,11},{1,10},{2,9},{3,8},{4,15},{5,14},{6,13},{7,12},{8,3},{9,2},... | collective-permute-start | bytes 417800 | tf_op jit(solution)/shard_map/ppermute | solution.py:333
  43.3 11.7 %collective-permute-start.20 = (bf16[272,256]{1,0:T(8,128)(2,1)S(1)}, bf16[272,256]{1,0:T(8,128)(2,1)S(1)}, u32[]{:S(2)}, u32[]{:S(2)}) collective-permute-start(bf16[272,256]{1,0:T(8,128)(2,1)S(1)} %after.16), channel_id=1, source_target_pairs={{0,1},{1,0},{2,3},{3,2},{4,5},{5,4},{6,7},{7,6},{8,9},{9,8},{10,11... | collective-permute-start | bytes 417800 | tf_op jit(solution)/shard_map/ppermute | solution.py:333
  44.0 16.0 %collective-permute-start.22 = (bf16[272,256]{1,0:T(8,128)(2,1)S(1)}, bf16[272,256]{1,0:T(8,128)(2,1)S(1)}, u32[]{:S(2)}, u32[]{:S(2)}) collective-permute-start(bf16[272,256]{1,0:T(8,128)(2,1)S(1)} %after.18), channel_id=1, source_target_pairs={{0,2},{1,3},{2,0},{3,1},{4,6},{5,7},{6,4},{7,5},{8,10},{9,11},{10,... | collective-permute-start | bytes 417800 | tf_op jit(solution)/shard_map/ppermute | solution.py:333
  52.2 18.3 %collective-permute-start.4 = (bf16[512,512]{1,0:T(8,128)(2,1)S(1)}, bf16[512,512]{1,0:T(8,128)(2,1)S(1)}, u32[]{:S(2)}, u32[]{:S(2)}) collective-permute-start(bf16[512,512]{1,0:T(8,128)(2,1)S(1)} %bundle.3.refs_2_), channel_id=1, source_target_pairs={{0,16},{16,0},{1,17},{17,1},{2,18},{18,2},{3,19},{19,3},{4,20},{20... | collective-permute-start | bytes 1572872 | tf_op jit(solution)/shard_map/ppermute | solution.py:302
  55.0 15.5 %collective-permute-start.3 = (bf16[512,512]{1,0:T(8,128)(2,1)S(1)}, bf16[512,512]{1,0:T(8,128)(2,1)S(1)}, u32[]{:S(2)}, u32[]{:S(2)}) collective-permute-start(bf16[512,512]{1,0:T(8,128)(2,1)S(1)} %bundle.3.refs_2_), channel_id=1, source_target_pairs={{0,1},{1,0},{2,3},{3,2},{4,5},{5,4},{6,7},{7,6},{8,9},{9,8},{10,11... | collective-permute-start | bytes 1572872 | tf_op jit(solution)/shard_map/ppermute | solution.py:302
  55.0 8.0 %collective-permute-start.27 = (bf16[272,256]{1,0:T(8,128)(2,1)S(1)}, bf16[272,256]{1,0:T(8,128)(2,1)S(1)}, u32[]{:S(2)}, u32[]{:S(2)}) collective-permute-start(bf16[272,256]{1,0:T(8,128)(2,1)S(1)} %after.23), channel_id=1, source_target_pairs={{0,12},{1,13},{2,14},{3,15},{4,8},{5,9},{6,10},{7,11},{8,4},{9,5},... | collective-permute-start | bytes 417800 | tf_op jit(solution)/shard_map/ppermute | solution.py:333
  59.9 6.8 %collective-permute-start.29 = (bf16[272,256]{1,0:T(8,128)(2,1)S(1)}, bf16[272,256]{1,0:T(8,128)(2,1)S(1)}, u32[]{:S(2)}, u32[]{:S(2)}) collective-permute-start(bf16[272,256]{1,0:T(8,128)(2,1)S(1)} %after.25), channel_id=1, source_target_pairs={{0,13},{1,12},{2,15},{3,14},{4,9},{5,8},{6,11},{7,10},{8,5},{9,4},... | collective-permute-start | bytes 417800 | tf_op jit(solution)/shard_map/ppermute | solution.py:333
  63.0 6.0 %collective-permute-start.24 = (bf16[272,256]{1,0:T(8,128)(2,1)S(1)}, bf16[272,256]{1,0:T(8,128)(2,1)S(1)}, u32[]{:S(2)}, u32[]{:S(2)}) collective-permute-start(bf16[272,256]{1,0:T(8,128)(2,1)S(1)} %after.20), channel_id=1, source_target_pairs={{0,3},{1,2},{2,1},{3,0},{4,7},{5,6},{6,5},{7,4},{8,11},{9,10},{10,... | collective-permute-start | bytes 417800 | tf_op jit(solution)/shard_map/ppermute | solution.py:333
  66.7 37.5 %collective-permute-start.9 = (bf16[512,512]{1,0:T(8,128)(2,1)S(1)}, bf16[512,512]{1,0:T(8,128)(2,1)S(1)}, u32[]{:S(2)}, u32[]{:S(2)}) collective-permute-start(bf16[512,512]{1,0:T(8,128)(2,1)S(1)} %bundle.4.refs_6_), channel_id=1, source_target_pairs={{0,16},{16,0},{1,17},{17,1},{2,18},{18,2},{3,19},{19,3},{4,20},{20... | collective-permute-start | bytes 1572872 | tf_op jit(solution)/shard_map/ppermute | solution.py:302
  68.2 36.5 %collective-permute-start.17 = (bf16[512,512]{1,0:T(8,128)(2,1)S(1)}, bf16[512,512]{1,0:T(8,128)(2,1)S(1)}, u32[]{:S(2)}, u32[]{:S(2)}) collective-permute-start(bf16[512,512]{1,0:T(8,128)(2,1)S(1)} %collective-permute-done.15.refs_14_), channel_id=1, source_target_pairs={{0,16},{16,0},{1,17},{17,1},{2,18},{18,2},{3,19},{19,3},{4,20},{20... | collective-permute-start | bytes 1572872 | tf_op jit(solution)/shard_map/ppermute | solution.py:302
  68.9 27.4 %collective-permute-start.13 = (bf16[256,512]{1,0:T(8,128)(2,1)S(1)}, bf16[256,512]{1,0:T(8,128)(2,1)S(1)}, u32[]{:S(2)}, u32[]{:S(2)}) collective-permute-start(bf16[256,512]{1,0:T(8,128)(2,1)S(1)} %collective-permute-done.11.refs_1_.refs_10_), channel_id=1, source_target_pairs={{0,16},{16,0},{1,17},{17,1},{2,18},{18,2},{3,19},{19,3},{4,20},{20... | collective-permute-start | bytes 786440 | tf_op jit(solution)/shard_map/ppermute | solution.py:302
  70.4 34.4 %collective-permute-start.8 = (bf16[512,512]{1,0:T(8,128)(2,1)S(1)}, bf16[512,512]{1,0:T(8,128)(2,1)S(1)}, u32[]{:S(2)}, u32[]{:S(2)}) collective-permute-start(bf16[512,512]{1,0:T(8,128)(2,1)S(1)} %bundle.4.refs_6_), channel_id=1, source_target_pairs={{0,1},{1,0},{2,3},{3,2},{4,5},{5,4},{6,7},{7,6},{8,9},{9,8},{10,11... | collective-permute-start | bytes 1572872 | tf_op jit(solution)/shard_map/ppermute | solution.py:302
  70.4 28.2 %collective-permute-start.12 = (bf16[256,512]{1,0:T(8,128)(2,1)S(1)}, bf16[256,512]{1,0:T(8,128)(2,1)S(1)}, u32[]{:S(2)}, u32[]{:S(2)}) collective-permute-start(bf16[256,512]{1,0:T(8,128)(2,1)S(1)} %collective-permute-done.11.refs_1_.refs_10_), channel_id=1, source_target_pairs={{0,1},{1,0},{2,3},{3,2},{4,5},{5,4},{6,7},{7,6},{8,9},{9,8},{10,11... | collective-permute-start | bytes 786440 | tf_op jit(solution)/shard_map/ppermute | solution.py:302
  96.3 7.9 %collective-permute-start.31 = (bf16[272,256]{1,0:T(8,128)(2,1)S(1)}, bf16[272,256]{1,0:T(8,128)(2,1)S(1)}, u32[]{:S(2)}, u32[]{:S(2)}) collective-permute-start(bf16[272,256]{1,0:T(8,128)(2,1)S(1)} %after.27), channel_id=1, source_target_pairs={{0,14},{1,15},{2,12},{3,13},{4,10},{5,11},{6,8},{7,9},{8,6},{9,7},... | collective-permute-start | bytes 417800 | tf_op jit(solution)/shard_map/ppermute | solution.py:333
  98.7 12.6 %collective-permute-start.5 = (bf16[512,512]{1,0:T(8,128)(2,1)S(1)}, bf16[512,512]{1,0:T(8,128)(2,1)S(1)}, u32[]{:S(2)}, u32[]{:S(2)}) collective-permute-start(bf16[512,512]{1,0:T(8,128)(2,1)S(1)} %collective-permute-done.4.refs_4_), channel_id=1, source_target_pairs={{0,1},{1,0},{2,3},{3,2},{4,5},{5,4},{6,7},{7,6},{8,9},{9,8},{10,11... | collective-permute-start | bytes 1572872 | tf_op jit(solution)/shard_map/ppermute | solution.py:302
  104.2 7.0 %collective-permute-start.16 = (bf16[512,512]{1,0:T(8,128)(2,1)S(1)}, bf16[512,512]{1,0:T(8,128)(2,1)S(1)}, u32[]{:S(2)}, u32[]{:S(2)}) collective-permute-start(bf16[512,512]{1,0:T(8,128)(2,1)S(1)} %collective-permute-done.15.refs_14_), channel_id=1, source_target_pairs={{0,1},{1,0},{2,3},{3,2},{4,5},{5,4},{6,7},{7,6},{8,9},{9,8},{10,11... | collective-permute-start | bytes 1572872 | tf_op jit(solution)/shard_map/ppermute | solution.py:302
  104.2 9.0 %collective-permute-start.10 = (bf16[512,512]{1,0:T(8,128)(2,1)S(1)}, bf16[512,512]{1,0:T(8,128)(2,1)S(1)}, u32[]{:S(2)}, u32[]{:S(2)}) collective-permute-start(bf16[512,512]{1,0:T(8,128)(2,1)S(1)} %collective-permute-done.9.refs_8_), channel_id=1, source_target_pairs={{0,1},{1,0},{2,3},{3,2},{4,5},{5,4},{6,7},{7,6},{8,9},{9,8},{10,11... | collective-permute-start | bytes 1572872 | tf_op jit(solution)/shard_map/ppermute | solution.py:302
  104.7 10.8 %collective-permute-start.18 = (bf16[512,512]{1,0:T(8,128)(2,1)S(1)}, bf16[512,512]{1,0:T(8,128)(2,1)S(1)}, u32[]{:S(2)}, u32[]{:S(2)}) collective-permute-start(bf16[512,512]{1,0:T(8,128)(2,1)S(1)} %collective-permute-done.17.refs_16_), channel_id=1, source_target_pairs={{0,1},{1,0},{2,3},{3,2},{4,5},{5,4},{6,7},{7,6},{8,9},{9,8},{10,11... | collective-permute-start | bytes 1572872 | tf_op jit(solution)/shard_map/ppermute | solution.py:302
  104.8 3.2 %collective-permute-start.14 = (bf16[256,512]{1,0:T(8,128)(2,1)S(1)}, bf16[256,512]{1,0:T(8,128)(2,1)S(1)}, u32[]{:S(2)}, u32[]{:S(2)}) collective-permute-start(bf16[256,512]{1,0:T(8,128)(2,1)S(1)} %collective-permute-done.13.refs_12_), channel_id=1, source_target_pairs={{0,1},{1,0},{2,3},{3,2},{4,5},{5,4},{6,7},{7,6},{8,9},{9,8},{10,11... | collective-permute-start | bytes 786440 | tf_op jit(solution)/shard_map/ppermute | solution.py:302
  108.0 12.1 %collective-permute-start.26 = (bf16[272,256]{1,0:T(8,128)(2,1)S(1)}, bf16[272,256]{1,0:T(8,128)(2,1)S(1)}, u32[]{:S(2)}, u32[]{:S(2)}) collective-permute-start(bf16[272,256]{1,0:T(8,128)(2,1)S(1)} %after.22), channel_id=1, source_target_pairs={{0,4},{1,5},{2,6},{3,7},{4,0},{5,1},{6,2},{7,3},{8,12},{9,13},{10,... | collective-permute-start | bytes 417800 | tf_op jit(solution)/shard_map/ppermute | solution.py:333
  111.2 8.8 %collective-permute-start.28 = (bf16[272,256]{1,0:T(8,128)(2,1)S(1)}, bf16[272,256]{1,0:T(8,128)(2,1)S(1)}, u32[]{:S(2)}, u32[]{:S(2)}) collective-permute-start(bf16[272,256]{1,0:T(8,128)(2,1)S(1)} %after.24), channel_id=1, source_target_pairs={{0,5},{1,4},{2,7},{3,6},{4,1},{5,0},{6,3},{7,2},{8,13},{9,12},{10,... | collective-permute-start | bytes 417800 | tf_op jit(solution)/shard_map/ppermute | solution.py:333
  111.2 10.9 %collective-permute-start.30 = (bf16[272,256]{1,0:T(8,128)(2,1)S(1)}, bf16[272,256]{1,0:T(8,128)(2,1)S(1)}, u32[]{:S(2)}, u32[]{:S(2)}) collective-permute-start(bf16[272,256]{1,0:T(8,128)(2,1)S(1)} %after.26), channel_id=1, source_target_pairs={{0,6},{1,7},{2,4},{3,5},{4,2},{5,3},{6,0},{7,1},{8,14},{9,15},{10,... | collective-permute-start | bytes 417800 | tf_op jit(solution)/shard_map/ppermute | solution.py:333
  113.2 12.2 %collective-permute-start.33 = (bf16[272,256]{1,0:T(8,128)(2,1)S(1)}, bf16[272,256]{1,0:T(8,128)(2,1)S(1)}, u32[]{:S(2)}, u32[]{:S(2)}) collective-permute-start(bf16[272,256]{1,0:T(8,128)(2,1)S(1)} %after.29), channel_id=1, source_target_pairs={{0,15},{1,14},{2,13},{3,12},{4,11},{5,10},{6,9},{7,8},{8,7},{9,6},... | collective-permute-start | bytes 417800 | tf_op jit(solution)/shard_map/ppermute | solution.py:333
  115.5 11.6 %collective-permute-start.32 = (bf16[272,256]{1,0:T(8,128)(2,1)S(1)}, bf16[272,256]{1,0:T(8,128)(2,1)S(1)}, u32[]{:S(2)}, u32[]{:S(2)}) collective-permute-start(bf16[272,256]{1,0:T(8,128)(2,1)S(1)} %after.28), channel_id=1, source_target_pairs={{0,7},{1,6},{2,5},{3,4},{4,3},{5,2},{6,1},{7,0},{8,15},{9,14},{10,... | collective-permute-start | bytes 417800 | tf_op jit(solution)/shard_map/ppermute | solution.py:333

commit v6 on v5

v6 whole, which is shorter than its diff:
```python
import functools

import jax
import jax.numpy as jnp
from jax import lax
from jax.experimental import pallas as pl
from jax.experimental.pallas import tpu as pltpu
from jax.sharding import Mesh
from jax.sharding import PartitionSpec as P

HALF = 256
MIB = 1024 * 1024
AXES = ("parts", "line", "plane", "core")


def in_vmem(value):
    return pltpu.with_memory_space_constraint(value, pltpu.VMEM)


def in_hbm(value):
    return pltpu.with_memory_space_constraint(value, pltpu.HBM)


def store_index():
    return (lax.axis_index("line") * 2 + lax.axis_index("plane")) * 2 + lax.axis_index("core")


ROUNDS = ((4, 1), (2, 6), (5, 3), (7, 7))


def message_targets(round_):
    chip, core = store_index() // 2, lax.axis_index("core")
    own = jnp.where(core == 0, *ROUNDS[round_])
    other = jnp.where(core == 0, *ROUNDS[round_][::-1])
    return [(chip ^ own) * 2, (chip ^ own) * 2 + 1], [(chip ^ other) * 2, (chip ^ other) * 2 + 1]


def send_kernel(rounds, wanted, down, up, weight, *refs):
    outs, whole, half = refs[: 2 * rounds + 1], refs[2 * rounds + 1], refs[2 * rounds + 2]
    table, pick, even_rows, odd_rows, table_sem, sems = refs[2 * rounds + 3 :]
    choices, groups = wanted.shape
    rank = down.shape[1]
    halves = down.shape[2] // HALF
    length = outs[0].shape[0] // 2
    me = store_index()
    places = []
    for n in range(rounds):
        own, other = message_targets(n)
        places += [(own[i], outs[2 * n], i) for i in range(2)]
        places += [(other[i], outs[2 * n + 1], i) for i in range(2)]
    places += [(me, outs[-1], 0), (me ^ 1, outs[-1], 1)]
    copies = []

    def begin(source, target):
        copy = pltpu.make_async_copy(source, target, sems.at[len(copies)])
        copy.start()
        copies.append(copy)

    begin(weight.at[pl.ds(lax.axis_index("parts") * HALF, HALF), :], half)
    begin(weight, whole)
    for target, out, i in places:
        for choice in range(choices):
            adapter = wanted[choice, target]
            for part in range(halves):
                start = i * length + (part * choices + choice) * rank
                begin(
                    down.at[adapter, :, pl.ds(part * HALF, HALF)], out.at[pl.ds(start, rank), :]
                )
    table_copy = pltpu.make_async_copy(up, table, table_sem)
    table_copy.start()

    ids = lax.broadcasted_iota(jnp.int32, (1, up.shape[1]), 1)
    for choice in range(choices):
        for group in range(groups):
            here = (ids == wanted[choice, group]).astype(jnp.float32)
            pick[pl.ds(choice * groups + group, 1), :] = here
    table_copy.wait()
    rows = lax.dot_general(
        pick[...].astype(jnp.bfloat16),
        table[...],
        (((1,), (1,)), ((), ())),
        preferred_element_type=jnp.float32,
    )
    first, second = rows[:groups], rows[groups:]
    low = lax.broadcasted_iota(jnp.int32, (groups, 2 * rank), 1) < rank
    count = even_rows.shape[0] // groups
    for i in range(count):
        a = first[:, 2 * rank * i : 2 * rank * (i + 1)]
        b = second[:, 2 * rank * i : 2 * rank * (i + 1)]
        even_rows[pl.ds(i, groups, stride=count), :] = jnp.where(low, a, pltpu.roll(b, rank, 1))
        odd_rows[pl.ds(i, groups, stride=count), :] = jnp.where(low, pltpu.roll(a, rank, 1), b)
    for target, out, i in places:
        own = pl.ds(pl.multiple_of(target * count, count), count)
        to = pl.ds((i + 1) * length - count, count)
        out[to, : 2 * rank] = even_rows[own, :].astype(jnp.bfloat16)
        out[to, 2 * rank :] = odd_rows[own, :].astype(jnp.bfloat16)
    for copy in copies:
        copy.wait()


def make_messages(wanted, down, up, weight, shard_width):
    choices, groups = wanted.shape
    rank, depth = down.shape[1:]
    halves = depth // HALF
    count = shard_width * choices * rank // HALF
    length = choices * rank * halves + count
    rounds = len(ROUNDS)
    *messages, local, whole, half = pl.pallas_call(
        functools.partial(send_kernel, rounds),
        out_shape=[pltpu.VMEM((2 * length, HALF), jnp.bfloat16)] * (2 * rounds + 1)
        + [
            pltpu.VMEM(weight.shape, weight.dtype),
            pltpu.VMEM((HALF, weight.shape[1]), weight.dtype),
        ],
        in_specs=[pl.BlockSpec(memory_space=pltpu.SMEM)]
        + [pl.BlockSpec(memory_space=pltpu.HBM)] * 3,
        out_specs=[pl.BlockSpec(memory_space=pltpu.VMEM)] * (2 * rounds + 3),
        scratch_shapes=[
            pltpu.VMEM(up.shape, up.dtype),
            pltpu.VMEM((choices * groups, up.shape[1]), jnp.float32),
            pltpu.VMEM((groups * count, 2 * rank), jnp.float32),
            pltpu.VMEM((groups * count, 2 * rank), jnp.float32),
            pltpu.SemaphoreType.DMA,
            pltpu.SemaphoreType.DMA(((4 * rounds + 2) * choices * halves + 2,)),
        ],
        compiler_params=pltpu.CompilerParams(vmem_limit_bytes=16 * MIB),
        name="make_messages",
    )(wanted, *[in_hbm(value) for value in (down, up, weight)])
    return messages[::2], messages[1::2], local, whole, half


def base_product(tokens, bundles, start=None):
    rows, depth = tokens.shape
    width = bundles[0][1].shape[1]
    count = len(bundles)
    total_rows = sum(bundle.shape[0] for _, bundle in bundles)

    def kernel(tokens_ref, *refs):
        parts, out = refs[:count], refs[-1]
        place = dict(zip(AXES, [lax.axis_index(name) for name in AXES]))
        first = True
        for (masks, _), part in zip(bundles, parts):
            left = []
            for x, z, y, core in masks:
                z, y, core = place["line"] ^ z, place["plane"] ^ y, place["core"] ^ core
                owner = (z * 2 + y) * 2 + core
                if x is None:
                    column, size = pl.multiple_of(owner * 2 * HALF, 2 * HALF), 2 * HALF
                else:
                    column = pl.multiple_of((owner * 2 + (place["parts"] ^ x)) * HALF, HALF)
                    size = HALF
                left.append(tokens_ref[:, pl.ds(column, size)])
            total = jnp.dot(
                jnp.concatenate(left, axis=1), part[...], preferred_element_type=jnp.float32
            )
            if first:
                out[...] = total if start is None else refs[count][...] + total
            else:
                out[...] += total
            first = False

    extra = [] if start is None else [start]
    return pl.pallas_call(
        kernel,
        out_shape=pltpu.VMEM((rows, width), jnp.float32),
        in_specs=[pl.BlockSpec(memory_space=pltpu.VMEM)] * (1 + count + len(extra)),
        out_specs=pl.BlockSpec(memory_space=pltpu.VMEM),
        compiler_params=pltpu.CompilerParams(vmem_limit_bytes=16 * MIB),
        cost_estimate=pl.CostEstimate(
            flops=2 * rows * total_rows * width,
            bytes_accessed=2 * rows * total_rows + 2 * total_rows * width + 4 * rows * width,
            transcendentals=0,
        ),
        name="base_product",
    )(*[in_vmem(value) for value in (tokens, *[bundle for _, bundle in bundles], *extra)])


def adapt_kernel(rounds, tokens, mask, base, *refs):
    across, handed = refs[:rounds], refs[rounds : 2 * rounds]
    local, swapped, out, ups, wide = refs[2 * rounds :]
    length = local.shape[0] // 2
    pair = mask.shape[1]
    step = HALF // pair
    groups = wide.shape[0] * step // ups.shape[0] // 2
    depth = tokens.shape[1] // groups
    halves = depth // HALF
    core = lax.axis_index("core")
    chip = store_index() // 2

    def at(ref, place):
        return ref[pl.ds(pl.multiple_of(place * length, 16), length), :]

    messages = [(chip * 2 + core, at(local, 0)), (chip * 2 + 1 - core, swapped[-length:, :])]
    for n in range(rounds):
        own, other = jnp.where(core == 0, *ROUNDS[n]), jnp.where(core == 0, *ROUNDS[n][::-1])
        if ROUNDS[n][0] != ROUNDS[n][1]:
            for i in range(2):
                messages.append(((chip ^ own) * 2 + (core ^ i), at(across[n], 2 * i + core)))
                messages.append(((chip ^ other) * 2 + (core ^ 1 ^ i), at(handed[n], i)))
        else:
            for i in range(2):
                both = at(across[n], 2 * i + core) + at(handed[n], 1 - i)
                messages.append(((chip ^ own) * 2 + (core ^ i), both))

    shrink = jnp.zeros(mask.shape, jnp.float32)
    for source, message in messages:
        column = pl.multiple_of(source * depth, depth)
        down = jnp.concatenate(
            [message[half * pair : (half + 1) * pair, :] for half in range(halves)], axis=1
        )
        shrink += lax.dot_general(
            tokens[:, pl.ds(column, depth)],
            down,
            (((1,), (1,)), ((), ())),
            preferred_element_type=jnp.float32,
        )
        up = message[halves * pair :, :].astype(jnp.float32)
        count = up.shape[0]
        for i in range(step):
            ups[pl.ds(i, count, stride=step), :] = up[:, i * pair : (i + 1) * pair]
        own = pl.ds(pl.multiple_of(source * count * step, count * step), count * step)
        wide[own, :] = ups[...].astype(jnp.bfloat16)
    picked = (shrink * mask[...]).astype(jnp.bfloat16)
    delta = lax.dot_general(
        picked, wide[...], (((1,), (1,)), ((), ())), preferred_element_type=jnp.float32
    )
    out[...] = (base[...] + delta).astype(out.dtype)


def adapt(tokens, across, handed, local, swapped, mask, base, shard_width):
    rows, width = base.shape
    pair = mask.shape[1]
    values = (tokens, mask, base, *across, *handed, local, swapped)
    return pl.pallas_call(
        functools.partial(adapt_kernel, len(across)),
        out_shape=jax.ShapeDtypeStruct((rows, width), jnp.bfloat16),
        in_specs=[pl.BlockSpec(memory_space=pltpu.VMEM)] * len(values),
        out_specs=pl.BlockSpec(memory_space=pltpu.VMEM),
        scratch_shapes=[
            pltpu.VMEM((shard_width, pair), jnp.float32),
            pltpu.VMEM((width, pair), jnp.bfloat16),
        ],
        compiler_params=pltpu.CompilerParams(vmem_limit_bytes=16 * MIB),
        cost_estimate=pl.CostEstimate(
            flops=2 * rows * tokens.shape[1] * pair,
            bytes_accessed=2 * tokens.size + 2 * tokens.shape[1] * pair + 6 * rows * width,
            transcendentals=0,
        ),
        name="adapt",
    )(*[in_vmem(value) for value in values])


def bundle(pieces, others=()):
    pieces = [piece if isinstance(piece, tuple) else (piece, None, piece.shape[0]) for piece in pieces]
    count = len(pieces)
    width, dtype = pieces[0][0].shape[1], pieces[0][0].dtype

    def kernel(*refs):
        place = 0
        for ref, (_, begin, size) in zip(refs[:count], pieces):
            first = 0 if begin is None else begin()
            refs[-1][place : place + size, :] = ref[pl.ds(first, size), :]
            place += size

    values = [array for array, _, _ in pieces] + list(others)
    return pl.pallas_call(
        kernel,
        out_shape=pltpu.VMEM((sum(size for _, _, size in pieces), width), dtype),
        in_specs=[pl.BlockSpec(memory_space=pltpu.VMEM)] * len(values),
        out_specs=pl.BlockSpec(memory_space=pltpu.VMEM),
        compiler_params=pltpu.CompilerParams(vmem_limit_bytes=2 * MIB),
        name="bundle",
    )(*[in_vmem(value) for value in values])


def row_mask(lengths, slots, rows, choices, rank):
    requests = lengths.shape[1]

    def kernel(lengths_ref, slots_ref, out):
        group = store_index()
        position = lax.broadcasted_iota(jnp.int32, out.shape, 0)
        lane_slot = lax.broadcasted_iota(jnp.int32, out.shape, 1) // rank
        chosen = jnp.full(out.shape, slots_ref[group, 0], jnp.int32)
        begin = lengths_ref[0, 0]
        for request in range(1, requests):
            change = slots_ref[group, request] - slots_ref[group, request - 1]
            chosen += jnp.where(position >= begin, change, 0)
            begin += lengths_ref[0, request]
        out[...] = (chosen == lane_slot).astype(jnp.float32)

    return pl.pallas_call(
        kernel,
        out_shape=pltpu.VMEM((rows, choices * rank), jnp.float32),
        in_specs=[pl.BlockSpec(memory_space=pltpu.SMEM)] * 2,
        out_specs=pl.BlockSpec(memory_space=pltpu.VMEM),
        compiler_params=pltpu.CompilerParams(vmem_limit_bytes=2 * MIB),
        name="row_mask",
    )(lengths, slots)


def row_slots(lengths, slots, rows):
    ends = jnp.cumsum(lengths)
    starts = ends - lengths
    position = jnp.arange(rows, dtype=jnp.int32)[:, None]
    member = (position >= starts[None, :]) & (position < ends[None, :])
    return jnp.sum(jnp.where(member, slots[None, :], 0), axis=1)


def swap(block, axis, bit):
    size = lax.axis_size(axis)
    return lax.ppermute(block, axis, [(i, i ^ bit) for i in range(size)])


def gather_rows(whole, own):
    z2 = swap(own, "line", 2)
    z1 = swap(own, "line", 1)
    y0 = swap(own, "plane", 1)
    z3 = swap(z2, "line", 1)
    y1 = swap(bundle([z1], [y0]), "plane", 1)
    y23 = swap(bundle([z2, z3], [y1]), "plane", 1)
    y2, y3 = (y23, lambda: 0, HALF), (y23, lambda: HALF, HALF)
    bundles = [([(None, 0, 0, 0)], whole), ([(None, 0, 0, 1)], swap(whole, "core", 1))]
    before = []
    for places, blocks in (
        ([(1, 0), (0, 1)], [z1, y0]),
        ([(2, 0), (1, 1)], [z2, y1]),
        ([(3, 0), (2, 1)], [z3, y2]),
        ([(3, 1)], [y3]),
    ):
        sent = bundle(blocks, before)
        got = swap(sent, "parts", 1)
        both = [(x, z, y) for x in range(2) for z, y in places]
        other = swap(bundle([sent, got]), "core", 1)
        bundles.append(([(0, z, y, 0) for z, y in places], sent))
        bundles.append(([(1, z, y, 0) for z, y in places], got))
        bundles.append(([(x, z, y, 1) for x, z, y in both], other))
        before = [got]
    return bundles, z2


def exchange(mine, theirs, local, first):
    length = local.shape[0] // 2
    size = 2 * lax.axis_size("line") * lax.axis_size("plane")
    early = swap(theirs[0], "core", 1)
    later = swap(bundle([*theirs[1:], (local, lambda: length, length)]), "core", 1)
    across, handed = [], []
    before = [[], [first]]
    for n, masks in enumerate(ROUNDS):
        if n == 0:
            got = early
        else:
            got = (later, functools.partial(int, (n - 1) * 2 * length), 2 * length)
        payload = bundle([mine[n], got], before[n])
        cores = (0, 1) if masks[0] != masks[1] else (1,)
        pairs = [
            (chip * 2 + core, (chip ^ masks[core]) * 2 + core)
            for chip in range(size // 2)
            for core in cores
        ]
        across.append(lax.ppermute(payload, AXES[1:], pairs))
        before.append([across[n]])

        def place(i):
            return pl.multiple_of((2 * i + 1 - lax.axis_index("core")) * length, 16)

        parts = [(across[n], functools.partial(place, i), length) for i in range(2)]
        handed.append(swap(bundle(parts), "core", 1))
    return across, handed, later


def body(
    tokens, base_weight, adapter_down, adapter_up, request_lengths, group_adapters, request_slot
):
    rank = adapter_down.shape[2]
    choices = group_adapters.shape[1]
    shard_width = adapter_up.shape[1]
    mine, theirs, local, whole, half = make_messages(
        jnp.transpose(group_adapters),
        jnp.swapaxes(adapter_down, 1, 2),
        jnp.transpose(adapter_up, (1, 2, 0)).reshape(shard_width * rank, adapter_up.shape[0]),
        base_weight,
        shard_width,
    )
    bundles, first = gather_rows(whole, half)
    across, handed, swapped = exchange(mine, theirs, local, first)
    mask = row_mask(request_lengths, request_slot, tokens.shape[0], choices, rank)
    base = base_product(tokens, bundles[:9])
    base = base_product(tokens, bundles[9:], base)
    return adapt(tokens, across, handed, local, swapped, mask, base, shard_width)


def plain_body(
    tokens, base_weight, adapter_down, adapter_up, request_lengths, group_adapters, request_slot
):
    store = AXES[1:]
    rank = adapter_down.shape[2]
    choices = group_adapters.shape[1]
    group = lax.axis_index(store)
    wanted = jnp.transpose(group_adapters)
    slots = lax.dynamic_index_in_dim(request_slot, group, 0, keepdims=False)
    slot_of_row = row_slots(request_lengths[0], slots, tokens.shape[0])
    lane_slot = jnp.arange(choices * rank, dtype=jnp.int32)[None, :] // rank
    mask = (slot_of_row[:, None] == lane_slot).astype(jnp.float32)
    exchange = functools.partial(
        lax.all_to_all, axis_name=store, split_axis=1, concat_axis=1, tiled=True
    )
    down = exchange(jnp.take(adapter_down, wanted, axis=0))
    up = exchange(jnp.take(adapter_up, wanted, axis=0))
    weight = lax.all_gather(base_weight, store, axis=0, tiled=True)
    down = down.reshape(choices, tokens.shape[1], rank)
    up = up.reshape(choices, base_weight.shape[1], rank)
    base = jnp.dot(tokens, weight, preferred_element_type=jnp.float32)
    shrink = jnp.einsum("td,kdr->tkr", tokens, down, preferred_element_type=jnp.float32)
    picked = (shrink.reshape(mask.shape) * mask).astype(jnp.bfloat16)
    picked = picked.reshape(shrink.shape)
    delta = jnp.einsum("tkr,kvr->tv", picked, up, preferred_element_type=jnp.float32)
    return (base + delta).astype(jnp.bfloat16)


def solution(mesh):
    parts, size = mesh.shape["parts"], mesh.shape["store"]
    chips = size // 2
    plane = 1
    while 4 * plane * plane <= chips:
        plane *= 2
    lines = chips // plane
    split = Mesh(mesh.devices.reshape(parts, lines, plane, 2), AXES)
    store = AXES[1:]

    def run(tokens, base_weight, *rest):
        small = (parts, lines, plane) == (2, 4, 2) and base_weight.shape[0] // size == 2 * HALF
        return jax.shard_map(
            body if small else plain_body,
            mesh=split,
            in_specs=(
                P(AXES, None),
                P(store, None),
                P(None, store, None),
                P(None, store, None),
                P(AXES, None),
                P("parts", None),
                P("parts", None),
            ),
            out_specs=P(AXES, None),
            check_vma=False,
        )(tokens, base_weight, *rest)

    return run
```

time: 131 us -> 91.1 us (0.70)
  the two profiles are of different devices: /device:TPU:0 before, /device:TPU:7 now
where the time goes in v6:
time: 91.1 us; the launch traced here: 90.9 us
  waiting for transfers between devices  39.1 us (43%)
  starting transfers between devices  37 us (41%)
  Pallas kernels  13.9 us (15%)
    ppermute x21, waiting for transfers between devices, swap(): return lax.ppermute(block, axis, [(i, i ^ bit) for i in range(size)])  34.4 us
    ppermute x21, starting transfers between devices, swap(): return lax.ppermute(block, axis, [(i, i ^ bit) for i in range(size)])  32.2 us
    ppermute x4, starting transfers between devices, exchange(): across.append(lax.ppermute(payload, AXES[1:], pairs))  4.81 us
    ppermute x4, waiting for transfers between devices, exchange(): across.append(lax.ppermute(payload, AXES[1:], pairs))  4.73 us
    pallas_call x2, Pallas kernels, base_product(): pl.pallas_call(kernel, out_shape=pltpu.VMEM((rows, width), jnp.float32),...  4.66 us
    pallas_call x1, Pallas kernels, make_messages(): pl.pallas_call(functools.partial(send_kernel, rounds), out_shape=[pltpu.V...  3.78 us
    pallas_call x1, Pallas kernels, adapt(): pl.pallas_call(functools.partial(adapt_kernel, len(across)), out_shape=ja...  3.55 us
  transfers between devices with their start and end apart: 25, of which 9 were waited for; matrix products, arithmetic and copies ran while one was open for 0% of the time, Pallas kernels for 7%

profile of v6, /device:TPU:7, one launch (start us, length us, event | category | flops | bytes accessed | tf_op | source)
XLA Modules:
  0.0 90.9 jit_solution(972919969630244688)
XLA Ops:
  0.0 0.7 copy-done.1
  0.7 3.8 %make_messages.1 = (bf16[544,256]{1,0:T(8,128)(2,1)S(1)}, bf16[544,256]{1,0:T(8,128)(2,1)S(1)}, bf16[544,256]{1,0:T(8,128)(2,1)S(1)}, bf16[544,256]{1,0:T(8,128)...) custom-call(s32[2,16]{1,0:T(2,128)S(1)} %bitcast.7, ...), custom_call_target="tpu_custom_call" | custom-call | tf_op jit(solution)/shard_map/make_messages/pallas_call | solution.py:108
  4.5 1.4 %collective-permute-start.2 = (bf16[256,512]{1,0:T(8,128)(2,1)S(1)}, bf16[256,512]{1,0:T(8,128)(2,1)S(1)}, u32[]{:S(2)}, u32[]{:S(2)}) collective-permute-start(bf16[256,512]{1,0:T(8,128)(2,1)S(1)} %get-tuple-element.16), channel_id=1, source_target_pairs={{0,4},{4,0},{8,12},{12,8},{1,5},{5,1},{9,13},{13,9},{2,6},{6,2},{1... | collective-permute-start | bytes 786440 | tf_op jit(solution)/shard_map/ppermute | solution.py:311
  5.8 0.2 collective-permute-start.3
  6.1 0.1 bundle.30
  6.1 1.3 %collective-permute-start.17 = (bf16[1904,256]{1,0:T(8,128)(2,1)S(1)}, bf16[1904,256]{1,0:T(8,128)(2,1)S(1)}, u32[]{:S(2)}, u32[]{:S(2)}) collective-permute-start(bf16[1904,256]{1,0:T(8,128)(2,1)S(1)} %bundle.30), channel_id=1, source_target_pairs={{0,1},{1,0},{2,3},{3,2},{4,5},{5,4},{6,7},{7,6},{8,9},{9,8},{10,11... | collective-permute-start | bytes 2924552 | tf_op jit(solution)/shard_map/ppermute | solution.py:311
  7.4 2.3 %collective-permute-start = (bf16[256,512]{1,0:T(8,128)(2,1)S(1)}, bf16[256,512]{1,0:T(8,128)(2,1)S(1)}, u32[]{:S(2)}, u32[]{:S(2)}) collective-permute-start(bf16[256,512]{1,0:T(8,128)(2,1)S(1)} %get-tuple-element.16), channel_id=1, source_target_pairs={{0,8},{4,12},{8,0},{12,4},{1,9},{5,13},{9,1},{13,5},{2,10},{6,14},... | collective-permute-start | bytes 786440 | tf_op jit(solution)/shard_map/ppermute | solution.py:311
  9.7 5.2 %collective-permute-done.2.refs_0_ = bf16[256,512]{1,0:T(8,128)(2,1)S(1)} collective-permute-done((bf16[256,512]{1,0:T(8,128)(2,1)S(1)}, bf16[256,512]{1,0:T(8,128)(2,1)S(1)}, u32[]{:S(2)}, u32[]{:S(2)}) %collective-permute-start.2) | collective-permute-done | bytes 262176 | tf_op jit(solution)/shard_map/ppermute | solution.py:311
  14.9 0.0 collective-permute-done.3.refs_1_
  15.0 0.3 collective-permute-start.6
  15.3 2.5 %collective-permute-start.15 = (bf16[544,256]{1,0:T(8,128)(2,1)S(1)}, bf16[544,256]{1,0:T(8,128)(2,1)S(1)}, u32[]{:S(2)}, u32[]{:S(2)}) collective-permute-start(bf16[544,256]{1,0:T(8,128)(2,1)S(1)} %get-tuple-element.19), channel_id=1, source_target_pairs={{0,1},{1,0},{2,3},{3,2},{4,5},{5,4},{6,7},{7,6},{8,9},{9,8},{10,11... | collective-permute-start | bytes 835592 | tf_op jit(solution)/shard_map/ppermute | solution.py:311
  17.8 0.1 collective-permute-start.4
  17.9 4.0 %collective-permute-done.refs_0_.refs_2_ = bf16[256,512]{1,0:T(8,128)(2,1)S(1)} collective-permute-done((bf16[256,512]{1,0:T(8,128)(2,1)S(1)}, bf16[256,512]{1,0:T(8,128)(2,1)S(1)}, u32[]{:S(2)}, u32[]{:S(2)}) %collective-permute-start) | collective-permute-done | bytes 262176 | tf_op jit(solution)/shard_map/ppermute | solution.py:311
  21.9 0.0 collective-permute-start.1
  21.9 0.0 collective-permute-done.15.refs_1_
  21.9 1.3 %collective-permute-start.16 = (bf16[1088,256]{1,0:T(8,128)(2,1)S(1)}, bf16[1088,256]{1,0:T(8,128)(2,1)S(1)}, u32[]{:S(2)}, u32[]{:S(2)}) collective-permute-start(bf16[1088,256]{1,0:T(8,128)(2,1)S(1)} %bundle.29), channel_id=1, source_target_pairs={{0,8},{1,3},{2,10},{3,1},{4,12},{5,7},{6,14},{7,5},{8,0},{9,11},{1... | collective-permute-start | bytes 1671176 | tf_op jit(solution)/shard_map/ppermute | solution.py:360
  23.2 2.6 %collective-permute-done.4.refs_2_.refs_1_ = bf16[256,512]{1,0:T(8,128)(2,1)S(1)} collective-permute-done((bf16[256,512]{1,0:T(8,128)(2,1)S(1)}, bf16[256,512]{1,0:T(8,128)(2,1)S(1)}, u32[]{:S(2)}, u32[]{:S(2)}) %collective-permute-start.4) | collective-permute-done | bytes 262176 | tf_op jit(solution)/shard_map/ppermute | solution.py:311
  25.8 7.0 %collective-permute-done.1.refs_1_.refs_0_ = bf16[256,512]{1,0:T(8,128)(2,1)S(1)} collective-permute-done((bf16[256,512]{1,0:T(8,128)(2,1)S(1)}, bf16[256,512]{1,0:T(8,128)(2,1)S(1)}, u32[]{:S(2)}, u32[]{:S(2)}) %collective-permute-start.1) | collective-permute-done | bytes 262176 | tf_op jit(solution)/shard_map/ppermute | solution.py:311
  32.8 1.3 %collective-permute-start.5 = (bf16[512,512]{1,0:T(8,128)(2,1)S(1)}, bf16[512,512]{1,0:T(8,128)(2,1)S(1)}, u32[]{:S(2)}, u32[]{:S(2)}) collective-permute-start(bf16[512,512]{1,0:T(8,128)(2,1)S(1)} %bundle.20), channel_id=1, source_target_pairs={{0,2},{2,0},{1,3},{3,1},{4,6},{6,4},{5,7},{7,5},{8,10},{10,8},{9,1... | collective-permute-start | bytes 1572872 | tf_op jit(solution)/shard_map/ppermute | solution.py:311
  34.2 0.0 collective-permute-done.6.refs_2_.refs_1_.refs_3_
  34.2 0.3 collective-permute-start.7
  34.5 0.0 collective-permute-done.17.refs_1_.refs_9_
  34.5 1.3 %collective-permute-start.18 = (bf16[1088,256]{1,0:T(8,128)(2,1)S(1)}, bf16[1088,256]{1,0:T(8,128)(2,1)S(1)}, u32[]{:S(2)}, u32[]{:S(2)}) collective-permute-start(bf16[1088,256]{1,0:T(8,128)(2,1)S(1)} %bundle.31), channel_id=1, source_target_pairs={{0,4},{1,13},{2,6},{3,15},{4,0},{5,9},{6,2},{7,11},{8,12},{9,5},{1... | collective-permute-start | bytes 1671176 | tf_op jit(solution)/shard_map/ppermute | solution.py:360
  35.8 0.0 collective-permute-done.16.refs_2_.refs_0_.refs_1_
  35.8 0.1 collective-permute-start.19
  35.9 9.5 %collective-permute-done.5.refs_1_.refs_0_ = bf16[512,512]{1,0:T(8,128)(2,1)S(1)} collective-permute-done((bf16[512,512]{1,0:T(8,128)(2,1)S(1)}, bf16[512,512]{1,0:T(8,128)(2,1)S(1)}, u32[]{:S(2)}, u32[]{:S(2)}) %collective-permute-start.5) | collective-permute-done | bytes 524320 | tf_op jit(solution)/shard_map/ppermute | solution.py:311
  45.4 0.3 collective-permute-done.7.refs_2_.refs_1_.refs_6_
  45.7 0.3 collective-permute-start.8
  46.0 4.7 %collective-permute-done.18.refs_2_.refs_0_.refs_1_ = bf16[1088,256]{1,0:T(8,128)(2,1)S(1)} collective-permute-done((bf16[1088,256]{1,0:T(8,128)(2,1)S(1)}, bf16[1088,256]{1,0:T(8,128)(2,1)S(1)}, u32[]{:S(2)}, u32[]{:S(2)}) %collective-permute-start.18) | collective-permute-done | bytes 557088 | tf_op jit(solution)/shard_map/ppermute | solution.py:360
  50.8 2.2 %collective-permute-start.20 = (bf16[1088,256]{1,0:T(8,128)(2,1)S(1)}, bf16[1088,256]{1,0:T(8,128)(2,1)S(1)}, u32[]{:S(2)}, u32[]{:S(2)}) collective-permute-start(bf16[1088,256]{1,0:T(8,128)(2,1)S(1)} %bundle.33), channel_id=1, source_target_pairs={{1,15},{3,13},{5,11},{7,9},{9,7},{11,5},{13,3},{15,1},{17,31},{19,... | collective-permute-start | bytes 1671176 | tf_op jit(solution)/shard_map/ppermute | solution.py:360
  53.0 0.1 bundle.27
  53.0 18.0 %collective-permute-start.13 = (bf16[1024,512]{1,0:T(8,128)(2,1)S(1)}, bf16[1024,512]{1,0:T(8,128)(2,1)S(1)}, u32[]{:S(2)}, u32[]{:S(2)}) collective-permute-start(bf16[1024,512]{1,0:T(8,128)(2,1)S(1)} %bundle.27), channel_id=1, source_target_pairs={{0,1},{1,0},{2,3},{3,2},{4,5},{5,4},{6,7},{7,6},{8,9},{9,8},{10,11... | collective-permute-start | bytes 3145736 | tf_op jit(solution)/shard_map/ppermute | solution.py:311
  71.0 0.1 bundle.28
  71.1 0.1 collective-permute-start.14
  71.2 0.0 collective-permute-done.8.refs_1_.refs_0_
  71.2 0.0 slice-start.1
  71.2 0.1 collective-permute-start.10
  71.3 0.1 bundle.24
  71.4 0.0 collective-permute-done.19.refs_0_.refs_1_.refs_2_
  71.4 1.6 %collective-permute-start.9 = (bf16[1024,512]{1,0:T(8,128)(2,1)S(1)}, bf16[1024,512]{1,0:T(8,128)(2,1)S(1)}, u32[]{:S(2)}, u32[]{:S(2)}) collective-permute-start(bf16[1024,512]{1,0:T(8,128)(2,1)S(1)} %bundle.24), channel_id=1, source_target_pairs={{0,1},{1,0},{2,3},{3,2},{4,5},{5,4},{6,7},{7,6},{8,9},{9,8},{10,11... | collective-permute-start | bytes 3145736 | tf_op jit(solution)/shard_map/ppermute | solution.py:311
  72.9 5.7 %collective-permute-done.10.refs_1_.refs_3_ = bf16[256,512]{1,0:T(8,128)(2,1)S(1)} collective-permute-done((bf16[256,512]{1,0:T(8,128)(2,1)S(1)}, bf16[256,512]{1,0:T(8,128)(2,1)S(1)}, u32[]{:S(2)}, u32[]{:S(2)}) %collective-permute-start.10) | collective-permute-done | bytes 262176 | tf_op jit(solution)/shard_map/ppermute | solution.py:311
  78.7 1.3 %collective-permute-start.12 = (bf16[512,512]{1,0:T(8,128)(2,1)S(1)}, bf16[512,512]{1,0:T(8,128)(2,1)S(1)}, u32[]{:S(2)}, u32[]{:S(2)}) collective-permute-start(bf16[512,512]{1,0:T(8,128)(2,1)S(1)} %get-tuple-element.17.refs_0_), channel_id=1, source_target_pairs={{0,1},{1,0},{2,3},{3,2},{4,5},{5,4},{6,7},{7,6},{8,9},{9,8},{10,11... | collective-permute-start | bytes 1572872 | tf_op jit(solution)/shard_map/ppermute | solution.py:311
  80.0 0.0 collective-permute-done.20.refs_0_.refs_1_.refs_3_
  80.0 0.1 collective-permute-start.11
  80.1 0.0 copy-done
  80.1 0.0 copy-done.2
  80.1 1.1 %row_mask.1.mask = f32[512,128]{1,0:T(8,128)S(1)} custom-call(s32[1,16]{1,0:T(1,128)S(1)} %copy-done.2, s32[16,16]{1,0:T(8,128)S(1)} %copy-done), custom_call_target="tpu_custom_call" | custom-call | tf_op jit(solution)/shard_map/row_mask/pallas_call | solution.py:291
  81.4 0.1 collective-permute-done.12.refs_1_
  81.5 0.4 collective-permute-start.21
  82.0 0.0 collective-permute-done.13.refs_4_
  82.0 0.1 collective-permute-start.23
  82.1 0.0 collective-permute-done.14.refs_7_
  82.1 0.4 collective-permute-start.22
  82.5 0.0 collective-permute-done.11.refs_4_
  82.5 0.2 collective-permute-start.24
  82.7 0.0 slice-done
  82.7 3.1 %base_product.2.refs_5_ = f32[512,512]{1,0:T(8,128)S(1)} custom-call(bf16[512,8192]{1,0:T(8,128)(2,1)S(1)} %bitcast.6, bf16[512,512]{1,0:T(8,128)(2,1)S(1)} %get-tuple-element.17.refs_0_, bf16[512,512]{1,0:T(8,128)(2,1)S(1)} %collective-permute-done.12.refs_1_, bf16[512,512]{1,0:T(8,128)(2,1)S(1)} %bundle.21.refs_0_.refs_2_, ...), custom_call_target="tpu_custom_call" | custom-call | flops 2952790016 | bytes 12582912 | tf_op jit(solution)/shard_map/base_product/pallas_call | solution.py:163
  85.8 0.0 collective-permute-done.9.refs_1_
  85.8 1.5 %base_product.3.base = f32[512,512]{1,0:T(8,128)S(1)} custom-call(bf16[512,8192]{1,0:T(8,128)(2,1)S(1)} %bitcast.6, bf16[512,512]{1,0:T(8,128)(2,1)S(1)} %collective-permute-done.8.refs_1_.refs_0_, bf16[1024,512]{1,0:T(8,128)(2,1)S(1)} %collective-permute-done.9.refs_1_, bf16[256,512]{1,0:T(8,128)(2,1)S(1)} %bundle.25.refs_0_.refs_2_, ...), custom_call_target="tpu_custom_call" | custom-call | flops 1342177280 | bytes 6291456 | tf_op jit(solution)/shard_map/base_product/pallas_call | solution.py:163
  87.4 0.0 collective-permute-done.21.refs_4_
  87.4 0.0 collective-permute-done.23.refs_6_
  87.4 0.0 collective-permute-done.22.refs_5_
  87.4 0.0 collective-permute-done.24.refs_7_
  87.4 3.5 %adapt.1 = bf16[512,512]{1,0:T(8,128)(2,1)} custom-call(bf16[512,8192]{1,0:T(8,128)(2,1)S(1)} %bitcast.6, f32[512,128]{1,0:T(8,128)S(1)} %row_mask.1.mask, f32[512,512]{1,0:T(8,128)S(1)} %base_product.3.base, bf16[1088,256]{1,0:T(8,128)(2,1)S(1)} %collective-permute-done.16.refs_2_.refs_0_.refs_1_, ...), custom_call_target="tpu_custom_call" | custom-call | flops 1073741824 | bytes 12058624 | tf_op jit(solution)/shard_map/adapt/pallas_call | solution.py:234
  (21 shorter events, 0.5 us)
Async XLA Ops:
  0.0 0.7 copy-start.1
  4.5 10.5 %collective-permute-start.2 = (bf16[256,512]{1,0:T(8,128)(2,1)S(1)}, bf16[256,512]{1,0:T(8,128)(2,1)S(1)}, u32[]{:S(2)}, u32[]{:S(2)}) collective-permute-start(bf16[256,512]{1,0:T(8,128)(2,1)S(1)} %get-tuple-element.16), channel_id=1, source_target_pairs={{0,4},{4,0},{8,12},{12,8},{1,5},{5,1},{9,13},{13,9},{2,6},{6,2},{1... | collective-permute-start | bytes 786440 | tf_op jit(solution)/shard_map/ppermute | solution.py:311
  5.8 9.1 %collective-permute-start.3 = (bf16[256,512]{1,0:T(8,128)(2,1)S(1)}, bf16[256,512]{1,0:T(8,128)(2,1)S(1)}, u32[]{:S(2)}, u32[]{:S(2)}) collective-permute-start(bf16[256,512]{1,0:T(8,128)(2,1)S(1)} %get-tuple-element.16), channel_id=1, source_target_pairs={{0,2},{2,0},{1,3},{3,1},{4,6},{6,4},{5,7},{7,5},{8,10},{10,8},{9,1... | collective-permute-start | bytes 786440 | tf_op jit(solution)/shard_map/ppermute | solution.py:311
  6.1 28.4 %collective-permute-start.17 = (bf16[1904,256]{1,0:T(8,128)(2,1)S(1)}, bf16[1904,256]{1,0:T(8,128)(2,1)S(1)}, u32[]{:S(2)}, u32[]{:S(2)}) collective-permute-start(bf16[1904,256]{1,0:T(8,128)(2,1)S(1)} %bundle.30), channel_id=1, source_target_pairs={{0,1},{1,0},{2,3},{3,2},{4,5},{5,4},{6,7},{7,6},{8,9},{9,8},{10,11... | collective-permute-start | bytes 2924552 | tf_op jit(solution)/shard_map/ppermute | solution.py:311
  7.4 14.4 %collective-permute-start = (bf16[256,512]{1,0:T(8,128)(2,1)S(1)}, bf16[256,512]{1,0:T(8,128)(2,1)S(1)}, u32[]{:S(2)}, u32[]{:S(2)}) collective-permute-start(bf16[256,512]{1,0:T(8,128)(2,1)S(1)} %get-tuple-element.16), channel_id=1, source_target_pairs={{0,8},{4,12},{8,0},{12,4},{1,9},{5,13},{9,1},{13,5},{2,10},{6,14},... | collective-permute-start | bytes 786440 | tf_op jit(solution)/shard_map/ppermute | solution.py:311
  15.0 19.2 %collective-permute-start.6 = (bf16[512,512]{1,0:T(8,128)(2,1)S(1)}, bf16[512,512]{1,0:T(8,128)(2,1)S(1)}, u32[]{:S(2)}, u32[]{:S(2)}) collective-permute-start(bf16[512,512]{1,0:T(8,128)(2,1)S(1)} %bundle.21.refs_0_.refs_2_), channel_id=1, source_target_pairs={{0,16},{16,0},{1,17},{17,1},{2,18},{18,2},{3,19},{19,3},{4,20},{20... | collective-permute-start | bytes 1572872 | tf_op jit(solution)/shard_map/ppermute | solution.py:311
  15.3 6.6 %collective-permute-start.15 = (bf16[544,256]{1,0:T(8,128)(2,1)S(1)}, bf16[544,256]{1,0:T(8,128)(2,1)S(1)}, u32[]{:S(2)}, u32[]{:S(2)}) collective-permute-start(bf16[544,256]{1,0:T(8,128)(2,1)S(1)} %get-tuple-element.19), channel_id=1, source_target_pairs={{0,1},{1,0},{2,3},{3,2},{4,5},{5,4},{6,7},{7,6},{8,9},{9,8},{10,11... | collective-permute-start | bytes 835592 | tf_op jit(solution)/shard_map/ppermute | solution.py:311
  17.8 8.0 %collective-permute-start.4 = (bf16[256,512]{1,0:T(8,128)(2,1)S(1)}, bf16[256,512]{1,0:T(8,128)(2,1)S(1)}, u32[]{:S(2)}, u32[]{:S(2)}) collective-permute-start(bf16[256,512]{1,0:T(8,128)(2,1)S(1)} %bundle.19), channel_id=1, source_target_pairs={{0,2},{2,0},{1,3},{3,1},{4,6},{6,4},{5,7},{7,5},{8,10},{10,8},{9,1... | collective-permute-start | bytes 786440 | tf_op jit(solution)/shard_map/ppermute | solution.py:311
  21.9 10.9 %collective-permute-start.1 = (bf16[256,512]{1,0:T(8,128)(2,1)S(1)}, bf16[256,512]{1,0:T(8,128)(2,1)S(1)}, u32[]{:S(2)}, u32[]{:S(2)}) collective-permute-start(bf16[256,512]{1,0:T(8,128)(2,1)S(1)} %collective-permute-done.refs_0_.refs_2_), channel_id=1, source_target_pairs={{0,4},{4,0},{8,12},{12,8},{1,5},{5,1},{9,13},{13,9},{2,6},{6,2},{1... | collective-permute-start | bytes 786440 | tf_op jit(solution)/shard_map/ppermute | solution.py:311
  21.9 13.9 %collective-permute-start.16 = (bf16[1088,256]{1,0:T(8,128)(2,1)S(1)}, bf16[1088,256]{1,0:T(8,128)(2,1)S(1)}, u32[]{:S(2)}, u32[]{:S(2)}) collective-permute-start(bf16[1088,256]{1,0:T(8,128)(2,1)S(1)} %bundle.29), channel_id=1, source_target_pairs={{0,8},{1,3},{2,10},{3,1},{4,12},{5,7},{6,14},{7,5},{8,0},{9,11},{1... | collective-permute-start | bytes 1671176 | tf_op jit(solution)/shard_map/ppermute | solution.py:360
  32.8 12.6 %collective-permute-start.5 = (bf16[512,512]{1,0:T(8,128)(2,1)S(1)}, bf16[512,512]{1,0:T(8,128)(2,1)S(1)}, u32[]{:S(2)}, u32[]{:S(2)}) collective-permute-start(bf16[512,512]{1,0:T(8,128)(2,1)S(1)} %bundle.20), channel_id=1, source_target_pairs={{0,2},{2,0},{1,3},{3,1},{4,6},{6,4},{5,7},{7,5},{8,10},{10,8},{9,1... | collective-permute-start | bytes 1572872 | tf_op jit(solution)/shard_map/ppermute | solution.py:311
  34.2 11.5 %collective-permute-start.7 = (bf16[512,512]{1,0:T(8,128)(2,1)S(1)}, bf16[512,512]{1,0:T(8,128)(2,1)S(1)}, u32[]{:S(2)}, u32[]{:S(2)}) collective-permute-start(bf16[512,512]{1,0:T(8,128)(2,1)S(1)} %bundle.22.refs_0_.refs_5_), channel_id=1, source_target_pairs={{0,16},{16,0},{1,17},{17,1},{2,18},{18,2},{3,19},{19,3},{4,20},{20... | collective-permute-start | bytes 1572872 | tf_op jit(solution)/shard_map/ppermute | solution.py:311
  34.5 45.6 %copy-start = (s32[16,16]{1,0:T(8,128)S(1)}, s32[16,16]{1,0:T(8,128)}, u32[]{:S(2)}) copy-start(s32[16,16]{1,0:T(8,128)} %slots_ref.1) | copy-start | bytes 3076
  34.5 45.6 %copy-start.2 = (s32[1,16]{1,0:T(1,128)S(1)}, s32[1,16]{1,0:T(1,128)}, u32[]{:S(2)}) copy-start(s32[1,16]{1,0:T(1,128)} %lengths_ref.1) | copy-start | bytes 196
  34.5 16.2 %collective-permute-start.18 = (bf16[1088,256]{1,0:T(8,128)(2,1)S(1)}, bf16[1088,256]{1,0:T(8,128)(2,1)S(1)}, u32[]{:S(2)}, u32[]{:S(2)}) collective-permute-start(bf16[1088,256]{1,0:T(8,128)(2,1)S(1)} %bundle.31), channel_id=1, source_target_pairs={{0,4},{1,13},{2,6},{3,15},{4,0},{5,9},{6,2},{7,11},{8,12},{9,5},{1... | collective-permute-start | bytes 1671176 | tf_op jit(solution)/shard_map/ppermute | solution.py:360
  35.8 35.5 %collective-permute-start.19 = (bf16[1088,256]{1,0:T(8,128)(2,1)S(1)}, bf16[1088,256]{1,0:T(8,128)(2,1)S(1)}, u32[]{:S(2)}, u32[]{:S(2)}) collective-permute-start(bf16[1088,256]{1,0:T(8,128)(2,1)S(1)} %bundle.32), channel_id=1, source_target_pairs={{0,10},{1,7},{2,8},{3,5},{4,14},{5,3},{6,12},{7,1},{8,2},{9,15},{1... | collective-permute-start | bytes 1671176 | tf_op jit(solution)/shard_map/ppermute | solution.py:360
  45.7 25.5 %collective-permute-start.8 = (bf16[512,512]{1,0:T(8,128)(2,1)S(1)}, bf16[512,512]{1,0:T(8,128)(2,1)S(1)}, u32[]{:S(2)}, u32[]{:S(2)}) collective-permute-start(bf16[512,512]{1,0:T(8,128)(2,1)S(1)} %bundle.23.refs_0_.refs_8_), channel_id=1, source_target_pairs={{0,16},{16,0},{1,17},{17,1},{2,18},{18,2},{3,19},{19,3},{4,20},{20... | collective-permute-start | bytes 1572872 | tf_op jit(solution)/shard_map/ppermute | solution.py:311
  50.7 31.9 %slice-start = ((s8[8388608]{0:T(1024)(128)(4,1)}), s8[4194304]{0:T(1024)(128)(4,1)S(1)}, s32[]{:S(2)}) async-start(s8[8388608]{0:T(1024)(128)(4,1)} %bitcast.5), calls=%async_computation | async-start | bytes 8388608
  50.8 29.3 %collective-permute-start.20 = (bf16[1088,256]{1,0:T(8,128)(2,1)S(1)}, bf16[1088,256]{1,0:T(8,128)(2,1)S(1)}, u32[]{:S(2)}, u32[]{:S(2)}) collective-permute-start(bf16[1088,256]{1,0:T(8,128)(2,1)S(1)} %bundle.33), channel_id=1, source_target_pairs={{1,15},{3,13},{5,11},{7,9},{9,7},{11,5},{13,3},{15,1},{17,31},{19,... | collective-permute-start | bytes 1671176 | tf_op jit(solution)/shard_map/ppermute | solution.py:360
  53.0 28.9 %collective-permute-start.13 = (bf16[1024,512]{1,0:T(8,128)(2,1)S(1)}, bf16[1024,512]{1,0:T(8,128)(2,1)S(1)}, u32[]{:S(2)}, u32[]{:S(2)}) collective-permute-start(bf16[1024,512]{1,0:T(8,128)(2,1)S(1)} %bundle.27), channel_id=1, source_target_pairs={{0,1},{1,0},{2,3},{3,2},{4,5},{5,4},{6,7},{7,6},{8,9},{9,8},{10,11... | collective-permute-start | bytes 3145736 | tf_op jit(solution)/shard_map/ppermute | solution.py:311
  71.1 11.0 %collective-permute-start.14 = (bf16[1024,512]{1,0:T(8,128)(2,1)S(1)}, bf16[1024,512]{1,0:T(8,128)(2,1)S(1)}, u32[]{:S(2)}, u32[]{:S(2)}) collective-permute-start(bf16[1024,512]{1,0:T(8,128)(2,1)S(1)} %bundle.28), channel_id=1, source_target_pairs={{0,1},{1,0},{2,3},{3,2},{4,5},{5,4},{6,7},{7,6},{8,9},{9,8},{10,11... | collective-permute-start | bytes 3145736 | tf_op jit(solution)/shard_map/ppermute | solution.py:311
  71.2 11.5 %slice-start.1 = ((s8[8388608]{0:T(1024)(128)(4,1)}), s8[4194304]{0:T(1024)(128)(4,1)S(1)}, s32[]{:S(2)}) async-start(s8[8388608]{0:T(1024)(128)(4,1)} %bitcast.5), calls=%async_computation.1 | async-start | bytes 8388608
  71.2 7.5 %collective-permute-start.10 = (bf16[256,512]{1,0:T(8,128)(2,1)S(1)}, bf16[256,512]{1,0:T(8,128)(2,1)S(1)}, u32[]{:S(2)}, u32[]{:S(2)}) collective-permute-start(bf16[256,512]{1,0:T(8,128)(2,1)S(1)} %bundle.25.refs_0_.refs_2_), channel_id=1, source_target_pairs={{0,16},{16,0},{1,17},{17,1},{2,18},{18,2},{3,19},{19,3},{4,20},{20... | collective-permute-start | bytes 786440 | tf_op jit(solution)/shard_map/ppermute | solution.py:311
  71.4 14.4 %collective-permute-start.9 = (bf16[1024,512]{1,0:T(8,128)(2,1)S(1)}, bf16[1024,512]{1,0:T(8,128)(2,1)S(1)}, u32[]{:S(2)}, u32[]{:S(2)}) collective-permute-start(bf16[1024,512]{1,0:T(8,128)(2,1)S(1)} %bundle.24), channel_id=1, source_target_pairs={{0,1},{1,0},{2,3},{3,2},{4,5},{5,4},{6,7},{7,6},{8,9},{9,8},{10,11... | collective-permute-start | bytes 3145736 | tf_op jit(solution)/shard_map/ppermute | solution.py:311
  78.7 2.9 %collective-permute-start.12 = (bf16[512,512]{1,0:T(8,128)(2,1)S(1)}, bf16[512,512]{1,0:T(8,128)(2,1)S(1)}, u32[]{:S(2)}, u32[]{:S(2)}) collective-permute-start(bf16[512,512]{1,0:T(8,128)(2,1)S(1)} %get-tuple-element.17.refs_0_), channel_id=1, source_target_pairs={{0,1},{1,0},{2,3},{3,2},{4,5},{5,4},{6,7},{7,6},{8,9},{9,8},{10,11... | collective-permute-start | bytes 1572872 | tf_op jit(solution)/shard_map/ppermute | solution.py:311
  80.0 2.5 %collective-permute-start.11 = (bf16[512,512]{1,0:T(8,128)(2,1)S(1)}, bf16[512,512]{1,0:T(8,128)(2,1)S(1)}, u32[]{:S(2)}, u32[]{:S(2)}) collective-permute-start(bf16[512,512]{1,0:T(8,128)(2,1)S(1)} %bundle.26), channel_id=1, source_target_pairs={{0,1},{1,0},{2,3},{3,2},{4,5},{5,4},{6,7},{7,6},{8,9},{9,8},{10,11... | collective-permute-start | bytes 1572872 | tf_op jit(solution)/shard_map/ppermute | solution.py:311
  81.5 5.8 %collective-permute-start.21 = (bf16[544,256]{1,0:T(8,128)(2,1)S(1)}, bf16[544,256]{1,0:T(8,128)(2,1)S(1)}, u32[]{:S(2)}, u32[]{:S(2)}) collective-permute-start(bf16[544,256]{1,0:T(8,128)(2,1)S(1)} %bundle.34), channel_id=1, source_target_pairs={{0,1},{1,0},{2,3},{3,2},{4,5},{5,4},{6,7},{7,6},{8,9},{9,8},{10,11... | collective-permute-start | bytes 835592 | tf_op jit(solution)/shard_map/ppermute | solution.py:311
  82.0 5.4 %collective-permute-start.23 = (bf16[544,256]{1,0:T(8,128)(2,1)S(1)}, bf16[544,256]{1,0:T(8,128)(2,1)S(1)}, u32[]{:S(2)}, u32[]{:S(2)}) collective-permute-start(bf16[544,256]{1,0:T(8,128)(2,1)S(1)} %bundle.36), channel_id=1, source_target_pairs={{0,1},{1,0},{2,3},{3,2},{4,5},{5,4},{6,7},{7,6},{8,9},{9,8},{10,11... | collective-permute-start | bytes 835592 | tf_op jit(solution)/shard_map/ppermute | solution.py:311
  82.1 5.3 %collective-permute-start.22 = (bf16[544,256]{1,0:T(8,128)(2,1)S(1)}, bf16[544,256]{1,0:T(8,128)(2,1)S(1)}, u32[]{:S(2)}, u32[]{:S(2)}) collective-permute-start(bf16[544,256]{1,0:T(8,128)(2,1)S(1)} %bundle.35), channel_id=1, source_target_pairs={{0,1},{1,0},{2,3},{3,2},{4,5},{5,4},{6,7},{7,6},{8,9},{9,8},{10,11... | collective-permute-start | bytes 835592 | tf_op jit(solution)/shard_map/ppermute | solution.py:311
  82.5 4.9 %collective-permute-start.24 = (bf16[544,256]{1,0:T(8,128)(2,1)S(1)}, bf16[544,256]{1,0:T(8,128)(2,1)S(1)}, u32[]{:S(2)}, u32[]{:S(2)}) collective-permute-start(bf16[544,256]{1,0:T(8,128)(2,1)S(1)} %bundle.37), channel_id=1, source_target_pairs={{0,1},{1,0},{2,3},{3,2},{4,5},{5,4},{6,7},{7,6},{8,9},{9,8},{10,11... | collective-permute-start | bytes 835592 | tf_op jit(solution)/shard_map/ppermute | solution.py:311

commit v7 on v6

v7 whole, which is shorter than its diff:
```python
import functools

import jax
import jax.numpy as jnp
from jax import lax
from jax.experimental import pallas as pl
from jax.experimental.pallas import tpu as pltpu
from jax.sharding import Mesh
from jax.sharding import PartitionSpec as P

HALF = 256
MIB = 1024 * 1024
COST = 4
AXES = ("parts", "line", "plane", "core")


def in_vmem(value):
    return pltpu.with_memory_space_constraint(value, pltpu.VMEM)


def in_hbm(value):
    return pltpu.with_memory_space_constraint(value, pltpu.HBM)


def store_index():
    return (lax.axis_index("line") * 2 + lax.axis_index("plane")) * 2 + lax.axis_index("core")


DIRECT_FIRST, DIRECT_LAST, DIRECT_NEAR = 4, 7, 1
ROUNDS = ((2, 6), (5, 3))


def direct_targets(mask):
    return [store_index() ^ (2 * mask + i) for i in range(2)]


def round_targets(masks, core):
    chip = store_index() // 2
    mask = jnp.where(core == 0, *masks)
    return [(chip ^ mask) * 2 + i for i in range(2)]


def send_kernel(targets_of, wanted, down, up, weight, *refs):
    targets = targets_of()
    *outs, whole, half = refs[:-6]
    table, pick, even_rows, odd_rows, table_sem, sems = refs[-6:]
    choices = wanted.shape[0]
    rank = down.shape[1]
    halves = down.shape[2] // HALF
    padded = pick.shape[0] // choices
    count = even_rows.shape[0] // padded
    length = choices * halves * rank + count
    copies = []

    def begin(source, target):
        copy = pltpu.make_async_copy(source, target, sems.at[len(copies)])
        copy.start()
        copies.append(copy)

    begin(weight.at[pl.ds(lax.axis_index("parts") * HALF, HALF), :], half)
    begin(weight, whole)
    places = []
    for out, target in targets:
        places.append((outs[out], sum(place[0] is outs[out] for place in places) * length))
        for choice in range(choices):
            adapter = wanted[choice, target]
            for part in range(halves):
                start = places[-1][1] + (part * choices + choice) * rank
                begin(
                    down.at[adapter, :, pl.ds(part * HALF, HALF)],
                    outs[out].at[pl.ds(start, rank), :],
                )
    table_copy = pltpu.make_async_copy(up, table, table_sem)
    table_copy.start()

    ids = lax.broadcasted_iota(jnp.int32, (1, up.shape[1]), 1)
    pick[...] = jnp.zeros_like(pick)
    for choice in range(choices):
        for n, (_, target) in enumerate(targets):
            here = (ids == wanted[choice, target]).astype(jnp.float32)
            pick[pl.ds(choice * padded + n, 1), :] = here
    table_copy.wait()
    rows = lax.dot_general(
        pick[...].astype(jnp.bfloat16),
        table[...],
        (((1,), (1,)), ((), ())),
        preferred_element_type=jnp.float32,
    )
    first, second = rows[:padded], rows[padded:]
    low = lax.broadcasted_iota(jnp.int32, (padded, 2 * rank), 1) < rank
    for i in range(count):
        a = first[:, 2 * rank * i : 2 * rank * (i + 1)]
        b = second[:, 2 * rank * i : 2 * rank * (i + 1)]
        even_rows[pl.ds(i, padded, stride=count), :] = jnp.where(low, a, pltpu.roll(b, rank, 1))
        odd_rows[pl.ds(i, padded, stride=count), :] = jnp.where(low, pltpu.roll(a, rank, 1), b)
    for n, (out, start) in enumerate(places):
        own = pl.ds(n * count, count)
        to = pl.ds(start + length - count, count)
        out[to, : 2 * rank] = even_rows[own, :].astype(jnp.bfloat16)
        out[to, 2 * rank :] = odd_rows[own, :].astype(jnp.bfloat16)
    for copy in copies:
        copy.wait()


def make_messages(wanted, down, up, weight, shard_width, counts, targets_of, cost, others=()):
    choices = wanted.shape[0]
    rank, depth = down.shape[1:]
    halves = depth // HALF
    count = shard_width * choices * rank // HALF
    length = choices * rank * halves + count
    padded = -(-sum(counts) // 8) * 8

    def kernel(*refs):
        send_kernel(targets_of, *refs[:4], *refs[4 + len(others) :])

    *messages, whole, half = pl.pallas_call(
        kernel,
        out_shape=[pltpu.VMEM((n * length, HALF), jnp.bfloat16) for n in counts]
        + [
            pltpu.VMEM(weight.shape, weight.dtype),
            pltpu.VMEM((HALF, weight.shape[1]), weight.dtype),
        ],
        in_specs=[pl.BlockSpec(memory_space=pltpu.SMEM)]
        + [pl.BlockSpec(memory_space=pltpu.HBM)] * 3
        + [pl.BlockSpec(memory_space=pltpu.VMEM)] * len(others),
        out_specs=[pl.BlockSpec(memory_space=pltpu.VMEM)] * (len(counts) + 2),
        scratch_shapes=[
            pltpu.VMEM(up.shape, up.dtype),
            pltpu.VMEM((choices * padded, up.shape[1]), jnp.float32),
            pltpu.VMEM((padded * count, 2 * rank), jnp.float32),
            pltpu.VMEM((padded * count, 2 * rank), jnp.float32),
            pltpu.SemaphoreType.DMA,
            pltpu.SemaphoreType.DMA((sum(counts) * choices * halves + 2,)),
        ],
        compiler_params=pltpu.CompilerParams(vmem_limit_bytes=16 * MIB),
        cost_estimate=pl.CostEstimate(
            flops=0, bytes_accessed=4 * cost * sum(counts) * length * HALF, transcendentals=0
        ),
        name="make_messages",
    )(
        wanted,
        *[in_hbm(value) for value in (down, up, weight)],
        *[in_vmem(other) for other in others],
    )
    return messages, whole, half


def base_product(tokens, bundles, start=None):
    rows, depth = tokens.shape
    width = bundles[0][1].shape[1]
    count = len(bundles)
    total_rows = sum(bundle.shape[0] for _, bundle in bundles)

    def kernel(tokens_ref, *refs):
        parts, out = refs[:count], refs[-1]
        place = dict(zip(AXES, [lax.axis_index(name) for name in AXES]))
        first = True
        for (masks, _), part in zip(bundles, parts):
            left = []
            for x, z, y, core in masks:
                z, y, core = place["line"] ^ z, place["plane"] ^ y, place["core"] ^ core
                owner = (z * 2 + y) * 2 + core
                if x is None:
                    column, size = pl.multiple_of(owner * 2 * HALF, 2 * HALF), 2 * HALF
                else:
                    column = pl.multiple_of((owner * 2 + (place["parts"] ^ x)) * HALF, HALF)
                    size = HALF
                left.append(tokens_ref[:, pl.ds(column, size)])
            total = jnp.dot(
                jnp.concatenate(left, axis=1), part[...], preferred_element_type=jnp.float32
            )
            if first:
                out[...] = total if start is None else refs[count][...] + total
            else:
                out[...] += total
            first = False

    extra = [] if start is None else [start]
    return pl.pallas_call(
        kernel,
        out_shape=pltpu.VMEM((rows, width), jnp.float32),
        in_specs=[pl.BlockSpec(memory_space=pltpu.VMEM)] * (1 + count + len(extra)),
        out_specs=pl.BlockSpec(memory_space=pltpu.VMEM),
        compiler_params=pltpu.CompilerParams(vmem_limit_bytes=16 * MIB),
        cost_estimate=pl.CostEstimate(
            flops=2 * rows * total_rows * width,
            bytes_accessed=2 * rows * total_rows + 2 * total_rows * width + 4 * rows * width,
            transcendentals=0,
        ),
        name="base_product",
    )(*[in_vmem(value) for value in (tokens, *[bundle for _, bundle in bundles], *extra)])


def shrink_part(sources, length, tokens, messages, wide, ups):
    pair = wide.shape[1]
    step = HALF // pair
    groups = wide.shape[0] // ups.shape[0]
    depth = tokens.shape[1] // groups
    halves = depth // HALF
    total = None
    for n, start, source in sources():
        begin = start if isinstance(start, int) else pl.multiple_of(start, 16)
        message = messages[n][pl.ds(begin, length), :]
        column = pl.multiple_of(source * depth, depth)
        down = jnp.concatenate(
            [message[half * pair : (half + 1) * pair, :] for half in range(halves)], axis=1
        )
        part = lax.dot_general(
            tokens[:, pl.ds(column, depth)],
            down,
            (((1,), (1,)), ((), ())),
            preferred_element_type=jnp.float32,
        )
        total = part if total is None else total + part
        up = message[halves * pair :, :].astype(jnp.float32)
        count = up.shape[0]
        for i in range(step):
            ups[pl.ds(i, count, stride=step), :] = up[:, i * pair : (i + 1) * pair]
        own = pl.ds(pl.multiple_of(source * count * step, count * step), count * step)
        wide[own, :] = ups[...].astype(jnp.bfloat16)
    return total


def adapt_cost(tokens, pair, share):
    return pl.CostEstimate(
        flops=int(4 * tokens.size * pair * share),
        bytes_accessed=int(2 * tokens.size * share),
        transcendentals=0,
    )


def adapt_begin(tokens, messages, sources, length, pair, shard_width, width, share):
    rows = tokens.shape[0]
    count = len(messages)

    def kernel(tokens_ref, *refs):
        shrink, wide, ups = refs[count:]
        wide[...] = jnp.zeros_like(wide)
        shrink[...] = shrink_part(sources, length, tokens_ref, refs[:count], wide, ups)

    return pl.pallas_call(
        kernel,
        out_shape=[
            pltpu.VMEM((rows, pair), jnp.float32),
            pltpu.VMEM((width, pair), jnp.bfloat16),
        ],
        in_specs=[pl.BlockSpec(memory_space=pltpu.VMEM)] * (1 + count),
        out_specs=[pl.BlockSpec(memory_space=pltpu.VMEM)] * 2,
        scratch_shapes=[pltpu.VMEM((shard_width, pair), jnp.float32)],
        compiler_params=pltpu.CompilerParams(vmem_limit_bytes=16 * MIB),
        cost_estimate=adapt_cost(tokens, pair, share),
        name="adapt_begin",
    )(*[in_vmem(value) for value in (tokens, *messages)])


def adapt_end(tokens, messages, sources, length, mask, base, begun, shard_width, share):
    rows, width = base.shape
    pair = mask.shape[1]
    count = len(messages)

    def kernel(tokens_ref, mask_ref, base_ref, shrunk, widened, *refs):
        out, wide, ups = refs[count:]
        wide[...] = widened[...]
        shrink = shrunk[...]
        shrink += shrink_part(sources, length, tokens_ref, refs[:count], wide, ups)
        picked = (shrink * mask_ref[...]).astype(jnp.bfloat16)
        delta = lax.dot_general(
            picked, wide[...], (((1,), (1,)), ((), ())), preferred_element_type=jnp.float32
        )
        out[...] = (base_ref[...] + delta).astype(out.dtype)

    values = (tokens, mask, base, *begun, *messages)
    return pl.pallas_call(
        kernel,
        out_shape=jax.ShapeDtypeStruct((rows, width), jnp.bfloat16),
        in_specs=[pl.BlockSpec(memory_space=pltpu.VMEM)] * len(values),
        out_specs=pl.BlockSpec(memory_space=pltpu.VMEM),
        scratch_shapes=[
            pltpu.VMEM((width, pair), jnp.bfloat16),
            pltpu.VMEM((shard_width, pair), jnp.float32),
        ],
        compiler_params=pltpu.CompilerParams(vmem_limit_bytes=16 * MIB),
        cost_estimate=adapt_cost(tokens, pair, share),
        name="adapt_end",
    )(*[in_vmem(value) for value in values])


def after(value, *others):
    def kernel(*refs):
        pass

    return pl.pallas_call(
        kernel,
        out_shape=pltpu.VMEM(value.shape, value.dtype),
        in_specs=[pl.BlockSpec(memory_space=pl.ANY)] * (1 + len(others)),
        out_specs=pl.BlockSpec(memory_space=pl.ANY),
        input_output_aliases={0: 0},
        compiler_params=pltpu.CompilerParams(vmem_limit_bytes=MIB),
        name="after",
    )(*[in_vmem(other) for other in (value, *others)])


def bundle(pieces, others=()):
    pieces = [piece if isinstance(piece, tuple) else (piece, None, piece.shape[0]) for piece in pieces]
    count = len(pieces)
    width, dtype = pieces[0][0].shape[1], pieces[0][0].dtype

    def kernel(*refs):
        place = 0
        for ref, (_, begin, size) in zip(refs[:count], pieces):
            first = 0 if begin is None else begin()
            refs[-1][place : place + size, :] = ref[pl.ds(first, size), :]
            place += size

    values = [array for array, _, _ in pieces] + list(others)
    return pl.pallas_call(
        kernel,
        out_shape=pltpu.VMEM((sum(size for _, _, size in pieces), width), dtype),
        in_specs=[pl.BlockSpec(memory_space=pltpu.VMEM)] * len(values),
        out_specs=pl.BlockSpec(memory_space=pltpu.VMEM),
        compiler_params=pltpu.CompilerParams(vmem_limit_bytes=2 * MIB),
        name="bundle",
    )(*[in_vmem(value) for value in values])


def row_mask(lengths, slots, rows, choices, rank):
    requests = lengths.shape[1]

    def kernel(lengths_ref, slots_ref, out):
        group = store_index()
        position = lax.broadcasted_iota(jnp.int32, out.shape, 0)
        lane_slot = lax.broadcasted_iota(jnp.int32, out.shape, 1) // rank
        chosen = jnp.full(out.shape, slots_ref[group, 0], jnp.int32)
        begin = lengths_ref[0, 0]
        for request in range(1, requests):
            change = slots_ref[group, request] - slots_ref[group, request - 1]
            chosen += jnp.where(position >= begin, change, 0)
            begin += lengths_ref[0, request]
        out[...] = (chosen == lane_slot).astype(jnp.float32)

    return pl.pallas_call(
        kernel,
        out_shape=pltpu.VMEM((rows, choices * rank), jnp.float32),
        in_specs=[pl.BlockSpec(memory_space=pltpu.SMEM)] * 2,
        out_specs=pl.BlockSpec(memory_space=pltpu.VMEM),
        compiler_params=pltpu.CompilerParams(vmem_limit_bytes=2 * MIB),
        name="row_mask",
    )(lengths, slots)


def row_slots(lengths, slots, rows):
    ends = jnp.cumsum(lengths)
    starts = ends - lengths
    position = jnp.arange(rows, dtype=jnp.int32)[:, None]
    member = (position >= starts[None, :]) & (position < ends[None, :])
    return jnp.sum(jnp.where(member, slots[None, :], 0), axis=1)


def swap(block, axis, bit):
    size = lax.axis_size(axis)
    return lax.ppermute(block, axis, [(i, i ^ bit) for i in range(size)])


def gather_rows(whole, half, paces, plane_pace):
    z2 = swap(half, "line", 2)
    z1 = swap(half, "line", 1)
    y0 = swap(half, "plane", 1)
    z3 = swap(bundle([z2], [z1]), "line", 1)
    y1 = swap(bundle([z1], [y0, *plane_pace]), "plane", 1)
    y23 = swap(bundle([z2, z3], [y1]), "plane", 1)
    y2, y3 = (y23, lambda: 0, HALF), (y23, lambda: HALF, HALF)
    bundles = [([(None, 0, 0, 0)], whole), ([(None, 0, 0, 1)], swap(whole, "core", 1))]
    before = []
    for n, (places, blocks) in enumerate(
        (
            ([(1, 0), (0, 1)], [z1, y0]),
            ([(2, 0), (1, 1)], [z2, y1]),
            ([(3, 0), (2, 1)], [z3, y2]),
            ([(3, 1)], [y3]),
        )
    ):
        sent = bundle(blocks, before + paces[n])
        got = swap(sent, "parts", 1)
        bundles.append(([(0, z, y, 0) for z, y in places], sent))
        bundles.append(([(1, z, y, 0) for z, y in places], got))

        def from_core(*others, places=places, held=(sent, got)):
            masks = [(x, z, y, 1) for x in range(2) for z, y in places]
            return masks, swap(bundle(held, others), "core", 1)

        if n < 3:
            bundles.append(from_core())
        before = [got]
    return bundles, from_core


def send_chip(mask, messages, *others):
    size = 2 * lax.axis_size("line") * lax.axis_size("plane")
    payload = after(messages, *others) if others else messages
    return lax.ppermute(payload, AXES[1:], [(i, i ^ (2 * mask)) for i in range(size)])


def hand_on(*arrived):
    length = arrived[0].shape[0] // 2

    return swap(bundle([(pair, lambda: length, length) for pair in arrived]), "core", 1)


def send_round(masks, mine, theirs, *others):
    size = 2 * lax.axis_size("line") * lax.axis_size("plane")
    length = mine.shape[0] // 2
    pairs = [
        (chip * 2 + core, (chip ^ masks[core]) * 2 + core)
        for chip in range(size // 2)
        for core in range(2)
    ]
    got = lax.ppermute(bundle([mine, theirs], others), AXES[1:], pairs)

    def place(i):
        return pl.multiple_of((2 * i + 1 - lax.axis_index("core")) * length, 16)

    parts = [(got, functools.partial(place, i), length) for i in range(2)]
    return got, swap(bundle(parts), "core", 1)


def body(
    tokens, base_weight, adapter_down, adapter_up, request_lengths, group_adapters, request_slot
):
    rank = adapter_down.shape[2]
    choices = group_adapters.shape[1]
    width = base_weight.shape[1]
    shard_width = adapter_up.shape[1]
    mask = row_mask(request_lengths, request_slot, tokens.shape[0], choices, rank)
    operands = (
        jnp.transpose(group_adapters),
        jnp.swapaxes(adapter_down, 1, 2),
        jnp.transpose(adapter_up, (1, 2, 0)).reshape(shard_width * rank, adapter_up.shape[0]),
        base_weight,
        shard_width,
    )

    def first_targets():
        return [(0, target) for target in direct_targets(DIRECT_FIRST)]

    def other_targets():
        core = lax.axis_index("core")
        targets = [(0, target) for target in direct_targets(DIRECT_LAST)]
        targets += [(1, target) for target in direct_targets(DIRECT_NEAR)]
        for n, masks in enumerate(ROUNDS):
            targets += [(2 + n, target) for target in round_targets(masks, core)]
        for masks in ROUNDS:
            targets += [(4, target) for target in round_targets(masks, 1 - core)]
        me = store_index()
        return targets + [(4, me ^ 1), (5, me)]

    (pair_first,), whole, half = make_messages(*operands, (2,), first_targets, 1)
    (pair_last, pair_near, mine_a, mine_b, theirs, local), _, _ = make_messages(
        *operands, (2, 2, 2, 2, 5, 1), other_targets, COST, [half]
    )
    length = local.shape[0]

    got_first = send_chip(DIRECT_FIRST, pair_first)
    swapped = swap(theirs, "core", 1)
    got_a, handed_a = send_round(ROUNDS[0], mine_a, (swapped, lambda: 0, 2 * length))
    got_near = send_chip(DIRECT_NEAR, pair_near, got_first)
    handed_first = hand_on(got_first, got_near)
    got_b, handed_b = send_round(
        ROUNDS[1], mine_b, (swapped, lambda: 2 * length, 2 * length), got_first, mask
    )
    paces = [[], [], [got_a], [got_b, handed_first]]
    bundles, last_rows = gather_rows(whole, half, paces, [got_first])
    base = base_product(tokens, bundles[:4])
    base = base_product(tokens, bundles[4:7], base)
    got_last = send_chip(DIRECT_LAST, pair_last, got_a, base)
    handed_last = hand_on(got_last)
    bundles.append(last_rows(got_last))
    base = base_product(tokens, bundles[7:10], base)
    base = base_product(tokens, bundles[10:], base)

    def round_sources(masks, first):
        core, chip = lax.axis_index("core"), store_index() // 2
        own, other = jnp.where(core == 0, *masks), jnp.where(core == 0, *masks[::-1])
        places = []
        for i in range(2):
            places.append((first, (2 * i + core) * length, (chip ^ own) * 2 + (core ^ i)))
            places.append((first + 1, i * length, (chip ^ other) * 2 + (core ^ 1 ^ i)))
        return places

    def direct_sources(mask, n, handed, start):
        core, chip = lax.axis_index("core"), store_index() // 2
        source = (chip ^ mask) * 2
        return [(n, 0, source + core), (handed, start, source + 1 - core)]

    def begin_sources():
        me = store_index()
        places = [(0, 0, me), (1, 4 * length, me ^ 1)]
        places += direct_sources(DIRECT_FIRST, 2, 4, 0)
        places += direct_sources(DIRECT_NEAR, 3, 4, length)
        return places + round_sources(ROUNDS[0], 5)

    def end_sources():
        return round_sources(ROUNDS[1], 0) + direct_sources(DIRECT_LAST, 2, 3, 0)

    begun = adapt_begin(
        tokens,
        (local, swapped, got_first, got_near, handed_first, got_a, handed_a),
        begin_sources,
        length,
        choices * rank,
        shard_width,
        width,
        0.6,
    )
    return adapt_end(
        tokens,
        (got_b, handed_b, got_last, handed_last),
        end_sources,
        length,
        mask,
        base,
        begun,
        shard_width,
        0.4,
    )


def plain_body(
    tokens, base_weight, adapter_down, adapter_up, request_lengths, group_adapters, request_slot
):
    store = AXES[1:]
    rank = adapter_down.shape[2]
    choices = group_adapters.shape[1]
    group = lax.axis_index(store)
    wanted = jnp.transpose(group_adapters)
    slots = lax.dynamic_index_in_dim(request_slot, group, 0, keepdims=False)
    slot_of_row = row_slots(request_lengths[0], slots, tokens.shape[0])
    lane_slot = jnp.arange(choices * rank, dtype=jnp.int32)[None, :] // rank
    mask = (slot_of_row[:, None] == lane_slot).astype(jnp.float32)
    exchange = functools.partial(
        lax.all_to_all, axis_name=store, split_axis=1, concat_axis=1, tiled=True
    )
    down = exchange(jnp.take(adapter_down, wanted, axis=0))
    up = exchange(jnp.take(adapter_up, wanted, axis=0))
    weight = lax.all_gather(base_weight, store, axis=0, tiled=True)
    down = down.reshape(choices, tokens.shape[1], rank)
    up = up.reshape(choices, base_weight.shape[1], rank)
    base = jnp.dot(tokens, weight, preferred_element_type=jnp.float32)
    shrink = jnp.einsum("td,kdr->tkr", tokens, down, preferred_element_type=jnp.float32)
    picked = (shrink.reshape(mask.shape) * mask).astype(jnp.bfloat16)
    picked = picked.reshape(shrink.shape)
    delta = jnp.einsum("tkr,kvr->tv", picked, up, preferred_element_type=jnp.float32)
    return (base + delta).astype(jnp.bfloat16)


def solution(mesh):
    parts, size = mesh.shape["parts"], mesh.shape["store"]
    chips = size // 2
    plane = 1
    while 4 * plane * plane <= chips:
        plane *= 2
    lines = chips // plane
    split = Mesh(mesh.devices.reshape(parts, lines, plane, 2), AXES)
    store = AXES[1:]

    def run(tokens, base_weight, *rest):
        small = (parts, lines, plane) == (2, 4, 2) and base_weight.shape[0] // size == 2 * HALF
        return jax.shard_map(
            body if small else plain_body,
            mesh=split,
            in_specs=(
                P(AXES, None),
                P(store, None),
                P(None, store, None),
                P(None, store, None),
                P(AXES, None),
                P("parts", None),
                P("parts", None),
            ),
            out_specs=P(AXES, None),
            check_vma=False,
        )(tokens, base_weight, *rest)

    return run
```

time: 91.1 us -> 111 us (1.22)
  the two profiles are of different devices: /device:TPU:7 before, /device:TPU:9 now
where the time goes in v7:
time: 111 us
  waiting for transfers between devices  67.5 us (61%)
  starting transfers between devices  25.3 us (23%)
  Pallas kernels  16.8 us (15%)
    ppermute x20, waiting for transfers between devices, swap(): return lax.ppermute(block, axis, [(i, i ^ bit) for i in range(size)])  44.2 us
    ppermute x3, waiting for transfers between devices, send_chip(): lax.ppermute(payload, AXES[1:], [(i, i ^ 2 * mask) for i in range(size)])  23.3 us
    ppermute x20, starting transfers between devices, swap(): return lax.ppermute(block, axis, [(i, i ^ bit) for i in range(size)])  18.7 us
    pallas_call x2, Pallas kernels, make_messages(): pl.pallas_call(kernel, out_shape=[pltpu.VMEM((n * length, HALF), jnp.bflo...  6.65 us
    ppermute x3, starting transfers between devices, send_chip(): lax.ppermute(payload, AXES[1:], [(i, i ^ 2 * mask) for i in range(size)])  5.14 us
    pallas_call x4, Pallas kernels, base_product(): pl.pallas_call(kernel, out_shape=pltpu.VMEM((rows, width), jnp.float32),...  4.99 us
  transfers between devices with their start and end apart: 25, of which 8 were waited for; matrix products, arithmetic and copies ran while one was open for 0% of the time, Pallas kernels for 11%

profile of v7, /device:TPU:9, one launch (start us, length us, event | category | flops | bytes accessed | tf_op | source)
XLA Modules:
  0.0 110.6 jit_solution(14765301427592139069)
XLA Ops:
  0.0 0.7 copy-done.1
  0.7 2.4 %make_messages.2 = (bf16[544,256]{1,0:T(8,128)(2,1)S(1)}, bf16[512,512]{1,0:T(8,128)(2,1)S(1)}, bf16[256,512]{1,0:T(8,128)(2,1)S(1)}) custom-call(s32[2,16]{1,0:T(2,128)S(1)} %bitcast.7, bf16[128,64,512]{2,1,0:T(8,128)(2,1)} %bitcast.9, bf16[2048,128]{1,0:T(8,128)(2,1)} %bitcast.11, bf16[512,512]{1,0:T(8,128)(2,1)} %refs_3_.3), custom_call_target="tpu_custom_call" | custom-call | bytes 557056 | tf_op jit(solution)/shard_map/make_messages/pallas_call | solution.py:116
  3.1 1.3 %collective-permute-start.3 = (bf16[256,512]{1,0:T(8,128)(2,1)S(1)}, bf16[256,512]{1,0:T(8,128)(2,1)S(1)}, u32[]{:S(2)}, u32[]{:S(2)}) collective-permute-start(bf16[256,512]{1,0:T(8,128)(2,1)S(1)} %get-tuple-element.16.refs_4_), channel_id=1, source_target_pairs={{0,2},{2,0},{1,3},{3,1},{4,6},{6,4},{5,7},{7,5},{8,10},{10,8},{9,1... | collective-permute-start | bytes 786440 | tf_op jit(solution)/shard_map/ppermute | solution.py:361
  4.4 0.2 collective-permute-start.1
  4.5 4.3 %make_messages.3 = (bf16[544,256]{1,0:T(8,128)(2,1)S(1)}, bf16[544,256]{1,0:T(8,128)(2,1)S(1)}, bf16[544,256]{1,0:T(8,128)(2,1)S(1)}, bf16[544,256]{1,0:T(8,128)...) custom-call(s32[2,16]{1,0:T(2,128)S(1)} %bitcast.8, ...), custom_call_target="tpu_custom_call" | custom-call | bytes 15597568 | tf_op jit(solution)/shard_map/make_messages/pallas_call | solution.py:116
  8.8 0.0 copy-start
  8.8 0.0 copy-start.2
  8.8 1.3 %collective-permute-start.9 = (bf16[1360,256]{1,0:T(8,128)(2,1)S(1)}, bf16[1360,256]{1,0:T(8,128)(2,1)S(1)}, u32[]{:S(2)}, u32[]{:S(2)}) collective-permute-start(bf16[1360,256]{1,0:T(8,128)(2,1)S(1)} %get-tuple-element.19), channel_id=1, source_target_pairs={{0,1},{1,0},{2,3},{3,2},{4,5},{5,4},{6,7},{7,6},{8,9},{9,8},{10,11... | collective-permute-start | bytes 2088968 | tf_op jit(solution)/shard_map/ppermute | solution.py:361
  10.2 2.3 %collective-permute-start.4 = (bf16[544,256]{1,0:T(8,128)(2,1)S(1)}, bf16[544,256]{1,0:T(8,128)(2,1)S(1)}, u32[]{:S(2)}, u32[]{:S(2)}) collective-permute-start(bf16[544,256]{1,0:T(8,128)(2,1)S(1)} %get-tuple-element.17), channel_id=1, source_target_pairs={{0,8},{1,9},{2,10},{3,11},{4,12},{5,13},{6,14},{7,15},{8,0},{9,1},... | collective-permute-start | bytes 835592 | tf_op jit(solution)/shard_map/ppermute | solution.py:400
  12.5 0.1 collective-permute-start
  12.5 0.0 collective-permute-done.3.refs_1_
  12.5 0.0 collective-permute-done.1.refs_1_.refs_0_
  12.6 1.3 %collective-permute-start.7 = (bf16[512,512]{1,0:T(8,128)(2,1)S(1)}, bf16[512,512]{1,0:T(8,128)(2,1)S(1)}, u32[]{:S(2)}, u32[]{:S(2)}) collective-permute-start(bf16[512,512]{1,0:T(8,128)(2,1)S(1)} %bundle.20.refs_0_.refs_2_), channel_id=1, source_target_pairs={{0,16},{16,0},{1,17},{17,1},{2,18},{18,2},{3,19},{19,3},{4,20},{20... | collective-permute-start | bytes 1572872 | tf_op jit(solution)/shard_map/ppermute | solution.py:361
  13.9 21.8 %collective-permute-done.refs_0_ = bf16[256,512]{1,0:T(8,128)(2,1)S(1)} collective-permute-done((bf16[256,512]{1,0:T(8,128)(2,1)S(1)}, bf16[256,512]{1,0:T(8,128)(2,1)S(1)}, u32[]{:S(2)}, u32[]{:S(2)}) %collective-permute-start) | collective-permute-done | bytes 262176 | tf_op jit(solution)/shard_map/ppermute | solution.py:361
  35.7 2.4 %collective-permute-start.2 = (bf16[256,512]{1,0:T(8,128)(2,1)S(1)}, bf16[256,512]{1,0:T(8,128)(2,1)S(1)}, u32[]{:S(2)}, u32[]{:S(2)}) collective-permute-start(bf16[256,512]{1,0:T(8,128)(2,1)S(1)} %bundle.17), channel_id=1, source_target_pairs={{0,4},{4,0},{8,12},{12,8},{1,5},{5,1},{9,13},{13,9},{2,6},{6,2},{1... | collective-permute-start | bytes 786440 | tf_op jit(solution)/shard_map/ppermute | solution.py:361
  38.2 0.0 collective-permute-done.4.refs_2_.refs_1_.refs_0_
  38.2 0.2 collective-permute-start.5
  38.4 0.0 collective-permute-done.9.refs_1_
  38.5 1.1 %collective-permute-start.10 = (bf16[1088,256]{1,0:T(8,128)(2,1)S(1)}, bf16[1088,256]{1,0:T(8,128)(2,1)S(1)}, u32[]{:S(2)}, u32[]{:S(2)}) collective-permute-start(bf16[1088,256]{1,0:T(8,128)(2,1)S(1)} %bundle.22), channel_id=1, source_target_pairs={{0,4},{1,13},{2,6},{3,15},{4,0},{5,9},{6,2},{7,11},{8,12},{9,5},{1... | collective-permute-start | bytes 1671176 | tf_op jit(solution)/shard_map/ppermute | solution.py:417
  39.6 4.9 %collective-permute-done.2.refs_1_.refs_0_ = bf16[256,512]{1,0:T(8,128)(2,1)S(1)} collective-permute-done((bf16[256,512]{1,0:T(8,128)(2,1)S(1)}, bf16[256,512]{1,0:T(8,128)(2,1)S(1)}, u32[]{:S(2)}, u32[]{:S(2)}) %collective-permute-start.2) | collective-permute-done | bytes 262176 | tf_op jit(solution)/shard_map/ppermute | solution.py:361
  44.5 0.9 collective-permute-done.5.refs_2_.refs_1_
  45.4 0.2 collective-permute-start.6
  45.7 0.0 collective-permute-done.7.refs_2_.refs_1_.refs_3_
  45.7 1.3 %collective-permute-start.8 = (bf16[512,512]{1,0:T(8,128)(2,1)S(1)}, bf16[512,512]{1,0:T(8,128)(2,1)S(1)}, u32[]{:S(2)}, u32[]{:S(2)}) collective-permute-start(bf16[512,512]{1,0:T(8,128)(2,1)S(1)} %bundle.21.refs_1_.refs_0_), channel_id=1, source_target_pairs={{0,16},{16,0},{1,17},{17,1},{2,18},{18,2},{3,19},{19,3},{4,20},{20... | collective-permute-start | bytes 1572872 | tf_op jit(solution)/shard_map/ppermute | solution.py:361
  47.0 0.1 bundle.28
  47.1 0.0 slice-start.1
  47.1 2.2 %collective-permute-start.17 = (bf16[1024,512]{1,0:T(8,128)(2,1)S(1)}, bf16[1024,512]{1,0:T(8,128)(2,1)S(1)}, u32[]{:S(2)}, u32[]{:S(2)}) collective-permute-start(bf16[1024,512]{1,0:T(8,128)(2,1)S(1)} %bundle.28), channel_id=1, source_target_pairs={{0,1},{1,0},{2,3},{3,2},{4,5},{5,4},{6,7},{7,6},{8,9},{9,8},{10,11... | collective-permute-start | bytes 3145736 | tf_op jit(solution)/shard_map/ppermute | solution.py:361
  49.3 7.9 %collective-permute-done.6.refs_1_.refs_0_ = bf16[512,512]{1,0:T(8,128)(2,1)S(1)} collective-permute-done((bf16[512,512]{1,0:T(8,128)(2,1)S(1)}, bf16[512,512]{1,0:T(8,128)(2,1)S(1)}, u32[]{:S(2)}, u32[]{:S(2)}) %collective-permute-start.6) | collective-permute-done | bytes 524320 | tf_op jit(solution)/shard_map/ppermute | solution.py:361
  57.3 0.0 collective-permute-done.10.refs_3_.refs_1_.refs_0_.refs_5_
  57.3 0.0 collective-permute-done.8.refs_2_.refs_1_
  57.3 1.3 %collective-permute-start.11 = (bf16[512,512]{1,0:T(8,128)(2,1)S(1)}, bf16[512,512]{1,0:T(8,128)(2,1)S(1)}, u32[]{:S(2)}, u32[]{:S(2)}) collective-permute-start(bf16[512,512]{1,0:T(8,128)(2,1)S(1)} %bundle.23.refs_0_.refs_1_), channel_id=1, source_target_pairs={{0,16},{16,0},{1,17},{17,1},{2,18},{18,2},{3,19},{19,3},{4,20},{20... | collective-permute-start | bytes 1572872 | tf_op jit(solution)/shard_map/ppermute | solution.py:361
  58.7 3.1 %collective-permute-start.18 = (bf16[512,512]{1,0:T(8,128)(2,1)S(1)}, bf16[512,512]{1,0:T(8,128)(2,1)S(1)}, u32[]{:S(2)}, u32[]{:S(2)}) collective-permute-start(bf16[512,512]{1,0:T(8,128)(2,1)S(1)} %get-tuple-element.23.refs_0_), channel_id=1, source_target_pairs={{0,1},{1,0},{2,3},{3,2},{4,5},{5,4},{6,7},{7,6},{8,9},{9,8},{10,11... | collective-permute-start | bytes 1572872 | tf_op jit(solution)/shard_map/ppermute | solution.py:361
  61.8 1.2 %collective-permute-start.14 = (bf16[544,256]{1,0:T(8,128)(2,1)S(1)}, bf16[544,256]{1,0:T(8,128)(2,1)S(1)}, u32[]{:S(2)}, u32[]{:S(2)}) collective-permute-start(bf16[544,256]{1,0:T(8,128)(2,1)S(1)} %after.2), channel_id=1, source_target_pairs={{0,2},{1,3},{2,0},{3,1},{4,6},{5,7},{6,4},{7,5},{8,10},{9,11},{10,... | collective-permute-start | bytes 835592 | tf_op jit(solution)/shard_map/ppermute | solution.py:400
  63.0 1.1 %row_mask.1.refs_3_.mask_ref = f32[512,128]{1,0:T(8,128)S(1)} custom-call(s32[1,16]{1,0:T(1,128)S(1)} %copy-done.2, s32[16,16]{1,0:T(8,128)S(1)} %copy-done), custom_call_target="tpu_custom_call" | custom-call | tf_op jit(solution)/shard_map/row_mask/pallas_call | solution.py:341
  64.2 0.4 collective-permute-start.13
  64.5 0.1 bundle.30
  64.6 17.4 %collective-permute-done.14.refs_1_.refs_3_ = bf16[544,256]{1,0:T(8,128)(2,1)S(1)} collective-permute-done((bf16[544,256]{1,0:T(8,128)(2,1)S(1)}, bf16[544,256]{1,0:T(8,128)(2,1)S(1)}, u32[]{:S(2)}, u32[]{:S(2)}) %collective-permute-start.14) | collective-permute-done | bytes 278560 | tf_op jit(solution)/shard_map/ppermute | solution.py:400
  82.0 0.8 collective-permute-start.21
  82.8 0.0 collective-permute-done.11.refs_1_.refs_2_
  82.8 0.1 collective-permute-start.15
  82.9 0.1 bundle.24
  83.0 0.0 collective-permute-done.18.refs_1_
  83.0 0.6 collective-permute-start.12
  83.5 1.2 %base_product.4.refs_3_ = f32[512,512]{1,0:T(8,128)S(1)} custom-call(bf16[512,8192]{1,0:T(8,128)(2,1)S(1)} %bitcast.6, bf16[512,512]{1,0:T(8,128)(2,1)S(1)} %get-tuple-element.23.refs_0_, bf16[512,512]{1,0:T(8,128)(2,1)S(1)} %collective-permute-done.18.refs_1_, bf16[512,512]{1,0:T(8,128)(2,1)S(1)} %bundle.20.refs_0_.refs_2_, ...), custom_call_target="tpu_custom_call" | custom-call | flops 1073741824 | bytes 5242880 | tf_op jit(solution)/shard_map/base_product/pallas_call | solution.py:179
  84.8 1.2 %base_product.5.refs_2_.refs_3_ = f32[512,512]{1,0:T(8,128)S(1)} custom-call(bf16[512,8192]{1,0:T(8,128)(2,1)S(1)} %bitcast.6, bf16[1024,512]{1,0:T(8,128)(2,1)S(1)} %collective-permute-done.17.refs_0_, bf16[512,512]{1,0:T(8,128)(2,1)S(1)} %bundle.21.refs_1_.refs_0_, bf16[512,512]{1,0:T(8,128)(2,1)S(1)} %collective-permute-done.8.refs_2_.refs_1_, ...), custom_call_target="tpu_custom_call" | custom-call | flops 1073741824 | bytes 5242880 | tf_op jit(solution)/shard_map/base_product/pallas_call | solution.py:179
  86.1 1.6 %collective-permute-start.19 = (bf16[544,256]{1,0:T(8,128)(2,1)S(1)}, bf16[544,256]{1,0:T(8,128)(2,1)S(1)}, u32[]{:S(2)}, u32[]{:S(2)}) collective-permute-start(bf16[544,256]{1,0:T(8,128)(2,1)S(1)} %after.3), channel_id=1, source_target_pairs={{0,14},{1,15},{2,12},{3,13},{4,10},{5,11},{6,8},{7,9},{8,6},{9,7},... | collective-permute-start | bytes 835592 | tf_op jit(solution)/shard_map/ppermute | solution.py:400
  87.6 0.0 collective-permute-done.15.refs_3_.refs_4_
  87.6 0.0 collective-permute-done.13.refs_2_.refs_0_.refs_1_
  87.7 0.3 collective-permute-start.16
  88.0 7.3 %collective-permute-done.16.refs_1_.refs_2_ = bf16[256,512]{1,0:T(8,128)(2,1)S(1)} collective-permute-done((bf16[256,512]{1,0:T(8,128)(2,1)S(1)}, bf16[256,512]{1,0:T(8,128)(2,1)S(1)}, u32[]{:S(2)}, u32[]{:S(2)}) %collective-permute-start.16) | collective-permute-done | bytes 262176 | tf_op jit(solution)/shard_map/ppermute | solution.py:361
  95.3 5.9 %collective-permute-done.19.refs_2_.refs_0_ = bf16[544,256]{1,0:T(8,128)(2,1)S(1)} collective-permute-done((bf16[544,256]{1,0:T(8,128)(2,1)S(1)}, bf16[544,256]{1,0:T(8,128)(2,1)S(1)}, u32[]{:S(2)}, u32[]{:S(2)}) %collective-permute-start.19) | collective-permute-done | bytes 278560 | tf_op jit(solution)/shard_map/ppermute | solution.py:400
  101.3 0.9 collective-permute-start.20
  102.2 0.1 collective-permute-start.22
  102.3 0.5 collective-permute-start.23
  102.9 1.2 %collective-permute-done.22.refs_6_ = bf16[544,256]{1,0:T(8,128)(2,1)S(1)} collective-permute-done((bf16[544,256]{1,0:T(8,128)(2,1)S(1)}, bf16[544,256]{1,0:T(8,128)(2,1)S(1)}, u32[]{:S(2)}, u32[]{:S(2)}) %collective-permute-start.22) | collective-permute-done | bytes 278560 | tf_op jit(solution)/shard_map/ppermute | solution.py:361
  104.1 1.5 %adapt_begin.1 = (f32[512,128]{1,0:T(8,128)S(1)}, bf16[512,128]{1,0:T(8,128)(2,1)S(1)}) custom-call(bf16[512,8192]{1,0:T(8,128)(2,1)S(1)} %bitcast.6, bf16[272,256]{1,0:T(8,128)(2,1)S(1)} %get-tuple-element.24.refs_0_, bf16[1360,256]{1,0:T(8,128)(2,1)S(1)} %collective-permute-done.9.refs_1_, ...), custom_call_target="tpu_custom_call" | custom-call | flops 1288490240 | bytes 5033164 | tf_op jit(solution)/shard_map/adapt_begin/pallas_call | solution.py:241
  105.7 0.4 collective-permute-start.24
  106.1 0.0 collective-permute-done.21.refs_0_
  106.1 1.2 %base_product.6.refs_4_ = f32[512,512]{1,0:T(8,128)S(1)} custom-call(bf16[512,8192]{1,0:T(8,128)(2,1)S(1)} %bitcast.6, bf16[1024,512]{1,0:T(8,128)(2,1)S(1)} %collective-permute-done.21.refs_0_, bf16[512,512]{1,0:T(8,128)(2,1)S(1)} %bundle.23.refs_0_.refs_1_, bf16[512,512]{1,0:T(8,128)(2,1)S(1)} %collective-permute-done.11.refs_1_.refs_2_, ...), custom_call_target="tpu_custom_call" | custom-call | flops 1073741824 | bytes 5242880 | tf_op jit(solution)/shard_map/base_product/pallas_call | solution.py:179
  107.4 0.0 collective-permute-done.20.refs_3_
  107.4 0.0 collective-permute-done.12.refs_0_
  107.4 1.3 %base_product.7.base_ref = f32[512,512]{1,0:T(8,128)S(1)} custom-call(bf16[512,8192]{1,0:T(8,128)(2,1)S(1)} %bitcast.6, bf16[1024,512]{1,0:T(8,128)(2,1)S(1)} %collective-permute-done.12.refs_0_, bf16[256,512]{1,0:T(8,128)(2,1)S(1)} %bundle.27.refs_0_.refs_1_, bf16[256,512]{1,0:T(8,128)(2,1)S(1)} %collective-permute-done.16.refs_1_.refs_2_, ...), custom_call_target="tpu_custom_call" | custom-call | flops 1073741824 | bytes 5242880 | tf_op jit(solution)/shard_map/base_product/pallas_call | solution.py:179
  108.6 0.0 collective-permute-done.24.refs_3_
  108.7 1.9 %adapt_end.1 = bf16[512,512]{1,0:T(8,128)(2,1)} custom-call(bf16[512,8192]{1,0:T(8,128)(2,1)S(1)} %bitcast.6, f32[512,128]{1,0:T(8,128)S(1)} %row_mask.1.refs_3_.mask_ref, f32[512,512]{1,0:T(8,128)S(1)} %base_product.7.base_ref, f32[512,128]{1,0:T(8,128)S(1)} %get-tuple-element.25.shrunk, bf16[512,128]{1,0:T(8,128)(2,1)S(1)} %get-tuple-element.26.widened, ...), custom_call_target="tpu_custom_call" | custom-call | flops 858993472 | bytes 3355443 | tf_op jit(solution)/shard_map/adapt_end/pallas_call | solution.py:273
  (25 shorter events, 0.4 us)
Async XLA Ops:
  0.0 0.7 copy-start.1
  3.1 9.5 %collective-permute-start.3 = (bf16[256,512]{1,0:T(8,128)(2,1)S(1)}, bf16[256,512]{1,0:T(8,128)(2,1)S(1)}, u32[]{:S(2)}, u32[]{:S(2)}) collective-permute-start(bf16[256,512]{1,0:T(8,128)(2,1)S(1)} %get-tuple-element.16.refs_4_), channel_id=1, source_target_pairs={{0,2},{2,0},{1,3},{3,1},{4,6},{6,4},{5,7},{7,5},{8,10},{10,8},{9,1... | collective-permute-start | bytes 786440 | tf_op jit(solution)/shard_map/ppermute | solution.py:361
  4.4 8.2 %collective-permute-start.1 = (bf16[256,512]{1,0:T(8,128)(2,1)S(1)}, bf16[256,512]{1,0:T(8,128)(2,1)S(1)}, u32[]{:S(2)}, u32[]{:S(2)}) collective-permute-start(bf16[256,512]{1,0:T(8,128)(2,1)S(1)} %get-tuple-element.16.refs_4_), channel_id=1, source_target_pairs={{0,4},{4,0},{8,12},{12,8},{1,5},{5,1},{9,13},{13,9},{2,6},{6,2},{1... | collective-permute-start | bytes 786440 | tf_op jit(solution)/shard_map/ppermute | solution.py:361
  8.8 54.2 %copy-start = (s32[16,16]{1,0:T(8,128)S(1)}, s32[16,16]{1,0:T(8,128)}, u32[]{:S(2)}) copy-start(s32[16,16]{1,0:T(8,128)} %slots_ref.1) | copy-start | bytes 3076
  8.8 54.2 %copy-start.2 = (s32[1,16]{1,0:T(1,128)S(1)}, s32[1,16]{1,0:T(1,128)}, u32[]{:S(2)}) copy-start(s32[1,16]{1,0:T(1,128)} %lengths_ref.1) | copy-start | bytes 196
  8.8 29.6 %collective-permute-start.9 = (bf16[1360,256]{1,0:T(8,128)(2,1)S(1)}, bf16[1360,256]{1,0:T(8,128)(2,1)S(1)}, u32[]{:S(2)}, u32[]{:S(2)}) collective-permute-start(bf16[1360,256]{1,0:T(8,128)(2,1)S(1)} %get-tuple-element.19), channel_id=1, source_target_pairs={{0,1},{1,0},{2,3},{3,2},{4,5},{5,4},{6,7},{7,6},{8,9},{9,8},{10,11... | collective-permute-start | bytes 2088968 | tf_op jit(solution)/shard_map/ppermute | solution.py:361
  10.2 28.0 %collective-permute-start.4 = (bf16[544,256]{1,0:T(8,128)(2,1)S(1)}, bf16[544,256]{1,0:T(8,128)(2,1)S(1)}, u32[]{:S(2)}, u32[]{:S(2)}) collective-permute-start(bf16[544,256]{1,0:T(8,128)(2,1)S(1)} %get-tuple-element.17), channel_id=1, source_target_pairs={{0,8},{1,9},{2,10},{3,11},{4,12},{5,13},{6,14},{7,15},{8,0},{9,1},... | collective-permute-start | bytes 835592 | tf_op jit(solution)/shard_map/ppermute | solution.py:400
  12.5 23.2 %collective-permute-start = (bf16[256,512]{1,0:T(8,128)(2,1)S(1)}, bf16[256,512]{1,0:T(8,128)(2,1)S(1)}, u32[]{:S(2)}, u32[]{:S(2)}) collective-permute-start(bf16[256,512]{1,0:T(8,128)(2,1)S(1)} %get-tuple-element.16.refs_4_), channel_id=1, source_target_pairs={{0,8},{4,12},{8,0},{12,4},{1,9},{5,13},{9,1},{13,5},{2,10},{6,14},... | collective-permute-start | bytes 786440 | tf_op jit(solution)/shard_map/ppermute | solution.py:361
  12.6 33.1 %collective-permute-start.7 = (bf16[512,512]{1,0:T(8,128)(2,1)S(1)}, bf16[512,512]{1,0:T(8,128)(2,1)S(1)}, u32[]{:S(2)}, u32[]{:S(2)}) collective-permute-start(bf16[512,512]{1,0:T(8,128)(2,1)S(1)} %bundle.20.refs_0_.refs_2_), channel_id=1, source_target_pairs={{0,16},{16,0},{1,17},{17,1},{2,18},{18,2},{3,19},{19,3},{4,20},{20... | collective-permute-start | bytes 1572872 | tf_op jit(solution)/shard_map/ppermute | solution.py:361
  35.7 8.7 %collective-permute-start.2 = (bf16[256,512]{1,0:T(8,128)(2,1)S(1)}, bf16[256,512]{1,0:T(8,128)(2,1)S(1)}, u32[]{:S(2)}, u32[]{:S(2)}) collective-permute-start(bf16[256,512]{1,0:T(8,128)(2,1)S(1)} %bundle.17), channel_id=1, source_target_pairs={{0,4},{4,0},{8,12},{12,8},{1,5},{5,1},{9,13},{13,9},{2,6},{6,2},{1... | collective-permute-start | bytes 786440 | tf_op jit(solution)/shard_map/ppermute | solution.py:361
  38.2 7.2 %collective-permute-start.5 = (bf16[256,512]{1,0:T(8,128)(2,1)S(1)}, bf16[256,512]{1,0:T(8,128)(2,1)S(1)}, u32[]{:S(2)}, u32[]{:S(2)}) collective-permute-start(bf16[256,512]{1,0:T(8,128)(2,1)S(1)} %bundle.18), channel_id=1, source_target_pairs={{0,2},{2,0},{1,3},{3,1},{4,6},{6,4},{5,7},{7,5},{8,10},{10,8},{9,1... | collective-permute-start | bytes 786440 | tf_op jit(solution)/shard_map/ppermute | solution.py:361
  38.4 45.1 %slice-start = ((s8[8388608]{0:T(1024)(128)(4,1)}), s8[4194304]{0:T(1024)(128)(4,1)S(1)}, s32[]{:S(2)}) async-start(s8[8388608]{0:T(1024)(128)(4,1)} %bitcast.5), calls=%async_computation | async-start | bytes 8388608
  38.5 18.8 %collective-permute-start.10 = (bf16[1088,256]{1,0:T(8,128)(2,1)S(1)}, bf16[1088,256]{1,0:T(8,128)(2,1)S(1)}, u32[]{:S(2)}, u32[]{:S(2)}) collective-permute-start(bf16[1088,256]{1,0:T(8,128)(2,1)S(1)} %bundle.22), channel_id=1, source_target_pairs={{0,4},{1,13},{2,6},{3,15},{4,0},{5,9},{6,2},{7,11},{8,12},{9,5},{1... | collective-permute-start | bytes 1671176 | tf_op jit(solution)/shard_map/ppermute | solution.py:417
  45.4 11.9 %collective-permute-start.6 = (bf16[512,512]{1,0:T(8,128)(2,1)S(1)}, bf16[512,512]{1,0:T(8,128)(2,1)S(1)}, u32[]{:S(2)}, u32[]{:S(2)}) collective-permute-start(bf16[512,512]{1,0:T(8,128)(2,1)S(1)} %bundle.19), channel_id=1, source_target_pairs={{0,2},{2,0},{1,3},{3,1},{4,6},{6,4},{5,7},{7,5},{8,10},{10,8},{9,1... | collective-permute-start | bytes 1572872 | tf_op jit(solution)/shard_map/ppermute | solution.py:361
  45.7 11.6 %collective-permute-start.8 = (bf16[512,512]{1,0:T(8,128)(2,1)S(1)}, bf16[512,512]{1,0:T(8,128)(2,1)S(1)}, u32[]{:S(2)}, u32[]{:S(2)}) collective-permute-start(bf16[512,512]{1,0:T(8,128)(2,1)S(1)} %bundle.21.refs_1_.refs_0_), channel_id=1, source_target_pairs={{0,16},{16,0},{1,17},{17,1},{2,18},{18,2},{3,19},{19,3},{4,20},{20... | collective-permute-start | bytes 1572872 | tf_op jit(solution)/shard_map/ppermute | solution.py:361
  47.1 36.4 %slice-start.1 = ((s8[8388608]{0:T(1024)(128)(4,1)}), s8[4194304]{0:T(1024)(128)(4,1)S(1)}, s32[]{:S(2)}) async-start(s8[8388608]{0:T(1024)(128)(4,1)} %bitcast.5), calls=%async_computation.1 | async-start | bytes 8388608
  47.1 37.7 %collective-permute-start.17 = (bf16[1024,512]{1,0:T(8,128)(2,1)S(1)}, bf16[1024,512]{1,0:T(8,128)(2,1)S(1)}, u32[]{:S(2)}, u32[]{:S(2)}) collective-permute-start(bf16[1024,512]{1,0:T(8,128)(2,1)S(1)} %bundle.28), channel_id=1, source_target_pairs={{0,1},{1,0},{2,3},{3,2},{4,5},{5,4},{6,7},{7,6},{8,9},{9,8},{10,11... | collective-permute-start | bytes 3145736 | tf_op jit(solution)/shard_map/ppermute | solution.py:361
  57.3 25.5 %collective-permute-start.11 = (bf16[512,512]{1,0:T(8,128)(2,1)S(1)}, bf16[512,512]{1,0:T(8,128)(2,1)S(1)}, u32[]{:S(2)}, u32[]{:S(2)}) collective-permute-start(bf16[512,512]{1,0:T(8,128)(2,1)S(1)} %bundle.23.refs_0_.refs_1_), channel_id=1, source_target_pairs={{0,16},{16,0},{1,17},{17,1},{2,18},{18,2},{3,19},{19,3},{4,20},{20... | collective-permute-start | bytes 1572872 | tf_op jit(solution)/shard_map/ppermute | solution.py:361
  58.7 24.3 %collective-permute-start.18 = (bf16[512,512]{1,0:T(8,128)(2,1)S(1)}, bf16[512,512]{1,0:T(8,128)(2,1)S(1)}, u32[]{:S(2)}, u32[]{:S(2)}) collective-permute-start(bf16[512,512]{1,0:T(8,128)(2,1)S(1)} %get-tuple-element.23.refs_0_), channel_id=1, source_target_pairs={{0,1},{1,0},{2,3},{3,2},{4,5},{5,4},{6,7},{7,6},{8,9},{9,8},{10,11... | collective-permute-start | bytes 1572872 | tf_op jit(solution)/shard_map/ppermute | solution.py:361
  61.8 20.2 %collective-permute-start.14 = (bf16[544,256]{1,0:T(8,128)(2,1)S(1)}, bf16[544,256]{1,0:T(8,128)(2,1)S(1)}, u32[]{:S(2)}, u32[]{:S(2)}) collective-permute-start(bf16[544,256]{1,0:T(8,128)(2,1)S(1)} %after.2), channel_id=1, source_target_pairs={{0,2},{1,3},{2,0},{3,1},{4,6},{5,7},{6,4},{7,5},{8,10},{9,11},{10,... | collective-permute-start | bytes 835592 | tf_op jit(solution)/shard_map/ppermute | solution.py:400
  64.2 23.5 %collective-permute-start.13 = (bf16[1088,256]{1,0:T(8,128)(2,1)S(1)}, bf16[1088,256]{1,0:T(8,128)(2,1)S(1)}, u32[]{:S(2)}, u32[]{:S(2)}) collective-permute-start(bf16[1088,256]{1,0:T(8,128)(2,1)S(1)} %bundle.25), channel_id=1, source_target_pairs={{0,10},{1,7},{2,8},{3,5},{4,14},{5,3},{6,12},{7,1},{8,2},{9,15},{1... | collective-permute-start | bytes 1671176 | tf_op jit(solution)/shard_map/ppermute | solution.py:417
  82.0 24.1 %collective-permute-start.21 = (bf16[1024,512]{1,0:T(8,128)(2,1)S(1)}, bf16[1024,512]{1,0:T(8,128)(2,1)S(1)}, u32[]{:S(2)}, u32[]{:S(2)}) collective-permute-start(bf16[1024,512]{1,0:T(8,128)(2,1)S(1)} %bundle.30), channel_id=1, source_target_pairs={{0,1},{1,0},{2,3},{3,2},{4,5},{5,4},{6,7},{7,6},{8,9},{9,8},{10,11... | collective-permute-start | bytes 3145736 | tf_op jit(solution)/shard_map/ppermute | solution.py:361
  82.8 4.8 %collective-permute-start.15 = (bf16[544,256]{1,0:T(8,128)(2,1)S(1)}, bf16[544,256]{1,0:T(8,128)(2,1)S(1)}, u32[]{:S(2)}, u32[]{:S(2)}) collective-permute-start(bf16[544,256]{1,0:T(8,128)(2,1)S(1)} %bundle.26), channel_id=1, source_target_pairs={{0,1},{1,0},{2,3},{3,2},{4,5},{5,4},{6,7},{7,6},{8,9},{9,8},{10,11... | collective-permute-start | bytes 835592 | tf_op jit(solution)/shard_map/ppermute | solution.py:361
  83.0 24.4 %collective-permute-start.12 = (bf16[1024,512]{1,0:T(8,128)(2,1)S(1)}, bf16[1024,512]{1,0:T(8,128)(2,1)S(1)}, u32[]{:S(2)}, u32[]{:S(2)}) collective-permute-start(bf16[1024,512]{1,0:T(8,128)(2,1)S(1)} %bundle.24), channel_id=1, source_target_pairs={{0,1},{1,0},{2,3},{3,2},{4,5},{5,4},{6,7},{7,6},{8,9},{9,8},{10,11... | collective-permute-start | bytes 3145736 | tf_op jit(solution)/shard_map/ppermute | solution.py:361
  86.1 15.2 %collective-permute-start.19 = (bf16[544,256]{1,0:T(8,128)(2,1)S(1)}, bf16[544,256]{1,0:T(8,128)(2,1)S(1)}, u32[]{:S(2)}, u32[]{:S(2)}) collective-permute-start(bf16[544,256]{1,0:T(8,128)(2,1)S(1)} %after.3), channel_id=1, source_target_pairs={{0,14},{1,15},{2,12},{3,13},{4,10},{5,11},{6,8},{7,9},{8,6},{9,7},... | collective-permute-start | bytes 835592 | tf_op jit(solution)/shard_map/ppermute | solution.py:400
  87.7 7.6 %collective-permute-start.16 = (bf16[256,512]{1,0:T(8,128)(2,1)S(1)}, bf16[256,512]{1,0:T(8,128)(2,1)S(1)}, u32[]{:S(2)}, u32[]{:S(2)}) collective-permute-start(bf16[256,512]{1,0:T(8,128)(2,1)S(1)} %bundle.27.refs_0_.refs_1_), channel_id=1, source_target_pairs={{0,16},{16,0},{1,17},{17,1},{2,18},{18,2},{3,19},{19,3},{4,20},{20... | collective-permute-start | bytes 786440 | tf_op jit(solution)/shard_map/ppermute | solution.py:361
  101.3 6.1 %collective-permute-start.20 = (bf16[512,512]{1,0:T(8,128)(2,1)S(1)}, bf16[512,512]{1,0:T(8,128)(2,1)S(1)}, u32[]{:S(2)}, u32[]{:S(2)}) collective-permute-start(bf16[512,512]{1,0:T(8,128)(2,1)S(1)} %bundle.29), channel_id=1, source_target_pairs={{0,1},{1,0},{2,3},{3,2},{4,5},{5,4},{6,7},{7,6},{8,9},{9,8},{10,11... | collective-permute-start | bytes 1572872 | tf_op jit(solution)/shard_map/ppermute | solution.py:361
  102.2 1.9 %collective-permute-start.22 = (bf16[544,256]{1,0:T(8,128)(2,1)S(1)}, bf16[544,256]{1,0:T(8,128)(2,1)S(1)}, u32[]{:S(2)}, u32[]{:S(2)}) collective-permute-start(bf16[544,256]{1,0:T(8,128)(2,1)S(1)} %bundle.31), channel_id=1, source_target_pairs={{0,1},{1,0},{2,3},{3,2},{4,5},{5,4},{6,7},{7,6},{8,9},{9,8},{10,11... | collective-permute-start | bytes 835592 | tf_op jit(solution)/shard_map/ppermute | solution.py:361
  102.3 6.3 %collective-permute-start.23 = (bf16[544,256]{1,0:T(8,128)(2,1)S(1)}, bf16[544,256]{1,0:T(8,128)(2,1)S(1)}, u32[]{:S(2)}, u32[]{:S(2)}) collective-permute-start(bf16[544,256]{1,0:T(8,128)(2,1)S(1)} %bundle.32), channel_id=1, source_target_pairs={{0,1},{1,0},{2,3},{3,2},{4,5},{5,4},{6,7},{7,6},{8,9},{9,8},{10,11... | collective-permute-start | bytes 835592 | tf_op jit(solution)/shard_map/ppermute | solution.py:361
  105.7 3.0 %collective-permute-start.24 = (bf16[272,256]{1,0:T(8,128)(2,1)S(1)}, bf16[272,256]{1,0:T(8,128)(2,1)S(1)}, u32[]{:S(2)}, u32[]{:S(2)}) collective-permute-start(bf16[272,256]{1,0:T(8,128)(2,1)S(1)} %bundle.33), channel_id=1, source_target_pairs={{0,1},{1,0},{2,3},{3,2},{4,5},{5,4},{6,7},{7,6},{8,9},{9,8},{10,11... | collective-permute-start | bytes 417800 | tf_op jit(solution)/shard_map/ppermute | solution.py:361

commit v8 on v7

--- a/solution.py
+++ b/solution.py
@@ -26,8 +26,22 @@
     return (lax.axis_index("line") * 2 + lax.axis_index("plane")) * 2 + lax.axis_index("core")
 
 
-DIRECT_FIRST, DIRECT_LAST, DIRECT_NEAR = 4, 7, 1
-ROUNDS = ((2, 6), (5, 3))
+EARLY, LATE = (5,), ()
+ROUNDS = ((1, 4), (3, 7), (2, 6))
+LAST = ('R1', 'P5')
+TIES = {
+    "Y2": ("B0", "T2", "X1",),
+    "X4": ("T2", "X3", "Y1",),
+    "C1": ("X2", "mask",),
+    "C2": ("X3",),
+    "C3": ("AB",),
+    "C4": ("AB", "B1", "F0", "R1", "Y2",),
+    "B1": ("R0",),
+    "F0": ("Y3",),
+    "T1": ("R0", "Y2", "Z3",),
+    "T2": ("P5", "Y1", "Z2",),
+    "mask": ("B0", "T1", "Y0",),
+}
 
 
 def direct_targets(mask):
@@ -145,7 +159,7 @@
     return messages, whole, half
 
 
-def base_product(tokens, bundles, start=None):
+def base_product(tokens, bundles, start=None, others=()):
     rows, depth = tokens.shape
     width = bundles[0][1].shape[1]
     count = len(bundles)
@@ -175,7 +189,7 @@
                 out[...] += total
             first = False
 
-    extra = [] if start is None else [start]
+    extra = ([] if start is None else [start]) + list(others)
     return pl.pallas_call(
         kernel,
         out_shape=pltpu.VMEM((rows, width), jnp.float32),
@@ -323,10 +337,11 @@
     )(*[in_vmem(value) for value in values])
 
 
-def row_mask(lengths, slots, rows, choices, rank):
+def row_mask(lengths, slots, rows, choices, rank, others):
     requests = lengths.shape[1]
 
-    def kernel(lengths_ref, slots_ref, out):
+    def kernel(lengths_ref, slots_ref, *refs):
+        out = refs[-1]
         group = store_index()
         position = lax.broadcasted_iota(jnp.int32, out.shape, 0)
         lane_slot = lax.broadcasted_iota(jnp.int32, out.shape, 1) // rank
@@ -341,11 +356,12 @@
     return pl.pallas_call(
         kernel,
         out_shape=pltpu.VMEM((rows, choices * rank), jnp.float32),
-        in_specs=[pl.BlockSpec(memory_space=pltpu.SMEM)] * 2,
+        in_specs=[pl.BlockSpec(memory_space=pltpu.SMEM)] * 2
+        + [pl.BlockSpec(memory_space=pltpu.VMEM)] * len(others),
         out_specs=pl.BlockSpec(memory_space=pltpu.VMEM),
         compiler_params=pltpu.CompilerParams(vmem_limit_bytes=2 * MIB),
         name="row_mask",
-    )(lengths, slots)
+    )(lengths, slots, *[in_vmem(other) for other in others])
 
 
 def row_slots(lengths, slots, rows):
@@ -361,66 +377,26 @@
     return lax.ppermute(block, axis, [(i, i ^ bit) for i in range(size)])
 
 
-def gather_rows(whole, half, paces, plane_pace):
-    z2 = swap(half, "line", 2)
-    z1 = swap(half, "line", 1)
-    y0 = swap(half, "plane", 1)
-    z3 = swap(bundle([z2], [z1]), "line", 1)
-    y1 = swap(bundle([z1], [y0, *plane_pace]), "plane", 1)
-    y23 = swap(bundle([z2, z3], [y1]), "plane", 1)
-    y2, y3 = (y23, lambda: 0, HALF), (y23, lambda: HALF, HALF)
-    bundles = [([(None, 0, 0, 0)], whole), ([(None, 0, 0, 1)], swap(whole, "core", 1))]
-    before = []
-    for n, (places, blocks) in enumerate(
-        (
-            ([(1, 0), (0, 1)], [z1, y0]),
-            ([(2, 0), (1, 1)], [z2, y1]),
-            ([(3, 0), (2, 1)], [z3, y2]),
-            ([(3, 1)], [y3]),
-        )
-    ):
-        sent = bundle(blocks, before + paces[n])
-        got = swap(sent, "parts", 1)
-        bundles.append(([(0, z, y, 0) for z, y in places], sent))
-        bundles.append(([(1, z, y, 0) for z, y in places], got))
-
-        def from_core(*others, places=places, held=(sent, got)):
-            masks = [(x, z, y, 1) for x in range(2) for z, y in places]
-            return masks, swap(bundle(held, others), "core", 1)
-
-        if n < 3:
-            bundles.append(from_core())
-        before = [got]
-    return bundles, from_core
-
-
-def send_chip(mask, messages, *others):
+def send_pairs(payload, target):
     size = 2 * lax.axis_size("line") * lax.axis_size("plane")
-    payload = after(messages, *others) if others else messages
-    return lax.ppermute(payload, AXES[1:], [(i, i ^ (2 * mask)) for i in range(size)])
-
-
-def hand_on(*arrived):
-    length = arrived[0].shape[0] // 2
-
-    return swap(bundle([(pair, lambda: length, length) for pair in arrived]), "core", 1)
-
-
-def send_round(masks, mine, theirs, *others):
-    size = 2 * lax.axis_size("line") * lax.axis_size("plane")
-    length = mine.shape[0] // 2
-    pairs = [
-        (chip * 2 + core, (chip ^ masks[core]) * 2 + core)
-        for chip in range(size // 2)
-        for core in range(2)
-    ]
-    got = lax.ppermute(bundle([mine, theirs], others), AXES[1:], pairs)
-
-    def place(i):
-        return pl.multiple_of((2 * i + 1 - lax.axis_index("core")) * length, 16)
-
-    parts = [(got, functools.partial(place, i), length) for i in range(2)]
-    return got, swap(bundle(parts), "core", 1)
+    return lax.ppermute(payload, AXES[1:], [(i, target(i)) for i in range(size)])
+
+
+ROWS = {
+    "Z1": ("line", 1, ["own"]),
+    "Z2": ("line", 2, ["own"]),
+    "Z3": ("line", 1, ["Z2"]),
+    "Y0": ("plane", 1, ["own"]),
+    "Y1": ("plane", 1, ["Z1"]),
+    "Y2": ("plane", 1, ["Z2"]),
+    "Y3": ("plane", 1, ["Z3"]),
+    "X1": ("parts", 1, ["Z1", "Y0"]),
+    "X2": ("parts", 1, ["Z2", "Y1"]),
+    "X3": ("parts", 1, ["Z3", "Y2"]),
+    "X4": ("parts", 1, ["Y3"]),
+}
+PLACES = {name: (int(name[1]), int(name[0] == "Y")) for name in ROWS if name[0] in "ZY"}
+STEPS = (("whole", "CW", "S1", "X1"), ("C1", "S2", "X2"), ("C2", "S3", "X3"), ("C3", "S4", "X4", "C4"))
 
 
 def body(
@@ -430,7 +406,7 @@
     choices = group_adapters.shape[1]
     width = base_weight.shape[1]
     shard_width = adapter_up.shape[1]
-    mask = row_mask(request_lengths, request_slot, tokens.shape[0], choices, rank)
+    pair = choices * rank
     operands = (
         jnp.transpose(group_adapters),
         jnp.swapaxes(adapter_down, 1, 2),
@@ -439,86 +415,185 @@
         shard_width,
     )
 
-    def first_targets():
-        return [(0, target) for target in direct_targets(DIRECT_FIRST)]
-
-    def other_targets():
+    def early_targets():
+        targets = []
+        for n, mask in enumerate(EARLY):
+            targets += [(n, target) for target in direct_targets(mask)]
+        return targets
+
+    def late_targets():
         core = lax.axis_index("core")
-        targets = [(0, target) for target in direct_targets(DIRECT_LAST)]
-        targets += [(1, target) for target in direct_targets(DIRECT_NEAR)]
+        targets = []
+        for n, mask in enumerate(LATE):
+            targets += [(n, target) for target in direct_targets(mask)]
         for n, masks in enumerate(ROUNDS):
-            targets += [(2 + n, target) for target in round_targets(masks, core)]
-        for masks in ROUNDS:
-            targets += [(4, target) for target in round_targets(masks, 1 - core)]
+            targets += [(len(LATE) + n, target) for target in round_targets(masks, core)]
+            targets += [
+                (len(LATE) + len(ROUNDS) + n, target) for target in round_targets(masks, 1 - core)
+            ]
         me = store_index()
-        return targets + [(4, me ^ 1), (5, me)]
-
-    (pair_first,), whole, half = make_messages(*operands, (2,), first_targets, 1)
-    (pair_last, pair_near, mine_a, mine_b, theirs, local), _, _ = make_messages(
-        *operands, (2, 2, 2, 2, 5, 1), other_targets, COST, [half]
-    )
-    length = local.shape[0]
-
-    got_first = send_chip(DIRECT_FIRST, pair_first)
-    swapped = swap(theirs, "core", 1)
-    got_a, handed_a = send_round(ROUNDS[0], mine_a, (swapped, lambda: 0, 2 * length))
-    got_near = send_chip(DIRECT_NEAR, pair_near, got_first)
-    handed_first = hand_on(got_first, got_near)
-    got_b, handed_b = send_round(
-        ROUNDS[1], mine_b, (swapped, lambda: 2 * length, 2 * length), got_first, mask
-    )
-    paces = [[], [], [got_a], [got_b, handed_first]]
-    bundles, last_rows = gather_rows(whole, half, paces, [got_first])
-    base = base_product(tokens, bundles[:4])
-    base = base_product(tokens, bundles[4:7], base)
-    got_last = send_chip(DIRECT_LAST, pair_last, got_a, base)
-    handed_last = hand_on(got_last)
-    bundles.append(last_rows(got_last))
-    base = base_product(tokens, bundles[7:10], base)
-    base = base_product(tokens, bundles[10:], base)
-
-    def round_sources(masks, first):
+        last = len(LATE) + 2 * len(ROUNDS)
+        return targets + [(last - 1, me ^ 1), (last, me)]
+
+    early_count = len(EARLY)
+    late_counts = (2,) * len(LATE) + (2,) * (2 * len(ROUNDS) - 1) + (3, 1)
+    values = {}
+
+    def get(name):
+        if name not in values:
+            values[name] = make(name)
+        return values[name]
+
+    def wait(name):
+        return [get(other) for other in TIES.get(name, ())]
+
+    def first_messages():
+        messages, whole, half = make_messages(
+            *operands, (2,) * early_count, early_targets, 1, wait("early")
+        )
+        for mask, message in zip(EARLY, messages):
+            values[f"pair{mask}"] = message
+        values["whole"], values["own"] = whole, half
+
+    def other_messages():
+        messages, _, _ = make_messages(
+            *operands, late_counts, late_targets, COST, [get("own"), *wait("late")]
+        )
+        for mask, message in zip(LATE, messages):
+            values[f"pair{mask}"] = message
+        for n, message in enumerate(messages[len(LATE) :]):
+            kind, number = divmod(n, len(ROUNDS))
+            values[("mine", "theirs", "local")[kind] + str(number)] = message
+
+    def make(name):
+        kind, number = name[0], name[1:]
+        if name in ("whole", "own") or name in [f"pair{mask}" for mask in EARLY]:
+            first_messages()
+            return values[name]
+        if name[:4] in ("pair", "mine", "thei", "loca"):
+            other_messages()
+            return values[name]
+        if name in ROWS:
+            axis, mask, sources = ROWS[name]
+            others = wait(name)
+            if kind == "X":
+                payload = get("S" + number)
+            elif others:
+                payload = bundle([get(source) for source in sources], others)
+            else:
+                payload = get(sources[0])
+            return swap(payload, axis, mask)
+        if kind == "S":
+            return bundle([get(source) for source in ROWS["X" + number][2]], wait("X" + number))
+        if name == "CW":
+            others = wait(name)
+            return swap(bundle([get("whole")], others) if others else get("whole"), "core", 1)
+        if kind == "C":
+            return swap(bundle([get("S" + number), get("X" + number)], wait(name)), "core", 1)
+        if kind == "T":
+            return swap(after(get("theirs" + number), *wait(name)), "core", 1)
+        if kind == "P":
+            message = get("pair" + number)
+            others = wait(name)
+            payload = after(message, *others) if others else message
+            return send_pairs(payload, lambda i: i ^ (2 * int(number)))
+        if kind == "H":
+            got, length = get("P" + number), get("local0").shape[0]
+            return swap(bundle([(got, lambda: length, length)], wait(name)), "core", 1)
+        if kind == "R":
+            masks, length = ROUNDS[int(number)], get("local0").shape[0]
+            theirs = (get("T" + number), lambda: 0, 2 * length)
+            payload = bundle([get("mine" + number), theirs], wait(name))
+            return send_pairs(payload, lambda i: i ^ (2 * masks[i % 2]))
+        if kind == "F":
+            got, length = get("R" + number), get("local0").shape[0]
+
+            def place(i):
+                return pl.multiple_of((2 * i + 1 - lax.axis_index("core")) * length, 16)
+
+            parts = [(got, functools.partial(place, i), length) for i in range(2)]
+            return swap(bundle(parts, wait(name)), "core", 1)
+        if name == "mask":
+            return row_mask(
+                request_lengths, request_slot, tokens.shape[0], choices, rank, wait(name)
+            )
+        if name == "AB":
+            every = [f"P{mask}" for mask in EARLY + LATE] + [f"R{n}" for n in range(len(ROUNDS))]
+            buffers, places = arrivals([other for other in every if other not in LAST])
+
+            def sources():
+                me = store_index()
+                return [(0, 0, me), (1, 2 * length_rows, me ^ 1)] + places(2)
+
+            shrunk, values["second factors"] = adapt_begin(
+                tokens,
+                (get("local0"), get(f"T{len(ROUNDS) - 1}"), *buffers, *wait(name)),
+                sources,
+                length_rows,
+                pair,
+                shard_width,
+                width,
+                0.6,
+            )
+            return shrunk
+        if kind == "B":
+            step = int(number)
+            start = get(f"B{step - 1}") if step else None
+            bundles = [(masks_of(part), get(part)) for part in STEPS[step]]
+            return base_product(tokens, bundles, start, wait(name))
+        raise KeyError(name)
+
+    def masks_of(part):
+        if part == "whole":
+            return [(None, 0, 0, 0)]
+        if part == "CW":
+            return [(None, 0, 0, 1)]
+        places = [PLACES[source] for source in ROWS["X" + part[1]][2]]
+        if part[0] == "C":
+            return [(x, z, y, 1) for x in range(2) for z, y in places]
+        return [(int(part[0] == "X"), z, y, 0) for z, y in places]
+
+    length_rows = base_weight.shape[0] // HALF * pair + shard_width * pair // HALF
+
+    def pair_sources(mask, n):
+        core, chip = lax.axis_index("core"), store_index() // 2
+        source = (chip ^ mask) * 2
+        return [(n, 0, source + core), (n + 1, 0, source + 1 - core)]
+
+    def round_sources(masks, n):
         core, chip = lax.axis_index("core"), store_index() // 2
         own, other = jnp.where(core == 0, *masks), jnp.where(core == 0, *masks[::-1])
         places = []
         for i in range(2):
-            places.append((first, (2 * i + core) * length, (chip ^ own) * 2 + (core ^ i)))
-            places.append((first + 1, i * length, (chip ^ other) * 2 + (core ^ 1 ^ i)))
+            places.append((n, (2 * i + core) * length_rows, (chip ^ own) * 2 + (core ^ i)))
+            places.append((n + 1, i * length_rows, (chip ^ other) * 2 + (core ^ 1 ^ i)))
         return places
 
-    def direct_sources(mask, n, handed, start):
-        core, chip = lax.axis_index("core"), store_index() // 2
-        source = (chip ^ mask) * 2
-        return [(n, 0, source + core), (handed, start, source + 1 - core)]
-
-    def begin_sources():
-        me = store_index()
-        places = [(0, 0, me), (1, 4 * length, me ^ 1)]
-        places += direct_sources(DIRECT_FIRST, 2, 4, 0)
-        places += direct_sources(DIRECT_NEAR, 3, 4, length)
-        return places + round_sources(ROUNDS[0], 5)
-
-    def end_sources():
-        return round_sources(ROUNDS[1], 0) + direct_sources(DIRECT_LAST, 2, 3, 0)
-
-    begun = adapt_begin(
-        tokens,
-        (local, swapped, got_first, got_near, handed_first, got_a, handed_a),
-        begin_sources,
-        length,
-        choices * rank,
-        shard_width,
-        width,
-        0.6,
-    )
+    def arrivals(names):
+        buffers = []
+        for name in names:
+            buffers += [get(name), get(("H" if name[0] == "P" else "F") + name[1:])]
+
+        def sources(offset=0):
+            places = []
+            for n, name in enumerate(names):
+                if name[0] == "P":
+                    places += pair_sources(int(name[1:]), offset + 2 * n)
+                else:
+                    places += round_sources(ROUNDS[int(name[1:])], offset + 2 * n)
+            return places
+
+        return buffers, sources
+
+    end_buffers, end_places = arrivals(list(LAST))
     return adapt_end(
         tokens,
-        (got_b, handed_b, got_last, handed_last),
-        end_sources,
-        length,
-        mask,
-        base,
-        begun,
+        tuple(end_buffers),
+        end_places,
+        length_rows,
+        get("mask"),
+        get(f"B{len(STEPS) - 1}"),
+        (get("AB"), values["second factors"]),
         shard_width,
         0.4,
     )

time: 111 us -> 84.6 us (0.76)
  the two profiles are of different devices: /device:TPU:9 before, /device:TPU:0 now
where the time goes in v8:
time: 84.6 us; the launch traced here: 84.4 us
  waiting for transfers between devices  36.3 us (43%)
  starting transfers between devices  30.1 us (36%)
  Pallas kernels  17.1 us (20%)
    ppermute x23, waiting for transfers between devices, swap(): return lax.ppermute(block, axis, [(i, i ^ bit) for i in range(size)])  29.6 us
    ppermute x23, starting transfers between devices, swap(): return lax.ppermute(block, axis, [(i, i ^ bit) for i in range(size)])  24.3 us
    pallas_call x2, Pallas kernels, make_messages(): pl.pallas_call(kernel, out_shape=[pltpu.VMEM((n * length, HALF), jnp.bflo...  6.93 us
    ppermute x4, waiting for transfers between devices, send_pairs(): lax.ppermute(payload, AXES[1:], [(i, target(i)) for i in range(size)])  6.63 us
    ppermute x4, starting transfers between devices, send_pairs(): lax.ppermute(payload, AXES[1:], [(i, target(i)) for i in range(size)])  5.75 us
    pallas_call x4, Pallas kernels, base_product(): pl.pallas_call(kernel, out_shape=pltpu.VMEM((rows, width), jnp.float32),...  4.99 us
    pallas_call x1, Pallas kernels, adapt_end(): pl.pallas_call(kernel, out_shape=jax.ShapeDtypeStruct((rows, width), jnp....  1.93 us
  transfers between devices with their start and end apart: 27, of which 9 were waited for; matrix products, arithmetic and copies ran while one was open for 0% of the time, Pallas kernels for 15%

profile of v8, /device:TPU:0, one launch (start us, length us, event | category | flops | bytes accessed | tf_op | source)
XLA Modules:
  0.0 84.4 jit_solution(17584303172743311580)
XLA Ops:
  0.0 0.7 copy-done.1
  0.7 2.7 %make_messages.2 = (bf16[544,256]{1,0:T(8,128)(2,1)S(1)}, bf16[512,512]{1,0:T(8,128)(2,1)S(1)}, bf16[256,512]{1,0:T(8,128)(2,1)S(1)}) custom-call(s32[2,16]{1,0:T(2,128)S(1)} %bitcast.7, bf16[128,64,512]{2,1,0:T(8,128)(2,1)} %bitcast.9, bf16[2048,128]{1,0:T(8,128)(2,1)} %bitcast.11, bf16[512,512]{1,0:T(8,128)(2,1)} %refs_3_.3), custom_call_target="tpu_custom_call" | custom-call | bytes 557056 | tf_op jit(solution)/shard_map/make_messages/pallas_call | solution.py:130
  3.3 3.1 %collective-permute-start.1 = (bf16[256,512]{1,0:T(8,128)(2,1)S(1)}, bf16[256,512]{1,0:T(8,128)(2,1)S(1)}, u32[]{:S(2)}, u32[]{:S(2)}) collective-permute-start(bf16[256,512]{1,0:T(8,128)(2,1)S(1)} %get-tuple-element.18.refs_4_), channel_id=1, source_target_pairs={{0,4},{4,0},{8,12},{12,8},{1,5},{5,1},{9,13},{13,9},{2,6},{6,2},{1... | collective-permute-start | bytes 786440 | tf_op jit(solution)/shard_map/ppermute | solution.py:377
  6.4 1.5 %collective-permute-start.2 = (bf16[256,512]{1,0:T(8,128)(2,1)S(1)}, bf16[256,512]{1,0:T(8,128)(2,1)S(1)}, u32[]{:S(2)}, u32[]{:S(2)}) collective-permute-start(bf16[256,512]{1,0:T(8,128)(2,1)S(1)} %get-tuple-element.18.refs_4_), channel_id=1, source_target_pairs={{0,2},{2,0},{1,3},{3,1},{4,6},{6,4},{5,7},{7,5},{8,10},{10,8},{9,1... | collective-permute-start | bytes 786440 | tf_op jit(solution)/shard_map/ppermute | solution.py:377
  8.0 2.6 %collective-permute-start.6 = (bf16[256,512]{1,0:T(8,128)(2,1)S(1)}, bf16[256,512]{1,0:T(8,128)(2,1)S(1)}, u32[]{:S(2)}, u32[]{:S(2)}) collective-permute-start(bf16[256,512]{1,0:T(8,128)(2,1)S(1)} %get-tuple-element.18.refs_4_), channel_id=1, source_target_pairs={{0,8},{4,12},{8,0},{12,4},{1,9},{5,13},{9,1},{13,5},{2,10},{6,14},... | collective-permute-start | bytes 786440 | tf_op jit(solution)/shard_map/ppermute | solution.py:377
  10.5 0.3 collective-permute-start.7
  10.8 6.2 %collective-permute-done.1.refs_0_ = bf16[256,512]{1,0:T(8,128)(2,1)S(1)} collective-permute-done((bf16[256,512]{1,0:T(8,128)(2,1)S(1)}, bf16[256,512]{1,0:T(8,128)(2,1)S(1)}, u32[]{:S(2)}, u32[]{:S(2)}) %collective-permute-start.1) | collective-permute-done | bytes 262176 | tf_op jit(solution)/shard_map/ppermute | solution.py:377
  17.0 2.7 %collective-permute-start.8 = (bf16[256,512]{1,0:T(8,128)(2,1)S(1)}, bf16[256,512]{1,0:T(8,128)(2,1)S(1)}, u32[]{:S(2)}, u32[]{:S(2)}) collective-permute-start(bf16[256,512]{1,0:T(8,128)(2,1)S(1)} %collective-permute-done.1.refs_0_), channel_id=1, source_target_pairs={{0,2},{2,0},{1,3},{3,1},{4,6},{6,4},{5,7},{7,5},{8,10},{10,8},{9,1... | collective-permute-start | bytes 786440 | tf_op jit(solution)/shard_map/ppermute | solution.py:377
  19.7 0.0 collective-permute-start
  19.7 0.0 collective-permute-done.2.refs_1_.refs_2_
  19.7 0.0 slice-start.1
  19.8 1.6 %collective-permute-start.3 = (bf16[512,512]{1,0:T(8,128)(2,1)S(1)}, bf16[512,512]{1,0:T(8,128)(2,1)S(1)}, u32[]{:S(2)}, u32[]{:S(2)}) collective-permute-start(bf16[512,512]{1,0:T(8,128)(2,1)S(1)} %bundle.16.refs_2_.refs_0_), channel_id=1, source_target_pairs={{0,16},{16,0},{1,17},{17,1},{2,18},{18,2},{3,19},{19,3},{4,20},{20... | collective-permute-start | bytes 1572872 | tf_op jit(solution)/shard_map/ppermute | solution.py:377
  21.3 4.3 %make_messages.3 = (bf16[544,256]{1,0:T(8,128)(2,1)S(1)}, bf16[544,256]{1,0:T(8,128)(2,1)S(1)}, bf16[544,256]{1,0:T(8,128)(2,1)S(1)}, bf16[544,256]{1,0:T(8,128)...) custom-call(s32[2,16]{1,0:T(2,128)S(1)} %bitcast.8, ...), custom_call_target="tpu_custom_call" | custom-call | bytes 15597568 | tf_op jit(solution)/shard_map/make_messages/pallas_call | solution.py:130
  25.6 4.1 %collective-permute-done.6.refs_3_.refs_0_ = bf16[256,512]{1,0:T(8,128)(2,1)S(1)} collective-permute-done((bf16[256,512]{1,0:T(8,128)(2,1)S(1)}, bf16[256,512]{1,0:T(8,128)(2,1)S(1)}, u32[]{:S(2)}, u32[]{:S(2)}) %collective-permute-start.6) | collective-permute-done | bytes 262176 | tf_op jit(solution)/shard_map/ppermute | solution.py:377
  29.7 0.0 collective-permute-start.4
  29.7 4.2 %collective-permute-done.7.refs_1_.refs_0_.refs_2_ = bf16[544,256]{1,0:T(8,128)(2,1)S(1)} collective-permute-done((bf16[544,256]{1,0:T(8,128)(2,1)S(1)}, bf16[544,256]{1,0:T(8,128)(2,1)S(1)}, u32[]{:S(2)}, u32[]{:S(2)}) %collective-permute-start.7) | collective-permute-done | bytes 278560 | tf_op jit(solution)/shard_map/ppermute | solution.py:382
  33.9 0.0 collective-permute-done.8.refs_2_.refs_3_.refs_1_
  33.9 0.0 collective-permute-start.9
  33.9 0.0 copy-start
  34.0 0.0 copy-start.2
  34.0 1.6 %collective-permute-start.5 = (bf16[1088,256]{1,0:T(8,128)(2,1)S(1)}, bf16[1088,256]{1,0:T(8,128)(2,1)S(1)}, u32[]{:S(2)}, u32[]{:S(2)}) collective-permute-start(bf16[1088,256]{1,0:T(8,128)(2,1)S(1)} %bundle.17), channel_id=1, source_target_pairs={{0,2},{1,9},{2,0},{3,11},{4,6},{5,13},{6,4},{7,15},{8,10},{9,1},{1... | collective-permute-start | bytes 1671176 | tf_op jit(solution)/shard_map/ppermute | solution.py:382
  35.6 0.0 collective-permute-start.11
  35.6 1.2 %base_product.4.refs_1_.refs_0_.refs_3_ = f32[512,512]{1,0:T(8,128)S(1)} custom-call(bf16[512,8192]{1,0:T(8,128)(2,1)S(1)} %bitcast.6, bf16[512,512]{1,0:T(8,128)(2,1)S(1)} %get-tuple-element.17.refs_0_, bf16[512,512]{1,0:T(8,128)(2,1)S(1)} %collective-permute-done.refs_1_, bf16[512,512]{1,0:T(8,128)(2,1)S(1)} %bundle.16.refs_2_.refs_0_, ...), custom_call_target="tpu_custom_call" | custom-call | flops 1073741824 | bytes 5242880 | tf_op jit(solution)/shard_map/base_product/pallas_call | solution.py:193
  36.8 0.0 collective-permute-done.9.refs_2_.refs_1_
  36.9 0.6 collective-permute-start.10
  37.5 1.6 %collective-permute-start.20 = (bf16[512,512]{1,0:T(8,128)(2,1)S(1)}, bf16[512,512]{1,0:T(8,128)(2,1)S(1)}, u32[]{:S(2)}, u32[]{:S(2)}) collective-permute-start(bf16[512,512]{1,0:T(8,128)(2,1)S(1)} %bundle.25.refs_1_.refs_0_), channel_id=1, source_target_pairs={{0,16},{16,0},{1,17},{17,1},{2,18},{18,2},{3,19},{19,3},{4,20},{20... | collective-permute-start | bytes 1572872 | tf_op jit(solution)/shard_map/ppermute | solution.py:377
  39.1 2.1 %collective-permute-start.16 = (bf16[1088,256]{1,0:T(8,128)(2,1)S(1)}, bf16[1088,256]{1,0:T(8,128)(2,1)S(1)}, u32[]{:S(2)}, u32[]{:S(2)}) collective-permute-start(bf16[1088,256]{1,0:T(8,128)(2,1)S(1)} %bundle.21), channel_id=1, source_target_pairs={{0,4},{1,13},{2,6},{3,15},{4,0},{5,9},{6,2},{7,11},{8,12},{9,5},{1... | collective-permute-start | bytes 1671176 | tf_op jit(solution)/shard_map/ppermute | solution.py:382
  41.2 6.7 %collective-permute-done.11.refs_3_.refs_0_ = bf16[256,512]{1,0:T(8,128)(2,1)S(1)} collective-permute-done((bf16[256,512]{1,0:T(8,128)(2,1)S(1)}, bf16[256,512]{1,0:T(8,128)(2,1)S(1)}, u32[]{:S(2)}, u32[]{:S(2)}) %collective-permute-start.11) | collective-permute-done | bytes 262176 | tf_op jit(solution)/shard_map/ppermute | solution.py:377
  47.9 0.0 collective-permute-done.5.refs_1_.refs_0_.refs_2_.refs_4_
  47.9 1.3 %collective-permute-done.10.refs_2_.refs_1_.refs_6_ = bf16[256,512]{1,0:T(8,128)(2,1)S(1)} collective-permute-done((bf16[256,512]{1,0:T(8,128)(2,1)S(1)}, bf16[256,512]{1,0:T(8,128)(2,1)S(1)}, u32[]{:S(2)}, u32[]{:S(2)}) %collective-permute-start.10) | collective-permute-done | bytes 262176 | tf_op jit(solution)/shard_map/ppermute | solution.py:377
  49.2 1.7 %collective-permute-start.12 = (bf16[544,256]{1,0:T(8,128)(2,1)S(1)}, bf16[544,256]{1,0:T(8,128)(2,1)S(1)}, u32[]{:S(2)}, u32[]{:S(2)}) collective-permute-start(bf16[544,256]{1,0:T(8,128)(2,1)S(1)} %after.5), channel_id=1, source_target_pairs={{0,1},{1,0},{2,3},{3,2},{4,5},{5,4},{6,7},{7,6},{8,9},{9,8},{10,11... | collective-permute-start | bytes 835592 | tf_op jit(solution)/shard_map/ppermute | solution.py:377
  50.8 1.6 %collective-permute-start.14 = (bf16[256,512]{1,0:T(8,128)(2,1)S(1)}, bf16[256,512]{1,0:T(8,128)(2,1)S(1)}, u32[]{:S(2)}, u32[]{:S(2)}) collective-permute-start(bf16[256,512]{1,0:T(8,128)(2,1)S(1)} %collective-permute-done.11.refs_3_.refs_0_), channel_id=1, source_target_pairs={{0,2},{2,0},{1,3},{3,1},{4,6},{6,4},{5,7},{7,5},{8,10},{10,8},{9,1... | collective-permute-start | bytes 786440 | tf_op jit(solution)/shard_map/ppermute | solution.py:377
  52.5 2.4 %collective-permute-start.13 = (bf16[512,512]{1,0:T(8,128)(2,1)S(1)}, bf16[512,512]{1,0:T(8,128)(2,1)S(1)}, u32[]{:S(2)}, u32[]{:S(2)}) collective-permute-start(bf16[512,512]{1,0:T(8,128)(2,1)S(1)} %bundle.19.refs_0_.refs_1_), channel_id=1, source_target_pairs={{0,16},{16,0},{1,17},{17,1},{2,18},{18,2},{3,19},{19,3},{4,20},{20... | collective-permute-start | bytes 1572872 | tf_op jit(solution)/shard_map/ppermute | solution.py:377
  54.9 0.0 collective-permute-done.12.refs_1_
  54.9 1.1 %row_mask.1.refs_3_.mask_ref = f32[512,128]{1,0:T(8,128)S(1)} custom-call(s32[1,16]{1,0:T(1,128)S(1)} %copy-done.2, s32[16,16]{1,0:T(8,128)S(1)} %copy-done, f32[512,512]{1,0:T(8,128)S(1)} %base_product.4.refs_1_.refs_0_.refs_3_, bf16[544,256]{1,0:T(8,128)(2,1)S(1)} %collective-permute-done.12.refs_1_, ...), custom_call_target="tpu_custom_call" | custom-call | tf_op jit(solution)/shard_map/row_mask/pallas_call | solution.py:356
  56.1 0.1 bundle.26
  56.1 0.1 collective-permute-start.21
  56.2 2.9 %collective-permute-done.14.refs_2_.refs_0_ = bf16[256,512]{1,0:T(8,128)(2,1)S(1)} collective-permute-done((bf16[256,512]{1,0:T(8,128)(2,1)S(1)}, bf16[256,512]{1,0:T(8,128)(2,1)S(1)}, u32[]{:S(2)}, u32[]{:S(2)}) %collective-permute-start.14) | collective-permute-done | bytes 262176 | tf_op jit(solution)/shard_map/ppermute | solution.py:377
  59.1 0.1 collective-permute-start.15
  59.2 2.4 %collective-permute-done.16.refs_0_.refs_1_.refs_4_ = bf16[1088,256]{1,0:T(8,128)(2,1)S(1)} collective-permute-done((bf16[1088,256]{1,0:T(8,128)(2,1)S(1)}, bf16[1088,256]{1,0:T(8,128)(2,1)S(1)}, u32[]{:S(2)}, u32[]{:S(2)}) %collective-permute-start.16) | collective-permute-done | bytes 557088 | tf_op jit(solution)/shard_map/ppermute | solution.py:382
  61.7 0.1 collective-permute-start.17
  61.8 1.8 %collective-permute-start.22 = (bf16[1088,256]{1,0:T(8,128)(2,1)S(1)}, bf16[1088,256]{1,0:T(8,128)(2,1)S(1)}, u32[]{:S(2)}, u32[]{:S(2)}) collective-permute-start(bf16[1088,256]{1,0:T(8,128)(2,1)S(1)} %bundle.27), channel_id=1, source_target_pairs={{0,6},{1,15},{2,4},{3,13},{4,2},{5,11},{6,0},{7,9},{8,14},{9,7},{1... | collective-permute-start | bytes 1671176 | tf_op jit(solution)/shard_map/ppermute | solution.py:382
  63.6 3.2 %collective-permute-done.13.refs_1_.refs_2_ = bf16[512,512]{1,0:T(8,128)(2,1)S(1)} collective-permute-done((bf16[512,512]{1,0:T(8,128)(2,1)S(1)}, bf16[512,512]{1,0:T(8,128)(2,1)S(1)}, u32[]{:S(2)}, u32[]{:S(2)}) %collective-permute-start.13) | collective-permute-done | bytes 524320 | tf_op jit(solution)/shard_map/ppermute | solution.py:377
  66.8 0.1 bundle.29
  66.9 0.1 collective-permute-start.24
  67.0 0.0 collective-permute-done.17.refs_5_
  67.0 1.5 %adapt_begin.1 = (f32[512,128]{1,0:T(8,128)S(1)}, bf16[512,128]{1,0:T(8,128)(2,1)S(1)}) custom-call(bf16[512,8192]{1,0:T(8,128)(2,1)S(1)} %bitcast.6, bf16[272,256]{1,0:T(8,128)(2,1)S(1)} %get-tuple-element.24.refs_0_, bf16[816,256]{1,0:T(8,128)(2,1)S(1)} %collective-permute-done.9.refs_2_.refs_1_, ...), custom_call_target="tpu_custom_call" | custom-call | flops 1288490240 | bytes 5033164 | tf_op jit(solution)/shard_map/adapt_begin/pallas_call | solution.py:255
  68.5 0.1 bundle.23
  68.6 0.5 collective-permute-start.18
  69.2 1.8 %collective-permute-start.19 = (bf16[256,512]{1,0:T(8,128)(2,1)S(1)}, bf16[256,512]{1,0:T(8,128)(2,1)S(1)}, u32[]{:S(2)}, u32[]{:S(2)}) collective-permute-start(bf16[256,512]{1,0:T(8,128)(2,1)S(1)} %bundle.24.refs_0_.refs_1_), channel_id=1, source_target_pairs={{0,16},{16,0},{1,17},{17,1},{2,18},{18,2},{3,19},{19,3},{4,20},{20... | collective-permute-start | bytes 786440 | tf_op jit(solution)/shard_map/ppermute | solution.py:377
  71.0 0.0 collective-permute-done.21.refs_0_
  71.0 1.2 %base_product.5.refs_3_ = f32[512,512]{1,0:T(8,128)S(1)} custom-call(bf16[512,8192]{1,0:T(8,128)(2,1)S(1)} %bitcast.6, bf16[1024,512]{1,0:T(8,128)(2,1)S(1)} %collective-permute-done.21.refs_0_, bf16[512,512]{1,0:T(8,128)(2,1)S(1)} %bundle.25.refs_1_.refs_0_, bf16[512,512]{1,0:T(8,128)(2,1)S(1)} %collective-permute-done.20.refs_2_.refs_1_, ...), custom_call_target="tpu_custom_call" | custom-call | flops 1073741824 | bytes 5242880 | tf_op jit(solution)/shard_map/base_product/pallas_call | solution.py:193
  72.2 5.2 %collective-permute-done.19.refs_1_.refs_2_ = bf16[256,512]{1,0:T(8,128)(2,1)S(1)} collective-permute-done((bf16[256,512]{1,0:T(8,128)(2,1)S(1)}, bf16[256,512]{1,0:T(8,128)(2,1)S(1)}, u32[]{:S(2)}, u32[]{:S(2)}) %collective-permute-start.19) | collective-permute-done | bytes 262176 | tf_op jit(solution)/shard_map/ppermute | solution.py:377
  77.5 0.0 collective-permute-done.22.refs_5_.refs_0_.refs_1_
  77.5 1.8 %collective-permute-start.23 = (bf16[512,512]{1,0:T(8,128)(2,1)S(1)}, bf16[512,512]{1,0:T(8,128)(2,1)S(1)}, u32[]{:S(2)}, u32[]{:S(2)}) collective-permute-start(bf16[512,512]{1,0:T(8,128)(2,1)S(1)} %bundle.28), channel_id=1, source_target_pairs={{0,1},{1,0},{2,3},{3,2},{4,5},{5,4},{6,7},{7,6},{8,9},{9,8},{10,11... | collective-permute-start | bytes 1572872 | tf_op jit(solution)/shard_map/ppermute | solution.py:377
  79.3 0.1 collective-permute-start.25
  79.4 0.5 collective-permute-start.26
  79.9 0.0 collective-permute-done.24.refs_0_
  79.9 1.2 %base_product.6.refs_4_ = f32[512,512]{1,0:T(8,128)S(1)} custom-call(bf16[512,8192]{1,0:T(8,128)(2,1)S(1)} %bitcast.6, bf16[1024,512]{1,0:T(8,128)(2,1)S(1)} %collective-permute-done.24.refs_0_, bf16[512,512]{1,0:T(8,128)(2,1)S(1)} %bundle.19.refs_0_.refs_1_, bf16[512,512]{1,0:T(8,128)(2,1)S(1)} %collective-permute-done.13.refs_1_.refs_2_, ...), custom_call_target="tpu_custom_call" | custom-call | flops 1073741824 | bytes 5242880 | tf_op jit(solution)/shard_map/base_product/pallas_call | solution.py:193
  81.2 0.0 collective-permute-done.18.refs_0_
  81.2 1.3 %base_product.7.base_ref = f32[512,512]{1,0:T(8,128)S(1)} custom-call(bf16[512,8192]{1,0:T(8,128)(2,1)S(1)} %bitcast.6, bf16[1024,512]{1,0:T(8,128)(2,1)S(1)} %collective-permute-done.18.refs_0_, bf16[256,512]{1,0:T(8,128)(2,1)S(1)} %bundle.24.refs_0_.refs_1_, bf16[256,512]{1,0:T(8,128)(2,1)S(1)} %collective-permute-done.19.refs_1_.refs_2_, ...), custom_call_target="tpu_custom_call" | custom-call | flops 1073741824 | bytes 5242880 | tf_op jit(solution)/shard_map/base_product/pallas_call | solution.py:193
  82.5 0.0 collective-permute-done.26.refs_3_
  82.5 0.0 collective-permute-done.25.refs_1_
  82.5 1.9 %adapt_end.1 = bf16[512,512]{1,0:T(8,128)(2,1)} custom-call(bf16[512,8192]{1,0:T(8,128)(2,1)S(1)} %bitcast.6, f32[512,128]{1,0:T(8,128)S(1)} %row_mask.1.refs_3_.mask_ref, f32[512,512]{1,0:T(8,128)S(1)} %base_product.7.base_ref, f32[512,128]{1,0:T(8,128)S(1)} %get-tuple-element.26.refs_2_.shrunk, bf16[512,128]{1,0:T(8,128)(2,1)S(1)} %get-tuple-element.28.widened, ...), custom_call_target="tpu_custom_call" | custom-call | flops 858993472 | bytes 3355443 | tf_op jit(solution)/shard_map/adapt_end/pallas_call | solution.py:287
  (29 shorter events, 0.4 us)
Async XLA Ops:
  0.0 0.7 copy-start.1
  0.7 34.9 %slice-start = ((s8[8388608]{0:T(1024)(128)(4,1)}), s8[4194304]{0:T(1024)(128)(4,1)S(1)}, s32[]{:S(2)}) async-start(s8[8388608]{0:T(1024)(128)(4,1)} %bitcast.5), calls=%async_computation | async-start | bytes 8388608
  3.3 13.7 %collective-permute-start.1 = (bf16[256,512]{1,0:T(8,128)(2,1)S(1)}, bf16[256,512]{1,0:T(8,128)(2,1)S(1)}, u32[]{:S(2)}, u32[]{:S(2)}) collective-permute-start(bf16[256,512]{1,0:T(8,128)(2,1)S(1)} %get-tuple-element.18.refs_4_), channel_id=1, source_target_pairs={{0,4},{4,0},{8,12},{12,8},{1,5},{5,1},{9,13},{13,9},{2,6},{6,2},{1... | collective-permute-start | bytes 786440 | tf_op jit(solution)/shard_map/ppermute | solution.py:377
  6.4 13.3 %collective-permute-start.2 = (bf16[256,512]{1,0:T(8,128)(2,1)S(1)}, bf16[256,512]{1,0:T(8,128)(2,1)S(1)}, u32[]{:S(2)}, u32[]{:S(2)}) collective-permute-start(bf16[256,512]{1,0:T(8,128)(2,1)S(1)} %get-tuple-element.18.refs_4_), channel_id=1, source_target_pairs={{0,2},{2,0},{1,3},{3,1},{4,6},{6,4},{5,7},{7,5},{8,10},{10,8},{9,1... | collective-permute-start | bytes 786440 | tf_op jit(solution)/shard_map/ppermute | solution.py:377
  8.0 21.7 %collective-permute-start.6 = (bf16[256,512]{1,0:T(8,128)(2,1)S(1)}, bf16[256,512]{1,0:T(8,128)(2,1)S(1)}, u32[]{:S(2)}, u32[]{:S(2)}) collective-permute-start(bf16[256,512]{1,0:T(8,128)(2,1)S(1)} %get-tuple-element.18.refs_4_), channel_id=1, source_target_pairs={{0,8},{4,12},{8,0},{12,4},{1,9},{5,13},{9,1},{13,5},{2,10},{6,14},... | collective-permute-start | bytes 786440 | tf_op jit(solution)/shard_map/ppermute | solution.py:377
  10.5 23.3 %collective-permute-start.7 = (bf16[544,256]{1,0:T(8,128)(2,1)S(1)}, bf16[544,256]{1,0:T(8,128)(2,1)S(1)}, u32[]{:S(2)}, u32[]{:S(2)}) collective-permute-start(bf16[544,256]{1,0:T(8,128)(2,1)S(1)} %get-tuple-element.23), channel_id=1, source_target_pairs={{0,10},{1,11},{2,8},{3,9},{4,14},{5,15},{6,12},{7,13},{8,2},{9,3},... | collective-permute-start | bytes 835592 | tf_op jit(solution)/shard_map/ppermute | solution.py:382
  17.0 16.9 %collective-permute-start.8 = (bf16[256,512]{1,0:T(8,128)(2,1)S(1)}, bf16[256,512]{1,0:T(8,128)(2,1)S(1)}, u32[]{:S(2)}, u32[]{:S(2)}) collective-permute-start(bf16[256,512]{1,0:T(8,128)(2,1)S(1)} %collective-permute-done.1.refs_0_), channel_id=1, source_target_pairs={{0,2},{2,0},{1,3},{3,1},{4,6},{6,4},{5,7},{7,5},{8,10},{10,8},{9,1... | collective-permute-start | bytes 786440 | tf_op jit(solution)/shard_map/ppermute | solution.py:377
  19.7 15.9 %collective-permute-start = (bf16[512,512]{1,0:T(8,128)(2,1)S(1)}, bf16[512,512]{1,0:T(8,128)(2,1)S(1)}, u32[]{:S(2)}, u32[]{:S(2)}) collective-permute-start(bf16[512,512]{1,0:T(8,128)(2,1)S(1)} %get-tuple-element.17.refs_0_), channel_id=1, source_target_pairs={{0,1},{1,0},{2,3},{3,2},{4,5},{5,4},{6,7},{7,6},{8,9},{9,8},{10,11... | collective-permute-start | bytes 1572872 | tf_op jit(solution)/shard_map/ppermute | solution.py:377
  19.7 15.8 %slice-start.1 = ((s8[8388608]{0:T(1024)(128)(4,1)}), s8[4194304]{0:T(1024)(128)(4,1)S(1)}, s32[]{:S(2)}) async-start(s8[8388608]{0:T(1024)(128)(4,1)} %bitcast.5), calls=%async_computation.1 | async-start | bytes 8388608
  19.8 15.8 %collective-permute-start.3 = (bf16[512,512]{1,0:T(8,128)(2,1)S(1)}, bf16[512,512]{1,0:T(8,128)(2,1)S(1)}, u32[]{:S(2)}, u32[]{:S(2)}) collective-permute-start(bf16[512,512]{1,0:T(8,128)(2,1)S(1)} %bundle.16.refs_2_.refs_0_), channel_id=1, source_target_pairs={{0,16},{16,0},{1,17},{17,1},{2,18},{18,2},{3,19},{19,3},{4,20},{20... | collective-permute-start | bytes 1572872 | tf_op jit(solution)/shard_map/ppermute | solution.py:377
  29.7 4.2 %collective-permute-start.4 = (bf16[544,256]{1,0:T(8,128)(2,1)S(1)}, bf16[544,256]{1,0:T(8,128)(2,1)S(1)}, u32[]{:S(2)}, u32[]{:S(2)}) collective-permute-start(bf16[544,256]{1,0:T(8,128)(2,1)S(1)} %after.3), channel_id=1, source_target_pairs={{0,1},{1,0},{2,3},{3,2},{4,5},{5,4},{6,7},{7,6},{8,9},{9,8},{10,11... | collective-permute-start | bytes 835592 | tf_op jit(solution)/shard_map/ppermute | solution.py:377
  33.9 3.0 %collective-permute-start.9 = (bf16[816,256]{1,0:T(8,128)(2,1)S(1)}, bf16[816,256]{1,0:T(8,128)(2,1)S(1)}, u32[]{:S(2)}, u32[]{:S(2)}) collective-permute-start(bf16[816,256]{1,0:T(8,128)(2,1)S(1)} %after.4), channel_id=1, source_target_pairs={{0,1},{1,0},{2,3},{3,2},{4,5},{5,4},{6,7},{7,6},{8,9},{9,8},{10,11... | collective-permute-start | bytes 1253384 | tf_op jit(solution)/shard_map/ppermute | solution.py:377
  33.9 21.0 %copy-start = (s32[16,16]{1,0:T(8,128)S(1)}, s32[16,16]{1,0:T(8,128)}, u32[]{:S(2)}) copy-start(s32[16,16]{1,0:T(8,128)} %slots_ref.1) | copy-start | bytes 3076
  34.0 21.0 %copy-start.2 = (s32[1,16]{1,0:T(1,128)S(1)}, s32[1,16]{1,0:T(1,128)}, u32[]{:S(2)}) copy-start(s32[1,16]{1,0:T(1,128)} %lengths_ref.1) | copy-start | bytes 196
  34.0 13.9 %collective-permute-start.5 = (bf16[1088,256]{1,0:T(8,128)(2,1)S(1)}, bf16[1088,256]{1,0:T(8,128)(2,1)S(1)}, u32[]{:S(2)}, u32[]{:S(2)}) collective-permute-start(bf16[1088,256]{1,0:T(8,128)(2,1)S(1)} %bundle.17), channel_id=1, source_target_pairs={{0,2},{1,9},{2,0},{3,11},{4,6},{5,13},{6,4},{7,15},{8,10},{9,1},{1... | collective-permute-start | bytes 1671176 | tf_op jit(solution)/shard_map/ppermute | solution.py:382
  35.6 12.3 %collective-permute-start.11 = (bf16[256,512]{1,0:T(8,128)(2,1)S(1)}, bf16[256,512]{1,0:T(8,128)(2,1)S(1)}, u32[]{:S(2)}, u32[]{:S(2)}) collective-permute-start(bf16[256,512]{1,0:T(8,128)(2,1)S(1)} %collective-permute-done.6.refs_3_.refs_0_), channel_id=1, source_target_pairs={{0,4},{4,0},{8,12},{12,8},{1,5},{5,1},{9,13},{13,9},{2,6},{6,2},{1... | collective-permute-start | bytes 786440 | tf_op jit(solution)/shard_map/ppermute | solution.py:377
  36.9 12.3 %collective-permute-start.10 = (bf16[256,512]{1,0:T(8,128)(2,1)S(1)}, bf16[256,512]{1,0:T(8,128)(2,1)S(1)}, u32[]{:S(2)}, u32[]{:S(2)}) collective-permute-start(bf16[256,512]{1,0:T(8,128)(2,1)S(1)} %bundle.18), channel_id=1, source_target_pairs={{0,2},{2,0},{1,3},{3,1},{4,6},{6,4},{5,7},{7,5},{8,10},{10,8},{9,1... | collective-permute-start | bytes 786440 | tf_op jit(solution)/shard_map/ppermute | solution.py:377
  37.5 18.6 %collective-permute-start.20 = (bf16[512,512]{1,0:T(8,128)(2,1)S(1)}, bf16[512,512]{1,0:T(8,128)(2,1)S(1)}, u32[]{:S(2)}, u32[]{:S(2)}) collective-permute-start(bf16[512,512]{1,0:T(8,128)(2,1)S(1)} %bundle.25.refs_1_.refs_0_), channel_id=1, source_target_pairs={{0,16},{16,0},{1,17},{17,1},{2,18},{18,2},{3,19},{19,3},{4,20},{20... | collective-permute-start | bytes 1572872 | tf_op jit(solution)/shard_map/ppermute | solution.py:377
  39.1 22.6 %collective-permute-start.16 = (bf16[1088,256]{1,0:T(8,128)(2,1)S(1)}, bf16[1088,256]{1,0:T(8,128)(2,1)S(1)}, u32[]{:S(2)}, u32[]{:S(2)}) collective-permute-start(bf16[1088,256]{1,0:T(8,128)(2,1)S(1)} %bundle.21), channel_id=1, source_target_pairs={{0,4},{1,13},{2,6},{3,15},{4,0},{5,9},{6,2},{7,11},{8,12},{9,5},{1... | collective-permute-start | bytes 1671176 | tf_op jit(solution)/shard_map/ppermute | solution.py:382
  49.2 5.7 %collective-permute-start.12 = (bf16[544,256]{1,0:T(8,128)(2,1)S(1)}, bf16[544,256]{1,0:T(8,128)(2,1)S(1)}, u32[]{:S(2)}, u32[]{:S(2)}) collective-permute-start(bf16[544,256]{1,0:T(8,128)(2,1)S(1)} %after.5), channel_id=1, source_target_pairs={{0,1},{1,0},{2,3},{3,2},{4,5},{5,4},{6,7},{7,6},{8,9},{9,8},{10,11... | collective-permute-start | bytes 835592 | tf_op jit(solution)/shard_map/ppermute | solution.py:377
  50.8 8.3 %collective-permute-start.14 = (bf16[256,512]{1,0:T(8,128)(2,1)S(1)}, bf16[256,512]{1,0:T(8,128)(2,1)S(1)}, u32[]{:S(2)}, u32[]{:S(2)}) collective-permute-start(bf16[256,512]{1,0:T(8,128)(2,1)S(1)} %collective-permute-done.11.refs_3_.refs_0_), channel_id=1, source_target_pairs={{0,2},{2,0},{1,3},{3,1},{4,6},{6,4},{5,7},{7,5},{8,10},{10,8},{9,1... | collective-permute-start | bytes 786440 | tf_op jit(solution)/shard_map/ppermute | solution.py:377
  52.5 14.3 %collective-permute-start.13 = (bf16[512,512]{1,0:T(8,128)(2,1)S(1)}, bf16[512,512]{1,0:T(8,128)(2,1)S(1)}, u32[]{:S(2)}, u32[]{:S(2)}) collective-permute-start(bf16[512,512]{1,0:T(8,128)(2,1)S(1)} %bundle.19.refs_0_.refs_1_), channel_id=1, source_target_pairs={{0,16},{16,0},{1,17},{17,1},{2,18},{18,2},{3,19},{19,3},{4,20},{20... | collective-permute-start | bytes 1572872 | tf_op jit(solution)/shard_map/ppermute | solution.py:377
  56.1 14.8 %collective-permute-start.21 = (bf16[1024,512]{1,0:T(8,128)(2,1)S(1)}, bf16[1024,512]{1,0:T(8,128)(2,1)S(1)}, u32[]{:S(2)}, u32[]{:S(2)}) collective-permute-start(bf16[1024,512]{1,0:T(8,128)(2,1)S(1)} %bundle.26), channel_id=1, source_target_pairs={{0,1},{1,0},{2,3},{3,2},{4,5},{5,4},{6,7},{7,6},{8,9},{9,8},{10,11... | collective-permute-start | bytes 3145736 | tf_op jit(solution)/shard_map/ppermute | solution.py:377
  59.1 7.8 %collective-permute-start.15 = (bf16[544,256]{1,0:T(8,128)(2,1)S(1)}, bf16[544,256]{1,0:T(8,128)(2,1)S(1)}, u32[]{:S(2)}, u32[]{:S(2)}) collective-permute-start(bf16[544,256]{1,0:T(8,128)(2,1)S(1)} %bundle.20), channel_id=1, source_target_pairs={{0,1},{1,0},{2,3},{3,2},{4,5},{5,4},{6,7},{7,6},{8,9},{9,8},{10,11... | collective-permute-start | bytes 835592 | tf_op jit(solution)/shard_map/ppermute | solution.py:377
  61.7 5.3 %collective-permute-start.17 = (bf16[544,256]{1,0:T(8,128)(2,1)S(1)}, bf16[544,256]{1,0:T(8,128)(2,1)S(1)}, u32[]{:S(2)}, u32[]{:S(2)}) collective-permute-start(bf16[544,256]{1,0:T(8,128)(2,1)S(1)} %bundle.22), channel_id=1, source_target_pairs={{0,1},{1,0},{2,3},{3,2},{4,5},{5,4},{6,7},{7,6},{8,9},{9,8},{10,11... | collective-permute-start | bytes 835592 | tf_op jit(solution)/shard_map/ppermute | solution.py:377
  61.8 15.7 %collective-permute-start.22 = (bf16[1088,256]{1,0:T(8,128)(2,1)S(1)}, bf16[1088,256]{1,0:T(8,128)(2,1)S(1)}, u32[]{:S(2)}, u32[]{:S(2)}) collective-permute-start(bf16[1088,256]{1,0:T(8,128)(2,1)S(1)} %bundle.27), channel_id=1, source_target_pairs={{0,6},{1,15},{2,4},{3,13},{4,2},{5,11},{6,0},{7,9},{8,14},{9,7},{1... | collective-permute-start | bytes 1671176 | tf_op jit(solution)/shard_map/ppermute | solution.py:382
  66.9 13.1 %collective-permute-start.24 = (bf16[1024,512]{1,0:T(8,128)(2,1)S(1)}, bf16[1024,512]{1,0:T(8,128)(2,1)S(1)}, u32[]{:S(2)}, u32[]{:S(2)}) collective-permute-start(bf16[1024,512]{1,0:T(8,128)(2,1)S(1)} %bundle.29), channel_id=1, source_target_pairs={{0,1},{1,0},{2,3},{3,2},{4,5},{5,4},{6,7},{7,6},{8,9},{9,8},{10,11... | collective-permute-start | bytes 3145736 | tf_op jit(solution)/shard_map/ppermute | solution.py:377
  68.6 12.6 %collective-permute-start.18 = (bf16[1024,512]{1,0:T(8,128)(2,1)S(1)}, bf16[1024,512]{1,0:T(8,128)(2,1)S(1)}, u32[]{:S(2)}, u32[]{:S(2)}) collective-permute-start(bf16[1024,512]{1,0:T(8,128)(2,1)S(1)} %bundle.23), channel_id=1, source_target_pairs={{0,1},{1,0},{2,3},{3,2},{4,5},{5,4},{6,7},{7,6},{8,9},{9,8},{10,11... | collective-permute-start | bytes 3145736 | tf_op jit(solution)/shard_map/ppermute | solution.py:377
  69.2 8.3 %collective-permute-start.19 = (bf16[256,512]{1,0:T(8,128)(2,1)S(1)}, bf16[256,512]{1,0:T(8,128)(2,1)S(1)}, u32[]{:S(2)}, u32[]{:S(2)}) collective-permute-start(bf16[256,512]{1,0:T(8,128)(2,1)S(1)} %bundle.24.refs_0_.refs_1_), channel_id=1, source_target_pairs={{0,16},{16,0},{1,17},{17,1},{2,18},{18,2},{3,19},{19,3},{4,20},{20... | collective-permute-start | bytes 786440 | tf_op jit(solution)/shard_map/ppermute | solution.py:377
  77.5 3.7 %collective-permute-start.23 = (bf16[512,512]{1,0:T(8,128)(2,1)S(1)}, bf16[512,512]{1,0:T(8,128)(2,1)S(1)}, u32[]{:S(2)}, u32[]{:S(2)}) collective-permute-start(bf16[512,512]{1,0:T(8,128)(2,1)S(1)} %bundle.28), channel_id=1, source_target_pairs={{0,1},{1,0},{2,3},{3,2},{4,5},{5,4},{6,7},{7,6},{8,9},{9,8},{10,11... | collective-permute-start | bytes 1572872 | tf_op jit(solution)/shard_map/ppermute | solution.py:377
  79.3 3.2 %collective-permute-start.25 = (bf16[544,256]{1,0:T(8,128)(2,1)S(1)}, bf16[544,256]{1,0:T(8,128)(2,1)S(1)}, u32[]{:S(2)}, u32[]{:S(2)}) collective-permute-start(bf16[544,256]{1,0:T(8,128)(2,1)S(1)} %bundle.30), channel_id=1, source_target_pairs={{0,1},{1,0},{2,3},{3,2},{4,5},{5,4},{6,7},{7,6},{8,9},{9,8},{10,11... | collective-permute-start | bytes 835592 | tf_op jit(solution)/shard_map/ppermute | solution.py:377
  79.4 3.1 %collective-permute-start.26 = (bf16[272,256]{1,0:T(8,128)(2,1)S(1)}, bf16[272,256]{1,0:T(8,128)(2,1)S(1)}, u32[]{:S(2)}, u32[]{:S(2)}) collective-permute-start(bf16[272,256]{1,0:T(8,128)(2,1)S(1)} %bundle.31), channel_id=1, source_target_pairs={{0,1},{1,0},{2,3},{3,2},{4,5},{5,4},{6,7},{7,6},{8,9},{9,8},{10,11... | collective-permute-start | bytes 417800 | tf_op jit(solution)/shard_map/ppermute | solution.py:377

commit v9 on v8

--- a/solution.py
+++ b/solution.py
@@ -10,7 +10,7 @@
 
 HALF = 256
 MIB = 1024 * 1024
-COST = 4
+COST = 1
 AXES = ("parts", "line", "plane", "core")
 
 
@@ -26,21 +26,25 @@
     return (lax.axis_index("line") * 2 + lax.axis_index("plane")) * 2 + lax.axis_index("core")
 
 
-EARLY, LATE = (5,), ()
+EARLY, LATE = (), (5,)
 ROUNDS = ((1, 4), (3, 7), (2, 6))
-LAST = ('R1', 'P5')
+SWAPS = ((0,), (1,), (2,))
+LAST = ("R1", "P5")
 TIES = {
-    "Y2": ("B0", "T2", "X1",),
-    "X4": ("T2", "X3", "Y1",),
+    "Y1": ("local",),
+    "Y2": ("B0", "T0", "T2",),
     "C1": ("X2", "mask",),
     "C2": ("X3",),
-    "C3": ("AB",),
-    "C4": ("AB", "B1", "F0", "R1", "Y2",),
-    "B1": ("R0",),
+    "C3": ("AB", "B0", "Y2",),
+    "C4": ("AB", "B1", "R1", "Y2",),
+    "B0": ("CW", "Y1", "Z1", "Z2",),
+    "B1": ("Y2",),
+    "B2": ("B1", "T0",),
     "F0": ("Y3",),
+    "R2": ("P5",),
     "T1": ("R0", "Y2", "Z3",),
-    "T2": ("P5", "Y1", "Z2",),
-    "mask": ("B0", "T1", "Y0",),
+    "T2": ("Y1", "Z2",),
+    "mask": ("B0", "T1", "Z2",),
 }
 
 
@@ -54,9 +58,9 @@
     return [(chip ^ mask) * 2 + i for i in range(2)]
 
 
-def send_kernel(targets_of, wanted, down, up, weight, *refs):
+def send_kernel(targets_of, wanted, down, up, *refs):
     targets = targets_of()
-    *outs, whole, half = refs[:-6]
+    outs = refs[:-6]
     table, pick, even_rows, odd_rows, table_sem, sems = refs[-6:]
     choices = wanted.shape[0]
     rank = down.shape[1]
@@ -71,8 +75,6 @@
         copy.start()
         copies.append(copy)
 
-    begin(weight.at[pl.ds(lax.axis_index("parts") * HALF, HALF), :], half)
-    begin(weight, whole)
     places = []
     for out, target in targets:
         places.append((outs[out], sum(place[0] is outs[out] for place in places) * length))
@@ -116,7 +118,7 @@
         copy.wait()
 
 
-def make_messages(wanted, down, up, weight, shard_width, counts, targets_of, cost, others=()):
+def make_messages(wanted, down, up, shard_width, counts, targets_of, cost, others=()):
     choices = wanted.shape[0]
     rank, depth = down.shape[1:]
     halves = depth // HALF
@@ -125,38 +127,53 @@
     padded = -(-sum(counts) // 8) * 8
 
     def kernel(*refs):
-        send_kernel(targets_of, *refs[:4], *refs[4 + len(others) :])
-
-    *messages, whole, half = pl.pallas_call(
-        kernel,
-        out_shape=[pltpu.VMEM((n * length, HALF), jnp.bfloat16) for n in counts]
-        + [
-            pltpu.VMEM(weight.shape, weight.dtype),
-            pltpu.VMEM((HALF, weight.shape[1]), weight.dtype),
-        ],
+        send_kernel(targets_of, *refs[:3], *refs[3 + len(others) :])
+
+    return pl.pallas_call(
+        kernel,
+        out_shape=[pltpu.VMEM((n * length, HALF), jnp.bfloat16) for n in counts],
         in_specs=[pl.BlockSpec(memory_space=pltpu.SMEM)]
-        + [pl.BlockSpec(memory_space=pltpu.HBM)] * 3
+        + [pl.BlockSpec(memory_space=pltpu.HBM)] * 2
         + [pl.BlockSpec(memory_space=pltpu.VMEM)] * len(others),
-        out_specs=[pl.BlockSpec(memory_space=pltpu.VMEM)] * (len(counts) + 2),
+        out_specs=[pl.BlockSpec(memory_space=pltpu.VMEM)] * len(counts),
         scratch_shapes=[
             pltpu.VMEM(up.shape, up.dtype),
             pltpu.VMEM((choices * padded, up.shape[1]), jnp.float32),
             pltpu.VMEM((padded * count, 2 * rank), jnp.float32),
             pltpu.VMEM((padded * count, 2 * rank), jnp.float32),
             pltpu.SemaphoreType.DMA,
-            pltpu.SemaphoreType.DMA((sum(counts) * choices * halves + 2,)),
+            pltpu.SemaphoreType.DMA((sum(counts) * choices * halves,)),
         ],
         compiler_params=pltpu.CompilerParams(vmem_limit_bytes=16 * MIB),
         cost_estimate=pl.CostEstimate(
             flops=0, bytes_accessed=4 * cost * sum(counts) * length * HALF, transcendentals=0
         ),
         name="make_messages",
-    )(
-        wanted,
-        *[in_hbm(value) for value in (down, up, weight)],
-        *[in_vmem(other) for other in others],
-    )
-    return messages, whole, half
+    )(wanted, in_hbm(down), in_hbm(up), *[in_vmem(other) for other in others])
+
+
+def load_rows(weight):
+    def kernel(source, whole, half, sems):
+        x = lax.axis_index("parts")
+        own = pltpu.make_async_copy(source.at[pl.ds(x * HALF, HALF), :], half, sems.at[0])
+        rest = pltpu.make_async_copy(source, whole, sems.at[1])
+        own.start()
+        rest.start()
+        own.wait()
+        rest.wait()
+
+    return pl.pallas_call(
+        kernel,
+        out_shape=[
+            pltpu.VMEM(weight.shape, weight.dtype),
+            pltpu.VMEM((HALF, weight.shape[1]), weight.dtype),
+        ],
+        in_specs=[pl.BlockSpec(memory_space=pltpu.HBM)],
+        out_specs=[pl.BlockSpec(memory_space=pltpu.VMEM)] * 2,
+        scratch_shapes=[pltpu.SemaphoreType.DMA((2,))],
+        compiler_params=pltpu.CompilerParams(vmem_limit_bytes=2 * MIB),
+        name="load_rows",
+    )(in_hbm(weight))
 
 
 def base_product(tokens, bundles, start=None, others=()):
@@ -411,7 +428,6 @@
         jnp.transpose(group_adapters),
         jnp.swapaxes(adapter_down, 1, 2),
         jnp.transpose(adapter_up, (1, 2, 0)).reshape(shard_width * rank, adapter_up.shape[0]),
-        base_weight,
         shard_width,
     )
 
@@ -428,15 +444,19 @@
             targets += [(n, target) for target in direct_targets(mask)]
         for n, masks in enumerate(ROUNDS):
             targets += [(len(LATE) + n, target) for target in round_targets(masks, core)]
-            targets += [
-                (len(LATE) + len(ROUNDS) + n, target) for target in round_targets(masks, 1 - core)
-            ]
+        first = len(LATE) + len(ROUNDS)
+        for n, rounds in enumerate(SWAPS):
+            for number in rounds:
+                targets += [
+                    (first + n, target) for target in round_targets(ROUNDS[number], 1 - core)
+                ]
         me = store_index()
-        last = len(LATE) + 2 * len(ROUNDS)
+        last = first + len(SWAPS)
         return targets + [(last - 1, me ^ 1), (last, me)]
 
-    early_count = len(EARLY)
-    late_counts = (2,) * len(LATE) + (2,) * (2 * len(ROUNDS) - 1) + (3, 1)
+    swap_counts = [2 * len(rounds) for rounds in SWAPS]
+    swap_counts[-1] += 1
+    late_counts = (2,) * (len(LATE) + len(ROUNDS)) + tuple(swap_counts) + (1,)
     values = {}
 
     def get(name):
@@ -447,31 +467,28 @@
     def wait(name):
         return [get(other) for other in TIES.get(name, ())]
 
-    def first_messages():
-        messages, whole, half = make_messages(
-            *operands, (2,) * early_count, early_targets, 1, wait("early")
-        )
+    def early_messages():
+        counts = (2,) * len(EARLY)
+        messages = make_messages(*operands, counts, early_targets, 1, wait("early"))
         for mask, message in zip(EARLY, messages):
             values[f"pair{mask}"] = message
-        values["whole"], values["own"] = whole, half
-
-    def other_messages():
-        messages, _, _ = make_messages(
-            *operands, late_counts, late_targets, COST, [get("own"), *wait("late")]
-        )
-        for mask, message in zip(LATE, messages):
-            values[f"pair{mask}"] = message
-        for n, message in enumerate(messages[len(LATE) :]):
-            kind, number = divmod(n, len(ROUNDS))
-            values[("mine", "theirs", "local")[kind] + str(number)] = message
+
+    def late_messages():
+        messages = make_messages(*operands, late_counts, late_targets, COST, wait("late"))
+        names = [f"pair{mask}" for mask in LATE] + [f"mine{n}" for n in range(len(ROUNDS))]
+        names += [f"theirs{n}" for n in range(len(SWAPS))] + ["local"]
+        values.update(zip(names, messages))
 
     def make(name):
         kind, number = name[0], name[1:]
-        if name in ("whole", "own") or name in [f"pair{mask}" for mask in EARLY]:
-            first_messages()
+        if name in ("whole", "own"):
+            values["whole"], values["own"] = load_rows(base_weight)
+            return values[name]
+        if name in [f"pair{mask}" for mask in EARLY]:
+            early_messages()
             return values[name]
         if name[:4] in ("pair", "mine", "thei", "loca"):
-            other_messages()
+            late_messages()
             return values[name]
         if name in ROWS:
             axis, mask, sources = ROWS[name]
@@ -498,15 +515,17 @@
             payload = after(message, *others) if others else message
             return send_pairs(payload, lambda i: i ^ (2 * int(number)))
         if kind == "H":
-            got, length = get("P" + number), get("local0").shape[0]
+            got, length = get("P" + number), get("local").shape[0]
             return swap(bundle([(got, lambda: length, length)], wait(name)), "core", 1)
         if kind == "R":
-            masks, length = ROUNDS[int(number)], get("local0").shape[0]
-            theirs = (get("T" + number), lambda: 0, 2 * length)
+            masks, length = ROUNDS[int(number)], get("local").shape[0]
+            group = [n for n, rounds in enumerate(SWAPS) if int(number) in rounds][0]
+            begin = SWAPS[group].index(int(number)) * 2 * length
+            theirs = (get(f"T{group}"), lambda: begin, 2 * length)
             payload = bundle([get("mine" + number), theirs], wait(name))
             return send_pairs(payload, lambda i: i ^ (2 * masks[i % 2]))
         if kind == "F":
-            got, length = get("R" + number), get("local0").shape[0]
+            got, length = get("R" + number), get("local").shape[0]
 
             def place(i):
                 return pl.multiple_of((2 * i + 1 - lax.axis_index("core")) * length, 16)
@@ -523,11 +542,11 @@
 
             def sources():
                 me = store_index()
-                return [(0, 0, me), (1, 2 * length_rows, me ^ 1)] + places(2)
+                return [(0, 0, me), (1, 2 * len(SWAPS[-1]) * length_rows, me ^ 1)] + places(2)
 
             shrunk, values["second factors"] = adapt_begin(
                 tokens,
-                (get("local0"), get(f"T{len(ROUNDS) - 1}"), *buffers, *wait(name)),
+                (get("local"), get(f"T{len(SWAPS) - 1}"), *buffers, *wait(name)),
                 sources,
                 length_rows,
                 pair,

time: 84.6 us -> 85.6 us (1.012)
  starting transfers between devices: 30.1 us -> 34.6 us
  Pallas kernels: 17.1 us -> 14.9 us
  waiting for transfers between devices: 36.3 us -> 35 us
    ppermute x23, waiting for transfers between devices: 29.6 us -> 22.6 us  [swap(): return lax.ppermute(block, axis, [(i, i ^ bit) for i in range(size)])]
    ppermute x4, waiting for transfers between devices: 6.63 us -> 12.4 us  [send_pairs(): lax.ppermute(payload, AXES[1:], [(i, target(i)) for i in range(size)])]
    ppermute x23, starting transfers between devices: 24.3 us -> 29.5 us  [swap(): return lax.ppermute(block, axis, [(i, i ^ bit) for i in range(size)])]
    pallas_call x2 -> x1, Pallas kernels: 6.93 us -> 3.42 us  [make_messages(): pl.pallas_call(kernel, out_shape=[pltpu.VMEM((n * length, HALF), jnp.bflo...]
    pallas_call x0 -> x1, Pallas kernels: none -> 1.29 us  [load_rows(): pl.pallas_call(kernel, out_shape=[pltpu.VMEM(weight.shape, weight.dtype),...]
  transfers between devices with their start and end apart: 27 -> 27, of which waited for: 9 -> 10; matrix products, arithmetic and copies ran while one was open for 0% -> 0% of each run, Pallas kernels for 15% -> 14%
where the time goes in v9:
time: 85.6 us; the launch traced here: 85.4 us
  waiting for transfers between devices  35 us (41%)
  starting transfers between devices  34.6 us (40%)
  Pallas kernels  14.9 us (17%)
    ppermute x23, starting transfers between devices, swap(): return lax.ppermute(block, axis, [(i, i ^ bit) for i in range(size)])  29.5 us
    ppermute x23, waiting for transfers between devices, swap(): return lax.ppermute(block, axis, [(i, i ^ bit) for i in range(size)])  22.6 us
    ppermute x4, waiting for transfers between devices, send_pairs(): lax.ppermute(payload, AXES[1:], [(i, target(i)) for i in range(size)])  12.4 us
    ppermute x4, starting transfers between devices, send_pairs(): lax.ppermute(payload, AXES[1:], [(i, target(i)) for i in range(size)])  5.15 us
    pallas_call x4, Pallas kernels, base_product(): pl.pallas_call(kernel, out_shape=pltpu.VMEM((rows, width), jnp.float32),...  4.99 us
    pallas_call x1, Pallas kernels, make_messages(): pl.pallas_call(kernel, out_shape=[pltpu.VMEM((n * length, HALF), jnp.bflo...  3.42 us
    pallas_call x1, Pallas kernels, adapt_end(): pl.pallas_call(kernel, out_shape=jax.ShapeDtypeStruct((rows, width), jnp....  1.93 us
  transfers between devices with their start and end apart: 27, of which 10 were waited for; matrix products, arithmetic and copies ran while one was open for 0% of the time, Pallas kernels for 14%

profile of v9, /device:TPU:0, one launch (start us, length us, event | category | flops | bytes accessed | tf_op | source)
XLA Modules:
  0.0 85.4 jit_solution(1565818129076756648)
XLA Ops:
  0.0 1.3 %load_rows.1 = (bf16[512,512]{1,0:T(8,128)(2,1)S(1)}, bf16[256,512]{1,0:T(8,128)(2,1)S(1)}) custom-call(bf16[512,512]{1,0:T(8,128)(2,1)} %source.1), custom_call_target="tpu_custom_call" | custom-call | tf_op jit(solution)/shard_map/load_rows/pallas_call | solution.py:165
  1.3 3.1 %collective-permute-start.1 = (bf16[256,512]{1,0:T(8,128)(2,1)S(1)}, bf16[256,512]{1,0:T(8,128)(2,1)S(1)}, u32[]{:S(2)}, u32[]{:S(2)}) collective-permute-start(bf16[256,512]{1,0:T(8,128)(2,1)S(1)} %get-tuple-element.18), channel_id=1, source_target_pairs={{0,4},{4,0},{8,12},{12,8},{1,5},{5,1},{9,13},{13,9},{2,6},{6,2},{1... | collective-permute-start | bytes 786440 | tf_op jit(solution)/shard_map/ppermute | solution.py:394
  4.4 1.5 %collective-permute-start.2 = (bf16[256,512]{1,0:T(8,128)(2,1)S(1)}, bf16[256,512]{1,0:T(8,128)(2,1)S(1)}, u32[]{:S(2)}, u32[]{:S(2)}) collective-permute-start(bf16[256,512]{1,0:T(8,128)(2,1)S(1)} %get-tuple-element.18), channel_id=1, source_target_pairs={{0,2},{2,0},{1,3},{3,1},{4,6},{6,4},{5,7},{7,5},{8,10},{10,8},{9,1... | collective-permute-start | bytes 786440 | tf_op jit(solution)/shard_map/ppermute | solution.py:394
  5.9 2.6 %collective-permute-start.5 = (bf16[256,512]{1,0:T(8,128)(2,1)S(1)}, bf16[256,512]{1,0:T(8,128)(2,1)S(1)}, u32[]{:S(2)}, u32[]{:S(2)}) collective-permute-start(bf16[256,512]{1,0:T(8,128)(2,1)S(1)} %get-tuple-element.18), channel_id=1, source_target_pairs={{0,8},{4,12},{8,0},{12,4},{1,9},{5,13},{9,1},{13,5},{2,10},{6,14},... | collective-permute-start | bytes 786440 | tf_op jit(solution)/shard_map/ppermute | solution.py:394
  8.5 0.7 copy-done.2
  9.2 3.4 %make_messages.1 = (bf16[544,256]{1,0:T(8,128)(2,1)S(1)}, bf16[544,256]{1,0:T(8,128)(2,1)S(1)}, bf16[544,256]{1,0:T(8,128)(2,1)S(1)}, bf16[544,256]{1,0:T(8,128)...) custom-call(s32[2,16]{1,0:T(2,128)S(1)} %bitcast.5, ...), custom_call_target="tpu_custom_call" | custom-call | bytes 4456448 | tf_op jit(solution)/shard_map/make_messages/pallas_call | solution.py:132
  12.6 2.3 %collective-permute-done.1.refs_0_.refs_6_ = bf16[256,512]{1,0:T(8,128)(2,1)S(1)} collective-permute-done((bf16[256,512]{1,0:T(8,128)(2,1)S(1)}, bf16[256,512]{1,0:T(8,128)(2,1)S(1)}, u32[]{:S(2)}, u32[]{:S(2)}) %collective-permute-start.1) | collective-permute-done | bytes 262176 | tf_op jit(solution)/shard_map/ppermute | solution.py:394
  15.0 2.8 %collective-permute-start.4 = (bf16[256,512]{1,0:T(8,128)(2,1)S(1)}, bf16[256,512]{1,0:T(8,128)(2,1)S(1)}, u32[]{:S(2)}, u32[]{:S(2)}) collective-permute-start(bf16[256,512]{1,0:T(8,128)(2,1)S(1)} %bundle.18), channel_id=1, source_target_pairs={{0,2},{2,0},{1,3},{3,1},{4,6},{6,4},{5,7},{7,5},{8,10},{10,8},{9,1... | collective-permute-start | bytes 786440 | tf_op jit(solution)/shard_map/ppermute | solution.py:394
  17.7 0.0 collective-permute-start
  17.7 0.0 collective-permute-done.2.refs_1_
  17.8 1.6 %collective-permute-start.3 = (bf16[512,512]{1,0:T(8,128)(2,1)S(1)}, bf16[512,512]{1,0:T(8,128)(2,1)S(1)}, u32[]{:S(2)}, u32[]{:S(2)}) collective-permute-start(bf16[512,512]{1,0:T(8,128)(2,1)S(1)} %bundle.17.refs_2_.refs_0_), channel_id=1, source_target_pairs={{0,16},{16,0},{1,17},{17,1},{2,18},{18,2},{3,19},{19,3},{4,20},{20... | collective-permute-start | bytes 1572872 | tf_op jit(solution)/shard_map/ppermute | solution.py:394
  19.3 0.2 collective-permute-start.6
  19.6 0.4 collective-permute-done.5.refs_7_.refs_2_.refs_0_
  20.0 3.2 %collective-permute-done.4.refs_5_.refs_1_ = bf16[256,512]{1,0:T(8,128)(2,1)S(1)} collective-permute-done((bf16[256,512]{1,0:T(8,128)(2,1)S(1)}, bf16[256,512]{1,0:T(8,128)(2,1)S(1)}, u32[]{:S(2)}, u32[]{:S(2)}) %collective-permute-start.4) | collective-permute-done | bytes 262176 | tf_op jit(solution)/shard_map/ppermute | solution.py:394
  23.2 0.0 collective-permute-start.8
  23.2 0.0 collective-permute-done.6.refs_1_.refs_2_.refs_5_
  23.2 1.8 %collective-permute-start.7 = (bf16[1088,256]{1,0:T(8,128)(2,1)S(1)}, bf16[1088,256]{1,0:T(8,128)(2,1)S(1)}, u32[]{:S(2)}, u32[]{:S(2)}) collective-permute-start(bf16[1088,256]{1,0:T(8,128)(2,1)S(1)} %bundle.19), channel_id=1, source_target_pairs={{0,2},{1,9},{2,0},{3,11},{4,6},{5,13},{6,4},{7,15},{8,10},{9,1},{1... | collective-permute-start | bytes 1671176 | tf_op jit(solution)/shard_map/ppermute | solution.py:399
  25.0 0.3 collective-permute-start.15
  25.3 0.0 collective-permute-done.refs_1_.refs_4_
  25.3 2.5 %collective-permute-start.10 = (bf16[256,512]{1,0:T(8,128)(2,1)S(1)}, bf16[256,512]{1,0:T(8,128)(2,1)S(1)}, u32[]{:S(2)}, u32[]{:S(2)}) collective-permute-start(bf16[256,512]{1,0:T(8,128)(2,1)S(1)} %collective-permute-done.5.refs_7_.refs_2_.refs_0_), channel_id=1, source_target_pairs={{0,4},{4,0},{8,12},{12,8},{1,5},{5,1},{9,13},{13,9},{2,6},{6,2},{1... | collective-permute-start | bytes 786440 | tf_op jit(solution)/shard_map/ppermute | solution.py:394
  27.8 4.4 %collective-permute-done.3.refs_3_.refs_1_ = bf16[512,512]{1,0:T(8,128)(2,1)S(1)} collective-permute-done((bf16[512,512]{1,0:T(8,128)(2,1)S(1)}, bf16[512,512]{1,0:T(8,128)(2,1)S(1)}, u32[]{:S(2)}, u32[]{:S(2)}) %collective-permute-start.3) | collective-permute-done | bytes 524320 | tf_op jit(solution)/shard_map/ppermute | solution.py:394
  32.2 1.2 %base_product.4.refs_1_.refs_0_.refs_3_ = f32[512,512]{1,0:T(8,128)S(1)} custom-call(bf16[512,8192]{1,0:T(8,128)(2,1)S(1)} %copy-done, bf16[512,512]{1,0:T(8,128)(2,1)S(1)} %get-tuple-element.17.refs_0_, bf16[512,512]{1,0:T(8,128)(2,1)S(1)} %collective-permute-done.refs_1_.refs_4_, bf16[512,512]{1,0:T(8,128)(2,1)S(1)} %bundle.17.refs_2_.refs_0_, ...), custom_call_target="tpu_custom_call" | custom-call | flops 1073741824 | bytes 5242880 | tf_op jit(solution)/shard_map/base_product/pallas_call | solution.py:210
  33.4 0.0 collective-permute-done.8.refs_3_.refs_1_
  33.5 0.1 collective-permute-start.9
  33.7 1.6 %collective-permute-start.20 = (bf16[512,512]{1,0:T(8,128)(2,1)S(1)}, bf16[512,512]{1,0:T(8,128)(2,1)S(1)}, u32[]{:S(2)}, u32[]{:S(2)}) collective-permute-start(bf16[512,512]{1,0:T(8,128)(2,1)S(1)} %bundle.27.refs_1_.refs_0_), channel_id=1, source_target_pairs={{0,16},{16,0},{1,17},{17,1},{2,18},{18,2},{3,19},{19,3},{4,20},{20... | collective-permute-start | bytes 1572872 | tf_op jit(solution)/shard_map/ppermute | solution.py:394
  35.2 11.1 %collective-permute-done.15.refs_2_.refs_0_ = bf16[544,256]{1,0:T(8,128)(2,1)S(1)} collective-permute-done((bf16[544,256]{1,0:T(8,128)(2,1)S(1)}, bf16[544,256]{1,0:T(8,128)(2,1)S(1)}, u32[]{:S(2)}, u32[]{:S(2)}) %collective-permute-start.15) | collective-permute-done | bytes 278560 | tf_op jit(solution)/shard_map/ppermute | solution.py:399
  46.3 0.1 collective-permute-start.16
  46.4 0.0 collective-permute-done.10.refs_3_.refs_0_
  46.4 0.0 collective-permute-done.7.refs_1_.refs_0_.refs_2_
  46.4 0.0 collective-permute-done.9.refs_2_.refs_1_.refs_4_.refs_5_
  46.5 7.2 %collective-permute-start.11 = (bf16[544,256]{1,0:T(8,128)(2,1)S(1)}, bf16[544,256]{1,0:T(8,128)(2,1)S(1)}, u32[]{:S(2)}, u32[]{:S(2)}) collective-permute-start(bf16[544,256]{1,0:T(8,128)(2,1)S(1)} %after.5), channel_id=1, source_target_pairs={{0,1},{1,0},{2,3},{3,2},{4,5},{5,4},{6,7},{7,6},{8,9},{9,8},{10,11... | collective-permute-start | bytes 835592 | tf_op jit(solution)/shard_map/ppermute | solution.py:394
  53.6 0.3 collective-permute-start.13
  54.0 1.6 %collective-permute-start.12 = (bf16[512,512]{1,0:T(8,128)(2,1)S(1)}, bf16[512,512]{1,0:T(8,128)(2,1)S(1)}, u32[]{:S(2)}, u32[]{:S(2)}) collective-permute-start(bf16[512,512]{1,0:T(8,128)(2,1)S(1)} %bundle.21.refs_0_.refs_1_), channel_id=1, source_target_pairs={{0,16},{16,0},{1,17},{17,1},{2,18},{18,2},{3,19},{19,3},{4,20},{20... | collective-permute-start | bytes 1572872 | tf_op jit(solution)/shard_map/ppermute | solution.py:394
  55.5 0.0 collective-permute-done.11.refs_1_
  55.5 1.1 %row_mask.1.refs_3_.mask_ref = f32[512,128]{1,0:T(8,128)S(1)} custom-call(s32[1,16]{1,0:T(1,128)S(1)} %copy-done.3, s32[16,16]{1,0:T(8,128)S(1)} %copy-done.1, f32[512,512]{1,0:T(8,128)S(1)} %base_product.4.refs_1_.refs_0_.refs_3_, bf16[544,256]{1,0:T(8,128)(2,1)S(1)} %collective-permute-done.11.refs_1_, ...), custom_call_target="tpu_custom_call" | custom-call | tf_op jit(solution)/shard_map/row_mask/pallas_call | solution.py:373
  56.7 0.0 collective-permute-done.20.refs_2_.refs_1_
  56.7 0.1 bundle.28
  56.7 0.1 collective-permute-start.21
  56.8 5.1 %collective-permute-done.13.refs_2_.refs_0_ = bf16[256,512]{1,0:T(8,128)(2,1)S(1)} collective-permute-done((bf16[256,512]{1,0:T(8,128)(2,1)S(1)}, bf16[256,512]{1,0:T(8,128)(2,1)S(1)}, u32[]{:S(2)}, u32[]{:S(2)}) %collective-permute-start.13) | collective-permute-done | bytes 262176 | tf_op jit(solution)/shard_map/ppermute | solution.py:394
  61.9 0.1 collective-permute-start.14
  62.0 0.9 %collective-permute-done.16.refs_0_.refs_1_.refs_4_ = bf16[1088,256]{1,0:T(8,128)(2,1)S(1)} collective-permute-done((bf16[1088,256]{1,0:T(8,128)(2,1)S(1)}, bf16[1088,256]{1,0:T(8,128)(2,1)S(1)}, u32[]{:S(2)}, u32[]{:S(2)}) %collective-permute-start.16) | collective-permute-done | bytes 557088 | tf_op jit(solution)/shard_map/ppermute | solution.py:399
  63.0 0.1 collective-permute-start.17
  63.1 3.0 %collective-permute-start.22 = (bf16[1088,256]{1,0:T(8,128)(2,1)S(1)}, bf16[1088,256]{1,0:T(8,128)(2,1)S(1)}, u32[]{:S(2)}, u32[]{:S(2)}) collective-permute-start(bf16[1088,256]{1,0:T(8,128)(2,1)S(1)} %bundle.29), channel_id=1, source_target_pairs={{0,6},{1,15},{2,4},{3,13},{4,2},{5,11},{6,0},{7,9},{8,14},{9,7},{1... | collective-permute-start | bytes 1671176 | tf_op jit(solution)/shard_map/ppermute | solution.py:399
  66.1 1.6 %collective-permute-done.12.refs_1_.refs_2_ = bf16[512,512]{1,0:T(8,128)(2,1)S(1)} collective-permute-done((bf16[512,512]{1,0:T(8,128)(2,1)S(1)}, bf16[512,512]{1,0:T(8,128)(2,1)S(1)}, u32[]{:S(2)}, u32[]{:S(2)}) %collective-permute-start.12) | collective-permute-done | bytes 524320 | tf_op jit(solution)/shard_map/ppermute | solution.py:394
  67.7 0.1 bundle.31
  67.7 0.1 collective-permute-start.24
  67.8 0.0 collective-permute-done.14.refs_3_
  67.8 0.0 collective-permute-done.17.refs_5_
  67.8 1.5 %adapt_begin.1 = (f32[512,128]{1,0:T(8,128)S(1)}, bf16[512,128]{1,0:T(8,128)(2,1)S(1)}) custom-call(bf16[512,8192]{1,0:T(8,128)(2,1)S(1)} %copy-done, bf16[272,256]{1,0:T(8,128)(2,1)S(1)} %get-tuple-element.19.refs_1_.refs_0_, bf16[816,256]{1,0:T(8,128)(2,1)S(1)} %collective-permute-done.8.refs_3_.refs_1_, ...), custom_call_target="tpu_custom_call" | custom-call | flops 1288490240 | bytes 5033164 | tf_op jit(solution)/shard_map/adapt_begin/pallas_call | solution.py:272
  69.4 0.1 bundle.25
  69.4 0.6 collective-permute-start.18
  70.0 1.6 %collective-permute-start.19 = (bf16[256,512]{1,0:T(8,128)(2,1)S(1)}, bf16[256,512]{1,0:T(8,128)(2,1)S(1)}, u32[]{:S(2)}, u32[]{:S(2)}) collective-permute-start(bf16[256,512]{1,0:T(8,128)(2,1)S(1)} %bundle.26.refs_0_.refs_1_), channel_id=1, source_target_pairs={{0,16},{16,0},{1,17},{17,1},{2,18},{18,2},{3,19},{19,3},{4,20},{20... | collective-permute-start | bytes 786440 | tf_op jit(solution)/shard_map/ppermute | solution.py:394
  71.6 1.2 %base_product.5.refs_3_.refs_4_ = f32[512,512]{1,0:T(8,128)S(1)} custom-call(bf16[512,8192]{1,0:T(8,128)(2,1)S(1)} %copy-done, bf16[1024,512]{1,0:T(8,128)(2,1)S(1)} %collective-permute-done.21.refs_0_, bf16[512,512]{1,0:T(8,128)(2,1)S(1)} %bundle.27.refs_1_.refs_0_, bf16[512,512]{1,0:T(8,128)(2,1)S(1)} %collective-permute-done.20.refs_2_.refs_1_, ...), custom_call_target="tpu_custom_call" | custom-call | flops 1073741824 | bytes 5242880 | tf_op jit(solution)/shard_map/base_product/pallas_call | solution.py:210
  72.8 5.5 %collective-permute-done.19.refs_1_.refs_2_ = bf16[256,512]{1,0:T(8,128)(2,1)S(1)} collective-permute-done((bf16[256,512]{1,0:T(8,128)(2,1)S(1)}, bf16[256,512]{1,0:T(8,128)(2,1)S(1)}, u32[]{:S(2)}, u32[]{:S(2)}) %collective-permute-start.19) | collective-permute-done | bytes 262176 | tf_op jit(solution)/shard_map/ppermute | solution.py:394
  78.3 0.4 collective-permute-done.22.refs_4_.refs_0_.refs_1_
  78.8 1.5 %collective-permute-start.23 = (bf16[512,512]{1,0:T(8,128)(2,1)S(1)}, bf16[512,512]{1,0:T(8,128)(2,1)S(1)}, u32[]{:S(2)}, u32[]{:S(2)}) collective-permute-start(bf16[512,512]{1,0:T(8,128)(2,1)S(1)} %bundle.30), channel_id=1, source_target_pairs={{0,1},{1,0},{2,3},{3,2},{4,5},{5,4},{6,7},{7,6},{8,9},{9,8},{10,11... | collective-permute-start | bytes 1572872 | tf_op jit(solution)/shard_map/ppermute | solution.py:394
  80.3 0.1 collective-permute-start.25
  80.4 0.5 collective-permute-start.26
  81.0 1.2 %base_product.6.refs_4_ = f32[512,512]{1,0:T(8,128)S(1)} custom-call(bf16[512,8192]{1,0:T(8,128)(2,1)S(1)} %copy-done, bf16[1024,512]{1,0:T(8,128)(2,1)S(1)} %collective-permute-done.24.refs_0_, bf16[512,512]{1,0:T(8,128)(2,1)S(1)} %bundle.21.refs_0_.refs_1_, bf16[512,512]{1,0:T(8,128)(2,1)S(1)} %collective-permute-done.12.refs_1_.refs_2_, ...), custom_call_target="tpu_custom_call" | custom-call | flops 1073741824 | bytes 5242880 | tf_op jit(solution)/shard_map/base_product/pallas_call | solution.py:210
  82.2 0.0 collective-permute-done.18.refs_0_
  82.2 1.3 %base_product.7.base_ref = f32[512,512]{1,0:T(8,128)S(1)} custom-call(bf16[512,8192]{1,0:T(8,128)(2,1)S(1)} %copy-done, bf16[1024,512]{1,0:T(8,128)(2,1)S(1)} %collective-permute-done.18.refs_0_, bf16[256,512]{1,0:T(8,128)(2,1)S(1)} %bundle.26.refs_0_.refs_1_, bf16[256,512]{1,0:T(8,128)(2,1)S(1)} %collective-permute-done.19.refs_1_.refs_2_, ...), custom_call_target="tpu_custom_call" | custom-call | flops 1073741824 | bytes 5242880 | tf_op jit(solution)/shard_map/base_product/pallas_call | solution.py:210
  83.5 0.0 collective-permute-done.26.refs_3_
  83.5 0.0 collective-permute-done.25.refs_1_
  83.5 1.9 %adapt_end.1 = bf16[512,512]{1,0:T(8,128)(2,1)} custom-call(bf16[512,8192]{1,0:T(8,128)(2,1)S(1)} %copy-done, f32[512,128]{1,0:T(8,128)S(1)} %row_mask.1.refs_3_.mask_ref, f32[512,512]{1,0:T(8,128)S(1)} %base_product.7.base_ref, f32[512,128]{1,0:T(8,128)S(1)} %get-tuple-element.26.refs_2_.shrunk, bf16[512,128]{1,0:T(8,128)(2,1)S(1)} %get-tuple-element.28.widened, ...), custom_call_target="tpu_custom_call" | custom-call | flops 858993472 | bytes 3355443 | tf_op jit(solution)/shard_map/adapt_end/pallas_call | solution.py:304
  (27 shorter events, 0.4 us)
Async XLA Ops:
  0.0 32.2 %copy-start = (bf16[512,8192]{1,0:T(8,128)(2,1)S(1)}, bf16[512,8192]{1,0:T(8,128)(2,1)}, u32[]{:S(2)}) copy-start(bf16[512,8192]{1,0:T(8,128)(2,1)} %tokens_ref.11) | copy-start | bytes 25165828
  1.3 13.7 %collective-permute-start.1 = (bf16[256,512]{1,0:T(8,128)(2,1)S(1)}, bf16[256,512]{1,0:T(8,128)(2,1)S(1)}, u32[]{:S(2)}, u32[]{:S(2)}) collective-permute-start(bf16[256,512]{1,0:T(8,128)(2,1)S(1)} %get-tuple-element.18), channel_id=1, source_target_pairs={{0,4},{4,0},{8,12},{12,8},{1,5},{5,1},{9,13},{13,9},{2,6},{6,2},{1... | collective-permute-start | bytes 786440 | tf_op jit(solution)/shard_map/ppermute | solution.py:394
  4.4 13.4 %collective-permute-start.2 = (bf16[256,512]{1,0:T(8,128)(2,1)S(1)}, bf16[256,512]{1,0:T(8,128)(2,1)S(1)}, u32[]{:S(2)}, u32[]{:S(2)}) collective-permute-start(bf16[256,512]{1,0:T(8,128)(2,1)S(1)} %get-tuple-element.18), channel_id=1, source_target_pairs={{0,2},{2,0},{1,3},{3,1},{4,6},{6,4},{5,7},{7,5},{8,10},{10,8},{9,1... | collective-permute-start | bytes 786440 | tf_op jit(solution)/shard_map/ppermute | solution.py:394
  5.9 14.1 %collective-permute-start.5 = (bf16[256,512]{1,0:T(8,128)(2,1)S(1)}, bf16[256,512]{1,0:T(8,128)(2,1)S(1)}, u32[]{:S(2)}, u32[]{:S(2)}) collective-permute-start(bf16[256,512]{1,0:T(8,128)(2,1)S(1)} %get-tuple-element.18), channel_id=1, source_target_pairs={{0,8},{4,12},{8,0},{12,4},{1,9},{5,13},{9,1},{13,5},{2,10},{6,14},... | collective-permute-start | bytes 786440 | tf_op jit(solution)/shard_map/ppermute | solution.py:394
  8.5 0.7 copy-start.2
  15.0 8.2 %collective-permute-start.4 = (bf16[256,512]{1,0:T(8,128)(2,1)S(1)}, bf16[256,512]{1,0:T(8,128)(2,1)S(1)}, u32[]{:S(2)}, u32[]{:S(2)}) collective-permute-start(bf16[256,512]{1,0:T(8,128)(2,1)S(1)} %bundle.18), channel_id=1, source_target_pairs={{0,2},{2,0},{1,3},{3,1},{4,6},{6,4},{5,7},{7,5},{8,10},{10,8},{9,1... | collective-permute-start | bytes 786440 | tf_op jit(solution)/shard_map/ppermute | solution.py:394
  17.7 7.6 %collective-permute-start = (bf16[512,512]{1,0:T(8,128)(2,1)S(1)}, bf16[512,512]{1,0:T(8,128)(2,1)S(1)}, u32[]{:S(2)}, u32[]{:S(2)}) collective-permute-start(bf16[512,512]{1,0:T(8,128)(2,1)S(1)} %get-tuple-element.17.refs_0_), channel_id=1, source_target_pairs={{0,1},{1,0},{2,3},{3,2},{4,5},{5,4},{6,7},{7,6},{8,9},{9,8},{10,11... | collective-permute-start | bytes 1572872 | tf_op jit(solution)/shard_map/ppermute | solution.py:394
  17.8 14.4 %collective-permute-start.3 = (bf16[512,512]{1,0:T(8,128)(2,1)S(1)}, bf16[512,512]{1,0:T(8,128)(2,1)S(1)}, u32[]{:S(2)}, u32[]{:S(2)}) collective-permute-start(bf16[512,512]{1,0:T(8,128)(2,1)S(1)} %bundle.17.refs_2_.refs_0_), channel_id=1, source_target_pairs={{0,16},{16,0},{1,17},{17,1},{2,18},{18,2},{3,19},{19,3},{4,20},{20... | collective-permute-start | bytes 1572872 | tf_op jit(solution)/shard_map/ppermute | solution.py:394
  19.3 3.8 %collective-permute-start.6 = (bf16[544,256]{1,0:T(8,128)(2,1)S(1)}, bf16[544,256]{1,0:T(8,128)(2,1)S(1)}, u32[]{:S(2)}, u32[]{:S(2)}) collective-permute-start(bf16[544,256]{1,0:T(8,128)(2,1)S(1)} %after.3), channel_id=1, source_target_pairs={{0,1},{1,0},{2,3},{3,2},{4,5},{5,4},{6,7},{7,6},{8,9},{9,8},{10,11... | collective-permute-start | bytes 835592 | tf_op jit(solution)/shard_map/ppermute | solution.py:394
  23.2 10.3 %collective-permute-start.8 = (bf16[816,256]{1,0:T(8,128)(2,1)S(1)}, bf16[816,256]{1,0:T(8,128)(2,1)S(1)}, u32[]{:S(2)}, u32[]{:S(2)}) collective-permute-start(bf16[816,256]{1,0:T(8,128)(2,1)S(1)} %after.4), channel_id=1, source_target_pairs={{0,1},{1,0},{2,3},{3,2},{4,5},{5,4},{6,7},{7,6},{8,9},{9,8},{10,11... | collective-permute-start | bytes 1253384 | tf_op jit(solution)/shard_map/ppermute | solution.py:394
  23.2 23.2 %collective-permute-start.7 = (bf16[1088,256]{1,0:T(8,128)(2,1)S(1)}, bf16[1088,256]{1,0:T(8,128)(2,1)S(1)}, u32[]{:S(2)}, u32[]{:S(2)}) collective-permute-start(bf16[1088,256]{1,0:T(8,128)(2,1)S(1)} %bundle.19), channel_id=1, source_target_pairs={{0,2},{1,9},{2,0},{3,11},{4,6},{5,13},{6,4},{7,15},{8,10},{9,1},{1... | collective-permute-start | bytes 1671176 | tf_op jit(solution)/shard_map/ppermute | solution.py:399
  25.0 30.5 %copy-start.1 = (s32[16,16]{1,0:T(8,128)S(1)}, s32[16,16]{1,0:T(8,128)}, u32[]{:S(2)}) copy-start(s32[16,16]{1,0:T(8,128)} %slots_ref.1) | copy-start | bytes 3076
  25.0 30.5 %copy-start.3 = (s32[1,16]{1,0:T(1,128)S(1)}, s32[1,16]{1,0:T(1,128)}, u32[]{:S(2)}) copy-start(s32[1,16]{1,0:T(1,128)} %lengths_ref.1) | copy-start | bytes 196
  25.0 21.3 %collective-permute-start.15 = (bf16[544,256]{1,0:T(8,128)(2,1)S(1)}, bf16[544,256]{1,0:T(8,128)(2,1)S(1)}, u32[]{:S(2)}, u32[]{:S(2)}) collective-permute-start(bf16[544,256]{1,0:T(8,128)(2,1)S(1)} %get-tuple-element.25), channel_id=1, source_target_pairs={{0,10},{1,11},{2,8},{3,9},{4,14},{5,15},{6,12},{7,13},{8,2},{9,3},... | collective-permute-start | bytes 835592 | tf_op jit(solution)/shard_map/ppermute | solution.py:399
  25.3 21.1 %collective-permute-start.10 = (bf16[256,512]{1,0:T(8,128)(2,1)S(1)}, bf16[256,512]{1,0:T(8,128)(2,1)S(1)}, u32[]{:S(2)}, u32[]{:S(2)}) collective-permute-start(bf16[256,512]{1,0:T(8,128)(2,1)S(1)} %collective-permute-done.5.refs_7_.refs_2_.refs_0_), channel_id=1, source_target_pairs={{0,4},{4,0},{8,12},{12,8},{1,5},{5,1},{9,13},{13,9},{2,6},{6,2},{1... | collective-permute-start | bytes 786440 | tf_op jit(solution)/shard_map/ppermute | solution.py:394
  33.5 13.0 %collective-permute-start.9 = (bf16[256,512]{1,0:T(8,128)(2,1)S(1)}, bf16[256,512]{1,0:T(8,128)(2,1)S(1)}, u32[]{:S(2)}, u32[]{:S(2)}) collective-permute-start(bf16[256,512]{1,0:T(8,128)(2,1)S(1)} %bundle.20), channel_id=1, source_target_pairs={{0,2},{2,0},{1,3},{3,1},{4,6},{6,4},{5,7},{7,5},{8,10},{10,8},{9,1... | collective-permute-start | bytes 786440 | tf_op jit(solution)/shard_map/ppermute | solution.py:394
  33.7 23.0 %collective-permute-start.20 = (bf16[512,512]{1,0:T(8,128)(2,1)S(1)}, bf16[512,512]{1,0:T(8,128)(2,1)S(1)}, u32[]{:S(2)}, u32[]{:S(2)}) collective-permute-start(bf16[512,512]{1,0:T(8,128)(2,1)S(1)} %bundle.27.refs_1_.refs_0_), channel_id=1, source_target_pairs={{0,16},{16,0},{1,17},{17,1},{2,18},{18,2},{3,19},{19,3},{4,20},{20... | collective-permute-start | bytes 1572872 | tf_op jit(solution)/shard_map/ppermute | solution.py:394
  46.3 16.6 %collective-permute-start.16 = (bf16[1088,256]{1,0:T(8,128)(2,1)S(1)}, bf16[1088,256]{1,0:T(8,128)(2,1)S(1)}, u32[]{:S(2)}, u32[]{:S(2)}) collective-permute-start(bf16[1088,256]{1,0:T(8,128)(2,1)S(1)} %bundle.23), channel_id=1, source_target_pairs={{0,4},{1,13},{2,6},{3,15},{4,0},{5,9},{6,2},{7,11},{8,12},{9,5},{1... | collective-permute-start | bytes 1671176 | tf_op jit(solution)/shard_map/ppermute | solution.py:399
  46.5 9.1 %collective-permute-start.11 = (bf16[544,256]{1,0:T(8,128)(2,1)S(1)}, bf16[544,256]{1,0:T(8,128)(2,1)S(1)}, u32[]{:S(2)}, u32[]{:S(2)}) collective-permute-start(bf16[544,256]{1,0:T(8,128)(2,1)S(1)} %after.5), channel_id=1, source_target_pairs={{0,1},{1,0},{2,3},{3,2},{4,5},{5,4},{6,7},{7,6},{8,9},{9,8},{10,11... | collective-permute-start | bytes 835592 | tf_op jit(solution)/shard_map/ppermute | solution.py:394
  53.6 8.3 %collective-permute-start.13 = (bf16[256,512]{1,0:T(8,128)(2,1)S(1)}, bf16[256,512]{1,0:T(8,128)(2,1)S(1)}, u32[]{:S(2)}, u32[]{:S(2)}) collective-permute-start(bf16[256,512]{1,0:T(8,128)(2,1)S(1)} %collective-permute-done.10.refs_3_.refs_0_), channel_id=1, source_target_pairs={{0,2},{2,0},{1,3},{3,1},{4,6},{6,4},{5,7},{7,5},{8,10},{10,8},{9,1... | collective-permute-start | bytes 786440 | tf_op jit(solution)/shard_map/ppermute | solution.py:394
  54.0 13.7 %collective-permute-start.12 = (bf16[512,512]{1,0:T(8,128)(2,1)S(1)}, bf16[512,512]{1,0:T(8,128)(2,1)S(1)}, u32[]{:S(2)}, u32[]{:S(2)}) collective-permute-start(bf16[512,512]{1,0:T(8,128)(2,1)S(1)} %bundle.21.refs_0_.refs_1_), channel_id=1, source_target_pairs={{0,16},{16,0},{1,17},{17,1},{2,18},{18,2},{3,19},{19,3},{4,20},{20... | collective-permute-start | bytes 1572872 | tf_op jit(solution)/shard_map/ppermute | solution.py:394
  56.7 14.8 %collective-permute-start.21 = (bf16[1024,512]{1,0:T(8,128)(2,1)S(1)}, bf16[1024,512]{1,0:T(8,128)(2,1)S(1)}, u32[]{:S(2)}, u32[]{:S(2)}) collective-permute-start(bf16[1024,512]{1,0:T(8,128)(2,1)S(1)} %bundle.28), channel_id=1, source_target_pairs={{0,1},{1,0},{2,3},{3,2},{4,5},{5,4},{6,7},{7,6},{8,9},{9,8},{10,11... | collective-permute-start | bytes 3145736 | tf_op jit(solution)/shard_map/ppermute | solution.py:394
  61.9 5.9 %collective-permute-start.14 = (bf16[544,256]{1,0:T(8,128)(2,1)S(1)}, bf16[544,256]{1,0:T(8,128)(2,1)S(1)}, u32[]{:S(2)}, u32[]{:S(2)}) collective-permute-start(bf16[544,256]{1,0:T(8,128)(2,1)S(1)} %bundle.22), channel_id=1, source_target_pairs={{0,1},{1,0},{2,3},{3,2},{4,5},{5,4},{6,7},{7,6},{8,9},{9,8},{10,11... | collective-permute-start | bytes 835592 | tf_op jit(solution)/shard_map/ppermute | solution.py:394
  63.0 4.9 %collective-permute-start.17 = (bf16[544,256]{1,0:T(8,128)(2,1)S(1)}, bf16[544,256]{1,0:T(8,128)(2,1)S(1)}, u32[]{:S(2)}, u32[]{:S(2)}) collective-permute-start(bf16[544,256]{1,0:T(8,128)(2,1)S(1)} %bundle.24), channel_id=1, source_target_pairs={{0,1},{1,0},{2,3},{3,2},{4,5},{5,4},{6,7},{7,6},{8,9},{9,8},{10,11... | collective-permute-start | bytes 835592 | tf_op jit(solution)/shard_map/ppermute | solution.py:394
  63.1 15.7 %collective-permute-start.22 = (bf16[1088,256]{1,0:T(8,128)(2,1)S(1)}, bf16[1088,256]{1,0:T(8,128)(2,1)S(1)}, u32[]{:S(2)}, u32[]{:S(2)}) collective-permute-start(bf16[1088,256]{1,0:T(8,128)(2,1)S(1)} %bundle.29), channel_id=1, source_target_pairs={{0,6},{1,15},{2,4},{3,13},{4,2},{5,11},{6,0},{7,9},{8,14},{9,7},{1... | collective-permute-start | bytes 1671176 | tf_op jit(solution)/shard_map/ppermute | solution.py:399
  67.7 13.2 %collective-permute-start.24 = (bf16[1024,512]{1,0:T(8,128)(2,1)S(1)}, bf16[1024,512]{1,0:T(8,128)(2,1)S(1)}, u32[]{:S(2)}, u32[]{:S(2)}) collective-permute-start(bf16[1024,512]{1,0:T(8,128)(2,1)S(1)} %bundle.31), channel_id=1, source_target_pairs={{0,1},{1,0},{2,3},{3,2},{4,5},{5,4},{6,7},{7,6},{8,9},{9,8},{10,11... | collective-permute-start | bytes 3145736 | tf_op jit(solution)/shard_map/ppermute | solution.py:394
  69.4 12.8 %collective-permute-start.18 = (bf16[1024,512]{1,0:T(8,128)(2,1)S(1)}, bf16[1024,512]{1,0:T(8,128)(2,1)S(1)}, u32[]{:S(2)}, u32[]{:S(2)}) collective-permute-start(bf16[1024,512]{1,0:T(8,128)(2,1)S(1)} %bundle.25), channel_id=1, source_target_pairs={{0,1},{1,0},{2,3},{3,2},{4,5},{5,4},{6,7},{7,6},{8,9},{9,8},{10,11... | collective-permute-start | bytes 3145736 | tf_op jit(solution)/shard_map/ppermute | solution.py:394
  70.0 8.3 %collective-permute-start.19 = (bf16[256,512]{1,0:T(8,128)(2,1)S(1)}, bf16[256,512]{1,0:T(8,128)(2,1)S(1)}, u32[]{:S(2)}, u32[]{:S(2)}) collective-permute-start(bf16[256,512]{1,0:T(8,128)(2,1)S(1)} %bundle.26.refs_0_.refs_1_), channel_id=1, source_target_pairs={{0,16},{16,0},{1,17},{17,1},{2,18},{18,2},{3,19},{19,3},{4,20},{20... | collective-permute-start | bytes 786440 | tf_op jit(solution)/shard_map/ppermute | solution.py:394
  78.8 3.4 %collective-permute-start.23 = (bf16[512,512]{1,0:T(8,128)(2,1)S(1)}, bf16[512,512]{1,0:T(8,128)(2,1)S(1)}, u32[]{:S(2)}, u32[]{:S(2)}) collective-permute-start(bf16[512,512]{1,0:T(8,128)(2,1)S(1)} %bundle.30), channel_id=1, source_target_pairs={{0,1},{1,0},{2,3},{3,2},{4,5},{5,4},{6,7},{7,6},{8,9},{9,8},{10,11... | collective-permute-start | bytes 1572872 | tf_op jit(solution)/shard_map/ppermute | solution.py:394
  80.3 3.2 %collective-permute-start.25 = (bf16[544,256]{1,0:T(8,128)(2,1)S(1)}, bf16[544,256]{1,0:T(8,128)(2,1)S(1)}, u32[]{:S(2)}, u32[]{:S(2)}) collective-permute-start(bf16[544,256]{1,0:T(8,128)(2,1)S(1)} %bundle.32), channel_id=1, source_target_pairs={{0,1},{1,0},{2,3},{3,2},{4,5},{5,4},{6,7},{7,6},{8,9},{9,8},{10,11... | collective-permute-start | bytes 835592 | tf_op jit(solution)/shard_map/ppermute | solution.py:394
  80.4 3.1 %collective-permute-start.26 = (bf16[272,256]{1,0:T(8,128)(2,1)S(1)}, bf16[272,256]{1,0:T(8,128)(2,1)S(1)}, u32[]{:S(2)}, u32[]{:S(2)}) collective-permute-start(bf16[272,256]{1,0:T(8,128)(2,1)S(1)} %bundle.33), channel_id=1, source_target_pairs={{0,1},{1,0},{2,3},{3,2},{4,5},{5,4},{6,7},{7,6},{8,9},{9,8},{10,11... | collective-permute-start | bytes 417800 | tf_op jit(solution)/shard_map/ppermute | solution.py:394

commit v10 on v9

--- a/solution.py
+++ b/solution.py
@@ -26,25 +26,26 @@
     return (lax.axis_index("line") * 2 + lax.axis_index("plane")) * 2 + lax.axis_index("core")
 
 
-EARLY, LATE = (), (5,)
-ROUNDS = ((1, 4), (3, 7), (2, 6))
-SWAPS = ((0,), (1,), (2,))
-LAST = ("R1", "P5")
+EARLY, LATE = (), (7,)
+ROUNDS = ((1, 4), (5, 2), (3, 6))
+SWAPS = ((0,), (1, 2))
+LAST = ("R2", "R1")
 TIES = {
-    "Y1": ("local",),
-    "Y2": ("B0", "T0", "T2",),
-    "C1": ("X2", "mask",),
-    "C2": ("X3",),
-    "C3": ("AB", "B0", "Y2",),
-    "C4": ("AB", "B1", "R1", "Y2",),
-    "B0": ("CW", "Y1", "Z1", "Z2",),
-    "B1": ("Y2",),
-    "B2": ("B1", "T0",),
-    "F0": ("Y3",),
-    "R2": ("P5",),
-    "T1": ("R0", "Y2", "Z3",),
-    "T2": ("Y1", "Z2",),
-    "mask": ("B0", "T1", "Z2",),
+    "Y1": ("Y0",),
+    "Y2": ("B0",),
+    "X1": ("Z2", "local", "mask",),
+    "X2": ("P7",),
+    "X3": ("R0", "X2",),
+    "X4": ("R1", "X3",),
+    "C4": ("AB", "B1", "R2",),
+    "B0": ("CW", "Y1",),
+    "B1": ("Y3",),
+    "F0": ("R1",),
+    "F1": ("AB", "B2",),
+    "F2": ("AB", "B2",),
+    "R1": ("P7", "R0",),
+    "R2": ("P7",),
+    "T1": ("T0",),
 }
 
 
@@ -413,7 +414,7 @@
     "X4": ("parts", 1, ["Y3"]),
 }
 PLACES = {name: (int(name[1]), int(name[0] == "Y")) for name in ROWS if name[0] in "ZY"}
-STEPS = (("whole", "CW", "S1", "X1"), ("C1", "S2", "X2"), ("C2", "S3", "X3"), ("C3", "S4", "X4", "C4"))
+STEPS = (("whole", "CW", "S1", "X1"), ("C1", "S2", "X2", "S3"), ("C2", "X3", "S4"), ("C3", "X4", "C4"))
 
 
 def body(

time: 85.6 us -> 82.9 us (0.968)
  starting transfers between devices: 34.6 us -> 28.7 us
  waiting for transfers between devices: 35 us -> 38 us
    ppermute x4, starting transfers between devices: 5.15 us -> 1.23 us  [send_pairs(): lax.ppermute(payload, AXES[1:], [(i, target(i)) for i in range(size)])]
    ppermute x23 -> x22, waiting for transfers between devices: 22.6 us -> 24.5 us  [swap(): return lax.ppermute(block, axis, [(i, i ^ bit) for i in range(size)])]
    ppermute x23 -> x22, starting transfers between devices: 29.5 us -> 27.5 us  [swap(): return lax.ppermute(block, axis, [(i, i ^ bit) for i in range(size)])]
    ppermute x4, waiting for transfers between devices: 12.4 us -> 13.5 us  [send_pairs(): lax.ppermute(payload, AXES[1:], [(i, target(i)) for i in range(size)])]
  transfers between devices with their start and end apart: 27 -> 26, of which waited for: 10 -> 13; matrix products, arithmetic and copies ran while one was open for 0% -> 0% of each run, Pallas kernels for 14% -> 14%
where the time goes in v10:
time: 82.9 us; the launch traced here: 82.7 us
  waiting for transfers between devices  38 us (46%)
  starting transfers between devices  28.7 us (35%)
  Pallas kernels  15.1 us (18%)
    ppermute x22, starting transfers between devices, swap(): return lax.ppermute(block, axis, [(i, i ^ bit) for i in range(size)])  27.5 us
    ppermute x22, waiting for transfers between devices, swap(): return lax.ppermute(block, axis, [(i, i ^ bit) for i in range(size)])  24.5 us
    ppermute x4, waiting for transfers between devices, send_pairs(): lax.ppermute(payload, AXES[1:], [(i, target(i)) for i in range(size)])  13.5 us
    pallas_call x4, Pallas kernels, base_product(): pl.pallas_call(kernel, out_shape=pltpu.VMEM((rows, width), jnp.float32),...  5 us
    pallas_call x1, Pallas kernels, make_messages(): pl.pallas_call(kernel, out_shape=[pltpu.VMEM((n * length, HALF), jnp.bflo...  3.62 us
    pallas_call x1, Pallas kernels, adapt_end(): pl.pallas_call(kernel, out_shape=jax.ShapeDtypeStruct((rows, width), jnp....  2.21 us
  transfers between devices with their start and end apart: 26, of which 13 were waited for; matrix products, arithmetic and copies ran while one was open for 0% of the time, Pallas kernels for 14%

profile of v10, /device:TPU:0, one launch (start us, length us, event | category | flops | bytes accessed | tf_op | source)
XLA Modules:
  0.0 82.7 jit_solution(12088493514627195395)
XLA Ops:
  0.0 1.3 %load_rows.1 = (bf16[512,512]{1,0:T(8,128)(2,1)S(1)}, bf16[256,512]{1,0:T(8,128)(2,1)S(1)}) custom-call(bf16[512,512]{1,0:T(8,128)(2,1)} %source.1), custom_call_target="tpu_custom_call" | custom-call | tf_op jit(solution)/shard_map/load_rows/pallas_call | solution.py:166
  1.3 4.1 %collective-permute-start = (bf16[256,512]{1,0:T(8,128)(2,1)S(1)}, bf16[256,512]{1,0:T(8,128)(2,1)S(1)}, u32[]{:S(2)}, u32[]{:S(2)}) collective-permute-start(bf16[256,512]{1,0:T(8,128)(2,1)S(1)} %get-tuple-element.16), channel_id=1, source_target_pairs={{0,8},{4,12},{8,0},{12,4},{1,9},{5,13},{9,1},{13,5},{2,10},{6,14},... | collective-permute-start | bytes 786440 | tf_op jit(solution)/shard_map/ppermute | solution.py:395
  5.4 1.6 %collective-permute-start.3 = (bf16[256,512]{1,0:T(8,128)(2,1)S(1)}, bf16[256,512]{1,0:T(8,128)(2,1)S(1)}, u32[]{:S(2)}, u32[]{:S(2)}) collective-permute-start(bf16[256,512]{1,0:T(8,128)(2,1)S(1)} %get-tuple-element.16), channel_id=1, source_target_pairs={{0,4},{4,0},{8,12},{12,8},{1,5},{5,1},{9,13},{13,9},{2,6},{6,2},{1... | collective-permute-start | bytes 786440 | tf_op jit(solution)/shard_map/ppermute | solution.py:395
  7.0 1.5 %collective-permute-start.4 = (bf16[256,512]{1,0:T(8,128)(2,1)S(1)}, bf16[256,512]{1,0:T(8,128)(2,1)S(1)}, u32[]{:S(2)}, u32[]{:S(2)}) collective-permute-start(bf16[256,512]{1,0:T(8,128)(2,1)S(1)} %get-tuple-element.16), channel_id=1, source_target_pairs={{0,2},{2,0},{1,3},{3,1},{4,6},{6,4},{5,7},{7,5},{8,10},{10,8},{9,1... | collective-permute-start | bytes 786440 | tf_op jit(solution)/shard_map/ppermute | solution.py:395
  8.5 0.7 copy-done.1
  9.2 3.6 %make_messages.1 = (bf16[544,256]{1,0:T(8,128)(2,1)S(1)}, bf16[544,256]{1,0:T(8,128)(2,1)S(1)}, bf16[544,256]{1,0:T(8,128)(2,1)S(1)}, bf16[544,256]{1,0:T(8,128)...) custom-call(s32[2,16]{1,0:T(2,128)S(1)} %bitcast.7, ...), custom_call_target="tpu_custom_call" | custom-call | bytes 4456448 | tf_op jit(solution)/shard_map/make_messages/pallas_call | solution.py:133
  12.8 0.1 collective-permute-start.8
  12.9 0.1 collective-permute-start.10
  13.0 1.1 %row_mask.1.refs_4_.mask_ref = f32[512,128]{1,0:T(8,128)S(1)} custom-call(s32[1,16]{1,0:T(1,128)S(1)} %copy-done.2, s32[16,16]{1,0:T(8,128)S(1)} %copy-done), custom_call_target="tpu_custom_call" | custom-call | tf_op jit(solution)/shard_map/row_mask/pallas_call | solution.py:374
  14.1 4.5 %collective-permute-done.refs_2_.refs_0_ = bf16[256,512]{1,0:T(8,128)(2,1)S(1)} collective-permute-done((bf16[256,512]{1,0:T(8,128)(2,1)S(1)}, bf16[256,512]{1,0:T(8,128)(2,1)S(1)}, u32[]{:S(2)}, u32[]{:S(2)}) %collective-permute-start) | collective-permute-done | bytes 262176 | tf_op jit(solution)/shard_map/ppermute | solution.py:395
  18.6 0.0 collective-permute-start.2
  18.6 0.0 collective-permute-done.3.refs_0_
  18.6 0.0 collective-permute-done.4.refs_1_
  18.6 7.5 %collective-permute-start.5 = (bf16[512,512]{1,0:T(8,128)(2,1)S(1)}, bf16[512,512]{1,0:T(8,128)(2,1)S(1)}, u32[]{:S(2)}, u32[]{:S(2)}) collective-permute-start(bf16[512,512]{1,0:T(8,128)(2,1)S(1)} %bundle.17.refs_2_.refs_0_), channel_id=1, source_target_pairs={{0,16},{16,0},{1,17},{17,1},{2,18},{18,2},{3,19},{19,3},{4,20},{20... | collective-permute-start | bytes 1572872 | tf_op jit(solution)/shard_map/ppermute | solution.py:395
  26.1 1.6 %collective-permute-start.6 = (bf16[256,512]{1,0:T(8,128)(2,1)S(1)}, bf16[256,512]{1,0:T(8,128)(2,1)S(1)}, u32[]{:S(2)}, u32[]{:S(2)}) collective-permute-start(bf16[256,512]{1,0:T(8,128)(2,1)S(1)} %bundle.18), channel_id=1, source_target_pairs={{0,2},{2,0},{1,3},{3,1},{4,6},{6,4},{5,7},{7,5},{8,10},{10,8},{9,1... | collective-permute-start | bytes 786440 | tf_op jit(solution)/shard_map/ppermute | solution.py:395
  27.7 0.0 collective-permute-done.8.refs_1_
  27.7 0.0 collective-permute-start.15
  27.8 0.0 collective-permute-done.10.refs_2_.refs_0_
  27.8 0.6 collective-permute-start.9
  28.4 6.3 %collective-permute-done.6.refs_5_.refs_1_ = bf16[256,512]{1,0:T(8,128)(2,1)S(1)} collective-permute-done((bf16[256,512]{1,0:T(8,128)(2,1)S(1)}, bf16[256,512]{1,0:T(8,128)(2,1)S(1)}, u32[]{:S(2)}, u32[]{:S(2)}) %collective-permute-start.6) | collective-permute-done | bytes 262176 | tf_op jit(solution)/shard_map/ppermute | solution.py:395
  34.7 0.4 collective-permute-start.11
  35.1 0.0 collective-permute-done.2.refs_1_.refs_4_
  35.1 0.0 collective-permute-start.1
  35.1 3.8 %collective-permute-done.5.refs_3_.refs_1_ = bf16[512,512]{1,0:T(8,128)(2,1)S(1)} collective-permute-done((bf16[512,512]{1,0:T(8,128)(2,1)S(1)}, bf16[512,512]{1,0:T(8,128)(2,1)S(1)}, u32[]{:S(2)}, u32[]{:S(2)}) %collective-permute-start.5) | collective-permute-done | bytes 524320 | tf_op jit(solution)/shard_map/ppermute | solution.py:395
  38.9 1.2 %base_product.4.refs_1_.refs_4_ = f32[512,512]{1,0:T(8,128)S(1)} custom-call(bf16[512,8192]{1,0:T(8,128)(2,1)S(1)} %bitcast.6, bf16[512,512]{1,0:T(8,128)(2,1)S(1)} %get-tuple-element.17.refs_0_, bf16[512,512]{1,0:T(8,128)(2,1)S(1)} %collective-permute-done.2.refs_1_.refs_4_, bf16[512,512]{1,0:T(8,128)(2,1)S(1)} %bundle.17.refs_2_.refs_0_, ...), custom_call_target="tpu_custom_call" | custom-call | flops 1073741824 | bytes 5242880 | tf_op jit(solution)/shard_map/base_product/pallas_call | solution.py:211
  40.2 2.0 %collective-permute-start.7 = (bf16[256,512]{1,0:T(8,128)(2,1)S(1)}, bf16[256,512]{1,0:T(8,128)(2,1)S(1)}, u32[]{:S(2)}, u32[]{:S(2)}) collective-permute-start(bf16[256,512]{1,0:T(8,128)(2,1)S(1)} %bundle.19), channel_id=1, source_target_pairs={{0,2},{2,0},{1,3},{3,1},{4,6},{6,4},{5,7},{7,5},{8,10},{10,8},{9,1... | collective-permute-start | bytes 786440 | tf_op jit(solution)/shard_map/ppermute | solution.py:395
  42.2 0.1 bundle.28
  42.3 0.0 collective-permute-done.9.refs_2_.refs_3_.refs_0_.refs_1_.refs_4_
  42.3 2.5 %collective-permute-start.20 = (bf16[1024,512]{1,0:T(8,128)(2,1)S(1)}, bf16[1024,512]{1,0:T(8,128)(2,1)S(1)}, u32[]{:S(2)}, u32[]{:S(2)}) collective-permute-start(bf16[1024,512]{1,0:T(8,128)(2,1)S(1)} %bundle.28), channel_id=1, source_target_pairs={{0,1},{1,0},{2,3},{3,2},{4,5},{5,4},{6,7},{7,6},{8,9},{9,8},{10,11... | collective-permute-start | bytes 3145736 | tf_op jit(solution)/shard_map/ppermute | solution.py:395
  44.8 0.0 collective-permute-done.15.refs_1_
  44.9 0.6 collective-permute-start.16
  45.5 4.1 %collective-permute-done.1.refs_0_ = bf16[256,512]{1,0:T(8,128)(2,1)S(1)} collective-permute-done((bf16[256,512]{1,0:T(8,128)(2,1)S(1)}, bf16[256,512]{1,0:T(8,128)(2,1)S(1)}, u32[]{:S(2)}, u32[]{:S(2)}) %collective-permute-start.1) | collective-permute-done | bytes 262176 | tf_op jit(solution)/shard_map/ppermute | solution.py:395
  49.6 0.0 collective-permute-done.7.refs_1_
  49.6 0.4 collective-permute-done.11.refs_3_.refs_2_.refs_1_
  50.0 1.8 %collective-permute-start.12 = (bf16[512,512]{1,0:T(8,128)(2,1)S(1)}, bf16[512,512]{1,0:T(8,128)(2,1)S(1)}, u32[]{:S(2)}, u32[]{:S(2)}) collective-permute-start(bf16[512,512]{1,0:T(8,128)(2,1)S(1)} %bundle.22.refs_0_.refs_3_), channel_id=1, source_target_pairs={{0,16},{16,0},{1,17},{17,1},{2,18},{18,2},{3,19},{19,3},{4,20},{20... | collective-permute-start | bytes 1572872 | tf_op jit(solution)/shard_map/ppermute | solution.py:395
  51.8 0.1 collective-permute-start.18
  51.9 0.1 bundle.31
  52.0 0.6 collective-permute-start.23
  52.5 0.7 collective-permute-done.18.refs_3_
  53.2 1.5 %collective-permute-start.14 = (bf16[256,512]{1,0:T(8,128)(2,1)S(1)}, bf16[256,512]{1,0:T(8,128)(2,1)S(1)}, u32[]{:S(2)}, u32[]{:S(2)}) collective-permute-start(bf16[256,512]{1,0:T(8,128)(2,1)S(1)} %collective-permute-done.1.refs_0_), channel_id=1, source_target_pairs={{0,2},{2,0},{1,3},{3,1},{4,6},{6,4},{5,7},{7,5},{8,10},{10,8},{9,1... | collective-permute-start | bytes 786440 | tf_op jit(solution)/shard_map/ppermute | solution.py:395
  54.8 6.1 %collective-permute-done.16.refs_1_.refs_2_.refs_0_ = bf16[1088,256]{1,0:T(8,128)(2,1)S(1)} collective-permute-done((bf16[1088,256]{1,0:T(8,128)(2,1)S(1)}, bf16[1088,256]{1,0:T(8,128)(2,1)S(1)}, u32[]{:S(2)}, u32[]{:S(2)}) %collective-permute-start.16) | collective-permute-done | bytes 557088 | tf_op jit(solution)/shard_map/ppermute | solution.py:400
  60.9 0.0 collective-permute-start.21
  61.0 2.9 %collective-permute-done.12.refs_1_.refs_2_ = bf16[512,512]{1,0:T(8,128)(2,1)S(1)} collective-permute-done((bf16[512,512]{1,0:T(8,128)(2,1)S(1)}, bf16[512,512]{1,0:T(8,128)(2,1)S(1)}, u32[]{:S(2)}, u32[]{:S(2)}) %collective-permute-start.12) | collective-permute-done | bytes 524320 | tf_op jit(solution)/shard_map/ppermute | solution.py:395
  63.8 0.0 collective-permute-start.19
  63.8 0.1 bundle.23
  63.9 0.8 %collective-permute-done.14.refs_0_.refs_5_ = bf16[256,512]{1,0:T(8,128)(2,1)S(1)} collective-permute-done((bf16[256,512]{1,0:T(8,128)(2,1)S(1)}, bf16[256,512]{1,0:T(8,128)(2,1)S(1)}, u32[]{:S(2)}, u32[]{:S(2)}) %collective-permute-start.14) | collective-permute-done | bytes 262176 | tf_op jit(solution)/shard_map/ppermute | solution.py:395
  64.7 0.0 collective-permute-start.13
  64.8 0.6 collective-permute-done.19.refs_5_
  65.4 1.5 %collective-permute-start.17 = (bf16[256,512]{1,0:T(8,128)(2,1)S(1)}, bf16[256,512]{1,0:T(8,128)(2,1)S(1)}, u32[]{:S(2)}, u32[]{:S(2)}) collective-permute-start(bf16[256,512]{1,0:T(8,128)(2,1)S(1)} %bundle.25.refs_0_.refs_2_), channel_id=1, source_target_pairs={{0,16},{16,0},{1,17},{17,1},{2,18},{18,2},{3,19},{19,3},{4,20},{20... | collective-permute-start | bytes 786440 | tf_op jit(solution)/shard_map/ppermute | solution.py:395
  66.9 1.3 %adapt_begin.1 = (f32[512,128]{1,0:T(8,128)S(1)}, bf16[512,128]{1,0:T(8,128)(2,1)S(1)}) custom-call(bf16[512,8192]{1,0:T(8,128)(2,1)S(1)} %bitcast.6, bf16[272,256]{1,0:T(8,128)(2,1)S(1)} %get-tuple-element.18.refs_3_.refs_0_, bf16[1360,256]{1,0:T(8,128)(2,1)S(1)} %collective-permute-done.15.refs_1_, ...), custom_call_target="tpu_custom_call" | custom-call | flops 1288490240 | bytes 5033164 | tf_op jit(solution)/shard_map/adapt_begin/pallas_call | solution.py:273
  68.2 0.0 collective-permute-done.20.refs_0_
  68.2 1.5 %base_product.5.refs_3_ = f32[512,512]{1,0:T(8,128)S(1)} custom-call(bf16[512,8192]{1,0:T(8,128)(2,1)S(1)} %bitcast.6, bf16[1024,512]{1,0:T(8,128)(2,1)S(1)} %collective-permute-done.20.refs_0_, bf16[512,512]{1,0:T(8,128)(2,1)S(1)} %bundle.21.refs_1_.refs_0_, bf16[512,512]{1,0:T(8,128)(2,1)S(1)} %collective-permute-done.11.refs_3_.refs_2_.refs_1_, ...), custom_call_target="tpu_custom_call" | custom-call | flops 1342177280 | bytes 6291456 | tf_op jit(solution)/shard_map/base_product/pallas_call | solution.py:211
  69.7 7.3 %collective-permute-done.21.refs_4_.refs_0_.refs_1_ = bf16[1088,256]{1,0:T(8,128)(2,1)S(1)} collective-permute-done((bf16[1088,256]{1,0:T(8,128)(2,1)S(1)}, bf16[1088,256]{1,0:T(8,128)(2,1)S(1)}, u32[]{:S(2)}, u32[]{:S(2)}) %collective-permute-start.21) | collective-permute-done | bytes 557088 | tf_op jit(solution)/shard_map/ppermute | solution.py:400
  77.0 0.0 collective-permute-done.17.refs_1_
  77.1 0.1 collective-permute-start.22
  77.2 0.0 collective-permute-done.23.refs_0_
  77.2 1.1 %base_product.6.refs_3_ = f32[512,512]{1,0:T(8,128)S(1)} custom-call(bf16[512,8192]{1,0:T(8,128)(2,1)S(1)} %bitcast.6, bf16[1024,512]{1,0:T(8,128)(2,1)S(1)} %collective-permute-done.23.refs_0_, bf16[512,512]{1,0:T(8,128)(2,1)S(1)} %collective-permute-done.12.refs_1_.refs_2_, bf16[256,512]{1,0:T(8,128)(2,1)S(1)} %bundle.25.refs_0_.refs_2_, ...), custom_call_target="tpu_custom_call" | custom-call | flops 939524096 | bytes 4718592 | tf_op jit(solution)/shard_map/base_product/pallas_call | solution.py:211
  78.3 0.6 collective-permute-start.25
  78.9 0.1 collective-permute-start.24
  79.0 0.1 collective-permute-done.22.refs_2_
  79.1 0.0 collective-permute-done.13.refs_0_
  79.1 1.1 %base_product.7.base_ref = f32[512,512]{1,0:T(8,128)S(1)} custom-call(bf16[512,8192]{1,0:T(8,128)(2,1)S(1)} %bitcast.6, bf16[1024,512]{1,0:T(8,128)(2,1)S(1)} %collective-permute-done.13.refs_0_, bf16[256,512]{1,0:T(8,128)(2,1)S(1)} %collective-permute-done.17.refs_1_, bf16[512,512]{1,0:T(8,128)(2,1)S(1)} %collective-permute-done.22.refs_2_, ...), custom_call_target="tpu_custom_call" | custom-call | flops 939524096 | bytes 4718592 | tf_op jit(solution)/shard_map/base_product/pallas_call | solution.py:211
  80.2 0.3 collective-permute-done.24.refs_1_
  80.5 2.2 %adapt_end.1 = bf16[512,512]{1,0:T(8,128)(2,1)} custom-call(bf16[512,8192]{1,0:T(8,128)(2,1)S(1)} %bitcast.6, f32[512,128]{1,0:T(8,128)S(1)} %row_mask.1.refs_4_.mask_ref, f32[512,512]{1,0:T(8,128)S(1)} %base_product.7.base_ref, f32[512,128]{1,0:T(8,128)S(1)} %get-tuple-element.24.refs_2_.shrunk, bf16[512,128]{1,0:T(8,128)(2,1)S(1)} %get-tuple-element.26.widened, ...), custom_call_target="tpu_custom_call" | custom-call | flops 858993472 | bytes 3355443 | tf_op jit(solution)/shard_map/adapt_end/pallas_call | solution.py:305
  (27 shorter events, 0.4 us)
Async XLA Ops:
  0.0 13.0 %copy-start = (s32[16,16]{1,0:T(8,128)S(1)}, s32[16,16]{1,0:T(8,128)}, u32[]{:S(2)}) copy-start(s32[16,16]{1,0:T(8,128)} %slots_ref.1) | copy-start | bytes 3076
  0.0 38.9 %slice-start = ((s8[8388608]{0:T(1024)(128)(4,1)}), s8[4194304]{0:T(1024)(128)(4,1)S(1)}, s32[]{:S(2)}) async-start(s8[8388608]{0:T(1024)(128)(4,1)} %bitcast.5), calls=%async_computation | async-start | bytes 8388608
  1.3 17.3 %collective-permute-start = (bf16[256,512]{1,0:T(8,128)(2,1)S(1)}, bf16[256,512]{1,0:T(8,128)(2,1)S(1)}, u32[]{:S(2)}, u32[]{:S(2)}) collective-permute-start(bf16[256,512]{1,0:T(8,128)(2,1)S(1)} %get-tuple-element.16), channel_id=1, source_target_pairs={{0,8},{4,12},{8,0},{12,4},{1,9},{5,13},{9,1},{13,5},{2,10},{6,14},... | collective-permute-start | bytes 786440 | tf_op jit(solution)/shard_map/ppermute | solution.py:395
  5.4 13.2 %collective-permute-start.3 = (bf16[256,512]{1,0:T(8,128)(2,1)S(1)}, bf16[256,512]{1,0:T(8,128)(2,1)S(1)}, u32[]{:S(2)}, u32[]{:S(2)}) collective-permute-start(bf16[256,512]{1,0:T(8,128)(2,1)S(1)} %get-tuple-element.16), channel_id=1, source_target_pairs={{0,4},{4,0},{8,12},{12,8},{1,5},{5,1},{9,13},{13,9},{2,6},{6,2},{1... | collective-permute-start | bytes 786440 | tf_op jit(solution)/shard_map/ppermute | solution.py:395
  7.0 11.6 %collective-permute-start.4 = (bf16[256,512]{1,0:T(8,128)(2,1)S(1)}, bf16[256,512]{1,0:T(8,128)(2,1)S(1)}, u32[]{:S(2)}, u32[]{:S(2)}) collective-permute-start(bf16[256,512]{1,0:T(8,128)(2,1)S(1)} %get-tuple-element.16), channel_id=1, source_target_pairs={{0,2},{2,0},{1,3},{3,1},{4,6},{6,4},{5,7},{7,5},{8,10},{10,8},{9,1... | collective-permute-start | bytes 786440 | tf_op jit(solution)/shard_map/ppermute | solution.py:395
  8.5 0.7 copy-start.1
  9.2 3.8 %copy-start.2 = (s32[1,16]{1,0:T(1,128)S(1)}, s32[1,16]{1,0:T(1,128)}, u32[]{:S(2)}) copy-start(s32[1,16]{1,0:T(1,128)} %lengths_ref.1) | copy-start | bytes 196
  9.2 29.7 %slice-start.1 = ((s8[8388608]{0:T(1024)(128)(4,1)}), s8[4194304]{0:T(1024)(128)(4,1)S(1)}, s32[]{:S(2)}) async-start(s8[8388608]{0:T(1024)(128)(4,1)} %bitcast.5), calls=%async_computation.1 | async-start | bytes 8388608
  12.8 14.9 %collective-permute-start.8 = (bf16[544,256]{1,0:T(8,128)(2,1)S(1)}, bf16[544,256]{1,0:T(8,128)(2,1)S(1)}, u32[]{:S(2)}, u32[]{:S(2)}) collective-permute-start(bf16[544,256]{1,0:T(8,128)(2,1)S(1)} %after.2), channel_id=1, source_target_pairs={{0,1},{1,0},{2,3},{3,2},{4,5},{5,4},{6,7},{7,6},{8,9},{9,8},{10,11... | collective-permute-start | bytes 835592 | tf_op jit(solution)/shard_map/ppermute | solution.py:395
  12.9 14.9 %collective-permute-start.10 = (bf16[544,256]{1,0:T(8,128)(2,1)S(1)}, bf16[544,256]{1,0:T(8,128)(2,1)S(1)}, u32[]{:S(2)}, u32[]{:S(2)}) collective-permute-start(bf16[544,256]{1,0:T(8,128)(2,1)S(1)} %get-tuple-element.21), channel_id=1, source_target_pairs={{0,14},{1,15},{2,12},{3,13},{4,10},{5,11},{6,8},{7,9},{8,6},{9,7},... | collective-permute-start | bytes 835592 | tf_op jit(solution)/shard_map/ppermute | solution.py:400
  18.6 16.5 %collective-permute-start.2 = (bf16[512,512]{1,0:T(8,128)(2,1)S(1)}, bf16[512,512]{1,0:T(8,128)(2,1)S(1)}, u32[]{:S(2)}, u32[]{:S(2)}) collective-permute-start(bf16[512,512]{1,0:T(8,128)(2,1)S(1)} %get-tuple-element.17.refs_0_), channel_id=1, source_target_pairs={{0,1},{1,0},{2,3},{3,2},{4,5},{5,4},{6,7},{7,6},{8,9},{9,8},{10,11... | collective-permute-start | bytes 1572872 | tf_op jit(solution)/shard_map/ppermute | solution.py:395
  18.6 20.3 %collective-permute-start.5 = (bf16[512,512]{1,0:T(8,128)(2,1)S(1)}, bf16[512,512]{1,0:T(8,128)(2,1)S(1)}, u32[]{:S(2)}, u32[]{:S(2)}) collective-permute-start(bf16[512,512]{1,0:T(8,128)(2,1)S(1)} %bundle.17.refs_2_.refs_0_), channel_id=1, source_target_pairs={{0,16},{16,0},{1,17},{17,1},{2,18},{18,2},{3,19},{19,3},{4,20},{20... | collective-permute-start | bytes 1572872 | tf_op jit(solution)/shard_map/ppermute | solution.py:395
  26.1 8.5 %collective-permute-start.6 = (bf16[256,512]{1,0:T(8,128)(2,1)S(1)}, bf16[256,512]{1,0:T(8,128)(2,1)S(1)}, u32[]{:S(2)}, u32[]{:S(2)}) collective-permute-start(bf16[256,512]{1,0:T(8,128)(2,1)S(1)} %bundle.18), channel_id=1, source_target_pairs={{0,2},{2,0},{1,3},{3,1},{4,6},{6,4},{5,7},{7,5},{8,10},{10,8},{9,1... | collective-permute-start | bytes 786440 | tf_op jit(solution)/shard_map/ppermute | solution.py:395
  27.7 17.1 %collective-permute-start.15 = (bf16[1360,256]{1,0:T(8,128)(2,1)S(1)}, bf16[1360,256]{1,0:T(8,128)(2,1)S(1)}, u32[]{:S(2)}, u32[]{:S(2)}) collective-permute-start(bf16[1360,256]{1,0:T(8,128)(2,1)S(1)} %after.3), channel_id=1, source_target_pairs={{0,1},{1,0},{2,3},{3,2},{4,5},{5,4},{6,7},{7,6},{8,9},{9,8},{10,11... | collective-permute-start | bytes 2088968 | tf_op jit(solution)/shard_map/ppermute | solution.py:395
  27.8 14.5 %collective-permute-start.9 = (bf16[1088,256]{1,0:T(8,128)(2,1)S(1)}, bf16[1088,256]{1,0:T(8,128)(2,1)S(1)}, u32[]{:S(2)}, u32[]{:S(2)}) collective-permute-start(bf16[1088,256]{1,0:T(8,128)(2,1)S(1)} %bundle.20), channel_id=1, source_target_pairs={{0,2},{1,9},{2,0},{3,11},{4,6},{5,13},{6,4},{7,15},{8,10},{9,1},{1... | collective-permute-start | bytes 1671176 | tf_op jit(solution)/shard_map/ppermute | solution.py:400
  34.7 15.3 %collective-permute-start.11 = (bf16[512,512]{1,0:T(8,128)(2,1)S(1)}, bf16[512,512]{1,0:T(8,128)(2,1)S(1)}, u32[]{:S(2)}, u32[]{:S(2)}) collective-permute-start(bf16[512,512]{1,0:T(8,128)(2,1)S(1)} %bundle.21.refs_1_.refs_0_), channel_id=1, source_target_pairs={{0,16},{16,0},{1,17},{17,1},{2,18},{18,2},{3,19},{19,3},{4,20},{20... | collective-permute-start | bytes 1572872 | tf_op jit(solution)/shard_map/ppermute | solution.py:395
  35.1 14.5 %collective-permute-start.1 = (bf16[256,512]{1,0:T(8,128)(2,1)S(1)}, bf16[256,512]{1,0:T(8,128)(2,1)S(1)}, u32[]{:S(2)}, u32[]{:S(2)}) collective-permute-start(bf16[256,512]{1,0:T(8,128)(2,1)S(1)} %collective-permute-done.refs_2_.refs_0_), channel_id=1, source_target_pairs={{0,4},{4,0},{8,12},{12,8},{1,5},{5,1},{9,13},{13,9},{2,6},{6,2},{1... | collective-permute-start | bytes 786440 | tf_op jit(solution)/shard_map/ppermute | solution.py:395
  40.2 9.4 %collective-permute-start.7 = (bf16[256,512]{1,0:T(8,128)(2,1)S(1)}, bf16[256,512]{1,0:T(8,128)(2,1)S(1)}, u32[]{:S(2)}, u32[]{:S(2)}) collective-permute-start(bf16[256,512]{1,0:T(8,128)(2,1)S(1)} %bundle.19), channel_id=1, source_target_pairs={{0,2},{2,0},{1,3},{3,1},{4,6},{6,4},{5,7},{7,5},{8,10},{10,8},{9,1... | collective-permute-start | bytes 786440 | tf_op jit(solution)/shard_map/ppermute | solution.py:395
  42.3 25.9 %collective-permute-start.20 = (bf16[1024,512]{1,0:T(8,128)(2,1)S(1)}, bf16[1024,512]{1,0:T(8,128)(2,1)S(1)}, u32[]{:S(2)}, u32[]{:S(2)}) collective-permute-start(bf16[1024,512]{1,0:T(8,128)(2,1)S(1)} %bundle.28), channel_id=1, source_target_pairs={{0,1},{1,0},{2,3},{3,2},{4,5},{5,4},{6,7},{7,6},{8,9},{9,8},{10,11... | collective-permute-start | bytes 3145736 | tf_op jit(solution)/shard_map/ppermute | solution.py:395
  44.9 16.0 %collective-permute-start.16 = (bf16[1088,256]{1,0:T(8,128)(2,1)S(1)}, bf16[1088,256]{1,0:T(8,128)(2,1)S(1)}, u32[]{:S(2)}, u32[]{:S(2)}) collective-permute-start(bf16[1088,256]{1,0:T(8,128)(2,1)S(1)} %bundle.24), channel_id=1, source_target_pairs={{0,10},{1,5},{2,8},{3,7},{4,14},{5,1},{6,12},{7,3},{8,2},{9,13},{1... | collective-permute-start | bytes 1671176 | tf_op jit(solution)/shard_map/ppermute | solution.py:400
  50.0 13.8 %collective-permute-start.12 = (bf16[512,512]{1,0:T(8,128)(2,1)S(1)}, bf16[512,512]{1,0:T(8,128)(2,1)S(1)}, u32[]{:S(2)}, u32[]{:S(2)}) collective-permute-start(bf16[512,512]{1,0:T(8,128)(2,1)S(1)} %bundle.22.refs_0_.refs_3_), channel_id=1, source_target_pairs={{0,16},{16,0},{1,17},{17,1},{2,18},{18,2},{3,19},{19,3},{4,20},{20... | collective-permute-start | bytes 1572872 | tf_op jit(solution)/shard_map/ppermute | solution.py:395
  51.8 1.4 %collective-permute-start.18 = (bf16[272,256]{1,0:T(8,128)(2,1)S(1)}, bf16[272,256]{1,0:T(8,128)(2,1)S(1)}, u32[]{:S(2)}, u32[]{:S(2)}) collective-permute-start(bf16[272,256]{1,0:T(8,128)(2,1)S(1)} %bundle.26), channel_id=1, source_target_pairs={{0,1},{1,0},{2,3},{3,2},{4,5},{5,4},{6,7},{7,6},{8,9},{9,8},{10,11... | collective-permute-start | bytes 417800 | tf_op jit(solution)/shard_map/ppermute | solution.py:395
  52.0 25.2 %collective-permute-start.23 = (bf16[1024,512]{1,0:T(8,128)(2,1)S(1)}, bf16[1024,512]{1,0:T(8,128)(2,1)S(1)}, u32[]{:S(2)}, u32[]{:S(2)}) collective-permute-start(bf16[1024,512]{1,0:T(8,128)(2,1)S(1)} %bundle.31), channel_id=1, source_target_pairs={{0,1},{1,0},{2,3},{3,2},{4,5},{5,4},{6,7},{7,6},{8,9},{9,8},{10,11... | collective-permute-start | bytes 3145736 | tf_op jit(solution)/shard_map/ppermute | solution.py:395
  53.2 11.5 %collective-permute-start.14 = (bf16[256,512]{1,0:T(8,128)(2,1)S(1)}, bf16[256,512]{1,0:T(8,128)(2,1)S(1)}, u32[]{:S(2)}, u32[]{:S(2)}) collective-permute-start(bf16[256,512]{1,0:T(8,128)(2,1)S(1)} %collective-permute-done.1.refs_0_), channel_id=1, source_target_pairs={{0,2},{2,0},{1,3},{3,1},{4,6},{6,4},{5,7},{7,5},{8,10},{10,8},{9,1... | collective-permute-start | bytes 786440 | tf_op jit(solution)/shard_map/ppermute | solution.py:395
  60.9 16.1 %collective-permute-start.21 = (bf16[1088,256]{1,0:T(8,128)(2,1)S(1)}, bf16[1088,256]{1,0:T(8,128)(2,1)S(1)}, u32[]{:S(2)}, u32[]{:S(2)}) collective-permute-start(bf16[1088,256]{1,0:T(8,128)(2,1)S(1)} %bundle.29), channel_id=1, source_target_pairs={{0,6},{1,13},{2,4},{3,15},{4,2},{5,9},{6,0},{7,11},{8,14},{9,5},{1... | collective-permute-start | bytes 1671176 | tf_op jit(solution)/shard_map/ppermute | solution.py:400
  63.8 1.6 %collective-permute-start.19 = (bf16[544,256]{1,0:T(8,128)(2,1)S(1)}, bf16[544,256]{1,0:T(8,128)(2,1)S(1)}, u32[]{:S(2)}, u32[]{:S(2)}) collective-permute-start(bf16[544,256]{1,0:T(8,128)(2,1)S(1)} %bundle.27), channel_id=1, source_target_pairs={{0,1},{1,0},{2,3},{3,2},{4,5},{5,4},{6,7},{7,6},{8,9},{9,8},{10,11... | collective-permute-start | bytes 835592 | tf_op jit(solution)/shard_map/ppermute | solution.py:395
  64.7 14.3 %collective-permute-start.13 = (bf16[1024,512]{1,0:T(8,128)(2,1)S(1)}, bf16[1024,512]{1,0:T(8,128)(2,1)S(1)}, u32[]{:S(2)}, u32[]{:S(2)}) collective-permute-start(bf16[1024,512]{1,0:T(8,128)(2,1)S(1)} %bundle.23), channel_id=1, source_target_pairs={{0,1},{1,0},{2,3},{3,2},{4,5},{5,4},{6,7},{7,6},{8,9},{9,8},{10,11... | collective-permute-start | bytes 3145736 | tf_op jit(solution)/shard_map/ppermute | solution.py:395
  65.4 11.7 %collective-permute-start.17 = (bf16[256,512]{1,0:T(8,128)(2,1)S(1)}, bf16[256,512]{1,0:T(8,128)(2,1)S(1)}, u32[]{:S(2)}, u32[]{:S(2)}) collective-permute-start(bf16[256,512]{1,0:T(8,128)(2,1)S(1)} %bundle.25.refs_0_.refs_2_), channel_id=1, source_target_pairs={{0,16},{16,0},{1,17},{17,1},{2,18},{18,2},{3,19},{19,3},{4,20},{20... | collective-permute-start | bytes 786440 | tf_op jit(solution)/shard_map/ppermute | solution.py:395
  77.1 2.0 %collective-permute-start.22 = (bf16[512,512]{1,0:T(8,128)(2,1)S(1)}, bf16[512,512]{1,0:T(8,128)(2,1)S(1)}, u32[]{:S(2)}, u32[]{:S(2)}) collective-permute-start(bf16[512,512]{1,0:T(8,128)(2,1)S(1)} %bundle.30), channel_id=1, source_target_pairs={{0,1},{1,0},{2,3},{3,2},{4,5},{5,4},{6,7},{7,6},{8,9},{9,8},{10,11... | collective-permute-start | bytes 1572872 | tf_op jit(solution)/shard_map/ppermute | solution.py:395
  78.3 1.9 %collective-permute-start.25 = (bf16[544,256]{1,0:T(8,128)(2,1)S(1)}, bf16[544,256]{1,0:T(8,128)(2,1)S(1)}, u32[]{:S(2)}, u32[]{:S(2)}) collective-permute-start(bf16[544,256]{1,0:T(8,128)(2,1)S(1)} %bundle.33), channel_id=1, source_target_pairs={{0,1},{1,0},{2,3},{3,2},{4,5},{5,4},{6,7},{7,6},{8,9},{9,8},{10,11... | collective-permute-start | bytes 835592 | tf_op jit(solution)/shard_map/ppermute | solution.py:395
  78.9 1.6 %collective-permute-start.24 = (bf16[544,256]{1,0:T(8,128)(2,1)S(1)}, bf16[544,256]{1,0:T(8,128)(2,1)S(1)}, u32[]{:S(2)}, u32[]{:S(2)}) collective-permute-start(bf16[544,256]{1,0:T(8,128)(2,1)S(1)} %bundle.32), channel_id=1, source_target_pairs={{0,1},{1,0},{2,3},{3,2},{4,5},{5,4},{6,7},{7,6},{8,9},{9,8},{10,11... | collective-permute-start | bytes 835592 | tf_op jit(solution)/shard_map/ppermute | solution.py:395

commit v11 on v10

--- a/solution.py
+++ b/solution.py
@@ -26,25 +26,24 @@
     return (lax.axis_index("line") * 2 + lax.axis_index("plane")) * 2 + lax.axis_index("core")
 
 
-EARLY, LATE = (), (7,)
-ROUNDS = ((1, 4), (5, 2), (3, 6))
+EARLY, LATE = (), (4,)
+ROUNDS = ((6, 1), (2, 7), (5, 3))
 SWAPS = ((0,), (1, 2))
 LAST = ("R2", "R1")
 TIES = {
     "Y1": ("Y0",),
     "Y2": ("B0",),
     "X1": ("Z2", "local", "mask",),
-    "X2": ("P7",),
+    "X2": ("P4",),
     "X3": ("R0", "X2",),
     "X4": ("R1", "X3",),
     "C4": ("AB", "B1", "R2",),
-    "B0": ("CW", "Y1",),
     "B1": ("Y3",),
     "F0": ("R1",),
     "F1": ("AB", "B2",),
     "F2": ("AB", "B2",),
-    "R1": ("P7", "R0",),
-    "R2": ("P7",),
+    "R1": ("P4", "R0",),
+    "R2": ("P4",),
     "T1": ("T0",),
 }
 
@@ -414,7 +413,7 @@
     "X4": ("parts", 1, ["Y3"]),
 }
 PLACES = {name: (int(name[1]), int(name[0] == "Y")) for name in ROWS if name[0] in "ZY"}
-STEPS = (("whole", "CW", "S1", "X1"), ("C1", "S2", "X2", "S3"), ("C2", "X3", "S4"), ("C3", "X4", "C4"))
+STEPS = (("whole", "CW", "S1", "X1"), ("C1", "S2", "X2", "S3"), ("C2", "X3"), ("C3", "S4", "X4", "C4"))
 
 
 def body(

time: 82.9 us -> 89.4 us (1.078)
  starting transfers between devices: 28.7 us -> 40.1 us
  waiting for transfers between devices: 38 us -> 33.1 us
    ppermute x4, starting transfers between devices: 1.23 us -> 10.9 us  [send_pairs(): lax.ppermute(payload, AXES[1:], [(i, target(i)) for i in range(size)])]
    ppermute x4, waiting for transfers between devices: 13.5 us -> 5.93 us  [send_pairs(): lax.ppermute(payload, AXES[1:], [(i, target(i)) for i in range(size)])]
    ppermute x22, waiting for transfers between devices: 24.5 us -> 27.1 us  [swap(): return lax.ppermute(block, axis, [(i, i ^ bit) for i in range(size)])]
    ppermute x22, starting transfers between devices: 27.5 us -> 29.1 us  [swap(): return lax.ppermute(block, axis, [(i, i ^ bit) for i in range(size)])]
  transfers between devices with their start and end apart: 26 -> 26, of which waited for: 13 -> 13; matrix products, arithmetic and copies ran while one was open for 0% -> 0% of each run, Pallas kernels for 14% -> 13%
where the time goes in v11:
time: 89.4 us; the launch traced here: 89.2 us
  starting transfers between devices  40.1 us (45%)
  waiting for transfers between devices  33.1 us (37%)
  Pallas kernels  15.1 us (17%)
    ppermute x22, starting transfers between devices, swap(): return lax.ppermute(block, axis, [(i, i ^ bit) for i in range(size)])  29.1 us
    ppermute x22, waiting for transfers between devices, swap(): return lax.ppermute(block, axis, [(i, i ^ bit) for i in range(size)])  27.1 us
    ppermute x4, starting transfers between devices, send_pairs(): lax.ppermute(payload, AXES[1:], [(i, target(i)) for i in range(size)])  10.9 us
    ppermute x4, waiting for transfers between devices, send_pairs(): lax.ppermute(payload, AXES[1:], [(i, target(i)) for i in range(size)])  5.93 us
    pallas_call x4, Pallas kernels, base_product(): pl.pallas_call(kernel, out_shape=pltpu.VMEM((rows, width), jnp.float32),...  5 us
    pallas_call x1, Pallas kernels, make_messages(): pl.pallas_call(kernel, out_shape=[pltpu.VMEM((n * length, HALF), jnp.bflo...  3.62 us
    pallas_call x1, Pallas kernels, adapt_end(): pl.pallas_call(kernel, out_shape=jax.ShapeDtypeStruct((rows, width), jnp....  2.21 us
  transfers between devices with their start and end apart: 26, of which 13 were waited for; matrix products, arithmetic and copies ran while one was open for 0% of the time, Pallas kernels for 13%

profile of v11, /device:TPU:0, one launch (start us, length us, event | category | flops | bytes accessed | tf_op | source)
XLA Modules:
  0.0 89.2 jit_solution(16325710017362511536)
XLA Ops:
  0.0 1.3 %load_rows.1 = (bf16[512,512]{1,0:T(8,128)(2,1)S(1)}, bf16[256,512]{1,0:T(8,128)(2,1)S(1)}) custom-call(bf16[512,512]{1,0:T(8,128)(2,1)} %source.1), custom_call_target="tpu_custom_call" | custom-call | tf_op jit(solution)/shard_map/load_rows/pallas_call | solution.py:165
  1.3 4.1 %collective-permute-start = (bf16[256,512]{1,0:T(8,128)(2,1)S(1)}, bf16[256,512]{1,0:T(8,128)(2,1)S(1)}, u32[]{:S(2)}, u32[]{:S(2)}) collective-permute-start(bf16[256,512]{1,0:T(8,128)(2,1)S(1)} %get-tuple-element.16), channel_id=1, source_target_pairs={{0,8},{4,12},{8,0},{12,4},{1,9},{5,13},{9,1},{13,5},{2,10},{6,14},... | collective-permute-start | bytes 786440 | tf_op jit(solution)/shard_map/ppermute | solution.py:394
  5.4 1.6 %collective-permute-start.3 = (bf16[256,512]{1,0:T(8,128)(2,1)S(1)}, bf16[256,512]{1,0:T(8,128)(2,1)S(1)}, u32[]{:S(2)}, u32[]{:S(2)}) collective-permute-start(bf16[256,512]{1,0:T(8,128)(2,1)S(1)} %get-tuple-element.16), channel_id=1, source_target_pairs={{0,4},{4,0},{8,12},{12,8},{1,5},{5,1},{9,13},{13,9},{2,6},{6,2},{1... | collective-permute-start | bytes 786440 | tf_op jit(solution)/shard_map/ppermute | solution.py:394
  7.0 1.5 %collective-permute-start.4 = (bf16[256,512]{1,0:T(8,128)(2,1)S(1)}, bf16[256,512]{1,0:T(8,128)(2,1)S(1)}, u32[]{:S(2)}, u32[]{:S(2)}) collective-permute-start(bf16[256,512]{1,0:T(8,128)(2,1)S(1)} %get-tuple-element.16), channel_id=1, source_target_pairs={{0,2},{2,0},{1,3},{3,1},{4,6},{6,4},{5,7},{7,5},{8,10},{10,8},{9,1... | collective-permute-start | bytes 786440 | tf_op jit(solution)/shard_map/ppermute | solution.py:394
  8.5 0.7 copy-done.1
  9.2 3.6 %make_messages.1 = (bf16[544,256]{1,0:T(8,128)(2,1)S(1)}, bf16[544,256]{1,0:T(8,128)(2,1)S(1)}, bf16[544,256]{1,0:T(8,128)(2,1)S(1)}, bf16[544,256]{1,0:T(8,128)...) custom-call(s32[2,16]{1,0:T(2,128)S(1)} %bitcast.7, ...), custom_call_target="tpu_custom_call" | custom-call | bytes 4456448 | tf_op jit(solution)/shard_map/make_messages/pallas_call | solution.py:132
  12.8 0.1 collective-permute-start.7
  12.9 0.4 collective-permute-start.10
  13.3 1.1 %row_mask.1.refs_4_.mask_ref = f32[512,128]{1,0:T(8,128)S(1)} custom-call(s32[1,16]{1,0:T(1,128)S(1)} %copy-done.2, s32[16,16]{1,0:T(8,128)S(1)} %copy-done), custom_call_target="tpu_custom_call" | custom-call | tf_op jit(solution)/shard_map/row_mask/pallas_call | solution.py:373
  14.4 3.8 %collective-permute-done.refs_2_.refs_0_ = bf16[256,512]{1,0:T(8,128)(2,1)S(1)} collective-permute-done((bf16[256,512]{1,0:T(8,128)(2,1)S(1)}, bf16[256,512]{1,0:T(8,128)(2,1)S(1)}, u32[]{:S(2)}, u32[]{:S(2)}) %collective-permute-start) | collective-permute-done | bytes 262176 | tf_op jit(solution)/shard_map/ppermute | solution.py:394
  18.2 0.0 collective-permute-start.2
  18.2 0.0 collective-permute-done.3.refs_0_
  18.2 0.0 collective-permute-done.4.refs_1_
  18.3 1.8 %collective-permute-start.5 = (bf16[512,512]{1,0:T(8,128)(2,1)S(1)}, bf16[512,512]{1,0:T(8,128)(2,1)S(1)}, u32[]{:S(2)}, u32[]{:S(2)}) collective-permute-start(bf16[512,512]{1,0:T(8,128)(2,1)S(1)} %bundle.17.refs_2_.refs_0_), channel_id=1, source_target_pairs={{0,16},{16,0},{1,17},{17,1},{2,18},{18,2},{3,19},{19,3},{4,20},{20... | collective-permute-start | bytes 1572872 | tf_op jit(solution)/shard_map/ppermute | solution.py:394
  20.0 7.7 %collective-permute-start.9 = (bf16[256,512]{1,0:T(8,128)(2,1)S(1)}, bf16[256,512]{1,0:T(8,128)(2,1)S(1)}, u32[]{:S(2)}, u32[]{:S(2)}) collective-permute-start(bf16[256,512]{1,0:T(8,128)(2,1)S(1)} %bundle.20), channel_id=1, source_target_pairs={{0,2},{2,0},{1,3},{3,1},{4,6},{6,4},{5,7},{7,5},{8,10},{10,8},{9,1... | collective-permute-start | bytes 786440 | tf_op jit(solution)/shard_map/ppermute | solution.py:394
  27.7 0.0 collective-permute-done.7.refs_1_
  27.7 0.0 collective-permute-start.15
  27.8 1.5 %collective-permute-done.10.refs_2_.refs_0_ = bf16[544,256]{1,0:T(8,128)(2,1)S(1)} collective-permute-done((bf16[544,256]{1,0:T(8,128)(2,1)S(1)}, bf16[544,256]{1,0:T(8,128)(2,1)S(1)}, u32[]{:S(2)}, u32[]{:S(2)}) %collective-permute-start.10) | collective-permute-done | bytes 278560 | tf_op jit(solution)/shard_map/ppermute | solution.py:399
  29.3 3.5 %collective-permute-start.8 = (bf16[1088,256]{1,0:T(8,128)(2,1)S(1)}, bf16[1088,256]{1,0:T(8,128)(2,1)S(1)}, u32[]{:S(2)}, u32[]{:S(2)}) collective-permute-start(bf16[1088,256]{1,0:T(8,128)(2,1)S(1)} %bundle.19), channel_id=1, source_target_pairs={{0,12},{1,3},{2,14},{3,1},{4,8},{5,7},{6,10},{7,5},{8,4},{9,11},{1... | collective-permute-start | bytes 1671176 | tf_op jit(solution)/shard_map/ppermute | solution.py:399
  32.8 2.0 %collective-permute-done.9.refs_1_ = bf16[256,512]{1,0:T(8,128)(2,1)S(1)} collective-permute-done((bf16[256,512]{1,0:T(8,128)(2,1)S(1)}, bf16[256,512]{1,0:T(8,128)(2,1)S(1)}, u32[]{:S(2)}, u32[]{:S(2)}) %collective-permute-start.9) | collective-permute-done | bytes 262176 | tf_op jit(solution)/shard_map/ppermute | solution.py:394
  34.9 0.6 collective-permute-start.11
  35.5 0.0 collective-permute-done.2.refs_1_
  35.5 0.0 collective-permute-start.1
  35.5 0.0 collective-permute-done.5.refs_3_.refs_1_
  35.5 1.2 %base_product.4.refs_1_.refs_4_ = f32[512,512]{1,0:T(8,128)S(1)} custom-call(bf16[512,8192]{1,0:T(8,128)(2,1)S(1)} %bitcast.6, bf16[512,512]{1,0:T(8,128)(2,1)S(1)} %get-tuple-element.17.refs_0_, bf16[512,512]{1,0:T(8,128)(2,1)S(1)} %collective-permute-done.2.refs_1_, bf16[512,512]{1,0:T(8,128)(2,1)S(1)} %bundle.17.refs_2_.refs_0_, ...), custom_call_target="tpu_custom_call" | custom-call | flops 1073741824 | bytes 5242880 | tf_op jit(solution)/shard_map/base_product/pallas_call | solution.py:210
  36.8 5.5 %collective-permute-start.6 = (bf16[256,512]{1,0:T(8,128)(2,1)S(1)}, bf16[256,512]{1,0:T(8,128)(2,1)S(1)}, u32[]{:S(2)}, u32[]{:S(2)}) collective-permute-start(bf16[256,512]{1,0:T(8,128)(2,1)S(1)} %bundle.18), channel_id=1, source_target_pairs={{0,2},{2,0},{1,3},{3,1},{4,6},{6,4},{5,7},{7,5},{8,10},{10,8},{9,1... | collective-permute-start | bytes 786440 | tf_op jit(solution)/shard_map/ppermute | solution.py:394
  42.2 0.1 bundle.28
  42.3 1.3 %collective-permute-done.8.refs_2_.refs_3_.refs_0_.refs_1_.refs_4_ = bf16[1088,256]{1,0:T(8,128)(2,1)S(1)} collective-permute-done((bf16[1088,256]{1,0:T(8,128)(2,1)S(1)}, bf16[1088,256]{1,0:T(8,128)(2,1)S(1)}, u32[]{:S(2)}, u32[]{:S(2)}) %collective-permute-start.8) | collective-permute-done | bytes 557088 | tf_op jit(solution)/shard_map/ppermute | solution.py:399
  43.6 0.0 collective-permute-start.20
  43.6 0.0 collective-permute-done.15.refs_1_
  43.6 2.0 %collective-permute-start.16 = (bf16[1088,256]{1,0:T(8,128)(2,1)S(1)}, bf16[1088,256]{1,0:T(8,128)(2,1)S(1)}, u32[]{:S(2)}, u32[]{:S(2)}) collective-permute-start(bf16[1088,256]{1,0:T(8,128)(2,1)S(1)} %bundle.24), channel_id=1, source_target_pairs={{0,4},{1,15},{2,6},{3,13},{4,0},{5,11},{6,2},{7,9},{8,12},{9,7},{1... | collective-permute-start | bytes 1671176 | tf_op jit(solution)/shard_map/ppermute | solution.py:399
  45.6 1.1 %collective-permute-done.1.refs_0_ = bf16[256,512]{1,0:T(8,128)(2,1)S(1)} collective-permute-done((bf16[256,512]{1,0:T(8,128)(2,1)S(1)}, bf16[256,512]{1,0:T(8,128)(2,1)S(1)}, u32[]{:S(2)}, u32[]{:S(2)}) %collective-permute-start.1) | collective-permute-done | bytes 262176 | tf_op jit(solution)/shard_map/ppermute | solution.py:394
  46.7 1.3 %collective-permute-done.6.refs_1_ = bf16[256,512]{1,0:T(8,128)(2,1)S(1)} collective-permute-done((bf16[256,512]{1,0:T(8,128)(2,1)S(1)}, bf16[256,512]{1,0:T(8,128)(2,1)S(1)}, u32[]{:S(2)}, u32[]{:S(2)}) %collective-permute-start.6) | collective-permute-done | bytes 262176 | tf_op jit(solution)/shard_map/ppermute | solution.py:394
  48.0 0.1 collective-permute-done.11.refs_3_.refs_2_.refs_1_
  48.1 1.5 %collective-permute-start.12 = (bf16[512,512]{1,0:T(8,128)(2,1)S(1)}, bf16[512,512]{1,0:T(8,128)(2,1)S(1)}, u32[]{:S(2)}, u32[]{:S(2)}) collective-permute-start(bf16[512,512]{1,0:T(8,128)(2,1)S(1)} %bundle.22.refs_0_.refs_3_), channel_id=1, source_target_pairs={{0,16},{16,0},{1,17},{17,1},{2,18},{18,2},{3,19},{19,3},{4,20},{20... | collective-permute-start | bytes 1572872 | tf_op jit(solution)/shard_map/ppermute | solution.py:394
  49.6 0.1 collective-permute-start.18
  49.7 3.8 %collective-permute-start.14 = (bf16[256,512]{1,0:T(8,128)(2,1)S(1)}, bf16[256,512]{1,0:T(8,128)(2,1)S(1)}, u32[]{:S(2)}, u32[]{:S(2)}) collective-permute-start(bf16[256,512]{1,0:T(8,128)(2,1)S(1)} %collective-permute-done.1.refs_0_), channel_id=1, source_target_pairs={{0,2},{2,0},{1,3},{3,1},{4,6},{6,4},{5,7},{7,5},{8,10},{10,8},{9,1... | collective-permute-start | bytes 786440 | tf_op jit(solution)/shard_map/ppermute | solution.py:394
  53.5 0.1 bundle.31
  53.5 0.0 collective-permute-done.18.refs_3_
  53.6 0.2 collective-permute-start.23
  53.8 3.1 %collective-permute-done.16.refs_1_.refs_2_.refs_0_ = bf16[1088,256]{1,0:T(8,128)(2,1)S(1)} collective-permute-done((bf16[1088,256]{1,0:T(8,128)(2,1)S(1)}, bf16[1088,256]{1,0:T(8,128)(2,1)S(1)}, u32[]{:S(2)}, u32[]{:S(2)}) %collective-permute-start.16) | collective-permute-done | bytes 557088 | tf_op jit(solution)/shard_map/ppermute | solution.py:399
  56.9 5.1 %collective-permute-start.21 = (bf16[1088,256]{1,0:T(8,128)(2,1)S(1)}, bf16[1088,256]{1,0:T(8,128)(2,1)S(1)}, u32[]{:S(2)}, u32[]{:S(2)}) collective-permute-start(bf16[1088,256]{1,0:T(8,128)(2,1)S(1)} %bundle.29), channel_id=1, source_target_pairs={{0,10},{1,7},{2,8},{3,5},{4,14},{5,3},{6,12},{7,1},{8,2},{9,15},{1... | collective-permute-start | bytes 1671176 | tf_op jit(solution)/shard_map/ppermute | solution.py:399
  62.0 0.2 collective-permute-done.12.refs_1_.refs_2_
  62.2 0.0 collective-permute-start.19
  62.3 0.1 bundle.23
  62.3 12.5 %collective-permute-done.14.refs_0_.refs_5_ = bf16[256,512]{1,0:T(8,128)(2,1)S(1)} collective-permute-done((bf16[256,512]{1,0:T(8,128)(2,1)S(1)}, bf16[256,512]{1,0:T(8,128)(2,1)S(1)}, u32[]{:S(2)}, u32[]{:S(2)}) %collective-permute-start.14) | collective-permute-done | bytes 262176 | tf_op jit(solution)/shard_map/ppermute | solution.py:394
  74.8 0.0 collective-permute-start.13
  74.9 0.0 collective-permute-done.19.refs_5_
  74.9 0.1 collective-permute-start.17
  75.0 1.3 %adapt_begin.1 = (f32[512,128]{1,0:T(8,128)S(1)}, bf16[512,128]{1,0:T(8,128)(2,1)S(1)}) custom-call(bf16[512,8192]{1,0:T(8,128)(2,1)S(1)} %bitcast.6, bf16[272,256]{1,0:T(8,128)(2,1)S(1)} %get-tuple-element.18.refs_3_.refs_0_, bf16[1360,256]{1,0:T(8,128)(2,1)S(1)} %collective-permute-done.15.refs_1_, ...), custom_call_target="tpu_custom_call" | custom-call | flops 1288490240 | bytes 5033164 | tf_op jit(solution)/shard_map/adapt_begin/pallas_call | solution.py:272
  76.2 0.0 collective-permute-done.20.refs_0_
  76.3 1.5 %base_product.5.refs_3_.refs_2_ = f32[512,512]{1,0:T(8,128)S(1)} custom-call(bf16[512,8192]{1,0:T(8,128)(2,1)S(1)} %bitcast.6, bf16[1024,512]{1,0:T(8,128)(2,1)S(1)} %collective-permute-done.20.refs_0_, bf16[512,512]{1,0:T(8,128)(2,1)S(1)} %bundle.21.refs_1_.refs_0_, bf16[512,512]{1,0:T(8,128)(2,1)S(1)} %collective-permute-done.11.refs_3_.refs_2_.refs_1_, ...), custom_call_target="tpu_custom_call" | custom-call | flops 1342177280 | bytes 6291456 | tf_op jit(solution)/shard_map/base_product/pallas_call | solution.py:210
  77.8 5.9 %collective-permute-done.17.refs_1_.refs_2_ = bf16[256,512]{1,0:T(8,128)(2,1)S(1)} collective-permute-done((bf16[256,512]{1,0:T(8,128)(2,1)S(1)}, bf16[256,512]{1,0:T(8,128)(2,1)S(1)}, u32[]{:S(2)}, u32[]{:S(2)}) %collective-permute-start.17) | collective-permute-done | bytes 262176 | tf_op jit(solution)/shard_map/ppermute | solution.py:394
  83.7 0.1 collective-permute-start.22
  83.8 0.0 collective-permute-done.23.refs_0_
  83.8 1.0 %base_product.6.refs_4_.refs_3_ = f32[512,512]{1,0:T(8,128)S(1)} custom-call(bf16[512,8192]{1,0:T(8,128)(2,1)S(1)} %bitcast.6, bf16[1024,512]{1,0:T(8,128)(2,1)S(1)} %collective-permute-done.23.refs_0_, bf16[512,512]{1,0:T(8,128)(2,1)S(1)} %collective-permute-done.12.refs_1_.refs_2_, f32[512,512]{1,0:T(8,128)S(1)} %base_product.5.refs_3_.refs_2_), custom_call_target="tpu_custom_call" | custom-call | flops 805306368 | bytes 4194304 | tf_op jit(solution)/shard_map/base_product/pallas_call | solution.py:210
  84.8 0.6 collective-permute-start.25
  85.4 0.1 collective-permute-start.24
  85.5 0.2 collective-permute-done.22.refs_3_
  85.7 0.0 collective-permute-done.13.refs_0_
  85.7 1.2 %base_product.7.base_ref = f32[512,512]{1,0:T(8,128)S(1)} custom-call(bf16[512,8192]{1,0:T(8,128)(2,1)S(1)} %bitcast.6, bf16[1024,512]{1,0:T(8,128)(2,1)S(1)} %collective-permute-done.13.refs_0_, bf16[256,512]{1,0:T(8,128)(2,1)S(1)} %bundle.25.refs_0_.refs_1_, bf16[256,512]{1,0:T(8,128)(2,1)S(1)} %collective-permute-done.17.refs_1_.refs_2_, ...), custom_call_target="tpu_custom_call" | custom-call | flops 1073741824 | bytes 5242880 | tf_op jit(solution)/shard_map/base_product/pallas_call | solution.py:210
  86.9 0.0 collective-permute-done.25.refs_3_
  86.9 0.1 collective-permute-done.24.refs_1_
  87.0 2.2 %adapt_end.1 = bf16[512,512]{1,0:T(8,128)(2,1)} custom-call(bf16[512,8192]{1,0:T(8,128)(2,1)S(1)} %bitcast.6, f32[512,128]{1,0:T(8,128)S(1)} %row_mask.1.refs_4_.mask_ref, f32[512,512]{1,0:T(8,128)S(1)} %base_product.7.base_ref, f32[512,128]{1,0:T(8,128)S(1)} %get-tuple-element.24.refs_2_.shrunk, bf16[512,128]{1,0:T(8,128)(2,1)S(1)} %get-tuple-element.26.widened, ...), custom_call_target="tpu_custom_call" | custom-call | flops 858993472 | bytes 3355443 | tf_op jit(solution)/shard_map/adapt_end/pallas_call | solution.py:304
  (27 shorter events, 0.4 us)
Async XLA Ops:
  0.0 13.3 %copy-start = (s32[16,16]{1,0:T(8,128)S(1)}, s32[16,16]{1,0:T(8,128)}, u32[]{:S(2)}) copy-start(s32[16,16]{1,0:T(8,128)} %slots_ref.1) | copy-start | bytes 3076
  0.0 35.5 %slice-start = ((s8[8388608]{0:T(1024)(128)(4,1)}), s8[4194304]{0:T(1024)(128)(4,1)S(1)}, s32[]{:S(2)}) async-start(s8[8388608]{0:T(1024)(128)(4,1)} %bitcast.5), calls=%async_computation | async-start | bytes 8388608
  1.3 16.9 %collective-permute-start = (bf16[256,512]{1,0:T(8,128)(2,1)S(1)}, bf16[256,512]{1,0:T(8,128)(2,1)S(1)}, u32[]{:S(2)}, u32[]{:S(2)}) collective-permute-start(bf16[256,512]{1,0:T(8,128)(2,1)S(1)} %get-tuple-element.16), channel_id=1, source_target_pairs={{0,8},{4,12},{8,0},{12,4},{1,9},{5,13},{9,1},{13,5},{2,10},{6,14},... | collective-permute-start | bytes 786440 | tf_op jit(solution)/shard_map/ppermute | solution.py:394
  5.4 12.8 %collective-permute-start.3 = (bf16[256,512]{1,0:T(8,128)(2,1)S(1)}, bf16[256,512]{1,0:T(8,128)(2,1)S(1)}, u32[]{:S(2)}, u32[]{:S(2)}) collective-permute-start(bf16[256,512]{1,0:T(8,128)(2,1)S(1)} %get-tuple-element.16), channel_id=1, source_target_pairs={{0,4},{4,0},{8,12},{12,8},{1,5},{5,1},{9,13},{13,9},{2,6},{6,2},{1... | collective-permute-start | bytes 786440 | tf_op jit(solution)/shard_map/ppermute | solution.py:394
  7.0 11.2 %collective-permute-start.4 = (bf16[256,512]{1,0:T(8,128)(2,1)S(1)}, bf16[256,512]{1,0:T(8,128)(2,1)S(1)}, u32[]{:S(2)}, u32[]{:S(2)}) collective-permute-start(bf16[256,512]{1,0:T(8,128)(2,1)S(1)} %get-tuple-element.16), channel_id=1, source_target_pairs={{0,2},{2,0},{1,3},{3,1},{4,6},{6,4},{5,7},{7,5},{8,10},{10,8},{9,1... | collective-permute-start | bytes 786440 | tf_op jit(solution)/shard_map/ppermute | solution.py:394
  8.5 0.7 copy-start.1
  9.2 4.1 %copy-start.2 = (s32[1,16]{1,0:T(1,128)S(1)}, s32[1,16]{1,0:T(1,128)}, u32[]{:S(2)}) copy-start(s32[1,16]{1,0:T(1,128)} %lengths_ref.1) | copy-start | bytes 196
  9.2 26.3 %slice-start.1 = ((s8[8388608]{0:T(1024)(128)(4,1)}), s8[4194304]{0:T(1024)(128)(4,1)S(1)}, s32[]{:S(2)}) async-start(s8[8388608]{0:T(1024)(128)(4,1)} %bitcast.5), calls=%async_computation.1 | async-start | bytes 8388608
  12.8 14.9 %collective-permute-start.7 = (bf16[544,256]{1,0:T(8,128)(2,1)S(1)}, bf16[544,256]{1,0:T(8,128)(2,1)S(1)}, u32[]{:S(2)}, u32[]{:S(2)}) collective-permute-start(bf16[544,256]{1,0:T(8,128)(2,1)S(1)} %after.2), channel_id=1, source_target_pairs={{0,1},{1,0},{2,3},{3,2},{4,5},{5,4},{6,7},{7,6},{8,9},{9,8},{10,11... | collective-permute-start | bytes 835592 | tf_op jit(solution)/shard_map/ppermute | solution.py:394
  12.9 16.4 %collective-permute-start.10 = (bf16[544,256]{1,0:T(8,128)(2,1)S(1)}, bf16[544,256]{1,0:T(8,128)(2,1)S(1)}, u32[]{:S(2)}, u32[]{:S(2)}) collective-permute-start(bf16[544,256]{1,0:T(8,128)(2,1)S(1)} %get-tuple-element.21), channel_id=1, source_target_pairs={{0,8},{1,9},{2,10},{3,11},{4,12},{5,13},{6,14},{7,15},{8,0},{9,1},... | collective-permute-start | bytes 835592 | tf_op jit(solution)/shard_map/ppermute | solution.py:399
  18.2 17.3 %collective-permute-start.2 = (bf16[512,512]{1,0:T(8,128)(2,1)S(1)}, bf16[512,512]{1,0:T(8,128)(2,1)S(1)}, u32[]{:S(2)}, u32[]{:S(2)}) collective-permute-start(bf16[512,512]{1,0:T(8,128)(2,1)S(1)} %get-tuple-element.17.refs_0_), channel_id=1, source_target_pairs={{0,1},{1,0},{2,3},{3,2},{4,5},{5,4},{6,7},{7,6},{8,9},{9,8},{10,11... | collective-permute-start | bytes 1572872 | tf_op jit(solution)/shard_map/ppermute | solution.py:394
  18.3 17.2 %collective-permute-start.5 = (bf16[512,512]{1,0:T(8,128)(2,1)S(1)}, bf16[512,512]{1,0:T(8,128)(2,1)S(1)}, u32[]{:S(2)}, u32[]{:S(2)}) collective-permute-start(bf16[512,512]{1,0:T(8,128)(2,1)S(1)} %bundle.17.refs_2_.refs_0_), channel_id=1, source_target_pairs={{0,16},{16,0},{1,17},{17,1},{2,18},{18,2},{3,19},{19,3},{4,20},{20... | collective-permute-start | bytes 1572872 | tf_op jit(solution)/shard_map/ppermute | solution.py:394
  20.0 14.8 %collective-permute-start.9 = (bf16[256,512]{1,0:T(8,128)(2,1)S(1)}, bf16[256,512]{1,0:T(8,128)(2,1)S(1)}, u32[]{:S(2)}, u32[]{:S(2)}) collective-permute-start(bf16[256,512]{1,0:T(8,128)(2,1)S(1)} %bundle.20), channel_id=1, source_target_pairs={{0,2},{2,0},{1,3},{3,1},{4,6},{6,4},{5,7},{7,5},{8,10},{10,8},{9,1... | collective-permute-start | bytes 786440 | tf_op jit(solution)/shard_map/ppermute | solution.py:394
  27.7 15.9 %collective-permute-start.15 = (bf16[1360,256]{1,0:T(8,128)(2,1)S(1)}, bf16[1360,256]{1,0:T(8,128)(2,1)S(1)}, u32[]{:S(2)}, u32[]{:S(2)}) collective-permute-start(bf16[1360,256]{1,0:T(8,128)(2,1)S(1)} %after.3), channel_id=1, source_target_pairs={{0,1},{1,0},{2,3},{3,2},{4,5},{5,4},{6,7},{7,6},{8,9},{9,8},{10,11... | collective-permute-start | bytes 2088968 | tf_op jit(solution)/shard_map/ppermute | solution.py:394
  29.3 14.3 %collective-permute-start.8 = (bf16[1088,256]{1,0:T(8,128)(2,1)S(1)}, bf16[1088,256]{1,0:T(8,128)(2,1)S(1)}, u32[]{:S(2)}, u32[]{:S(2)}) collective-permute-start(bf16[1088,256]{1,0:T(8,128)(2,1)S(1)} %bundle.19), channel_id=1, source_target_pairs={{0,12},{1,3},{2,14},{3,1},{4,8},{5,7},{6,10},{7,5},{8,4},{9,11},{1... | collective-permute-start | bytes 1671176 | tf_op jit(solution)/shard_map/ppermute | solution.py:399
  34.9 13.2 %collective-permute-start.11 = (bf16[512,512]{1,0:T(8,128)(2,1)S(1)}, bf16[512,512]{1,0:T(8,128)(2,1)S(1)}, u32[]{:S(2)}, u32[]{:S(2)}) collective-permute-start(bf16[512,512]{1,0:T(8,128)(2,1)S(1)} %bundle.21.refs_1_.refs_0_), channel_id=1, source_target_pairs={{0,16},{16,0},{1,17},{17,1},{2,18},{18,2},{3,19},{19,3},{4,20},{20... | collective-permute-start | bytes 1572872 | tf_op jit(solution)/shard_map/ppermute | solution.py:394
  35.5 11.2 %collective-permute-start.1 = (bf16[256,512]{1,0:T(8,128)(2,1)S(1)}, bf16[256,512]{1,0:T(8,128)(2,1)S(1)}, u32[]{:S(2)}, u32[]{:S(2)}) collective-permute-start(bf16[256,512]{1,0:T(8,128)(2,1)S(1)} %collective-permute-done.refs_2_.refs_0_), channel_id=1, source_target_pairs={{0,4},{4,0},{8,12},{12,8},{1,5},{5,1},{9,13},{13,9},{2,6},{6,2},{1... | collective-permute-start | bytes 786440 | tf_op jit(solution)/shard_map/ppermute | solution.py:394
  36.8 11.3 %collective-permute-start.6 = (bf16[256,512]{1,0:T(8,128)(2,1)S(1)}, bf16[256,512]{1,0:T(8,128)(2,1)S(1)}, u32[]{:S(2)}, u32[]{:S(2)}) collective-permute-start(bf16[256,512]{1,0:T(8,128)(2,1)S(1)} %bundle.18), channel_id=1, source_target_pairs={{0,2},{2,0},{1,3},{3,1},{4,6},{6,4},{5,7},{7,5},{8,10},{10,8},{9,1... | collective-permute-start | bytes 786440 | tf_op jit(solution)/shard_map/ppermute | solution.py:394
  43.6 32.7 %collective-permute-start.20 = (bf16[1024,512]{1,0:T(8,128)(2,1)S(1)}, bf16[1024,512]{1,0:T(8,128)(2,1)S(1)}, u32[]{:S(2)}, u32[]{:S(2)}) collective-permute-start(bf16[1024,512]{1,0:T(8,128)(2,1)S(1)} %bundle.28), channel_id=1, source_target_pairs={{0,1},{1,0},{2,3},{3,2},{4,5},{5,4},{6,7},{7,6},{8,9},{9,8},{10,11... | collective-permute-start | bytes 3145736 | tf_op jit(solution)/shard_map/ppermute | solution.py:394
  43.6 13.3 %collective-permute-start.16 = (bf16[1088,256]{1,0:T(8,128)(2,1)S(1)}, bf16[1088,256]{1,0:T(8,128)(2,1)S(1)}, u32[]{:S(2)}, u32[]{:S(2)}) collective-permute-start(bf16[1088,256]{1,0:T(8,128)(2,1)S(1)} %bundle.24), channel_id=1, source_target_pairs={{0,4},{1,15},{2,6},{3,13},{4,0},{5,11},{6,2},{7,9},{8,12},{9,7},{1... | collective-permute-start | bytes 1671176 | tf_op jit(solution)/shard_map/ppermute | solution.py:399
  48.1 14.1 %collective-permute-start.12 = (bf16[512,512]{1,0:T(8,128)(2,1)S(1)}, bf16[512,512]{1,0:T(8,128)(2,1)S(1)}, u32[]{:S(2)}, u32[]{:S(2)}) collective-permute-start(bf16[512,512]{1,0:T(8,128)(2,1)S(1)} %bundle.22.refs_0_.refs_3_), channel_id=1, source_target_pairs={{0,16},{16,0},{1,17},{17,1},{2,18},{18,2},{3,19},{19,3},{4,20},{20... | collective-permute-start | bytes 1572872 | tf_op jit(solution)/shard_map/ppermute | solution.py:394
  49.6 3.9 %collective-permute-start.18 = (bf16[272,256]{1,0:T(8,128)(2,1)S(1)}, bf16[272,256]{1,0:T(8,128)(2,1)S(1)}, u32[]{:S(2)}, u32[]{:S(2)}) collective-permute-start(bf16[272,256]{1,0:T(8,128)(2,1)S(1)} %bundle.26), channel_id=1, source_target_pairs={{0,1},{1,0},{2,3},{3,2},{4,5},{5,4},{6,7},{7,6},{8,9},{9,8},{10,11... | collective-permute-start | bytes 417800 | tf_op jit(solution)/shard_map/ppermute | solution.py:394
  49.7 25.1 %collective-permute-start.14 = (bf16[256,512]{1,0:T(8,128)(2,1)S(1)}, bf16[256,512]{1,0:T(8,128)(2,1)S(1)}, u32[]{:S(2)}, u32[]{:S(2)}) collective-permute-start(bf16[256,512]{1,0:T(8,128)(2,1)S(1)} %collective-permute-done.1.refs_0_), channel_id=1, source_target_pairs={{0,2},{2,0},{1,3},{3,1},{4,6},{6,4},{5,7},{7,5},{8,10},{10,8},{9,1... | collective-permute-start | bytes 786440 | tf_op jit(solution)/shard_map/ppermute | solution.py:394
  53.6 30.2 %collective-permute-start.23 = (bf16[1024,512]{1,0:T(8,128)(2,1)S(1)}, bf16[1024,512]{1,0:T(8,128)(2,1)S(1)}, u32[]{:S(2)}, u32[]{:S(2)}) collective-permute-start(bf16[1024,512]{1,0:T(8,128)(2,1)S(1)} %bundle.31), channel_id=1, source_target_pairs={{0,1},{1,0},{2,3},{3,2},{4,5},{5,4},{6,7},{7,6},{8,9},{9,8},{10,11... | collective-permute-start | bytes 3145736 | tf_op jit(solution)/shard_map/ppermute | solution.py:394
  56.9 20.9 %collective-permute-start.21 = (bf16[1088,256]{1,0:T(8,128)(2,1)S(1)}, bf16[1088,256]{1,0:T(8,128)(2,1)S(1)}, u32[]{:S(2)}, u32[]{:S(2)}) collective-permute-start(bf16[1088,256]{1,0:T(8,128)(2,1)S(1)} %bundle.29), channel_id=1, source_target_pairs={{0,10},{1,7},{2,8},{3,5},{4,14},{5,3},{6,12},{7,1},{8,2},{9,15},{1... | collective-permute-start | bytes 1671176 | tf_op jit(solution)/shard_map/ppermute | solution.py:399
  62.2 12.6 %collective-permute-start.19 = (bf16[544,256]{1,0:T(8,128)(2,1)S(1)}, bf16[544,256]{1,0:T(8,128)(2,1)S(1)}, u32[]{:S(2)}, u32[]{:S(2)}) collective-permute-start(bf16[544,256]{1,0:T(8,128)(2,1)S(1)} %bundle.27), channel_id=1, source_target_pairs={{0,1},{1,0},{2,3},{3,2},{4,5},{5,4},{6,7},{7,6},{8,9},{9,8},{10,11... | collective-permute-start | bytes 835592 | tf_op jit(solution)/shard_map/ppermute | solution.py:394
  74.8 10.8 %collective-permute-start.13 = (bf16[1024,512]{1,0:T(8,128)(2,1)S(1)}, bf16[1024,512]{1,0:T(8,128)(2,1)S(1)}, u32[]{:S(2)}, u32[]{:S(2)}) collective-permute-start(bf16[1024,512]{1,0:T(8,128)(2,1)S(1)} %bundle.23), channel_id=1, source_target_pairs={{0,1},{1,0},{2,3},{3,2},{4,5},{5,4},{6,7},{7,6},{8,9},{9,8},{10,11... | collective-permute-start | bytes 3145736 | tf_op jit(solution)/shard_map/ppermute | solution.py:394
  74.9 8.8 %collective-permute-start.17 = (bf16[256,512]{1,0:T(8,128)(2,1)S(1)}, bf16[256,512]{1,0:T(8,128)(2,1)S(1)}, u32[]{:S(2)}, u32[]{:S(2)}) collective-permute-start(bf16[256,512]{1,0:T(8,128)(2,1)S(1)} %bundle.25.refs_0_.refs_1_), channel_id=1, source_target_pairs={{0,16},{16,0},{1,17},{17,1},{2,18},{18,2},{3,19},{19,3},{4,20},{20... | collective-permute-start | bytes 786440 | tf_op jit(solution)/shard_map/ppermute | solution.py:394
  83.7 2.0 %collective-permute-start.22 = (bf16[512,512]{1,0:T(8,128)(2,1)S(1)}, bf16[512,512]{1,0:T(8,128)(2,1)S(1)}, u32[]{:S(2)}, u32[]{:S(2)}) collective-permute-start(bf16[512,512]{1,0:T(8,128)(2,1)S(1)} %bundle.30), channel_id=1, source_target_pairs={{0,1},{1,0},{2,3},{3,2},{4,5},{5,4},{6,7},{7,6},{8,9},{9,8},{10,11... | collective-permute-start | bytes 1572872 | tf_op jit(solution)/shard_map/ppermute | solution.py:394
  84.8 2.1 %collective-permute-start.25 = (bf16[544,256]{1,0:T(8,128)(2,1)S(1)}, bf16[544,256]{1,0:T(8,128)(2,1)S(1)}, u32[]{:S(2)}, u32[]{:S(2)}) collective-permute-start(bf16[544,256]{1,0:T(8,128)(2,1)S(1)} %bundle.33), channel_id=1, source_target_pairs={{0,1},{1,0},{2,3},{3,2},{4,5},{5,4},{6,7},{7,6},{8,9},{9,8},{10,11... | collective-permute-start | bytes 835592 | tf_op jit(solution)/shard_map/ppermute | solution.py:394
  85.4 1.6 %collective-permute-start.24 = (bf16[544,256]{1,0:T(8,128)(2,1)S(1)}, bf16[544,256]{1,0:T(8,128)(2,1)S(1)}, u32[]{:S(2)}, u32[]{:S(2)}) collective-permute-start(bf16[544,256]{1,0:T(8,128)(2,1)S(1)} %bundle.32), channel_id=1, source_target_pairs={{0,1},{1,0},{2,3},{3,2},{4,5},{5,4},{6,7},{7,6},{8,9},{9,8},{10,11... | collective-permute-start | bytes 835592 | tf_op jit(solution)/shard_map/ppermute | solution.py:394

commit v12 on v10

--- a/solution.py
+++ b/solution.py
@@ -27,7 +27,7 @@
 
 
 EARLY, LATE = (), (7,)
-ROUNDS = ((1, 4), (5, 2), (3, 6))
+ROUNDS = ((1, 4), (6, 2), (3, 5))
 SWAPS = ((0,), (1, 2))
 LAST = ("R2", "R1")
 TIES = {

time: 82.9 us -> 82.3 us (level)
    ppermute x4, waiting for transfers between devices: 13.5 us -> 11.9 us  [send_pairs(): lax.ppermute(payload, AXES[1:], [(i, target(i)) for i in range(size)])]
    ppermute x22, waiting for transfers between devices: 24.5 us -> 25.3 us  [swap(): return lax.ppermute(block, axis, [(i, i ^ bit) for i in range(size)])]
  transfers between devices with their start and end apart: 26 -> 26, of which waited for: 13 -> 12; matrix products, arithmetic and copies ran while one was open for 0% -> 0% of each run, Pallas kernels for 14% -> 14%
where the time goes in v12:
time: 82.3 us; the launch traced here: 82.1 us
  waiting for transfers between devices  37.2 us (45%)
  starting transfers between devices  28.8 us (35%)
  Pallas kernels  15.1 us (18%)
    ppermute x22, starting transfers between devices, swap(): return lax.ppermute(block, axis, [(i, i ^ bit) for i in range(size)])  28.1 us
    ppermute x22, waiting for transfers between devices, swap(): return lax.ppermute(block, axis, [(i, i ^ bit) for i in range(size)])  25.3 us
    ppermute x4, waiting for transfers between devices, send_pairs(): lax.ppermute(payload, AXES[1:], [(i, target(i)) for i in range(size)])  11.9 us
    pallas_call x4, Pallas kernels, base_product(): pl.pallas_call(kernel, out_shape=pltpu.VMEM((rows, width), jnp.float32),...  5 us
    pallas_call x1, Pallas kernels, make_messages(): pl.pallas_call(kernel, out_shape=[pltpu.VMEM((n * length, HALF), jnp.bflo...  3.62 us
    pallas_call x1, Pallas kernels, adapt_end(): pl.pallas_call(kernel, out_shape=jax.ShapeDtypeStruct((rows, width), jnp....  2.21 us
  transfers between devices with their start and end apart: 26, of which 12 were waited for; matrix products, arithmetic and copies ran while one was open for 0% of the time, Pallas kernels for 14%

profile of v12, /device:TPU:0, one launch (start us, length us, event | category | flops | bytes accessed | tf_op | source)
XLA Modules:
  0.0 82.1 jit_solution(14586042661251710013)
XLA Ops:
  0.0 1.3 %load_rows.1 = (bf16[512,512]{1,0:T(8,128)(2,1)S(1)}, bf16[256,512]{1,0:T(8,128)(2,1)S(1)}) custom-call(bf16[512,512]{1,0:T(8,128)(2,1)} %source.1), custom_call_target="tpu_custom_call" | custom-call | tf_op jit(solution)/shard_map/load_rows/pallas_call | solution.py:166
  1.3 4.1 %collective-permute-start = (bf16[256,512]{1,0:T(8,128)(2,1)S(1)}, bf16[256,512]{1,0:T(8,128)(2,1)S(1)}, u32[]{:S(2)}, u32[]{:S(2)}) collective-permute-start(bf16[256,512]{1,0:T(8,128)(2,1)S(1)} %get-tuple-element.16), channel_id=1, source_target_pairs={{0,8},{4,12},{8,0},{12,4},{1,9},{5,13},{9,1},{13,5},{2,10},{6,14},... | collective-permute-start | bytes 786440 | tf_op jit(solution)/shard_map/ppermute | solution.py:395
  5.4 1.6 %collective-permute-start.3 = (bf16[256,512]{1,0:T(8,128)(2,1)S(1)}, bf16[256,512]{1,0:T(8,128)(2,1)S(1)}, u32[]{:S(2)}, u32[]{:S(2)}) collective-permute-start(bf16[256,512]{1,0:T(8,128)(2,1)S(1)} %get-tuple-element.16), channel_id=1, source_target_pairs={{0,4},{4,0},{8,12},{12,8},{1,5},{5,1},{9,13},{13,9},{2,6},{6,2},{1... | collective-permute-start | bytes 786440 | tf_op jit(solution)/shard_map/ppermute | solution.py:395
  7.0 1.5 %collective-permute-start.4 = (bf16[256,512]{1,0:T(8,128)(2,1)S(1)}, bf16[256,512]{1,0:T(8,128)(2,1)S(1)}, u32[]{:S(2)}, u32[]{:S(2)}) collective-permute-start(bf16[256,512]{1,0:T(8,128)(2,1)S(1)} %get-tuple-element.16), channel_id=1, source_target_pairs={{0,2},{2,0},{1,3},{3,1},{4,6},{6,4},{5,7},{7,5},{8,10},{10,8},{9,1... | collective-permute-start | bytes 786440 | tf_op jit(solution)/shard_map/ppermute | solution.py:395
  8.5 0.7 copy-done.1
  9.2 3.6 %make_messages.1 = (bf16[544,256]{1,0:T(8,128)(2,1)S(1)}, bf16[544,256]{1,0:T(8,128)(2,1)S(1)}, bf16[544,256]{1,0:T(8,128)(2,1)S(1)}, bf16[544,256]{1,0:T(8,128)...) custom-call(s32[2,16]{1,0:T(2,128)S(1)} %bitcast.7, ...), custom_call_target="tpu_custom_call" | custom-call | bytes 4456448 | tf_op jit(solution)/shard_map/make_messages/pallas_call | solution.py:133
  12.8 0.1 collective-permute-start.8
  12.9 0.1 collective-permute-start.10
  13.0 1.1 %row_mask.1.refs_4_.mask_ref = f32[512,128]{1,0:T(8,128)S(1)} custom-call(s32[1,16]{1,0:T(1,128)S(1)} %copy-done.2, s32[16,16]{1,0:T(8,128)S(1)} %copy-done), custom_call_target="tpu_custom_call" | custom-call | tf_op jit(solution)/shard_map/row_mask/pallas_call | solution.py:374
  14.1 4.5 %collective-permute-done.refs_2_.refs_0_ = bf16[256,512]{1,0:T(8,128)(2,1)S(1)} collective-permute-done((bf16[256,512]{1,0:T(8,128)(2,1)S(1)}, bf16[256,512]{1,0:T(8,128)(2,1)S(1)}, u32[]{:S(2)}, u32[]{:S(2)}) %collective-permute-start) | collective-permute-done | bytes 262176 | tf_op jit(solution)/shard_map/ppermute | solution.py:395
  18.6 0.0 collective-permute-start.2
  18.6 0.0 collective-permute-done.3.refs_0_
  18.6 0.0 collective-permute-done.4.refs_1_
  18.6 7.5 %collective-permute-start.5 = (bf16[512,512]{1,0:T(8,128)(2,1)S(1)}, bf16[512,512]{1,0:T(8,128)(2,1)S(1)}, u32[]{:S(2)}, u32[]{:S(2)}) collective-permute-start(bf16[512,512]{1,0:T(8,128)(2,1)S(1)} %bundle.17.refs_2_.refs_0_), channel_id=1, source_target_pairs={{0,16},{16,0},{1,17},{17,1},{2,18},{18,2},{3,19},{19,3},{4,20},{20... | collective-permute-start | bytes 1572872 | tf_op jit(solution)/shard_map/ppermute | solution.py:395
  26.1 1.6 %collective-permute-start.6 = (bf16[256,512]{1,0:T(8,128)(2,1)S(1)}, bf16[256,512]{1,0:T(8,128)(2,1)S(1)}, u32[]{:S(2)}, u32[]{:S(2)}) collective-permute-start(bf16[256,512]{1,0:T(8,128)(2,1)S(1)} %bundle.18), channel_id=1, source_target_pairs={{0,2},{2,0},{1,3},{3,1},{4,6},{6,4},{5,7},{7,5},{8,10},{10,8},{9,1... | collective-permute-start | bytes 786440 | tf_op jit(solution)/shard_map/ppermute | solution.py:395
  27.7 0.0 collective-permute-done.8.refs_1_
  27.7 0.0 collective-permute-start.15
  27.8 0.0 collective-permute-done.10.refs_2_.refs_0_
  27.8 0.6 collective-permute-start.9
  28.4 6.3 %collective-permute-done.6.refs_5_.refs_1_ = bf16[256,512]{1,0:T(8,128)(2,1)S(1)} collective-permute-done((bf16[256,512]{1,0:T(8,128)(2,1)S(1)}, bf16[256,512]{1,0:T(8,128)(2,1)S(1)}, u32[]{:S(2)}, u32[]{:S(2)}) %collective-permute-start.6) | collective-permute-done | bytes 262176 | tf_op jit(solution)/shard_map/ppermute | solution.py:395
  34.7 0.4 collective-permute-start.11
  35.1 0.0 collective-permute-done.2.refs_1_.refs_4_
  35.1 0.0 collective-permute-start.1
  35.1 3.8 %collective-permute-done.5.refs_3_.refs_1_ = bf16[512,512]{1,0:T(8,128)(2,1)S(1)} collective-permute-done((bf16[512,512]{1,0:T(8,128)(2,1)S(1)}, bf16[512,512]{1,0:T(8,128)(2,1)S(1)}, u32[]{:S(2)}, u32[]{:S(2)}) %collective-permute-start.5) | collective-permute-done | bytes 524320 | tf_op jit(solution)/shard_map/ppermute | solution.py:395
  38.9 1.2 %base_product.4.refs_1_.refs_4_ = f32[512,512]{1,0:T(8,128)S(1)} custom-call(bf16[512,8192]{1,0:T(8,128)(2,1)S(1)} %bitcast.6, bf16[512,512]{1,0:T(8,128)(2,1)S(1)} %get-tuple-element.17.refs_0_, bf16[512,512]{1,0:T(8,128)(2,1)S(1)} %collective-permute-done.2.refs_1_.refs_4_, bf16[512,512]{1,0:T(8,128)(2,1)S(1)} %bundle.17.refs_2_.refs_0_, ...), custom_call_target="tpu_custom_call" | custom-call | flops 1073741824 | bytes 5242880 | tf_op jit(solution)/shard_map/base_product/pallas_call | solution.py:211
  40.2 2.0 %collective-permute-start.7 = (bf16[256,512]{1,0:T(8,128)(2,1)S(1)}, bf16[256,512]{1,0:T(8,128)(2,1)S(1)}, u32[]{:S(2)}, u32[]{:S(2)}) collective-permute-start(bf16[256,512]{1,0:T(8,128)(2,1)S(1)} %bundle.19), channel_id=1, source_target_pairs={{0,2},{2,0},{1,3},{3,1},{4,6},{6,4},{5,7},{7,5},{8,10},{10,8},{9,1... | collective-permute-start | bytes 786440 | tf_op jit(solution)/shard_map/ppermute | solution.py:395
  42.2 0.1 bundle.28
  42.3 0.0 collective-permute-done.9.refs_2_.refs_3_.refs_0_.refs_1_.refs_4_
  42.3 2.5 %collective-permute-start.20 = (bf16[1024,512]{1,0:T(8,128)(2,1)S(1)}, bf16[1024,512]{1,0:T(8,128)(2,1)S(1)}, u32[]{:S(2)}, u32[]{:S(2)}) collective-permute-start(bf16[1024,512]{1,0:T(8,128)(2,1)S(1)} %bundle.28), channel_id=1, source_target_pairs={{0,1},{1,0},{2,3},{3,2},{4,5},{5,4},{6,7},{7,6},{8,9},{9,8},{10,11... | collective-permute-start | bytes 3145736 | tf_op jit(solution)/shard_map/ppermute | solution.py:395
  44.8 0.0 collective-permute-done.15.refs_1_
  44.9 0.1 collective-permute-start.16
  45.0 4.6 %collective-permute-done.1.refs_0_ = bf16[256,512]{1,0:T(8,128)(2,1)S(1)} collective-permute-done((bf16[256,512]{1,0:T(8,128)(2,1)S(1)}, bf16[256,512]{1,0:T(8,128)(2,1)S(1)}, u32[]{:S(2)}, u32[]{:S(2)}) %collective-permute-start.1) | collective-permute-done | bytes 262176 | tf_op jit(solution)/shard_map/ppermute | solution.py:395
  49.6 0.0 collective-permute-done.7.refs_1_
  49.6 0.4 collective-permute-done.11.refs_3_.refs_2_.refs_1_
  50.0 1.8 %collective-permute-start.12 = (bf16[512,512]{1,0:T(8,128)(2,1)S(1)}, bf16[512,512]{1,0:T(8,128)(2,1)S(1)}, u32[]{:S(2)}, u32[]{:S(2)}) collective-permute-start(bf16[512,512]{1,0:T(8,128)(2,1)S(1)} %bundle.22.refs_0_.refs_3_), channel_id=1, source_target_pairs={{0,16},{16,0},{1,17},{17,1},{2,18},{18,2},{3,19},{19,3},{4,20},{20... | collective-permute-start | bytes 1572872 | tf_op jit(solution)/shard_map/ppermute | solution.py:395
  51.8 0.1 collective-permute-start.18
  51.9 0.1 bundle.31
  52.0 0.6 collective-permute-start.23
  52.5 0.7 collective-permute-done.18.refs_3_
  53.2 1.5 %collective-permute-start.14 = (bf16[256,512]{1,0:T(8,128)(2,1)S(1)}, bf16[256,512]{1,0:T(8,128)(2,1)S(1)}, u32[]{:S(2)}, u32[]{:S(2)}) collective-permute-start(bf16[256,512]{1,0:T(8,128)(2,1)S(1)} %collective-permute-done.1.refs_0_), channel_id=1, source_target_pairs={{0,2},{2,0},{1,3},{3,1},{4,6},{6,4},{5,7},{7,5},{8,10},{10,8},{9,1... | collective-permute-start | bytes 786440 | tf_op jit(solution)/shard_map/ppermute | solution.py:395
  54.8 5.2 %collective-permute-done.16.refs_1_.refs_2_.refs_0_ = bf16[1088,256]{1,0:T(8,128)(2,1)S(1)} collective-permute-done((bf16[1088,256]{1,0:T(8,128)(2,1)S(1)}, bf16[1088,256]{1,0:T(8,128)(2,1)S(1)}, u32[]{:S(2)}, u32[]{:S(2)}) %collective-permute-start.16) | collective-permute-done | bytes 557088 | tf_op jit(solution)/shard_map/ppermute | solution.py:400
  60.0 0.0 collective-permute-start.21
  60.0 3.8 %collective-permute-done.12.refs_1_.refs_2_ = bf16[512,512]{1,0:T(8,128)(2,1)S(1)} collective-permute-done((bf16[512,512]{1,0:T(8,128)(2,1)S(1)}, bf16[512,512]{1,0:T(8,128)(2,1)S(1)}, u32[]{:S(2)}, u32[]{:S(2)}) %collective-permute-start.12) | collective-permute-done | bytes 524320 | tf_op jit(solution)/shard_map/ppermute | solution.py:395
  63.8 0.0 collective-permute-start.19
  63.8 0.1 bundle.23
  63.9 0.0 collective-permute-done.14.refs_0_.refs_5_
  63.9 0.6 collective-permute-start.13
  64.5 0.9 %collective-permute-done.19.refs_5_ = bf16[544,256]{1,0:T(8,128)(2,1)S(1)} collective-permute-done((bf16[544,256]{1,0:T(8,128)(2,1)S(1)}, bf16[544,256]{1,0:T(8,128)(2,1)S(1)}, u32[]{:S(2)}, u32[]{:S(2)}) %collective-permute-start.19) | collective-permute-done | bytes 278560 | tf_op jit(solution)/shard_map/ppermute | solution.py:395
  65.4 1.5 %collective-permute-start.17 = (bf16[256,512]{1,0:T(8,128)(2,1)S(1)}, bf16[256,512]{1,0:T(8,128)(2,1)S(1)}, u32[]{:S(2)}, u32[]{:S(2)}) collective-permute-start(bf16[256,512]{1,0:T(8,128)(2,1)S(1)} %bundle.25.refs_0_.refs_2_), channel_id=1, source_target_pairs={{0,16},{16,0},{1,17},{17,1},{2,18},{18,2},{3,19},{19,3},{4,20},{20... | collective-permute-start | bytes 786440 | tf_op jit(solution)/shard_map/ppermute | solution.py:395
  66.9 1.3 %adapt_begin.1 = (f32[512,128]{1,0:T(8,128)S(1)}, bf16[512,128]{1,0:T(8,128)(2,1)S(1)}) custom-call(bf16[512,8192]{1,0:T(8,128)(2,1)S(1)} %bitcast.6, bf16[272,256]{1,0:T(8,128)(2,1)S(1)} %get-tuple-element.18.refs_3_.refs_0_, bf16[1360,256]{1,0:T(8,128)(2,1)S(1)} %collective-permute-done.15.refs_1_, ...), custom_call_target="tpu_custom_call" | custom-call | flops 1288490240 | bytes 5033164 | tf_op jit(solution)/shard_map/adapt_begin/pallas_call | solution.py:273
  68.2 0.0 collective-permute-done.20.refs_0_
  68.2 1.5 %base_product.5.refs_3_ = f32[512,512]{1,0:T(8,128)S(1)} custom-call(bf16[512,8192]{1,0:T(8,128)(2,1)S(1)} %bitcast.6, bf16[1024,512]{1,0:T(8,128)(2,1)S(1)} %collective-permute-done.20.refs_0_, bf16[512,512]{1,0:T(8,128)(2,1)S(1)} %bundle.21.refs_1_.refs_0_, bf16[512,512]{1,0:T(8,128)(2,1)S(1)} %collective-permute-done.11.refs_3_.refs_2_.refs_1_, ...), custom_call_target="tpu_custom_call" | custom-call | flops 1342177280 | bytes 6291456 | tf_op jit(solution)/shard_map/base_product/pallas_call | solution.py:211
  69.7 6.7 %collective-permute-done.21.refs_4_.refs_0_.refs_1_ = bf16[1088,256]{1,0:T(8,128)(2,1)S(1)} collective-permute-done((bf16[1088,256]{1,0:T(8,128)(2,1)S(1)}, bf16[1088,256]{1,0:T(8,128)(2,1)S(1)}, u32[]{:S(2)}, u32[]{:S(2)}) %collective-permute-start.21) | collective-permute-done | bytes 557088 | tf_op jit(solution)/shard_map/ppermute | solution.py:400
  76.4 0.0 collective-permute-done.17.refs_1_
  76.4 0.1 collective-permute-start.22
  76.5 1.1 %base_product.6.refs_3_ = f32[512,512]{1,0:T(8,128)S(1)} custom-call(bf16[512,8192]{1,0:T(8,128)(2,1)S(1)} %bitcast.6, bf16[1024,512]{1,0:T(8,128)(2,1)S(1)} %collective-permute-done.23.refs_0_, bf16[512,512]{1,0:T(8,128)(2,1)S(1)} %collective-permute-done.12.refs_1_.refs_2_, bf16[256,512]{1,0:T(8,128)(2,1)S(1)} %bundle.25.refs_0_.refs_2_, ...), custom_call_target="tpu_custom_call" | custom-call | flops 939524096 | bytes 4718592 | tf_op jit(solution)/shard_map/base_product/pallas_call | solution.py:211
  77.7 0.6 collective-permute-start.25
  78.3 0.1 collective-permute-start.24
  78.4 0.1 collective-permute-done.22.refs_2_
  78.4 0.0 collective-permute-done.13.refs_0_
  78.4 1.1 %base_product.7.base_ref = f32[512,512]{1,0:T(8,128)S(1)} custom-call(bf16[512,8192]{1,0:T(8,128)(2,1)S(1)} %bitcast.6, bf16[1024,512]{1,0:T(8,128)(2,1)S(1)} %collective-permute-done.13.refs_0_, bf16[256,512]{1,0:T(8,128)(2,1)S(1)} %collective-permute-done.17.refs_1_, bf16[512,512]{1,0:T(8,128)(2,1)S(1)} %collective-permute-done.22.refs_2_, ...), custom_call_target="tpu_custom_call" | custom-call | flops 939524096 | bytes 4718592 | tf_op jit(solution)/shard_map/base_product/pallas_call | solution.py:211
  79.5 0.0 collective-permute-done.25.refs_3_
  79.6 0.3 collective-permute-done.24.refs_1_
  79.9 2.2 %adapt_end.1 = bf16[512,512]{1,0:T(8,128)(2,1)} custom-call(bf16[512,8192]{1,0:T(8,128)(2,1)S(1)} %bitcast.6, f32[512,128]{1,0:T(8,128)S(1)} %row_mask.1.refs_4_.mask_ref, f32[512,512]{1,0:T(8,128)S(1)} %base_product.7.base_ref, f32[512,128]{1,0:T(8,128)S(1)} %get-tuple-element.24.refs_2_.shrunk, bf16[512,128]{1,0:T(8,128)(2,1)S(1)} %get-tuple-element.26.widened, ...), custom_call_target="tpu_custom_call" | custom-call | flops 858993472 | bytes 3355443 | tf_op jit(solution)/shard_map/adapt_end/pallas_call | solution.py:305
  (27 shorter events, 0.4 us)
Async XLA Ops:
  0.0 13.0 %copy-start = (s32[16,16]{1,0:T(8,128)S(1)}, s32[16,16]{1,0:T(8,128)}, u32[]{:S(2)}) copy-start(s32[16,16]{1,0:T(8,128)} %slots_ref.1) | copy-start | bytes 3076
  0.0 38.9 %slice-start = ((s8[8388608]{0:T(1024)(128)(4,1)}), s8[4194304]{0:T(1024)(128)(4,1)S(1)}, s32[]{:S(2)}) async-start(s8[8388608]{0:T(1024)(128)(4,1)} %bitcast.5), calls=%async_computation | async-start | bytes 8388608
  1.3 17.3 %collective-permute-start = (bf16[256,512]{1,0:T(8,128)(2,1)S(1)}, bf16[256,512]{1,0:T(8,128)(2,1)S(1)}, u32[]{:S(2)}, u32[]{:S(2)}) collective-permute-start(bf16[256,512]{1,0:T(8,128)(2,1)S(1)} %get-tuple-element.16), channel_id=1, source_target_pairs={{0,8},{4,12},{8,0},{12,4},{1,9},{5,13},{9,1},{13,5},{2,10},{6,14},... | collective-permute-start | bytes 786440 | tf_op jit(solution)/shard_map/ppermute | solution.py:395
  5.4 13.2 %collective-permute-start.3 = (bf16[256,512]{1,0:T(8,128)(2,1)S(1)}, bf16[256,512]{1,0:T(8,128)(2,1)S(1)}, u32[]{:S(2)}, u32[]{:S(2)}) collective-permute-start(bf16[256,512]{1,0:T(8,128)(2,1)S(1)} %get-tuple-element.16), channel_id=1, source_target_pairs={{0,4},{4,0},{8,12},{12,8},{1,5},{5,1},{9,13},{13,9},{2,6},{6,2},{1... | collective-permute-start | bytes 786440 | tf_op jit(solution)/shard_map/ppermute | solution.py:395
  7.0 11.6 %collective-permute-start.4 = (bf16[256,512]{1,0:T(8,128)(2,1)S(1)}, bf16[256,512]{1,0:T(8,128)(2,1)S(1)}, u32[]{:S(2)}, u32[]{:S(2)}) collective-permute-start(bf16[256,512]{1,0:T(8,128)(2,1)S(1)} %get-tuple-element.16), channel_id=1, source_target_pairs={{0,2},{2,0},{1,3},{3,1},{4,6},{6,4},{5,7},{7,5},{8,10},{10,8},{9,1... | collective-permute-start | bytes 786440 | tf_op jit(solution)/shard_map/ppermute | solution.py:395
  8.5 0.7 copy-start.1
  9.2 3.8 %copy-start.2 = (s32[1,16]{1,0:T(1,128)S(1)}, s32[1,16]{1,0:T(1,128)}, u32[]{:S(2)}) copy-start(s32[1,16]{1,0:T(1,128)} %lengths_ref.1) | copy-start | bytes 196
  9.2 29.7 %slice-start.1 = ((s8[8388608]{0:T(1024)(128)(4,1)}), s8[4194304]{0:T(1024)(128)(4,1)S(1)}, s32[]{:S(2)}) async-start(s8[8388608]{0:T(1024)(128)(4,1)} %bitcast.5), calls=%async_computation.1 | async-start | bytes 8388608
  12.8 14.9 %collective-permute-start.8 = (bf16[544,256]{1,0:T(8,128)(2,1)S(1)}, bf16[544,256]{1,0:T(8,128)(2,1)S(1)}, u32[]{:S(2)}, u32[]{:S(2)}) collective-permute-start(bf16[544,256]{1,0:T(8,128)(2,1)S(1)} %after.2), channel_id=1, source_target_pairs={{0,1},{1,0},{2,3},{3,2},{4,5},{5,4},{6,7},{7,6},{8,9},{9,8},{10,11... | collective-permute-start | bytes 835592 | tf_op jit(solution)/shard_map/ppermute | solution.py:395
  12.9 14.9 %collective-permute-start.10 = (bf16[544,256]{1,0:T(8,128)(2,1)S(1)}, bf16[544,256]{1,0:T(8,128)(2,1)S(1)}, u32[]{:S(2)}, u32[]{:S(2)}) collective-permute-start(bf16[544,256]{1,0:T(8,128)(2,1)S(1)} %get-tuple-element.21), channel_id=1, source_target_pairs={{0,14},{1,15},{2,12},{3,13},{4,10},{5,11},{6,8},{7,9},{8,6},{9,7},... | collective-permute-start | bytes 835592 | tf_op jit(solution)/shard_map/ppermute | solution.py:400
  18.6 16.5 %collective-permute-start.2 = (bf16[512,512]{1,0:T(8,128)(2,1)S(1)}, bf16[512,512]{1,0:T(8,128)(2,1)S(1)}, u32[]{:S(2)}, u32[]{:S(2)}) collective-permute-start(bf16[512,512]{1,0:T(8,128)(2,1)S(1)} %get-tuple-element.17.refs_0_), channel_id=1, source_target_pairs={{0,1},{1,0},{2,3},{3,2},{4,5},{5,4},{6,7},{7,6},{8,9},{9,8},{10,11... | collective-permute-start | bytes 1572872 | tf_op jit(solution)/shard_map/ppermute | solution.py:395
  18.6 20.3 %collective-permute-start.5 = (bf16[512,512]{1,0:T(8,128)(2,1)S(1)}, bf16[512,512]{1,0:T(8,128)(2,1)S(1)}, u32[]{:S(2)}, u32[]{:S(2)}) collective-permute-start(bf16[512,512]{1,0:T(8,128)(2,1)S(1)} %bundle.17.refs_2_.refs_0_), channel_id=1, source_target_pairs={{0,16},{16,0},{1,17},{17,1},{2,18},{18,2},{3,19},{19,3},{4,20},{20... | collective-permute-start | bytes 1572872 | tf_op jit(solution)/shard_map/ppermute | solution.py:395
  26.1 8.5 %collective-permute-start.6 = (bf16[256,512]{1,0:T(8,128)(2,1)S(1)}, bf16[256,512]{1,0:T(8,128)(2,1)S(1)}, u32[]{:S(2)}, u32[]{:S(2)}) collective-permute-start(bf16[256,512]{1,0:T(8,128)(2,1)S(1)} %bundle.18), channel_id=1, source_target_pairs={{0,2},{2,0},{1,3},{3,1},{4,6},{6,4},{5,7},{7,5},{8,10},{10,8},{9,1... | collective-permute-start | bytes 786440 | tf_op jit(solution)/shard_map/ppermute | solution.py:395
  27.7 17.1 %collective-permute-start.15 = (bf16[1360,256]{1,0:T(8,128)(2,1)S(1)}, bf16[1360,256]{1,0:T(8,128)(2,1)S(1)}, u32[]{:S(2)}, u32[]{:S(2)}) collective-permute-start(bf16[1360,256]{1,0:T(8,128)(2,1)S(1)} %after.3), channel_id=1, source_target_pairs={{0,1},{1,0},{2,3},{3,2},{4,5},{5,4},{6,7},{7,6},{8,9},{9,8},{10,11... | collective-permute-start | bytes 2088968 | tf_op jit(solution)/shard_map/ppermute | solution.py:395
  27.8 14.5 %collective-permute-start.9 = (bf16[1088,256]{1,0:T(8,128)(2,1)S(1)}, bf16[1088,256]{1,0:T(8,128)(2,1)S(1)}, u32[]{:S(2)}, u32[]{:S(2)}) collective-permute-start(bf16[1088,256]{1,0:T(8,128)(2,1)S(1)} %bundle.20), channel_id=1, source_target_pairs={{0,2},{1,9},{2,0},{3,11},{4,6},{5,13},{6,4},{7,15},{8,10},{9,1},{1... | collective-permute-start | bytes 1671176 | tf_op jit(solution)/shard_map/ppermute | solution.py:400
  34.7 15.3 %collective-permute-start.11 = (bf16[512,512]{1,0:T(8,128)(2,1)S(1)}, bf16[512,512]{1,0:T(8,128)(2,1)S(1)}, u32[]{:S(2)}, u32[]{:S(2)}) collective-permute-start(bf16[512,512]{1,0:T(8,128)(2,1)S(1)} %bundle.21.refs_1_.refs_0_), channel_id=1, source_target_pairs={{0,16},{16,0},{1,17},{17,1},{2,18},{18,2},{3,19},{19,3},{4,20},{20... | collective-permute-start | bytes 1572872 | tf_op jit(solution)/shard_map/ppermute | solution.py:395
  35.1 14.5 %collective-permute-start.1 = (bf16[256,512]{1,0:T(8,128)(2,1)S(1)}, bf16[256,512]{1,0:T(8,128)(2,1)S(1)}, u32[]{:S(2)}, u32[]{:S(2)}) collective-permute-start(bf16[256,512]{1,0:T(8,128)(2,1)S(1)} %collective-permute-done.refs_2_.refs_0_), channel_id=1, source_target_pairs={{0,4},{4,0},{8,12},{12,8},{1,5},{5,1},{9,13},{13,9},{2,6},{6,2},{1... | collective-permute-start | bytes 786440 | tf_op jit(solution)/shard_map/ppermute | solution.py:395
  40.2 9.4 %collective-permute-start.7 = (bf16[256,512]{1,0:T(8,128)(2,1)S(1)}, bf16[256,512]{1,0:T(8,128)(2,1)S(1)}, u32[]{:S(2)}, u32[]{:S(2)}) collective-permute-start(bf16[256,512]{1,0:T(8,128)(2,1)S(1)} %bundle.19), channel_id=1, source_target_pairs={{0,2},{2,0},{1,3},{3,1},{4,6},{6,4},{5,7},{7,5},{8,10},{10,8},{9,1... | collective-permute-start | bytes 786440 | tf_op jit(solution)/shard_map/ppermute | solution.py:395
  42.3 25.9 %collective-permute-start.20 = (bf16[1024,512]{1,0:T(8,128)(2,1)S(1)}, bf16[1024,512]{1,0:T(8,128)(2,1)S(1)}, u32[]{:S(2)}, u32[]{:S(2)}) collective-permute-start(bf16[1024,512]{1,0:T(8,128)(2,1)S(1)} %bundle.28), channel_id=1, source_target_pairs={{0,1},{1,0},{2,3},{3,2},{4,5},{5,4},{6,7},{7,6},{8,9},{9,8},{10,11... | collective-permute-start | bytes 3145736 | tf_op jit(solution)/shard_map/ppermute | solution.py:395
  44.9 15.1 %collective-permute-start.16 = (bf16[1088,256]{1,0:T(8,128)(2,1)S(1)}, bf16[1088,256]{1,0:T(8,128)(2,1)S(1)}, u32[]{:S(2)}, u32[]{:S(2)}) collective-permute-start(bf16[1088,256]{1,0:T(8,128)(2,1)S(1)} %bundle.24), channel_id=1, source_target_pairs={{0,12},{1,5},{2,14},{3,7},{4,8},{5,1},{6,10},{7,3},{8,4},{9,13},{1... | collective-permute-start | bytes 1671176 | tf_op jit(solution)/shard_map/ppermute | solution.py:400
  50.0 13.8 %collective-permute-start.12 = (bf16[512,512]{1,0:T(8,128)(2,1)S(1)}, bf16[512,512]{1,0:T(8,128)(2,1)S(1)}, u32[]{:S(2)}, u32[]{:S(2)}) collective-permute-start(bf16[512,512]{1,0:T(8,128)(2,1)S(1)} %bundle.22.refs_0_.refs_3_), channel_id=1, source_target_pairs={{0,16},{16,0},{1,17},{17,1},{2,18},{18,2},{3,19},{19,3},{4,20},{20... | collective-permute-start | bytes 1572872 | tf_op jit(solution)/shard_map/ppermute | solution.py:395
  51.8 1.4 %collective-permute-start.18 = (bf16[272,256]{1,0:T(8,128)(2,1)S(1)}, bf16[272,256]{1,0:T(8,128)(2,1)S(1)}, u32[]{:S(2)}, u32[]{:S(2)}) collective-permute-start(bf16[272,256]{1,0:T(8,128)(2,1)S(1)} %bundle.26), channel_id=1, source_target_pairs={{0,1},{1,0},{2,3},{3,2},{4,5},{5,4},{6,7},{7,6},{8,9},{9,8},{10,11... | collective-permute-start | bytes 417800 | tf_op jit(solution)/shard_map/ppermute | solution.py:395
  52.0 24.6 %collective-permute-start.23 = (bf16[1024,512]{1,0:T(8,128)(2,1)S(1)}, bf16[1024,512]{1,0:T(8,128)(2,1)S(1)}, u32[]{:S(2)}, u32[]{:S(2)}) collective-permute-start(bf16[1024,512]{1,0:T(8,128)(2,1)S(1)} %bundle.31), channel_id=1, source_target_pairs={{0,1},{1,0},{2,3},{3,2},{4,5},{5,4},{6,7},{7,6},{8,9},{9,8},{10,11... | collective-permute-start | bytes 3145736 | tf_op jit(solution)/shard_map/ppermute | solution.py:395
  53.2 10.7 %collective-permute-start.14 = (bf16[256,512]{1,0:T(8,128)(2,1)S(1)}, bf16[256,512]{1,0:T(8,128)(2,1)S(1)}, u32[]{:S(2)}, u32[]{:S(2)}) collective-permute-start(bf16[256,512]{1,0:T(8,128)(2,1)S(1)} %collective-permute-done.1.refs_0_), channel_id=1, source_target_pairs={{0,2},{2,0},{1,3},{3,1},{4,6},{6,4},{5,7},{7,5},{8,10},{10,8},{9,1... | collective-permute-start | bytes 786440 | tf_op jit(solution)/shard_map/ppermute | solution.py:395
  60.0 16.4 %collective-permute-start.21 = (bf16[1088,256]{1,0:T(8,128)(2,1)S(1)}, bf16[1088,256]{1,0:T(8,128)(2,1)S(1)}, u32[]{:S(2)}, u32[]{:S(2)}) collective-permute-start(bf16[1088,256]{1,0:T(8,128)(2,1)S(1)} %bundle.29), channel_id=1, source_target_pairs={{0,6},{1,11},{2,4},{3,9},{4,2},{5,15},{6,0},{7,13},{8,14},{9,3},{1... | collective-permute-start | bytes 1671176 | tf_op jit(solution)/shard_map/ppermute | solution.py:400
  63.8 1.6 %collective-permute-start.19 = (bf16[544,256]{1,0:T(8,128)(2,1)S(1)}, bf16[544,256]{1,0:T(8,128)(2,1)S(1)}, u32[]{:S(2)}, u32[]{:S(2)}) collective-permute-start(bf16[544,256]{1,0:T(8,128)(2,1)S(1)} %bundle.27), channel_id=1, source_target_pairs={{0,1},{1,0},{2,3},{3,2},{4,5},{5,4},{6,7},{7,6},{8,9},{9,8},{10,11... | collective-permute-start | bytes 835592 | tf_op jit(solution)/shard_map/ppermute | solution.py:395
  63.9 14.5 %collective-permute-start.13 = (bf16[1024,512]{1,0:T(8,128)(2,1)S(1)}, bf16[1024,512]{1,0:T(8,128)(2,1)S(1)}, u32[]{:S(2)}, u32[]{:S(2)}) collective-permute-start(bf16[1024,512]{1,0:T(8,128)(2,1)S(1)} %bundle.23), channel_id=1, source_target_pairs={{0,1},{1,0},{2,3},{3,2},{4,5},{5,4},{6,7},{7,6},{8,9},{9,8},{10,11... | collective-permute-start | bytes 3145736 | tf_op jit(solution)/shard_map/ppermute | solution.py:395
  65.4 11.0 %collective-permute-start.17 = (bf16[256,512]{1,0:T(8,128)(2,1)S(1)}, bf16[256,512]{1,0:T(8,128)(2,1)S(1)}, u32[]{:S(2)}, u32[]{:S(2)}) collective-permute-start(bf16[256,512]{1,0:T(8,128)(2,1)S(1)} %bundle.25.refs_0_.refs_2_), channel_id=1, source_target_pairs={{0,16},{16,0},{1,17},{17,1},{2,18},{18,2},{3,19},{19,3},{4,20},{20... | collective-permute-start | bytes 786440 | tf_op jit(solution)/shard_map/ppermute | solution.py:395
  76.4 2.0 %collective-permute-start.22 = (bf16[512,512]{1,0:T(8,128)(2,1)S(1)}, bf16[512,512]{1,0:T(8,128)(2,1)S(1)}, u32[]{:S(2)}, u32[]{:S(2)}) collective-permute-start(bf16[512,512]{1,0:T(8,128)(2,1)S(1)} %bundle.30), channel_id=1, source_target_pairs={{0,1},{1,0},{2,3},{3,2},{4,5},{5,4},{6,7},{7,6},{8,9},{9,8},{10,11... | collective-permute-start | bytes 1572872 | tf_op jit(solution)/shard_map/ppermute | solution.py:395
  77.7 1.9 %collective-permute-start.25 = (bf16[544,256]{1,0:T(8,128)(2,1)S(1)}, bf16[544,256]{1,0:T(8,128)(2,1)S(1)}, u32[]{:S(2)}, u32[]{:S(2)}) collective-permute-start(bf16[544,256]{1,0:T(8,128)(2,1)S(1)} %bundle.33), channel_id=1, source_target_pairs={{0,1},{1,0},{2,3},{3,2},{4,5},{5,4},{6,7},{7,6},{8,9},{9,8},{10,11... | collective-permute-start | bytes 835592 | tf_op jit(solution)/shard_map/ppermute | solution.py:395
  78.3 1.6 %collective-permute-start.24 = (bf16[544,256]{1,0:T(8,128)(2,1)S(1)}, bf16[544,256]{1,0:T(8,128)(2,1)S(1)}, u32[]{:S(2)}, u32[]{:S(2)}) collective-permute-start(bf16[544,256]{1,0:T(8,128)(2,1)S(1)} %bundle.32), channel_id=1, source_target_pairs={{0,1},{1,0},{2,3},{3,2},{4,5},{5,4},{6,7},{7,6},{8,9},{9,8},{10,11... | collective-permute-start | bytes 835592 | tf_op jit(solution)/shard_map/ppermute | solution.py:395

commit v13 on v12

--- a/solution.py
+++ b/solution.py
@@ -31,7 +31,7 @@
 SWAPS = ((0,), (1, 2))
 LAST = ("R2", "R1")
 TIES = {
-    "Y1": ("Y0",),
+    "Y1": ("Y0", "Z2",),
     "Y2": ("B0",),
     "X1": ("Z2", "local", "mask",),
     "X2": ("P7",),
@@ -40,6 +40,7 @@
     "C4": ("AB", "B1", "R2",),
     "B0": ("CW", "Y1",),
     "B1": ("Y3",),
+    "P7": ("Z2",),
     "F0": ("R1",),
     "F1": ("AB", "B2",),
     "F2": ("AB", "B2",),

time: 82.3 us -> 91.4 us (1.11)
  the two profiles are of different devices: /device:TPU:0 before, /device:TPU:11 now
where the time goes in v13:
time: 91.4 us; the launch traced here: 91.3 us
  starting transfers between devices  39 us (43%)
  waiting for transfers between devices  35.8 us (39%)
  Pallas kernels  15.4 us (17%)
    ppermute x22, starting transfers between devices, swap(): return lax.ppermute(block, axis, [(i, i ^ bit) for i in range(size)])  29.8 us
    ppermute x4, waiting for transfers between devices, send_pairs(): lax.ppermute(payload, AXES[1:], [(i, target(i)) for i in range(size)])  20.6 us
    ppermute x22, waiting for transfers between devices, swap(): return lax.ppermute(block, axis, [(i, i ^ bit) for i in range(size)])  15.2 us
    ppermute x4, starting transfers between devices, send_pairs(): lax.ppermute(payload, AXES[1:], [(i, target(i)) for i in range(size)])  9.23 us
    pallas_call x4, Pallas kernels, base_product(): pl.pallas_call(kernel, out_shape=pltpu.VMEM((rows, width), jnp.float32),...  5.01 us
    pallas_call x1, Pallas kernels, make_messages(): pl.pallas_call(kernel, out_shape=[pltpu.VMEM((n * length, HALF), jnp.bflo...  4 us
    pallas_call x1, Pallas kernels, adapt_end(): pl.pallas_call(kernel, out_shape=jax.ShapeDtypeStruct((rows, width), jnp....  2.21 us
  transfers between devices with their start and end apart: 26, of which 10 were waited for; matrix products, arithmetic and copies ran while one was open for 0% of the time, Pallas kernels for 13%

profile of v13, /device:TPU:11, one launch (start us, length us, event | category | flops | bytes accessed | tf_op | source)
XLA Modules:
  0.0 91.3 jit_solution(16931412619849857323)
XLA Ops:
  0.0 1.2 %load_rows.1 = (bf16[512,512]{1,0:T(8,128)(2,1)S(1)}, bf16[256,512]{1,0:T(8,128)(2,1)S(1)}) custom-call(bf16[512,512]{1,0:T(8,128)(2,1)} %source.1), custom_call_target="tpu_custom_call" | custom-call | tf_op jit(solution)/shard_map/load_rows/pallas_call | solution.py:167
  1.2 2.4 %collective-permute-start = (bf16[256,512]{1,0:T(8,128)(2,1)S(1)}, bf16[256,512]{1,0:T(8,128)(2,1)S(1)}, u32[]{:S(2)}, u32[]{:S(2)}) collective-permute-start(bf16[256,512]{1,0:T(8,128)(2,1)S(1)} %get-tuple-element.16), channel_id=1, source_target_pairs={{0,8},{4,12},{8,0},{12,4},{1,9},{5,13},{9,1},{13,5},{2,10},{6,14},... | collective-permute-start | bytes 786440 | tf_op jit(solution)/shard_map/ppermute | solution.py:396
  3.6 0.2 collective-permute-start.3
  3.7 1.2 %collective-permute-start.4 = (bf16[256,512]{1,0:T(8,128)(2,1)S(1)}, bf16[256,512]{1,0:T(8,128)(2,1)S(1)}, u32[]{:S(2)}, u32[]{:S(2)}) collective-permute-start(bf16[256,512]{1,0:T(8,128)(2,1)S(1)} %get-tuple-element.16), channel_id=1, source_target_pairs={{0,2},{2,0},{1,3},{3,1},{4,6},{6,4},{5,7},{7,5},{8,10},{10,8},{9,1... | collective-permute-start | bytes 786440 | tf_op jit(solution)/shard_map/ppermute | solution.py:396
  5.0 0.8 copy-done.1
  5.8 4.0 %make_messages.1 = (bf16[544,256]{1,0:T(8,128)(2,1)S(1)}, bf16[544,256]{1,0:T(8,128)(2,1)S(1)}, bf16[544,256]{1,0:T(8,128)(2,1)S(1)}, bf16[544,256]{1,0:T(8,128)...) custom-call(s32[2,16]{1,0:T(2,128)S(1)} %bitcast.7, ...), custom_call_target="tpu_custom_call" | custom-call | bytes 4456448 | tf_op jit(solution)/shard_map/make_messages/pallas_call | solution.py:134
  9.8 1.6 %collective-permute-start.8 = (bf16[544,256]{1,0:T(8,128)(2,1)S(1)}, bf16[544,256]{1,0:T(8,128)(2,1)S(1)}, u32[]{:S(2)}, u32[]{:S(2)}) collective-permute-start(bf16[544,256]{1,0:T(8,128)(2,1)S(1)} %after.3), channel_id=1, source_target_pairs={{0,1},{1,0},{2,3},{3,2},{4,5},{5,4},{6,7},{7,6},{8,9},{9,8},{10,11... | collective-permute-start | bytes 835592 | tf_op jit(solution)/shard_map/ppermute | solution.py:396
  11.4 3.7 %collective-permute-done.refs_2_.refs_0_.refs_1_ = bf16[256,512]{1,0:T(8,128)(2,1)S(1)} collective-permute-done((bf16[256,512]{1,0:T(8,128)(2,1)S(1)}, bf16[256,512]{1,0:T(8,128)(2,1)S(1)}, u32[]{:S(2)}, u32[]{:S(2)}) %collective-permute-start) | collective-permute-done | bytes 262176 | tf_op jit(solution)/shard_map/ppermute | solution.py:396
  15.1 0.0 collective-permute-done.3.refs_0_
  15.1 0.0 collective-permute-done.4.refs_1_
  15.1 1.3 %collective-permute-start.6 = (bf16[256,512]{1,0:T(8,128)(2,1)S(1)}, bf16[256,512]{1,0:T(8,128)(2,1)S(1)}, u32[]{:S(2)}, u32[]{:S(2)}) collective-permute-start(bf16[256,512]{1,0:T(8,128)(2,1)S(1)} %bundle.18), channel_id=1, source_target_pairs={{0,2},{2,0},{1,3},{3,1},{4,6},{6,4},{5,7},{7,5},{8,10},{10,8},{9,1... | collective-permute-start | bytes 786440 | tf_op jit(solution)/shard_map/ppermute | solution.py:396
  16.4 1.8 %collective-permute-start.2 = (bf16[512,512]{1,0:T(8,128)(2,1)S(1)}, bf16[512,512]{1,0:T(8,128)(2,1)S(1)}, u32[]{:S(2)}, u32[]{:S(2)}) collective-permute-start(bf16[512,512]{1,0:T(8,128)(2,1)S(1)} %get-tuple-element.17.refs_0_), channel_id=1, source_target_pairs={{0,1},{1,0},{2,3},{3,2},{4,5},{5,4},{6,7},{7,6},{8,9},{9,8},{10,11... | collective-permute-start | bytes 1572872 | tf_op jit(solution)/shard_map/ppermute | solution.py:396
  18.3 1.1 %row_mask.1.refs_4_.mask_ref = f32[512,128]{1,0:T(8,128)S(1)} custom-call(s32[1,16]{1,0:T(1,128)S(1)} %copy-done.2, s32[16,16]{1,0:T(8,128)S(1)} %copy-done), custom_call_target="tpu_custom_call" | custom-call | tf_op jit(solution)/shard_map/row_mask/pallas_call | solution.py:375
  19.4 0.3 collective-permute-start.5
  19.7 0.1 collective-permute-start.10
  19.9 0.0 collective-permute-done.8.refs_1_
  19.9 0.6 collective-permute-start.15
  20.5 1.0 %collective-permute-done.6.refs_5_.refs_1_ = bf16[256,512]{1,0:T(8,128)(2,1)S(1)} collective-permute-done((bf16[256,512]{1,0:T(8,128)(2,1)S(1)}, bf16[256,512]{1,0:T(8,128)(2,1)S(1)}, u32[]{:S(2)}, u32[]{:S(2)}) %collective-permute-start.6) | collective-permute-done | bytes 262176 | tf_op jit(solution)/shard_map/ppermute | solution.py:396
  21.4 4.2 %collective-permute-start.9 = (bf16[1088,256]{1,0:T(8,128)(2,1)S(1)}, bf16[1088,256]{1,0:T(8,128)(2,1)S(1)}, u32[]{:S(2)}, u32[]{:S(2)}) collective-permute-start(bf16[1088,256]{1,0:T(8,128)(2,1)S(1)} %bundle.20), channel_id=1, source_target_pairs={{0,2},{1,9},{2,0},{3,11},{4,6},{5,13},{6,4},{7,15},{8,10},{9,1},{1... | collective-permute-start | bytes 1671176 | tf_op jit(solution)/shard_map/ppermute | solution.py:401
  25.7 14.9 %collective-permute-done.10.refs_2_.refs_0_ = bf16[544,256]{1,0:T(8,128)(2,1)S(1)} collective-permute-done((bf16[544,256]{1,0:T(8,128)(2,1)S(1)}, bf16[544,256]{1,0:T(8,128)(2,1)S(1)}, u32[]{:S(2)}, u32[]{:S(2)}) %collective-permute-start.10) | collective-permute-done | bytes 278560 | tf_op jit(solution)/shard_map/ppermute | solution.py:401
  40.6 1.3 %collective-permute-start.11 = (bf16[512,512]{1,0:T(8,128)(2,1)S(1)}, bf16[512,512]{1,0:T(8,128)(2,1)S(1)}, u32[]{:S(2)}, u32[]{:S(2)}) collective-permute-start(bf16[512,512]{1,0:T(8,128)(2,1)S(1)} %bundle.21.refs_1_.refs_0_), channel_id=1, source_target_pairs={{0,16},{16,0},{1,17},{17,1},{2,18},{18,2},{3,19},{19,3},{4,20},{20... | collective-permute-start | bytes 1572872 | tf_op jit(solution)/shard_map/ppermute | solution.py:396
  41.9 0.0 collective-permute-done.2.refs_1_.refs_4_
  41.9 0.0 collective-permute-start.1
  41.9 0.0 collective-permute-done.5.refs_3_.refs_1_
  41.9 1.2 %base_product.4.refs_1_.refs_4_ = f32[512,512]{1,0:T(8,128)S(1)} custom-call(bf16[512,8192]{1,0:T(8,128)(2,1)S(1)} %bitcast.6, bf16[512,512]{1,0:T(8,128)(2,1)S(1)} %get-tuple-element.17.refs_0_, bf16[512,512]{1,0:T(8,128)(2,1)S(1)} %collective-permute-done.2.refs_1_.refs_4_, bf16[512,512]{1,0:T(8,128)(2,1)S(1)} %bundle.17.refs_2_.refs_0_, ...), custom_call_target="tpu_custom_call" | custom-call | flops 1073741824 | bytes 5242880 | tf_op jit(solution)/shard_map/base_product/pallas_call | solution.py:212
  43.2 0.3 collective-permute-start.7
  43.5 0.1 bundle.28
  43.5 0.8 collective-permute-done.9.refs_2_.refs_3_.refs_0_.refs_1_.refs_4_
  44.3 1.7 %collective-permute-start.20 = (bf16[1024,512]{1,0:T(8,128)(2,1)S(1)}, bf16[1024,512]{1,0:T(8,128)(2,1)S(1)}, u32[]{:S(2)}, u32[]{:S(2)}) collective-permute-start(bf16[1024,512]{1,0:T(8,128)(2,1)S(1)} %bundle.28), channel_id=1, source_target_pairs={{0,1},{1,0},{2,3},{3,2},{4,5},{5,4},{6,7},{7,6},{8,9},{9,8},{10,11... | collective-permute-start | bytes 3145736 | tf_op jit(solution)/shard_map/ppermute | solution.py:396
  46.0 0.0 collective-permute-done.15.refs_1_
  46.0 1.8 %collective-permute-start.16 = (bf16[1088,256]{1,0:T(8,128)(2,1)S(1)}, bf16[1088,256]{1,0:T(8,128)(2,1)S(1)}, u32[]{:S(2)}, u32[]{:S(2)}) collective-permute-start(bf16[1088,256]{1,0:T(8,128)(2,1)S(1)} %bundle.24), channel_id=1, source_target_pairs={{0,12},{1,5},{2,14},{3,7},{4,8},{5,1},{6,10},{7,3},{8,4},{9,13},{1... | collective-permute-start | bytes 1671176 | tf_op jit(solution)/shard_map/ppermute | solution.py:401
  47.8 2.9 %collective-permute-done.1.refs_0_ = bf16[256,512]{1,0:T(8,128)(2,1)S(1)} collective-permute-done((bf16[256,512]{1,0:T(8,128)(2,1)S(1)}, bf16[256,512]{1,0:T(8,128)(2,1)S(1)}, u32[]{:S(2)}, u32[]{:S(2)}) %collective-permute-start.1) | collective-permute-done | bytes 262176 | tf_op jit(solution)/shard_map/ppermute | solution.py:396
  50.8 0.0 collective-permute-done.7.refs_1_
  50.8 1.5 %collective-permute-done.11.refs_3_.refs_2_.refs_1_ = bf16[512,512]{1,0:T(8,128)(2,1)S(1)} collective-permute-done((bf16[512,512]{1,0:T(8,128)(2,1)S(1)}, bf16[512,512]{1,0:T(8,128)(2,1)S(1)}, u32[]{:S(2)}, u32[]{:S(2)}) %collective-permute-start.11) | collective-permute-done | bytes 524320 | tf_op jit(solution)/shard_map/ppermute | solution.py:396
  52.3 1.3 %collective-permute-start.12 = (bf16[512,512]{1,0:T(8,128)(2,1)S(1)}, bf16[512,512]{1,0:T(8,128)(2,1)S(1)}, u32[]{:S(2)}, u32[]{:S(2)}) collective-permute-start(bf16[512,512]{1,0:T(8,128)(2,1)S(1)} %bundle.22.refs_0_.refs_3_), channel_id=1, source_target_pairs={{0,16},{16,0},{1,17},{17,1},{2,18},{18,2},{3,19},{19,3},{4,20},{20... | collective-permute-start | bytes 1572872 | tf_op jit(solution)/shard_map/ppermute | solution.py:396
  53.6 3.1 %collective-permute-start.18 = (bf16[272,256]{1,0:T(8,128)(2,1)S(1)}, bf16[272,256]{1,0:T(8,128)(2,1)S(1)}, u32[]{:S(2)}, u32[]{:S(2)}) collective-permute-start(bf16[272,256]{1,0:T(8,128)(2,1)S(1)} %bundle.26), channel_id=1, source_target_pairs={{0,1},{1,0},{2,3},{3,2},{4,5},{5,4},{6,7},{7,6},{8,9},{9,8},{10,11... | collective-permute-start | bytes 417800 | tf_op jit(solution)/shard_map/ppermute | solution.py:396
  56.7 0.1 bundle.31
  56.7 0.1 collective-permute-start.23
  56.8 0.8 collective-permute-done.18.refs_3_
  57.7 0.2 collective-permute-start.14
  57.9 4.9 %collective-permute-done.16.refs_1_.refs_2_.refs_0_ = bf16[1088,256]{1,0:T(8,128)(2,1)S(1)} collective-permute-done((bf16[1088,256]{1,0:T(8,128)(2,1)S(1)}, bf16[1088,256]{1,0:T(8,128)(2,1)S(1)}, u32[]{:S(2)}, u32[]{:S(2)}) %collective-permute-start.16) | collective-permute-done | bytes 557088 | tf_op jit(solution)/shard_map/ppermute | solution.py:401
  62.8 3.1 %collective-permute-start.21 = (bf16[1088,256]{1,0:T(8,128)(2,1)S(1)}, bf16[1088,256]{1,0:T(8,128)(2,1)S(1)}, u32[]{:S(2)}, u32[]{:S(2)}) collective-permute-start(bf16[1088,256]{1,0:T(8,128)(2,1)S(1)} %bundle.29), channel_id=1, source_target_pairs={{0,6},{1,11},{2,4},{3,9},{4,2},{5,15},{6,0},{7,13},{8,14},{9,3},{1... | collective-permute-start | bytes 1671176 | tf_op jit(solution)/shard_map/ppermute | solution.py:401
  65.9 0.0 collective-permute-done.12.refs_1_.refs_2_
  65.9 0.8 collective-permute-start.19
  66.7 0.1 bundle.23
  66.8 0.0 collective-permute-done.14.refs_0_.refs_5_
  66.8 10.2 %collective-permute-start.13 = (bf16[1024,512]{1,0:T(8,128)(2,1)S(1)}, bf16[1024,512]{1,0:T(8,128)(2,1)S(1)}, u32[]{:S(2)}, u32[]{:S(2)}) collective-permute-start(bf16[1024,512]{1,0:T(8,128)(2,1)S(1)} %bundle.23), channel_id=1, source_target_pairs={{0,1},{1,0},{2,3},{3,2},{4,5},{5,4},{6,7},{7,6},{8,9},{9,8},{10,11... | collective-permute-start | bytes 3145736 | tf_op jit(solution)/shard_map/ppermute | solution.py:396
  77.0 0.0 collective-permute-done.19.refs_5_
  77.0 0.1 collective-permute-start.17
  77.1 1.3 %adapt_begin.1 = (f32[512,128]{1,0:T(8,128)S(1)}, bf16[512,128]{1,0:T(8,128)(2,1)S(1)}) custom-call(bf16[512,8192]{1,0:T(8,128)(2,1)S(1)} %bitcast.6, bf16[272,256]{1,0:T(8,128)(2,1)S(1)} %get-tuple-element.18.refs_3_.refs_0_, bf16[1360,256]{1,0:T(8,128)(2,1)S(1)} %collective-permute-done.15.refs_1_, ...), custom_call_target="tpu_custom_call" | custom-call | flops 1288490240 | bytes 5033164 | tf_op jit(solution)/shard_map/adapt_begin/pallas_call | solution.py:274
  78.3 0.0 collective-permute-done.20.refs_0_
  78.4 1.5 %base_product.5.refs_3_ = f32[512,512]{1,0:T(8,128)S(1)} custom-call(bf16[512,8192]{1,0:T(8,128)(2,1)S(1)} %bitcast.6, bf16[1024,512]{1,0:T(8,128)(2,1)S(1)} %collective-permute-done.20.refs_0_, bf16[512,512]{1,0:T(8,128)(2,1)S(1)} %bundle.21.refs_1_.refs_0_, bf16[512,512]{1,0:T(8,128)(2,1)S(1)} %collective-permute-done.11.refs_3_.refs_2_.refs_1_, ...), custom_call_target="tpu_custom_call" | custom-call | flops 1342177280 | bytes 6291456 | tf_op jit(solution)/shard_map/base_product/pallas_call | solution.py:212
  79.9 0.0 collective-permute-done.21.refs_4_.refs_0_.refs_1_
  79.9 5.1 %collective-permute-done.17.refs_1_ = bf16[256,512]{1,0:T(8,128)(2,1)S(1)} collective-permute-done((bf16[256,512]{1,0:T(8,128)(2,1)S(1)}, bf16[256,512]{1,0:T(8,128)(2,1)S(1)}, u32[]{:S(2)}, u32[]{:S(2)}) %collective-permute-start.17) | collective-permute-done | bytes 262176 | tf_op jit(solution)/shard_map/ppermute | solution.py:396
  85.0 0.8 collective-permute-start.22
  85.9 0.0 collective-permute-done.23.refs_0_
  85.9 1.1 %base_product.6.refs_3_ = f32[512,512]{1,0:T(8,128)S(1)} custom-call(bf16[512,8192]{1,0:T(8,128)(2,1)S(1)} %bitcast.6, bf16[1024,512]{1,0:T(8,128)(2,1)S(1)} %collective-permute-done.23.refs_0_, bf16[512,512]{1,0:T(8,128)(2,1)S(1)} %collective-permute-done.12.refs_1_.refs_2_, bf16[256,512]{1,0:T(8,128)(2,1)S(1)} %bundle.25.refs_0_.refs_2_, ...), custom_call_target="tpu_custom_call" | custom-call | flops 939524096 | bytes 4718592 | tf_op jit(solution)/shard_map/base_product/pallas_call | solution.py:212
  87.0 0.1 collective-permute-start.25
  87.1 0.5 collective-permute-start.24
  87.7 0.0 collective-permute-done.22.refs_2_
  87.7 1.1 %base_product.7.base_ref = f32[512,512]{1,0:T(8,128)S(1)} custom-call(bf16[512,8192]{1,0:T(8,128)(2,1)S(1)} %bitcast.6, bf16[1024,512]{1,0:T(8,128)(2,1)S(1)} %collective-permute-done.13.refs_0_, bf16[256,512]{1,0:T(8,128)(2,1)S(1)} %collective-permute-done.17.refs_1_, bf16[512,512]{1,0:T(8,128)(2,1)S(1)} %collective-permute-done.22.refs_2_, ...), custom_call_target="tpu_custom_call" | custom-call | flops 939524096 | bytes 4718592 | tf_op jit(solution)/shard_map/base_product/pallas_call | solution.py:212
  88.8 0.0 collective-permute-done.25.refs_3_
  88.8 0.2 collective-permute-done.24.refs_1_
  89.1 2.2 %adapt_end.1 = bf16[512,512]{1,0:T(8,128)(2,1)} custom-call(bf16[512,8192]{1,0:T(8,128)(2,1)S(1)} %bitcast.6, f32[512,128]{1,0:T(8,128)S(1)} %row_mask.1.refs_4_.mask_ref, f32[512,512]{1,0:T(8,128)S(1)} %base_product.7.base_ref, f32[512,128]{1,0:T(8,128)S(1)} %get-tuple-element.24.refs_2_.shrunk, bf16[512,128]{1,0:T(8,128)(2,1)S(1)} %get-tuple-element.26.widened, ...), custom_call_target="tpu_custom_call" | custom-call | flops 858993472 | bytes 3355443 | tf_op jit(solution)/shard_map/adapt_end/pallas_call | solution.py:306
  (28 shorter events, 0.4 us)
Async XLA Ops:
  0.0 18.2 %copy-start.2 = (s32[1,16]{1,0:T(1,128)S(1)}, s32[1,16]{1,0:T(1,128)}, u32[]{:S(2)}) copy-start(s32[1,16]{1,0:T(1,128)} %lengths_ref.1) | copy-start | bytes 196
  0.0 18.3 %copy-start = (s32[16,16]{1,0:T(8,128)S(1)}, s32[16,16]{1,0:T(8,128)}, u32[]{:S(2)}) copy-start(s32[16,16]{1,0:T(8,128)} %slots_ref.1) | copy-start | bytes 3076
  1.2 13.9 %collective-permute-start = (bf16[256,512]{1,0:T(8,128)(2,1)S(1)}, bf16[256,512]{1,0:T(8,128)(2,1)S(1)}, u32[]{:S(2)}, u32[]{:S(2)}) collective-permute-start(bf16[256,512]{1,0:T(8,128)(2,1)S(1)} %get-tuple-element.16), channel_id=1, source_target_pairs={{0,8},{4,12},{8,0},{12,4},{1,9},{5,13},{9,1},{13,5},{2,10},{6,14},... | collective-permute-start | bytes 786440 | tf_op jit(solution)/shard_map/ppermute | solution.py:396
  3.6 11.5 %collective-permute-start.3 = (bf16[256,512]{1,0:T(8,128)(2,1)S(1)}, bf16[256,512]{1,0:T(8,128)(2,1)S(1)}, u32[]{:S(2)}, u32[]{:S(2)}) collective-permute-start(bf16[256,512]{1,0:T(8,128)(2,1)S(1)} %get-tuple-element.16), channel_id=1, source_target_pairs={{0,4},{4,0},{8,12},{12,8},{1,5},{5,1},{9,13},{13,9},{2,6},{6,2},{1... | collective-permute-start | bytes 786440 | tf_op jit(solution)/shard_map/ppermute | solution.py:396
  3.7 11.4 %collective-permute-start.4 = (bf16[256,512]{1,0:T(8,128)(2,1)S(1)}, bf16[256,512]{1,0:T(8,128)(2,1)S(1)}, u32[]{:S(2)}, u32[]{:S(2)}) collective-permute-start(bf16[256,512]{1,0:T(8,128)(2,1)S(1)} %get-tuple-element.16), channel_id=1, source_target_pairs={{0,2},{2,0},{1,3},{3,1},{4,6},{6,4},{5,7},{7,5},{8,10},{10,8},{9,1... | collective-permute-start | bytes 786440 | tf_op jit(solution)/shard_map/ppermute | solution.py:396
  5.0 36.9 %slice-start = ((s8[8388608]{0:T(1024)(128)(4,1)}), s8[4194304]{0:T(1024)(128)(4,1)S(1)}, s32[]{:S(2)}) async-start(s8[8388608]{0:T(1024)(128)(4,1)} %bitcast.5), calls=%async_computation | async-start | bytes 8388608
  5.0 0.8 copy-start.1
  5.8 36.1 %slice-start.1 = ((s8[8388608]{0:T(1024)(128)(4,1)}), s8[4194304]{0:T(1024)(128)(4,1)S(1)}, s32[]{:S(2)}) async-start(s8[8388608]{0:T(1024)(128)(4,1)} %bitcast.5), calls=%async_computation.1 | async-start | bytes 8388608
  9.8 10.0 %collective-permute-start.8 = (bf16[544,256]{1,0:T(8,128)(2,1)S(1)}, bf16[544,256]{1,0:T(8,128)(2,1)S(1)}, u32[]{:S(2)}, u32[]{:S(2)}) collective-permute-start(bf16[544,256]{1,0:T(8,128)(2,1)S(1)} %after.3), channel_id=1, source_target_pairs={{0,1},{1,0},{2,3},{3,2},{4,5},{5,4},{6,7},{7,6},{8,9},{9,8},{10,11... | collective-permute-start | bytes 835592 | tf_op jit(solution)/shard_map/ppermute | solution.py:396
  15.1 6.3 %collective-permute-start.6 = (bf16[256,512]{1,0:T(8,128)(2,1)S(1)}, bf16[256,512]{1,0:T(8,128)(2,1)S(1)}, u32[]{:S(2)}, u32[]{:S(2)}) collective-permute-start(bf16[256,512]{1,0:T(8,128)(2,1)S(1)} %bundle.18), channel_id=1, source_target_pairs={{0,2},{2,0},{1,3},{3,1},{4,6},{6,4},{5,7},{7,5},{8,10},{10,8},{9,1... | collective-permute-start | bytes 786440 | tf_op jit(solution)/shard_map/ppermute | solution.py:396
  16.4 25.4 %collective-permute-start.2 = (bf16[512,512]{1,0:T(8,128)(2,1)S(1)}, bf16[512,512]{1,0:T(8,128)(2,1)S(1)}, u32[]{:S(2)}, u32[]{:S(2)}) collective-permute-start(bf16[512,512]{1,0:T(8,128)(2,1)S(1)} %get-tuple-element.17.refs_0_), channel_id=1, source_target_pairs={{0,1},{1,0},{2,3},{3,2},{4,5},{5,4},{6,7},{7,6},{8,9},{9,8},{10,11... | collective-permute-start | bytes 1572872 | tf_op jit(solution)/shard_map/ppermute | solution.py:396
  19.4 22.4 %collective-permute-start.5 = (bf16[512,512]{1,0:T(8,128)(2,1)S(1)}, bf16[512,512]{1,0:T(8,128)(2,1)S(1)}, u32[]{:S(2)}, u32[]{:S(2)}) collective-permute-start(bf16[512,512]{1,0:T(8,128)(2,1)S(1)} %bundle.17.refs_2_.refs_0_), channel_id=1, source_target_pairs={{0,16},{16,0},{1,17},{17,1},{2,18},{18,2},{3,19},{19,3},{4,20},{20... | collective-permute-start | bytes 1572872 | tf_op jit(solution)/shard_map/ppermute | solution.py:396
  19.7 20.8 %collective-permute-start.10 = (bf16[544,256]{1,0:T(8,128)(2,1)S(1)}, bf16[544,256]{1,0:T(8,128)(2,1)S(1)}, u32[]{:S(2)}, u32[]{:S(2)}) collective-permute-start(bf16[544,256]{1,0:T(8,128)(2,1)S(1)} %after.4), channel_id=1, source_target_pairs={{0,14},{1,15},{2,12},{3,13},{4,10},{5,11},{6,8},{7,9},{8,6},{9,7},... | collective-permute-start | bytes 835592 | tf_op jit(solution)/shard_map/ppermute | solution.py:401
  19.9 26.1 %collective-permute-start.15 = (bf16[1360,256]{1,0:T(8,128)(2,1)S(1)}, bf16[1360,256]{1,0:T(8,128)(2,1)S(1)}, u32[]{:S(2)}, u32[]{:S(2)}) collective-permute-start(bf16[1360,256]{1,0:T(8,128)(2,1)S(1)} %after.5), channel_id=1, source_target_pairs={{0,1},{1,0},{2,3},{3,2},{4,5},{5,4},{6,7},{7,6},{8,9},{9,8},{10,11... | collective-permute-start | bytes 2088968 | tf_op jit(solution)/shard_map/ppermute | solution.py:396
  21.4 22.9 %collective-permute-start.9 = (bf16[1088,256]{1,0:T(8,128)(2,1)S(1)}, bf16[1088,256]{1,0:T(8,128)(2,1)S(1)}, u32[]{:S(2)}, u32[]{:S(2)}) collective-permute-start(bf16[1088,256]{1,0:T(8,128)(2,1)S(1)} %bundle.20), channel_id=1, source_target_pairs={{0,2},{1,9},{2,0},{3,11},{4,6},{5,13},{6,4},{7,15},{8,10},{9,1},{1... | collective-permute-start | bytes 1671176 | tf_op jit(solution)/shard_map/ppermute | solution.py:401
  40.6 11.7 %collective-permute-start.11 = (bf16[512,512]{1,0:T(8,128)(2,1)S(1)}, bf16[512,512]{1,0:T(8,128)(2,1)S(1)}, u32[]{:S(2)}, u32[]{:S(2)}) collective-permute-start(bf16[512,512]{1,0:T(8,128)(2,1)S(1)} %bundle.21.refs_1_.refs_0_), channel_id=1, source_target_pairs={{0,16},{16,0},{1,17},{17,1},{2,18},{18,2},{3,19},{19,3},{4,20},{20... | collective-permute-start | bytes 1572872 | tf_op jit(solution)/shard_map/ppermute | solution.py:396
  41.9 8.9 %collective-permute-start.1 = (bf16[256,512]{1,0:T(8,128)(2,1)S(1)}, bf16[256,512]{1,0:T(8,128)(2,1)S(1)}, u32[]{:S(2)}, u32[]{:S(2)}) collective-permute-start(bf16[256,512]{1,0:T(8,128)(2,1)S(1)} %collective-permute-done.refs_2_.refs_0_.refs_1_), channel_id=1, source_target_pairs={{0,4},{4,0},{8,12},{12,8},{1,5},{5,1},{9,13},{13,9},{2,6},{6,2},{1... | collective-permute-start | bytes 786440 | tf_op jit(solution)/shard_map/ppermute | solution.py:396
  43.2 7.6 %collective-permute-start.7 = (bf16[256,512]{1,0:T(8,128)(2,1)S(1)}, bf16[256,512]{1,0:T(8,128)(2,1)S(1)}, u32[]{:S(2)}, u32[]{:S(2)}) collective-permute-start(bf16[256,512]{1,0:T(8,128)(2,1)S(1)} %bundle.19), channel_id=1, source_target_pairs={{0,2},{2,0},{1,3},{3,1},{4,6},{6,4},{5,7},{7,5},{8,10},{10,8},{9,1... | collective-permute-start | bytes 786440 | tf_op jit(solution)/shard_map/ppermute | solution.py:396
  44.3 34.0 %collective-permute-start.20 = (bf16[1024,512]{1,0:T(8,128)(2,1)S(1)}, bf16[1024,512]{1,0:T(8,128)(2,1)S(1)}, u32[]{:S(2)}, u32[]{:S(2)}) collective-permute-start(bf16[1024,512]{1,0:T(8,128)(2,1)S(1)} %bundle.28), channel_id=1, source_target_pairs={{0,1},{1,0},{2,3},{3,2},{4,5},{5,4},{6,7},{7,6},{8,9},{9,8},{10,11... | collective-permute-start | bytes 3145736 | tf_op jit(solution)/shard_map/ppermute | solution.py:396
  46.0 16.8 %collective-permute-start.16 = (bf16[1088,256]{1,0:T(8,128)(2,1)S(1)}, bf16[1088,256]{1,0:T(8,128)(2,1)S(1)}, u32[]{:S(2)}, u32[]{:S(2)}) collective-permute-start(bf16[1088,256]{1,0:T(8,128)(2,1)S(1)} %bundle.24), channel_id=1, source_target_pairs={{0,12},{1,5},{2,14},{3,7},{4,8},{5,1},{6,10},{7,3},{8,4},{9,13},{1... | collective-permute-start | bytes 1671176 | tf_op jit(solution)/shard_map/ppermute | solution.py:401
  52.3 13.6 %collective-permute-start.12 = (bf16[512,512]{1,0:T(8,128)(2,1)S(1)}, bf16[512,512]{1,0:T(8,128)(2,1)S(1)}, u32[]{:S(2)}, u32[]{:S(2)}) collective-permute-start(bf16[512,512]{1,0:T(8,128)(2,1)S(1)} %bundle.22.refs_0_.refs_3_), channel_id=1, source_target_pairs={{0,16},{16,0},{1,17},{17,1},{2,18},{18,2},{3,19},{19,3},{4,20},{20... | collective-permute-start | bytes 1572872 | tf_op jit(solution)/shard_map/ppermute | solution.py:396
  53.6 4.1 %collective-permute-start.18 = (bf16[272,256]{1,0:T(8,128)(2,1)S(1)}, bf16[272,256]{1,0:T(8,128)(2,1)S(1)}, u32[]{:S(2)}, u32[]{:S(2)}) collective-permute-start(bf16[272,256]{1,0:T(8,128)(2,1)S(1)} %bundle.26), channel_id=1, source_target_pairs={{0,1},{1,0},{2,3},{3,2},{4,5},{5,4},{6,7},{7,6},{8,9},{9,8},{10,11... | collective-permute-start | bytes 417800 | tf_op jit(solution)/shard_map/ppermute | solution.py:396
  56.7 29.1 %collective-permute-start.23 = (bf16[1024,512]{1,0:T(8,128)(2,1)S(1)}, bf16[1024,512]{1,0:T(8,128)(2,1)S(1)}, u32[]{:S(2)}, u32[]{:S(2)}) collective-permute-start(bf16[1024,512]{1,0:T(8,128)(2,1)S(1)} %bundle.31), channel_id=1, source_target_pairs={{0,1},{1,0},{2,3},{3,2},{4,5},{5,4},{6,7},{7,6},{8,9},{9,8},{10,11... | collective-permute-start | bytes 3145736 | tf_op jit(solution)/shard_map/ppermute | solution.py:396
  57.7 9.1 %collective-permute-start.14 = (bf16[256,512]{1,0:T(8,128)(2,1)S(1)}, bf16[256,512]{1,0:T(8,128)(2,1)S(1)}, u32[]{:S(2)}, u32[]{:S(2)}) collective-permute-start(bf16[256,512]{1,0:T(8,128)(2,1)S(1)} %collective-permute-done.1.refs_0_), channel_id=1, source_target_pairs={{0,2},{2,0},{1,3},{3,1},{4,6},{6,4},{5,7},{7,5},{8,10},{10,8},{9,1... | collective-permute-start | bytes 786440 | tf_op jit(solution)/shard_map/ppermute | solution.py:396
  62.8 17.1 %collective-permute-start.21 = (bf16[1088,256]{1,0:T(8,128)(2,1)S(1)}, bf16[1088,256]{1,0:T(8,128)(2,1)S(1)}, u32[]{:S(2)}, u32[]{:S(2)}) collective-permute-start(bf16[1088,256]{1,0:T(8,128)(2,1)S(1)} %bundle.29), channel_id=1, source_target_pairs={{0,6},{1,11},{2,4},{3,9},{4,2},{5,15},{6,0},{7,13},{8,14},{9,3},{1... | collective-permute-start | bytes 1671176 | tf_op jit(solution)/shard_map/ppermute | solution.py:401
  65.9 11.0 %collective-permute-start.19 = (bf16[544,256]{1,0:T(8,128)(2,1)S(1)}, bf16[544,256]{1,0:T(8,128)(2,1)S(1)}, u32[]{:S(2)}, u32[]{:S(2)}) collective-permute-start(bf16[544,256]{1,0:T(8,128)(2,1)S(1)} %bundle.27), channel_id=1, source_target_pairs={{0,1},{1,0},{2,3},{3,2},{4,5},{5,4},{6,7},{7,6},{8,9},{9,8},{10,11... | collective-permute-start | bytes 835592 | tf_op jit(solution)/shard_map/ppermute | solution.py:396
  66.8 20.9 %collective-permute-start.13 = (bf16[1024,512]{1,0:T(8,128)(2,1)S(1)}, bf16[1024,512]{1,0:T(8,128)(2,1)S(1)}, u32[]{:S(2)}, u32[]{:S(2)}) collective-permute-start(bf16[1024,512]{1,0:T(8,128)(2,1)S(1)} %bundle.23), channel_id=1, source_target_pairs={{0,1},{1,0},{2,3},{3,2},{4,5},{5,4},{6,7},{7,6},{8,9},{9,8},{10,11... | collective-permute-start | bytes 3145736 | tf_op jit(solution)/shard_map/ppermute | solution.py:396
  77.0 8.0 %collective-permute-start.17 = (bf16[256,512]{1,0:T(8,128)(2,1)S(1)}, bf16[256,512]{1,0:T(8,128)(2,1)S(1)}, u32[]{:S(2)}, u32[]{:S(2)}) collective-permute-start(bf16[256,512]{1,0:T(8,128)(2,1)S(1)} %bundle.25.refs_0_.refs_2_), channel_id=1, source_target_pairs={{0,16},{16,0},{1,17},{17,1},{2,18},{18,2},{3,19},{19,3},{4,20},{20... | collective-permute-start | bytes 786440 | tf_op jit(solution)/shard_map/ppermute | solution.py:396
  85.0 2.7 %collective-permute-start.22 = (bf16[512,512]{1,0:T(8,128)(2,1)S(1)}, bf16[512,512]{1,0:T(8,128)(2,1)S(1)}, u32[]{:S(2)}, u32[]{:S(2)}) collective-permute-start(bf16[512,512]{1,0:T(8,128)(2,1)S(1)} %bundle.30), channel_id=1, source_target_pairs={{0,1},{1,0},{2,3},{3,2},{4,5},{5,4},{6,7},{7,6},{8,9},{9,8},{10,11... | collective-permute-start | bytes 1572872 | tf_op jit(solution)/shard_map/ppermute | solution.py:396
  87.0 1.8 %collective-permute-start.25 = (bf16[544,256]{1,0:T(8,128)(2,1)S(1)}, bf16[544,256]{1,0:T(8,128)(2,1)S(1)}, u32[]{:S(2)}, u32[]{:S(2)}) collective-permute-start(bf16[544,256]{1,0:T(8,128)(2,1)S(1)} %bundle.33), channel_id=1, source_target_pairs={{0,1},{1,0},{2,3},{3,2},{4,5},{5,4},{6,7},{7,6},{8,9},{9,8},{10,11... | collective-permute-start | bytes 835592 | tf_op jit(solution)/shard_map/ppermute | solution.py:396
  87.1 1.9 %collective-permute-start.24 = (bf16[544,256]{1,0:T(8,128)(2,1)S(1)}, bf16[544,256]{1,0:T(8,128)(2,1)S(1)}, u32[]{:S(2)}, u32[]{:S(2)}) collective-permute-start(bf16[544,256]{1,0:T(8,128)(2,1)S(1)} %bundle.32), channel_id=1, source_target_pairs={{0,1},{1,0},{2,3},{3,2},{4,5},{5,4},{6,7},{7,6},{8,9},{9,8},{10,11... | collective-permute-start | bytes 835592 | tf_op jit(solution)/shard_map/ppermute | solution.py:396

commit v14 on v13

--- a/solution.py
+++ b/solution.py
@@ -47,6 +47,7 @@
     "R1": ("P7", "R0",),
     "R2": ("P7",),
     "T1": ("T0",),
+    "R0": ("P7",),
 }
 
 

time: 91.4 us -> 89.1 us (0.975)
  the two profiles are of different devices: /device:TPU:11 before, /device:TPU:9 now
where the time goes in v14:
time: 89.1 us; the launch traced here: 88.9 us
  starting transfers between devices  43.1 us (48%)
  waiting for transfers between devices  29.4 us (33%)
  Pallas kernels  15.4 us (17%)
    ppermute x22, starting transfers between devices, swap(): return lax.ppermute(block, axis, [(i, i ^ bit) for i in range(size)])  32 us
    ppermute x22, waiting for transfers between devices, swap(): return lax.ppermute(block, axis, [(i, i ^ bit) for i in range(size)])  19.5 us
    ppermute x4, starting transfers between devices, send_pairs(): lax.ppermute(payload, AXES[1:], [(i, target(i)) for i in range(size)])  11 us
    ppermute x4, waiting for transfers between devices, send_pairs(): lax.ppermute(payload, AXES[1:], [(i, target(i)) for i in range(size)])  9.86 us
    pallas_call x4, Pallas kernels, base_product(): pl.pallas_call(kernel, out_shape=pltpu.VMEM((rows, width), jnp.float32),...  4.99 us
    pallas_call x1, Pallas kernels, make_messages(): pl.pallas_call(kernel, out_shape=[pltpu.VMEM((n * length, HALF), jnp.bflo...  4 us
    pallas_call x1, Pallas kernels, adapt_end(): pl.pallas_call(kernel, out_shape=jax.ShapeDtypeStruct((rows, width), jnp....  2.2 us
  transfers between devices with their start and end apart: 26, of which 7 were waited for; matrix products, arithmetic and copies ran while one was open for 0% of the time, Pallas kernels for 13%

profile of v14, /device:TPU:9, one launch (start us, length us, event | category | flops | bytes accessed | tf_op | source)
XLA Modules:
  0.0 88.9 jit_solution(18007616611922836464)
XLA Ops:
  0.0 1.2 %load_rows.1 = (bf16[512,512]{1,0:T(8,128)(2,1)S(1)}, bf16[256,512]{1,0:T(8,128)(2,1)S(1)}) custom-call(bf16[512,512]{1,0:T(8,128)(2,1)} %source.1), custom_call_target="tpu_custom_call" | custom-call | tf_op jit(solution)/shard_map/load_rows/pallas_call | solution.py:168
  1.2 2.4 %collective-permute-start = (bf16[256,512]{1,0:T(8,128)(2,1)S(1)}, bf16[256,512]{1,0:T(8,128)(2,1)S(1)}, u32[]{:S(2)}, u32[]{:S(2)}) collective-permute-start(bf16[256,512]{1,0:T(8,128)(2,1)S(1)} %get-tuple-element.16), channel_id=1, source_target_pairs={{0,8},{4,12},{8,0},{12,4},{1,9},{5,13},{9,1},{13,5},{2,10},{6,14},... | collective-permute-start | bytes 786440 | tf_op jit(solution)/shard_map/ppermute | solution.py:397
  3.6 0.2 collective-permute-start.3
  3.7 1.2 %collective-permute-start.4 = (bf16[256,512]{1,0:T(8,128)(2,1)S(1)}, bf16[256,512]{1,0:T(8,128)(2,1)S(1)}, u32[]{:S(2)}, u32[]{:S(2)}) collective-permute-start(bf16[256,512]{1,0:T(8,128)(2,1)S(1)} %get-tuple-element.16), channel_id=1, source_target_pairs={{0,2},{2,0},{1,3},{3,1},{4,6},{6,4},{5,7},{7,5},{8,10},{10,8},{9,1... | collective-permute-start | bytes 786440 | tf_op jit(solution)/shard_map/ppermute | solution.py:397
  5.0 1.5 %collective-permute-start.2 = (bf16[512,512]{1,0:T(8,128)(2,1)S(1)}, bf16[512,512]{1,0:T(8,128)(2,1)S(1)}, u32[]{:S(2)}, u32[]{:S(2)}) collective-permute-start(bf16[512,512]{1,0:T(8,128)(2,1)S(1)} %get-tuple-element.17.refs_0_), channel_id=1, source_target_pairs={{0,1},{1,0},{2,3},{3,2},{4,5},{5,4},{6,7},{7,6},{8,9},{9,8},{10,11... | collective-permute-start | bytes 1572872 | tf_op jit(solution)/shard_map/ppermute | solution.py:397
  6.5 0.8 copy-done.1
  7.3 4.0 %make_messages.1 = (bf16[544,256]{1,0:T(8,128)(2,1)S(1)}, bf16[544,256]{1,0:T(8,128)(2,1)S(1)}, bf16[544,256]{1,0:T(8,128)(2,1)S(1)}, bf16[544,256]{1,0:T(8,128)...) custom-call(s32[2,16]{1,0:T(2,128)S(1)} %bitcast.7, ...), custom_call_target="tpu_custom_call" | custom-call | bytes 4456448 | tf_op jit(solution)/shard_map/make_messages/pallas_call | solution.py:135
  11.3 0.1 collective-permute-start.8
  11.4 1.1 %row_mask.1.refs_4_.mask_ref = f32[512,128]{1,0:T(8,128)S(1)} custom-call(s32[1,16]{1,0:T(1,128)S(1)} %copy-done.2, s32[16,16]{1,0:T(8,128)S(1)} %copy-done), custom_call_target="tpu_custom_call" | custom-call | tf_op jit(solution)/shard_map/row_mask/pallas_call | solution.py:376
  12.6 2.5 %collective-permute-done.refs_2_.refs_0_.refs_1_ = bf16[256,512]{1,0:T(8,128)(2,1)S(1)} collective-permute-done((bf16[256,512]{1,0:T(8,128)(2,1)S(1)}, bf16[256,512]{1,0:T(8,128)(2,1)S(1)}, u32[]{:S(2)}, u32[]{:S(2)}) %collective-permute-start) | collective-permute-done | bytes 262176 | tf_op jit(solution)/shard_map/ppermute | solution.py:397
  15.1 0.0 collective-permute-done.3.refs_0_
  15.1 0.0 collective-permute-done.4.refs_1_
  15.1 1.3 %collective-permute-start.5 = (bf16[512,512]{1,0:T(8,128)(2,1)S(1)}, bf16[512,512]{1,0:T(8,128)(2,1)S(1)}, u32[]{:S(2)}, u32[]{:S(2)}) collective-permute-start(bf16[512,512]{1,0:T(8,128)(2,1)S(1)} %bundle.17.refs_2_.refs_0_), channel_id=1, source_target_pairs={{0,16},{16,0},{1,17},{17,1},{2,18},{18,2},{3,19},{19,3},{4,20},{20... | collective-permute-start | bytes 1572872 | tf_op jit(solution)/shard_map/ppermute | solution.py:397
  16.4 1.2 %collective-permute-start.9 = (bf16[544,256]{1,0:T(8,128)(2,1)S(1)}, bf16[544,256]{1,0:T(8,128)(2,1)S(1)}, u32[]{:S(2)}, u32[]{:S(2)}) collective-permute-start(bf16[544,256]{1,0:T(8,128)(2,1)S(1)} %after.4), channel_id=1, source_target_pairs={{0,14},{1,15},{2,12},{3,13},{4,10},{5,11},{6,8},{7,9},{8,6},{9,7},... | collective-permute-start | bytes 835592 | tf_op jit(solution)/shard_map/ppermute | solution.py:402
  17.6 0.3 collective-permute-start.6
  17.9 0.0 collective-permute-done.8.refs_1_
  17.9 2.3 %collective-permute-start.15 = (bf16[1360,256]{1,0:T(8,128)(2,1)S(1)}, bf16[1360,256]{1,0:T(8,128)(2,1)S(1)}, u32[]{:S(2)}, u32[]{:S(2)}) collective-permute-start(bf16[1360,256]{1,0:T(8,128)(2,1)S(1)} %after.5), channel_id=1, source_target_pairs={{0,1},{1,0},{2,3},{3,2},{4,5},{5,4},{6,7},{7,6},{8,9},{9,8},{10,11... | collective-permute-start | bytes 2088968 | tf_op jit(solution)/shard_map/ppermute | solution.py:397
  20.2 9.9 %collective-permute-done.9.refs_2_.refs_0_ = bf16[544,256]{1,0:T(8,128)(2,1)S(1)} collective-permute-done((bf16[544,256]{1,0:T(8,128)(2,1)S(1)}, bf16[544,256]{1,0:T(8,128)(2,1)S(1)}, u32[]{:S(2)}, u32[]{:S(2)}) %collective-permute-start.9) | collective-permute-done | bytes 278560 | tf_op jit(solution)/shard_map/ppermute | solution.py:402
  30.1 0.1 collective-permute-start.10
  30.2 0.0 collective-permute-done.6.refs_5_.refs_1_
  30.3 0.3 collective-permute-start.11
  30.6 0.0 collective-permute-done.2.refs_1_.refs_4_
  30.6 4.2 %collective-permute-start.1 = (bf16[256,512]{1,0:T(8,128)(2,1)S(1)}, bf16[256,512]{1,0:T(8,128)(2,1)S(1)}, u32[]{:S(2)}, u32[]{:S(2)}) collective-permute-start(bf16[256,512]{1,0:T(8,128)(2,1)S(1)} %collective-permute-done.refs_2_.refs_0_.refs_1_), channel_id=1, source_target_pairs={{0,4},{4,0},{8,12},{12,8},{1,5},{5,1},{9,13},{13,9},{2,6},{6,2},{1... | collective-permute-start | bytes 786440 | tf_op jit(solution)/shard_map/ppermute | solution.py:397
  34.8 0.0 collective-permute-done.5.refs_3_.refs_1_
  34.9 1.2 %base_product.4.refs_1_.refs_4_ = f32[512,512]{1,0:T(8,128)S(1)} custom-call(bf16[512,8192]{1,0:T(8,128)(2,1)S(1)} %bitcast.6, bf16[512,512]{1,0:T(8,128)(2,1)S(1)} %get-tuple-element.17.refs_0_, bf16[512,512]{1,0:T(8,128)(2,1)S(1)} %collective-permute-done.2.refs_1_.refs_4_, bf16[512,512]{1,0:T(8,128)(2,1)S(1)} %bundle.17.refs_2_.refs_0_, ...), custom_call_target="tpu_custom_call" | custom-call | flops 1073741824 | bytes 5242880 | tf_op jit(solution)/shard_map/base_product/pallas_call | solution.py:213
  36.1 0.3 collective-permute-start.7
  36.5 0.1 bundle.28
  36.5 8.1 %collective-permute-done.1.refs_0_ = bf16[256,512]{1,0:T(8,128)(2,1)S(1)} collective-permute-done((bf16[256,512]{1,0:T(8,128)(2,1)S(1)}, bf16[256,512]{1,0:T(8,128)(2,1)S(1)}, u32[]{:S(2)}, u32[]{:S(2)}) %collective-permute-start.1) | collective-permute-done | bytes 262176 | tf_op jit(solution)/shard_map/ppermute | solution.py:397
  44.6 0.8 collective-permute-start.20
  45.4 0.0 collective-permute-done.7.refs_1_
  45.4 0.0 collective-permute-done.11.refs_3_.refs_2_.refs_1_
  45.5 1.3 %collective-permute-start.12 = (bf16[512,512]{1,0:T(8,128)(2,1)S(1)}, bf16[512,512]{1,0:T(8,128)(2,1)S(1)}, u32[]{:S(2)}, u32[]{:S(2)}) collective-permute-start(bf16[512,512]{1,0:T(8,128)(2,1)S(1)} %bundle.22.refs_0_.refs_3_), channel_id=1, source_target_pairs={{0,16},{16,0},{1,17},{17,1},{2,18},{18,2},{3,19},{19,3},{4,20},{20... | collective-permute-start | bytes 1572872 | tf_op jit(solution)/shard_map/ppermute | solution.py:397
  46.8 0.0 collective-permute-done.15.refs_1_
  46.8 2.3 %collective-permute-start.16 = (bf16[1088,256]{1,0:T(8,128)(2,1)S(1)}, bf16[1088,256]{1,0:T(8,128)(2,1)S(1)}, u32[]{:S(2)}, u32[]{:S(2)}) collective-permute-start(bf16[1088,256]{1,0:T(8,128)(2,1)S(1)} %bundle.24), channel_id=1, source_target_pairs={{0,12},{1,5},{2,14},{3,7},{4,8},{5,1},{6,10},{7,3},{8,4},{9,13},{1... | collective-permute-start | bytes 1671176 | tf_op jit(solution)/shard_map/ppermute | solution.py:402
  49.1 0.1 bundle.31
  49.1 0.5 collective-permute-start.23
  49.7 0.1 collective-permute-start.18
  49.8 2.4 %collective-permute-done.18.refs_3_ = bf16[272,256]{1,0:T(8,128)(2,1)S(1)} collective-permute-done((bf16[272,256]{1,0:T(8,128)(2,1)S(1)}, bf16[272,256]{1,0:T(8,128)(2,1)S(1)}, u32[]{:S(2)}, u32[]{:S(2)}) %collective-permute-start.18) | collective-permute-done | bytes 139296 | tf_op jit(solution)/shard_map/ppermute | solution.py:397
  52.2 0.6 collective-permute-start.14
  52.8 2.8 %collective-permute-done.12.refs_1_.refs_2_ = bf16[512,512]{1,0:T(8,128)(2,1)S(1)} collective-permute-done((bf16[512,512]{1,0:T(8,128)(2,1)S(1)}, bf16[512,512]{1,0:T(8,128)(2,1)S(1)}, u32[]{:S(2)}, u32[]{:S(2)}) %collective-permute-start.12) | collective-permute-done | bytes 524320 | tf_op jit(solution)/shard_map/ppermute | solution.py:397
  55.6 7.5 %collective-permute-start.21 = (bf16[1088,256]{1,0:T(8,128)(2,1)S(1)}, bf16[1088,256]{1,0:T(8,128)(2,1)S(1)}, u32[]{:S(2)}, u32[]{:S(2)}) collective-permute-start(bf16[1088,256]{1,0:T(8,128)(2,1)S(1)} %bundle.29), channel_id=1, source_target_pairs={{0,6},{1,11},{2,4},{3,9},{4,2},{5,15},{6,0},{7,13},{8,14},{9,3},{1... | collective-permute-start | bytes 1671176 | tf_op jit(solution)/shard_map/ppermute | solution.py:402
  63.1 0.1 bundle.23
  63.2 0.0 collective-permute-done.16.refs_1_.refs_2_.refs_0_
  63.2 11.3 %collective-permute-start.13 = (bf16[1024,512]{1,0:T(8,128)(2,1)S(1)}, bf16[1024,512]{1,0:T(8,128)(2,1)S(1)}, u32[]{:S(2)}, u32[]{:S(2)}) collective-permute-start(bf16[1024,512]{1,0:T(8,128)(2,1)S(1)} %bundle.23), channel_id=1, source_target_pairs={{0,1},{1,0},{2,3},{3,2},{4,5},{5,4},{6,7},{7,6},{8,9},{9,8},{10,11... | collective-permute-start | bytes 3145736 | tf_op jit(solution)/shard_map/ppermute | solution.py:397
  74.5 0.0 collective-permute-done.14.refs_0_.refs_5_
  74.5 0.1 collective-permute-start.19
  74.6 0.0 collective-permute-done.20.refs_0_
  74.7 1.1 %collective-permute-start.17 = (bf16[256,512]{1,0:T(8,128)(2,1)S(1)}, bf16[256,512]{1,0:T(8,128)(2,1)S(1)}, u32[]{:S(2)}, u32[]{:S(2)}) collective-permute-start(bf16[256,512]{1,0:T(8,128)(2,1)S(1)} %bundle.25.refs_0_.refs_2_), channel_id=1, source_target_pairs={{0,16},{16,0},{1,17},{17,1},{2,18},{18,2},{3,19},{19,3},{4,20},{20... | collective-permute-start | bytes 786440 | tf_op jit(solution)/shard_map/ppermute | solution.py:397
  75.8 1.5 %base_product.5.refs_3_ = f32[512,512]{1,0:T(8,128)S(1)} custom-call(bf16[512,8192]{1,0:T(8,128)(2,1)S(1)} %bitcast.6, bf16[1024,512]{1,0:T(8,128)(2,1)S(1)} %collective-permute-done.20.refs_0_, bf16[512,512]{1,0:T(8,128)(2,1)S(1)} %bundle.21.refs_1_.refs_0_, bf16[512,512]{1,0:T(8,128)(2,1)S(1)} %collective-permute-done.11.refs_3_.refs_2_.refs_1_, ...), custom_call_target="tpu_custom_call" | custom-call | flops 1342177280 | bytes 6291456 | tf_op jit(solution)/shard_map/base_product/pallas_call | solution.py:213
  77.3 0.0 collective-permute-done.19.refs_5_
  77.3 1.3 %adapt_begin.1 = (f32[512,128]{1,0:T(8,128)S(1)}, bf16[512,128]{1,0:T(8,128)(2,1)S(1)}) custom-call(bf16[512,8192]{1,0:T(8,128)(2,1)S(1)} %bitcast.6, bf16[272,256]{1,0:T(8,128)(2,1)S(1)} %get-tuple-element.18.refs_3_.refs_0_, bf16[1360,256]{1,0:T(8,128)(2,1)S(1)} %collective-permute-done.15.refs_1_, ...), custom_call_target="tpu_custom_call" | custom-call | flops 1288490240 | bytes 5033164 | tf_op jit(solution)/shard_map/adapt_begin/pallas_call | solution.py:275
  78.6 0.0 collective-permute-done.21.refs_4_.refs_0_.refs_1_
  78.6 3.5 %collective-permute-done.17.refs_1_ = bf16[256,512]{1,0:T(8,128)(2,1)S(1)} collective-permute-done((bf16[256,512]{1,0:T(8,128)(2,1)S(1)}, bf16[256,512]{1,0:T(8,128)(2,1)S(1)}, u32[]{:S(2)}, u32[]{:S(2)}) %collective-permute-start.17) | collective-permute-done | bytes 262176 | tf_op jit(solution)/shard_map/ppermute | solution.py:397
  82.1 1.4 %collective-permute-start.22 = (bf16[512,512]{1,0:T(8,128)(2,1)S(1)}, bf16[512,512]{1,0:T(8,128)(2,1)S(1)}, u32[]{:S(2)}, u32[]{:S(2)}) collective-permute-start(bf16[512,512]{1,0:T(8,128)(2,1)S(1)} %bundle.30), channel_id=1, source_target_pairs={{0,1},{1,0},{2,3},{3,2},{4,5},{5,4},{6,7},{7,6},{8,9},{9,8},{10,11... | collective-permute-start | bytes 1572872 | tf_op jit(solution)/shard_map/ppermute | solution.py:397
  83.5 0.0 collective-permute-done.23.refs_0_
  83.6 1.1 %base_product.6.refs_3_ = f32[512,512]{1,0:T(8,128)S(1)} custom-call(bf16[512,8192]{1,0:T(8,128)(2,1)S(1)} %bitcast.6, bf16[1024,512]{1,0:T(8,128)(2,1)S(1)} %collective-permute-done.23.refs_0_, bf16[512,512]{1,0:T(8,128)(2,1)S(1)} %collective-permute-done.12.refs_1_.refs_2_, bf16[256,512]{1,0:T(8,128)(2,1)S(1)} %bundle.25.refs_0_.refs_2_, ...), custom_call_target="tpu_custom_call" | custom-call | flops 939524096 | bytes 4718592 | tf_op jit(solution)/shard_map/base_product/pallas_call | solution.py:213
  84.7 0.1 collective-permute-start.25
  84.8 0.5 collective-permute-start.24
  85.4 0.0 collective-permute-done.22.refs_2_
  85.4 0.0 collective-permute-done.13.refs_0_
  85.4 1.1 %base_product.7.base_ref = f32[512,512]{1,0:T(8,128)S(1)} custom-call(bf16[512,8192]{1,0:T(8,128)(2,1)S(1)} %bitcast.6, bf16[1024,512]{1,0:T(8,128)(2,1)S(1)} %collective-permute-done.13.refs_0_, bf16[256,512]{1,0:T(8,128)(2,1)S(1)} %collective-permute-done.17.refs_1_, bf16[512,512]{1,0:T(8,128)(2,1)S(1)} %collective-permute-done.22.refs_2_, ...), custom_call_target="tpu_custom_call" | custom-call | flops 939524096 | bytes 4718592 | tf_op jit(solution)/shard_map/base_product/pallas_call | solution.py:213
  86.5 0.0 collective-permute-done.25.refs_3_
  86.5 0.2 collective-permute-done.24.refs_1_
  86.7 2.2 %adapt_end.1 = bf16[512,512]{1,0:T(8,128)(2,1)} custom-call(bf16[512,8192]{1,0:T(8,128)(2,1)S(1)} %bitcast.6, f32[512,128]{1,0:T(8,128)S(1)} %row_mask.1.refs_4_.mask_ref, f32[512,512]{1,0:T(8,128)S(1)} %base_product.7.base_ref, f32[512,128]{1,0:T(8,128)S(1)} %get-tuple-element.24.refs_2_.shrunk, bf16[512,128]{1,0:T(8,128)(2,1)S(1)} %get-tuple-element.26.widened, ...), custom_call_target="tpu_custom_call" | custom-call | flops 858993472 | bytes 3355443 | tf_op jit(solution)/shard_map/adapt_end/pallas_call | solution.py:307
  (28 shorter events, 0.4 us)
Async XLA Ops:
  0.0 11.4 %copy-start.2 = (s32[1,16]{1,0:T(1,128)S(1)}, s32[1,16]{1,0:T(1,128)}, u32[]{:S(2)}) copy-start(s32[1,16]{1,0:T(1,128)} %lengths_ref.1) | copy-start | bytes 196
  0.0 11.4 %copy-start = (s32[16,16]{1,0:T(8,128)S(1)}, s32[16,16]{1,0:T(8,128)}, u32[]{:S(2)}) copy-start(s32[16,16]{1,0:T(8,128)} %slots_ref.1) | copy-start | bytes 3076
  1.2 13.9 %collective-permute-start = (bf16[256,512]{1,0:T(8,128)(2,1)S(1)}, bf16[256,512]{1,0:T(8,128)(2,1)S(1)}, u32[]{:S(2)}, u32[]{:S(2)}) collective-permute-start(bf16[256,512]{1,0:T(8,128)(2,1)S(1)} %get-tuple-element.16), channel_id=1, source_target_pairs={{0,8},{4,12},{8,0},{12,4},{1,9},{5,13},{9,1},{13,5},{2,10},{6,14},... | collective-permute-start | bytes 786440 | tf_op jit(solution)/shard_map/ppermute | solution.py:397
  3.6 11.5 %collective-permute-start.3 = (bf16[256,512]{1,0:T(8,128)(2,1)S(1)}, bf16[256,512]{1,0:T(8,128)(2,1)S(1)}, u32[]{:S(2)}, u32[]{:S(2)}) collective-permute-start(bf16[256,512]{1,0:T(8,128)(2,1)S(1)} %get-tuple-element.16), channel_id=1, source_target_pairs={{0,4},{4,0},{8,12},{12,8},{1,5},{5,1},{9,13},{13,9},{2,6},{6,2},{1... | collective-permute-start | bytes 786440 | tf_op jit(solution)/shard_map/ppermute | solution.py:397
  3.7 11.4 %collective-permute-start.4 = (bf16[256,512]{1,0:T(8,128)(2,1)S(1)}, bf16[256,512]{1,0:T(8,128)(2,1)S(1)}, u32[]{:S(2)}, u32[]{:S(2)}) collective-permute-start(bf16[256,512]{1,0:T(8,128)(2,1)S(1)} %get-tuple-element.16), channel_id=1, source_target_pairs={{0,2},{2,0},{1,3},{3,1},{4,6},{6,4},{5,7},{7,5},{8,10},{10,8},{9,1... | collective-permute-start | bytes 786440 | tf_op jit(solution)/shard_map/ppermute | solution.py:397
  5.0 25.6 %collective-permute-start.2 = (bf16[512,512]{1,0:T(8,128)(2,1)S(1)}, bf16[512,512]{1,0:T(8,128)(2,1)S(1)}, u32[]{:S(2)}, u32[]{:S(2)}) collective-permute-start(bf16[512,512]{1,0:T(8,128)(2,1)S(1)} %get-tuple-element.17.refs_0_), channel_id=1, source_target_pairs={{0,1},{1,0},{2,3},{3,2},{4,5},{5,4},{6,7},{7,6},{8,9},{9,8},{10,11... | collective-permute-start | bytes 1572872 | tf_op jit(solution)/shard_map/ppermute | solution.py:397
  6.5 28.4 %slice-start = ((s8[8388608]{0:T(1024)(128)(4,1)}), s8[4194304]{0:T(1024)(128)(4,1)S(1)}, s32[]{:S(2)}) async-start(s8[8388608]{0:T(1024)(128)(4,1)} %bitcast.5), calls=%async_computation | async-start | bytes 8388608
  6.5 0.8 copy-start.1
  7.3 27.5 %slice-start.1 = ((s8[8388608]{0:T(1024)(128)(4,1)}), s8[4194304]{0:T(1024)(128)(4,1)S(1)}, s32[]{:S(2)}) async-start(s8[8388608]{0:T(1024)(128)(4,1)} %bitcast.5), calls=%async_computation.1 | async-start | bytes 8388608
  11.3 6.6 %collective-permute-start.8 = (bf16[544,256]{1,0:T(8,128)(2,1)S(1)}, bf16[544,256]{1,0:T(8,128)(2,1)S(1)}, u32[]{:S(2)}, u32[]{:S(2)}) collective-permute-start(bf16[544,256]{1,0:T(8,128)(2,1)S(1)} %after.3), channel_id=1, source_target_pairs={{0,1},{1,0},{2,3},{3,2},{4,5},{5,4},{6,7},{7,6},{8,9},{9,8},{10,11... | collective-permute-start | bytes 835592 | tf_op jit(solution)/shard_map/ppermute | solution.py:397
  15.1 19.7 %collective-permute-start.5 = (bf16[512,512]{1,0:T(8,128)(2,1)S(1)}, bf16[512,512]{1,0:T(8,128)(2,1)S(1)}, u32[]{:S(2)}, u32[]{:S(2)}) collective-permute-start(bf16[512,512]{1,0:T(8,128)(2,1)S(1)} %bundle.17.refs_2_.refs_0_), channel_id=1, source_target_pairs={{0,16},{16,0},{1,17},{17,1},{2,18},{18,2},{3,19},{19,3},{4,20},{20... | collective-permute-start | bytes 1572872 | tf_op jit(solution)/shard_map/ppermute | solution.py:397
  16.4 13.7 %collective-permute-start.9 = (bf16[544,256]{1,0:T(8,128)(2,1)S(1)}, bf16[544,256]{1,0:T(8,128)(2,1)S(1)}, u32[]{:S(2)}, u32[]{:S(2)}) collective-permute-start(bf16[544,256]{1,0:T(8,128)(2,1)S(1)} %after.4), channel_id=1, source_target_pairs={{0,14},{1,15},{2,12},{3,13},{4,10},{5,11},{6,8},{7,9},{8,6},{9,7},... | collective-permute-start | bytes 835592 | tf_op jit(solution)/shard_map/ppermute | solution.py:402
  17.6 12.6 %collective-permute-start.6 = (bf16[256,512]{1,0:T(8,128)(2,1)S(1)}, bf16[256,512]{1,0:T(8,128)(2,1)S(1)}, u32[]{:S(2)}, u32[]{:S(2)}) collective-permute-start(bf16[256,512]{1,0:T(8,128)(2,1)S(1)} %bundle.18), channel_id=1, source_target_pairs={{0,2},{2,0},{1,3},{3,1},{4,6},{6,4},{5,7},{7,5},{8,10},{10,8},{9,1... | collective-permute-start | bytes 786440 | tf_op jit(solution)/shard_map/ppermute | solution.py:397
  17.9 28.9 %collective-permute-start.15 = (bf16[1360,256]{1,0:T(8,128)(2,1)S(1)}, bf16[1360,256]{1,0:T(8,128)(2,1)S(1)}, u32[]{:S(2)}, u32[]{:S(2)}) collective-permute-start(bf16[1360,256]{1,0:T(8,128)(2,1)S(1)} %after.5), channel_id=1, source_target_pairs={{0,1},{1,0},{2,3},{3,2},{4,5},{5,4},{6,7},{7,6},{8,9},{9,8},{10,11... | collective-permute-start | bytes 2088968 | tf_op jit(solution)/shard_map/ppermute | solution.py:397
  30.1 15.3 %collective-permute-start.10 = (bf16[1088,256]{1,0:T(8,128)(2,1)S(1)}, bf16[1088,256]{1,0:T(8,128)(2,1)S(1)}, u32[]{:S(2)}, u32[]{:S(2)}) collective-permute-start(bf16[1088,256]{1,0:T(8,128)(2,1)S(1)} %bundle.20), channel_id=1, source_target_pairs={{0,2},{1,9},{2,0},{3,11},{4,6},{5,13},{6,4},{7,15},{8,10},{9,1},{1... | collective-permute-start | bytes 1671176 | tf_op jit(solution)/shard_map/ppermute | solution.py:402
  30.3 15.2 %collective-permute-start.11 = (bf16[512,512]{1,0:T(8,128)(2,1)S(1)}, bf16[512,512]{1,0:T(8,128)(2,1)S(1)}, u32[]{:S(2)}, u32[]{:S(2)}) collective-permute-start(bf16[512,512]{1,0:T(8,128)(2,1)S(1)} %bundle.21.refs_1_.refs_0_), channel_id=1, source_target_pairs={{0,16},{16,0},{1,17},{17,1},{2,18},{18,2},{3,19},{19,3},{4,20},{20... | collective-permute-start | bytes 1572872 | tf_op jit(solution)/shard_map/ppermute | solution.py:397
  30.6 14.0 %collective-permute-start.1 = (bf16[256,512]{1,0:T(8,128)(2,1)S(1)}, bf16[256,512]{1,0:T(8,128)(2,1)S(1)}, u32[]{:S(2)}, u32[]{:S(2)}) collective-permute-start(bf16[256,512]{1,0:T(8,128)(2,1)S(1)} %collective-permute-done.refs_2_.refs_0_.refs_1_), channel_id=1, source_target_pairs={{0,4},{4,0},{8,12},{12,8},{1,5},{5,1},{9,13},{13,9},{2,6},{6,2},{1... | collective-permute-start | bytes 786440 | tf_op jit(solution)/shard_map/ppermute | solution.py:397
  36.1 9.3 %collective-permute-start.7 = (bf16[256,512]{1,0:T(8,128)(2,1)S(1)}, bf16[256,512]{1,0:T(8,128)(2,1)S(1)}, u32[]{:S(2)}, u32[]{:S(2)}) collective-permute-start(bf16[256,512]{1,0:T(8,128)(2,1)S(1)} %bundle.19), channel_id=1, source_target_pairs={{0,2},{2,0},{1,3},{3,1},{4,6},{6,4},{5,7},{7,5},{8,10},{10,8},{9,1... | collective-permute-start | bytes 786440 | tf_op jit(solution)/shard_map/ppermute | solution.py:397
  44.6 30.1 %collective-permute-start.20 = (bf16[1024,512]{1,0:T(8,128)(2,1)S(1)}, bf16[1024,512]{1,0:T(8,128)(2,1)S(1)}, u32[]{:S(2)}, u32[]{:S(2)}) collective-permute-start(bf16[1024,512]{1,0:T(8,128)(2,1)S(1)} %bundle.28), channel_id=1, source_target_pairs={{0,1},{1,0},{2,3},{3,2},{4,5},{5,4},{6,7},{7,6},{8,9},{9,8},{10,11... | collective-permute-start | bytes 3145736 | tf_op jit(solution)/shard_map/ppermute | solution.py:397
  45.5 10.1 %collective-permute-start.12 = (bf16[512,512]{1,0:T(8,128)(2,1)S(1)}, bf16[512,512]{1,0:T(8,128)(2,1)S(1)}, u32[]{:S(2)}, u32[]{:S(2)}) collective-permute-start(bf16[512,512]{1,0:T(8,128)(2,1)S(1)} %bundle.22.refs_0_.refs_3_), channel_id=1, source_target_pairs={{0,16},{16,0},{1,17},{17,1},{2,18},{18,2},{3,19},{19,3},{4,20},{20... | collective-permute-start | bytes 1572872 | tf_op jit(solution)/shard_map/ppermute | solution.py:397
  46.8 16.4 %collective-permute-start.16 = (bf16[1088,256]{1,0:T(8,128)(2,1)S(1)}, bf16[1088,256]{1,0:T(8,128)(2,1)S(1)}, u32[]{:S(2)}, u32[]{:S(2)}) collective-permute-start(bf16[1088,256]{1,0:T(8,128)(2,1)S(1)} %bundle.24), channel_id=1, source_target_pairs={{0,12},{1,5},{2,14},{3,7},{4,8},{5,1},{6,10},{7,3},{8,4},{9,13},{1... | collective-permute-start | bytes 1671176 | tf_op jit(solution)/shard_map/ppermute | solution.py:402
  49.1 34.4 %collective-permute-start.23 = (bf16[1024,512]{1,0:T(8,128)(2,1)S(1)}, bf16[1024,512]{1,0:T(8,128)(2,1)S(1)}, u32[]{:S(2)}, u32[]{:S(2)}) collective-permute-start(bf16[1024,512]{1,0:T(8,128)(2,1)S(1)} %bundle.31), channel_id=1, source_target_pairs={{0,1},{1,0},{2,3},{3,2},{4,5},{5,4},{6,7},{7,6},{8,9},{9,8},{10,11... | collective-permute-start | bytes 3145736 | tf_op jit(solution)/shard_map/ppermute | solution.py:397
  49.7 2.5 %collective-permute-start.18 = (bf16[272,256]{1,0:T(8,128)(2,1)S(1)}, bf16[272,256]{1,0:T(8,128)(2,1)S(1)}, u32[]{:S(2)}, u32[]{:S(2)}) collective-permute-start(bf16[272,256]{1,0:T(8,128)(2,1)S(1)} %bundle.26), channel_id=1, source_target_pairs={{0,1},{1,0},{2,3},{3,2},{4,5},{5,4},{6,7},{7,6},{8,9},{9,8},{10,11... | collective-permute-start | bytes 417800 | tf_op jit(solution)/shard_map/ppermute | solution.py:397
  52.2 22.4 %collective-permute-start.14 = (bf16[256,512]{1,0:T(8,128)(2,1)S(1)}, bf16[256,512]{1,0:T(8,128)(2,1)S(1)}, u32[]{:S(2)}, u32[]{:S(2)}) collective-permute-start(bf16[256,512]{1,0:T(8,128)(2,1)S(1)} %collective-permute-done.1.refs_0_), channel_id=1, source_target_pairs={{0,2},{2,0},{1,3},{3,1},{4,6},{6,4},{5,7},{7,5},{8,10},{10,8},{9,1... | collective-permute-start | bytes 786440 | tf_op jit(solution)/shard_map/ppermute | solution.py:397
  55.6 23.0 %collective-permute-start.21 = (bf16[1088,256]{1,0:T(8,128)(2,1)S(1)}, bf16[1088,256]{1,0:T(8,128)(2,1)S(1)}, u32[]{:S(2)}, u32[]{:S(2)}) collective-permute-start(bf16[1088,256]{1,0:T(8,128)(2,1)S(1)} %bundle.29), channel_id=1, source_target_pairs={{0,6},{1,11},{2,4},{3,9},{4,2},{5,15},{6,0},{7,13},{8,14},{9,3},{1... | collective-permute-start | bytes 1671176 | tf_op jit(solution)/shard_map/ppermute | solution.py:402
  63.2 22.2 %collective-permute-start.13 = (bf16[1024,512]{1,0:T(8,128)(2,1)S(1)}, bf16[1024,512]{1,0:T(8,128)(2,1)S(1)}, u32[]{:S(2)}, u32[]{:S(2)}) collective-permute-start(bf16[1024,512]{1,0:T(8,128)(2,1)S(1)} %bundle.23), channel_id=1, source_target_pairs={{0,1},{1,0},{2,3},{3,2},{4,5},{5,4},{6,7},{7,6},{8,9},{9,8},{10,11... | collective-permute-start | bytes 3145736 | tf_op jit(solution)/shard_map/ppermute | solution.py:397
  74.5 2.8 %collective-permute-start.19 = (bf16[544,256]{1,0:T(8,128)(2,1)S(1)}, bf16[544,256]{1,0:T(8,128)(2,1)S(1)}, u32[]{:S(2)}, u32[]{:S(2)}) collective-permute-start(bf16[544,256]{1,0:T(8,128)(2,1)S(1)} %bundle.27), channel_id=1, source_target_pairs={{0,1},{1,0},{2,3},{3,2},{4,5},{5,4},{6,7},{7,6},{8,9},{9,8},{10,11... | collective-permute-start | bytes 835592 | tf_op jit(solution)/shard_map/ppermute | solution.py:397
  74.7 7.4 %collective-permute-start.17 = (bf16[256,512]{1,0:T(8,128)(2,1)S(1)}, bf16[256,512]{1,0:T(8,128)(2,1)S(1)}, u32[]{:S(2)}, u32[]{:S(2)}) collective-permute-start(bf16[256,512]{1,0:T(8,128)(2,1)S(1)} %bundle.25.refs_0_.refs_2_), channel_id=1, source_target_pairs={{0,16},{16,0},{1,17},{17,1},{2,18},{18,2},{3,19},{19,3},{4,20},{20... | collective-permute-start | bytes 786440 | tf_op jit(solution)/shard_map/ppermute | solution.py:397
  82.1 3.2 %collective-permute-start.22 = (bf16[512,512]{1,0:T(8,128)(2,1)S(1)}, bf16[512,512]{1,0:T(8,128)(2,1)S(1)}, u32[]{:S(2)}, u32[]{:S(2)}) collective-permute-start(bf16[512,512]{1,0:T(8,128)(2,1)S(1)} %bundle.30), channel_id=1, source_target_pairs={{0,1},{1,0},{2,3},{3,2},{4,5},{5,4},{6,7},{7,6},{8,9},{9,8},{10,11... | collective-permute-start | bytes 1572872 | tf_op jit(solution)/shard_map/ppermute | solution.py:397
  84.7 1.8 %collective-permute-start.25 = (bf16[544,256]{1,0:T(8,128)(2,1)S(1)}, bf16[544,256]{1,0:T(8,128)(2,1)S(1)}, u32[]{:S(2)}, u32[]{:S(2)}) collective-permute-start(bf16[544,256]{1,0:T(8,128)(2,1)S(1)} %bundle.33), channel_id=1, source_target_pairs={{0,1},{1,0},{2,3},{3,2},{4,5},{5,4},{6,7},{7,6},{8,9},{9,8},{10,11... | collective-permute-start | bytes 835592 | tf_op jit(solution)/shard_map/ppermute | solution.py:397
  84.8 1.9 %collective-permute-start.24 = (bf16[544,256]{1,0:T(8,128)(2,1)S(1)}, bf16[544,256]{1,0:T(8,128)(2,1)S(1)}, u32[]{:S(2)}, u32[]{:S(2)}) collective-permute-start(bf16[544,256]{1,0:T(8,128)(2,1)S(1)} %bundle.32), channel_id=1, source_target_pairs={{0,1},{1,0},{2,3},{3,2},{4,5},{5,4},{6,7},{7,6},{8,9},{9,8},{10,11... | collective-permute-start | bytes 835592 | tf_op jit(solution)/shard_map/ppermute | solution.py:397

commit v15 on v12

--- a/solution.py
+++ b/solution.py
@@ -41,8 +41,6 @@
     "B0": ("CW", "Y1",),
     "B1": ("Y3",),
     "F0": ("R1",),
-    "F1": ("AB", "B2",),
-    "F2": ("AB", "B2",),
     "R1": ("P7", "R0",),
     "R2": ("P7",),
     "T1": ("T0",),

time: 82.3 us -> 81.9 us (level)
  transfers between devices with their start and end apart: 26 -> 26, of which waited for: 12 -> 11; matrix products, arithmetic and copies ran while one was open for 0% -> 0% of each run, Pallas kernels for 14% -> 14%
where the time goes in v15:
time: 81.9 us; the launch traced here: 81.8 us
  waiting for transfers between devices  37.3 us (46%)
  starting transfers between devices  28.4 us (35%)
  Pallas kernels  15.1 us (18%)
    ppermute x22, starting transfers between devices, swap(): return lax.ppermute(block, axis, [(i, i ^ bit) for i in range(size)])  27.7 us
    ppermute x22, waiting for transfers between devices, swap(): return lax.ppermute(block, axis, [(i, i ^ bit) for i in range(size)])  25.6 us
    ppermute x4, waiting for transfers between devices, send_pairs(): lax.ppermute(payload, AXES[1:], [(i, target(i)) for i in range(size)])  11.7 us
    pallas_call x4, Pallas kernels, base_product(): pl.pallas_call(kernel, out_shape=pltpu.VMEM((rows, width), jnp.float32),...  4.99 us
    pallas_call x1, Pallas kernels, make_messages(): pl.pallas_call(kernel, out_shape=[pltpu.VMEM((n * length, HALF), jnp.bflo...  3.62 us
    pallas_call x1, Pallas kernels, adapt_end(): pl.pallas_call(kernel, out_shape=jax.ShapeDtypeStruct((rows, width), jnp....  2.22 us
  transfers between devices with their start and end apart: 26, of which 11 were waited for; matrix products, arithmetic and copies ran while one was open for 0% of the time, Pallas kernels for 14%

profile of v15, /device:TPU:0, one launch (start us, length us, event | category | flops | bytes accessed | tf_op | source)
XLA Modules:
  0.0 81.8 jit_solution(1265709409400196374)
XLA Ops:
  0.0 1.3 %load_rows.1 = (bf16[512,512]{1,0:T(8,128)(2,1)S(1)}, bf16[256,512]{1,0:T(8,128)(2,1)S(1)}) custom-call(bf16[512,512]{1,0:T(8,128)(2,1)} %source.1), custom_call_target="tpu_custom_call" | custom-call | tf_op jit(solution)/shard_map/load_rows/pallas_call | solution.py:164
  1.3 4.1 %collective-permute-start = (bf16[256,512]{1,0:T(8,128)(2,1)S(1)}, bf16[256,512]{1,0:T(8,128)(2,1)S(1)}, u32[]{:S(2)}, u32[]{:S(2)}) collective-permute-start(bf16[256,512]{1,0:T(8,128)(2,1)S(1)} %get-tuple-element.16), channel_id=1, source_target_pairs={{0,8},{4,12},{8,0},{12,4},{1,9},{5,13},{9,1},{13,5},{2,10},{6,14},... | collective-permute-start | bytes 786440 | tf_op jit(solution)/shard_map/ppermute | solution.py:393
  5.4 1.6 %collective-permute-start.3 = (bf16[256,512]{1,0:T(8,128)(2,1)S(1)}, bf16[256,512]{1,0:T(8,128)(2,1)S(1)}, u32[]{:S(2)}, u32[]{:S(2)}) collective-permute-start(bf16[256,512]{1,0:T(8,128)(2,1)S(1)} %get-tuple-element.16), channel_id=1, source_target_pairs={{0,4},{4,0},{8,12},{12,8},{1,5},{5,1},{9,13},{13,9},{2,6},{6,2},{1... | collective-permute-start | bytes 786440 | tf_op jit(solution)/shard_map/ppermute | solution.py:393
  7.0 1.5 %collective-permute-start.4 = (bf16[256,512]{1,0:T(8,128)(2,1)S(1)}, bf16[256,512]{1,0:T(8,128)(2,1)S(1)}, u32[]{:S(2)}, u32[]{:S(2)}) collective-permute-start(bf16[256,512]{1,0:T(8,128)(2,1)S(1)} %get-tuple-element.16), channel_id=1, source_target_pairs={{0,2},{2,0},{1,3},{3,1},{4,6},{6,4},{5,7},{7,5},{8,10},{10,8},{9,1... | collective-permute-start | bytes 786440 | tf_op jit(solution)/shard_map/ppermute | solution.py:393
  8.5 0.7 copy-done.1
  9.2 3.6 %make_messages.1 = (bf16[544,256]{1,0:T(8,128)(2,1)S(1)}, bf16[544,256]{1,0:T(8,128)(2,1)S(1)}, bf16[544,256]{1,0:T(8,128)(2,1)S(1)}, bf16[544,256]{1,0:T(8,128)...) custom-call(s32[2,16]{1,0:T(2,128)S(1)} %bitcast.7, ...), custom_call_target="tpu_custom_call" | custom-call | bytes 4456448 | tf_op jit(solution)/shard_map/make_messages/pallas_call | solution.py:131
  12.8 0.1 collective-permute-start.8
  12.9 0.1 collective-permute-start.10
  13.0 1.1 %row_mask.1.refs_4_.mask_ref = f32[512,128]{1,0:T(8,128)S(1)} custom-call(s32[1,16]{1,0:T(1,128)S(1)} %copy-done.2, s32[16,16]{1,0:T(8,128)S(1)} %copy-done), custom_call_target="tpu_custom_call" | custom-call | tf_op jit(solution)/shard_map/row_mask/pallas_call | solution.py:372
  14.1 4.5 %collective-permute-done.refs_2_.refs_0_ = bf16[256,512]{1,0:T(8,128)(2,1)S(1)} collective-permute-done((bf16[256,512]{1,0:T(8,128)(2,1)S(1)}, bf16[256,512]{1,0:T(8,128)(2,1)S(1)}, u32[]{:S(2)}, u32[]{:S(2)}) %collective-permute-start) | collective-permute-done | bytes 262176 | tf_op jit(solution)/shard_map/ppermute | solution.py:393
  18.6 0.0 collective-permute-start.2
  18.6 0.0 collective-permute-done.3.refs_0_
  18.6 0.0 collective-permute-done.4.refs_1_
  18.6 7.5 %collective-permute-start.5 = (bf16[512,512]{1,0:T(8,128)(2,1)S(1)}, bf16[512,512]{1,0:T(8,128)(2,1)S(1)}, u32[]{:S(2)}, u32[]{:S(2)}) collective-permute-start(bf16[512,512]{1,0:T(8,128)(2,1)S(1)} %bundle.17.refs_2_.refs_0_), channel_id=1, source_target_pairs={{0,16},{16,0},{1,17},{17,1},{2,18},{18,2},{3,19},{19,3},{4,20},{20... | collective-permute-start | bytes 1572872 | tf_op jit(solution)/shard_map/ppermute | solution.py:393
  26.1 1.6 %collective-permute-start.6 = (bf16[256,512]{1,0:T(8,128)(2,1)S(1)}, bf16[256,512]{1,0:T(8,128)(2,1)S(1)}, u32[]{:S(2)}, u32[]{:S(2)}) collective-permute-start(bf16[256,512]{1,0:T(8,128)(2,1)S(1)} %bundle.18), channel_id=1, source_target_pairs={{0,2},{2,0},{1,3},{3,1},{4,6},{6,4},{5,7},{7,5},{8,10},{10,8},{9,1... | collective-permute-start | bytes 786440 | tf_op jit(solution)/shard_map/ppermute | solution.py:393
  27.7 0.0 collective-permute-done.8.refs_1_
  27.7 0.0 collective-permute-start.15
  27.8 0.0 collective-permute-done.10.refs_2_.refs_0_
  27.8 0.6 collective-permute-start.9
  28.4 6.3 %collective-permute-done.6.refs_5_.refs_1_ = bf16[256,512]{1,0:T(8,128)(2,1)S(1)} collective-permute-done((bf16[256,512]{1,0:T(8,128)(2,1)S(1)}, bf16[256,512]{1,0:T(8,128)(2,1)S(1)}, u32[]{:S(2)}, u32[]{:S(2)}) %collective-permute-start.6) | collective-permute-done | bytes 262176 | tf_op jit(solution)/shard_map/ppermute | solution.py:393
  34.7 0.4 collective-permute-start.11
  35.1 0.0 collective-permute-done.2.refs_1_.refs_4_
  35.1 0.0 collective-permute-start.1
  35.1 3.8 %collective-permute-done.5.refs_3_.refs_1_ = bf16[512,512]{1,0:T(8,128)(2,1)S(1)} collective-permute-done((bf16[512,512]{1,0:T(8,128)(2,1)S(1)}, bf16[512,512]{1,0:T(8,128)(2,1)S(1)}, u32[]{:S(2)}, u32[]{:S(2)}) %collective-permute-start.5) | collective-permute-done | bytes 524320 | tf_op jit(solution)/shard_map/ppermute | solution.py:393
  38.9 1.2 %base_product.4.refs_1_.refs_4_ = f32[512,512]{1,0:T(8,128)S(1)} custom-call(bf16[512,8192]{1,0:T(8,128)(2,1)S(1)} %bitcast.6, bf16[512,512]{1,0:T(8,128)(2,1)S(1)} %get-tuple-element.17.refs_0_, bf16[512,512]{1,0:T(8,128)(2,1)S(1)} %collective-permute-done.2.refs_1_.refs_4_, bf16[512,512]{1,0:T(8,128)(2,1)S(1)} %bundle.17.refs_2_.refs_0_, ...), custom_call_target="tpu_custom_call" | custom-call | flops 1073741824 | bytes 5242880 | tf_op jit(solution)/shard_map/base_product/pallas_call | solution.py:209
  40.2 2.0 %collective-permute-start.7 = (bf16[256,512]{1,0:T(8,128)(2,1)S(1)}, bf16[256,512]{1,0:T(8,128)(2,1)S(1)}, u32[]{:S(2)}, u32[]{:S(2)}) collective-permute-start(bf16[256,512]{1,0:T(8,128)(2,1)S(1)} %bundle.19), channel_id=1, source_target_pairs={{0,2},{2,0},{1,3},{3,1},{4,6},{6,4},{5,7},{7,5},{8,10},{10,8},{9,1... | collective-permute-start | bytes 786440 | tf_op jit(solution)/shard_map/ppermute | solution.py:393
  42.2 0.1 bundle.28
  42.3 0.0 collective-permute-done.9.refs_2_.refs_3_.refs_0_.refs_1_.refs_4_
  42.3 2.5 %collective-permute-start.20 = (bf16[1024,512]{1,0:T(8,128)(2,1)S(1)}, bf16[1024,512]{1,0:T(8,128)(2,1)S(1)}, u32[]{:S(2)}, u32[]{:S(2)}) collective-permute-start(bf16[1024,512]{1,0:T(8,128)(2,1)S(1)} %bundle.28), channel_id=1, source_target_pairs={{0,1},{1,0},{2,3},{3,2},{4,5},{5,4},{6,7},{7,6},{8,9},{9,8},{10,11... | collective-permute-start | bytes 3145736 | tf_op jit(solution)/shard_map/ppermute | solution.py:393
  44.8 0.0 collective-permute-done.15.refs_1_
  44.9 0.1 collective-permute-start.16
  45.0 4.6 %collective-permute-done.1.refs_0_ = bf16[256,512]{1,0:T(8,128)(2,1)S(1)} collective-permute-done((bf16[256,512]{1,0:T(8,128)(2,1)S(1)}, bf16[256,512]{1,0:T(8,128)(2,1)S(1)}, u32[]{:S(2)}, u32[]{:S(2)}) %collective-permute-start.1) | collective-permute-done | bytes 262176 | tf_op jit(solution)/shard_map/ppermute | solution.py:393
  49.6 0.0 collective-permute-done.7.refs_1_
  49.6 0.4 collective-permute-done.11.refs_3_.refs_2_.refs_1_
  50.0 1.8 %collective-permute-start.12 = (bf16[512,512]{1,0:T(8,128)(2,1)S(1)}, bf16[512,512]{1,0:T(8,128)(2,1)S(1)}, u32[]{:S(2)}, u32[]{:S(2)}) collective-permute-start(bf16[512,512]{1,0:T(8,128)(2,1)S(1)} %bundle.22.refs_0_.refs_3_), channel_id=1, source_target_pairs={{0,16},{16,0},{1,17},{17,1},{2,18},{18,2},{3,19},{19,3},{4,20},{20... | collective-permute-start | bytes 1572872 | tf_op jit(solution)/shard_map/ppermute | solution.py:393
  51.8 1.5 %collective-permute-start.14 = (bf16[256,512]{1,0:T(8,128)(2,1)S(1)}, bf16[256,512]{1,0:T(8,128)(2,1)S(1)}, u32[]{:S(2)}, u32[]{:S(2)}) collective-permute-start(bf16[256,512]{1,0:T(8,128)(2,1)S(1)} %collective-permute-done.1.refs_0_), channel_id=1, source_target_pairs={{0,2},{2,0},{1,3},{3,1},{4,6},{6,4},{5,7},{7,5},{8,10},{10,8},{9,1... | collective-permute-start | bytes 786440 | tf_op jit(solution)/shard_map/ppermute | solution.py:393
  53.3 0.1 collective-permute-start.18
  53.4 0.1 bundle.31
  53.5 1.3 %collective-permute-done.18.refs_3_ = bf16[272,256]{1,0:T(8,128)(2,1)S(1)} collective-permute-done((bf16[272,256]{1,0:T(8,128)(2,1)S(1)}, bf16[272,256]{1,0:T(8,128)(2,1)S(1)}, u32[]{:S(2)}, u32[]{:S(2)}) %collective-permute-start.18) | collective-permute-done | bytes 139296 | tf_op jit(solution)/shard_map/ppermute | solution.py:393
  54.8 0.1 collective-permute-start.23
  54.9 5.1 %collective-permute-done.16.refs_1_.refs_2_.refs_0_ = bf16[1088,256]{1,0:T(8,128)(2,1)S(1)} collective-permute-done((bf16[1088,256]{1,0:T(8,128)(2,1)S(1)}, bf16[1088,256]{1,0:T(8,128)(2,1)S(1)}, u32[]{:S(2)}, u32[]{:S(2)}) %collective-permute-start.16) | collective-permute-done | bytes 557088 | tf_op jit(solution)/shard_map/ppermute | solution.py:398
  60.0 0.0 collective-permute-start.21
  60.0 3.8 %collective-permute-done.12.refs_1_.refs_2_ = bf16[512,512]{1,0:T(8,128)(2,1)S(1)} collective-permute-done((bf16[512,512]{1,0:T(8,128)(2,1)S(1)}, bf16[512,512]{1,0:T(8,128)(2,1)S(1)}, u32[]{:S(2)}, u32[]{:S(2)}) %collective-permute-start.12) | collective-permute-done | bytes 524320 | tf_op jit(solution)/shard_map/ppermute | solution.py:393
  63.8 0.0 collective-permute-start.19
  63.8 0.1 bundle.23
  63.9 0.0 collective-permute-done.14.refs_0_.refs_5_
  63.9 0.6 collective-permute-start.13
  64.5 0.9 %collective-permute-done.19.refs_5_ = bf16[544,256]{1,0:T(8,128)(2,1)S(1)} collective-permute-done((bf16[544,256]{1,0:T(8,128)(2,1)S(1)}, bf16[544,256]{1,0:T(8,128)(2,1)S(1)}, u32[]{:S(2)}, u32[]{:S(2)}) %collective-permute-start.19) | collective-permute-done | bytes 278560 | tf_op jit(solution)/shard_map/ppermute | solution.py:393
  65.4 1.5 %collective-permute-start.17 = (bf16[256,512]{1,0:T(8,128)(2,1)S(1)}, bf16[256,512]{1,0:T(8,128)(2,1)S(1)}, u32[]{:S(2)}, u32[]{:S(2)}) collective-permute-start(bf16[256,512]{1,0:T(8,128)(2,1)S(1)} %bundle.25.refs_0_.refs_2_), channel_id=1, source_target_pairs={{0,16},{16,0},{1,17},{17,1},{2,18},{18,2},{3,19},{19,3},{4,20},{20... | collective-permute-start | bytes 786440 | tf_op jit(solution)/shard_map/ppermute | solution.py:393
  66.9 1.3 %adapt_begin.1 = (f32[512,128]{1,0:T(8,128)S(1)}, bf16[512,128]{1,0:T(8,128)(2,1)S(1)}) custom-call(bf16[512,8192]{1,0:T(8,128)(2,1)S(1)} %bitcast.6, bf16[272,256]{1,0:T(8,128)(2,1)S(1)} %get-tuple-element.18.refs_3_.refs_0_, bf16[1360,256]{1,0:T(8,128)(2,1)S(1)} %collective-permute-done.15.refs_1_, ...), custom_call_target="tpu_custom_call" | custom-call | flops 1288490240 | bytes 5033164 | tf_op jit(solution)/shard_map/adapt_begin/pallas_call | solution.py:271
  68.2 0.0 collective-permute-done.20.refs_0_
  68.2 1.5 %base_product.5.refs_3_ = f32[512,512]{1,0:T(8,128)S(1)} custom-call(bf16[512,8192]{1,0:T(8,128)(2,1)S(1)} %bitcast.6, bf16[1024,512]{1,0:T(8,128)(2,1)S(1)} %collective-permute-done.20.refs_0_, bf16[512,512]{1,0:T(8,128)(2,1)S(1)} %bundle.21.refs_1_.refs_0_, bf16[512,512]{1,0:T(8,128)(2,1)S(1)} %collective-permute-done.11.refs_3_.refs_2_.refs_1_, ...), custom_call_target="tpu_custom_call" | custom-call | flops 1342177280 | bytes 6291456 | tf_op jit(solution)/shard_map/base_product/pallas_call | solution.py:209
  69.7 6.7 %collective-permute-done.21.refs_4_.refs_0_.refs_1_ = bf16[1088,256]{1,0:T(8,128)(2,1)S(1)} collective-permute-done((bf16[1088,256]{1,0:T(8,128)(2,1)S(1)}, bf16[1088,256]{1,0:T(8,128)(2,1)S(1)}, u32[]{:S(2)}, u32[]{:S(2)}) %collective-permute-start.21) | collective-permute-done | bytes 557088 | tf_op jit(solution)/shard_map/ppermute | solution.py:398
  76.4 0.0 collective-permute-done.17.refs_1_
  76.4 0.1 collective-permute-start.22
  76.6 0.5 collective-permute-start.25
  77.1 0.1 collective-permute-start.24
  77.2 0.0 collective-permute-done.23.refs_0_
  77.2 1.1 %base_product.6.refs_3_ = f32[512,512]{1,0:T(8,128)S(1)} custom-call(bf16[512,8192]{1,0:T(8,128)(2,1)S(1)} %bitcast.6, bf16[1024,512]{1,0:T(8,128)(2,1)S(1)} %collective-permute-done.23.refs_0_, bf16[512,512]{1,0:T(8,128)(2,1)S(1)} %collective-permute-done.12.refs_1_.refs_2_, bf16[256,512]{1,0:T(8,128)(2,1)S(1)} %bundle.25.refs_0_.refs_2_, ...), custom_call_target="tpu_custom_call" | custom-call | flops 939524096 | bytes 4718592 | tf_op jit(solution)/shard_map/base_product/pallas_call | solution.py:209
  78.3 0.1 collective-permute-done.22.refs_2_
  78.4 0.0 collective-permute-done.13.refs_0_
  78.4 1.1 %base_product.7.base_ref = f32[512,512]{1,0:T(8,128)S(1)} custom-call(bf16[512,8192]{1,0:T(8,128)(2,1)S(1)} %bitcast.6, bf16[1024,512]{1,0:T(8,128)(2,1)S(1)} %collective-permute-done.13.refs_0_, bf16[256,512]{1,0:T(8,128)(2,1)S(1)} %collective-permute-done.17.refs_1_, bf16[512,512]{1,0:T(8,128)(2,1)S(1)} %collective-permute-done.22.refs_2_, ...), custom_call_target="tpu_custom_call" | custom-call | flops 939524096 | bytes 4718592 | tf_op jit(solution)/shard_map/base_product/pallas_call | solution.py:209
  79.5 0.0 collective-permute-done.25.refs_3_
  79.6 2.2 %adapt_end.1 = bf16[512,512]{1,0:T(8,128)(2,1)} custom-call(bf16[512,8192]{1,0:T(8,128)(2,1)S(1)} %bitcast.6, f32[512,128]{1,0:T(8,128)S(1)} %row_mask.1.refs_4_.mask_ref, f32[512,512]{1,0:T(8,128)S(1)} %base_product.7.base_ref, f32[512,128]{1,0:T(8,128)S(1)} %get-tuple-element.24.refs_2_.shrunk, bf16[512,128]{1,0:T(8,128)(2,1)S(1)} %get-tuple-element.26.widened, ...), custom_call_target="tpu_custom_call" | custom-call | flops 858993472 | bytes 3355443 | tf_op jit(solution)/shard_map/adapt_end/pallas_call | solution.py:303
  (27 shorter events, 0.4 us)
Async XLA Ops:
  0.0 13.0 %copy-start = (s32[16,16]{1,0:T(8,128)S(1)}, s32[16,16]{1,0:T(8,128)}, u32[]{:S(2)}) copy-start(s32[16,16]{1,0:T(8,128)} %slots_ref.1) | copy-start | bytes 3076
  0.0 38.9 %slice-start = ((s8[8388608]{0:T(1024)(128)(4,1)}), s8[4194304]{0:T(1024)(128)(4,1)S(1)}, s32[]{:S(2)}) async-start(s8[8388608]{0:T(1024)(128)(4,1)} %bitcast.5), calls=%async_computation | async-start | bytes 8388608
  1.3 17.3 %collective-permute-start = (bf16[256,512]{1,0:T(8,128)(2,1)S(1)}, bf16[256,512]{1,0:T(8,128)(2,1)S(1)}, u32[]{:S(2)}, u32[]{:S(2)}) collective-permute-start(bf16[256,512]{1,0:T(8,128)(2,1)S(1)} %get-tuple-element.16), channel_id=1, source_target_pairs={{0,8},{4,12},{8,0},{12,4},{1,9},{5,13},{9,1},{13,5},{2,10},{6,14},... | collective-permute-start | bytes 786440 | tf_op jit(solution)/shard_map/ppermute | solution.py:393
  5.4 13.2 %collective-permute-start.3 = (bf16[256,512]{1,0:T(8,128)(2,1)S(1)}, bf16[256,512]{1,0:T(8,128)(2,1)S(1)}, u32[]{:S(2)}, u32[]{:S(2)}) collective-permute-start(bf16[256,512]{1,0:T(8,128)(2,1)S(1)} %get-tuple-element.16), channel_id=1, source_target_pairs={{0,4},{4,0},{8,12},{12,8},{1,5},{5,1},{9,13},{13,9},{2,6},{6,2},{1... | collective-permute-start | bytes 786440 | tf_op jit(solution)/shard_map/ppermute | solution.py:393
  7.0 11.6 %collective-permute-start.4 = (bf16[256,512]{1,0:T(8,128)(2,1)S(1)}, bf16[256,512]{1,0:T(8,128)(2,1)S(1)}, u32[]{:S(2)}, u32[]{:S(2)}) collective-permute-start(bf16[256,512]{1,0:T(8,128)(2,1)S(1)} %get-tuple-element.16), channel_id=1, source_target_pairs={{0,2},{2,0},{1,3},{3,1},{4,6},{6,4},{5,7},{7,5},{8,10},{10,8},{9,1... | collective-permute-start | bytes 786440 | tf_op jit(solution)/shard_map/ppermute | solution.py:393
  8.5 0.7 copy-start.1
  9.2 3.8 %copy-start.2 = (s32[1,16]{1,0:T(1,128)S(1)}, s32[1,16]{1,0:T(1,128)}, u32[]{:S(2)}) copy-start(s32[1,16]{1,0:T(1,128)} %lengths_ref.1) | copy-start | bytes 196
  9.2 29.7 %slice-start.1 = ((s8[8388608]{0:T(1024)(128)(4,1)}), s8[4194304]{0:T(1024)(128)(4,1)S(1)}, s32[]{:S(2)}) async-start(s8[8388608]{0:T(1024)(128)(4,1)} %bitcast.5), calls=%async_computation.1 | async-start | bytes 8388608
  12.8 14.9 %collective-permute-start.8 = (bf16[544,256]{1,0:T(8,128)(2,1)S(1)}, bf16[544,256]{1,0:T(8,128)(2,1)S(1)}, u32[]{:S(2)}, u32[]{:S(2)}) collective-permute-start(bf16[544,256]{1,0:T(8,128)(2,1)S(1)} %after.2), channel_id=1, source_target_pairs={{0,1},{1,0},{2,3},{3,2},{4,5},{5,4},{6,7},{7,6},{8,9},{9,8},{10,11... | collective-permute-start | bytes 835592 | tf_op jit(solution)/shard_map/ppermute | solution.py:393
  12.9 14.9 %collective-permute-start.10 = (bf16[544,256]{1,0:T(8,128)(2,1)S(1)}, bf16[544,256]{1,0:T(8,128)(2,1)S(1)}, u32[]{:S(2)}, u32[]{:S(2)}) collective-permute-start(bf16[544,256]{1,0:T(8,128)(2,1)S(1)} %get-tuple-element.21), channel_id=1, source_target_pairs={{0,14},{1,15},{2,12},{3,13},{4,10},{5,11},{6,8},{7,9},{8,6},{9,7},... | collective-permute-start | bytes 835592 | tf_op jit(solution)/shard_map/ppermute | solution.py:398
  18.6 16.5 %collective-permute-start.2 = (bf16[512,512]{1,0:T(8,128)(2,1)S(1)}, bf16[512,512]{1,0:T(8,128)(2,1)S(1)}, u32[]{:S(2)}, u32[]{:S(2)}) collective-permute-start(bf16[512,512]{1,0:T(8,128)(2,1)S(1)} %get-tuple-element.17.refs_0_), channel_id=1, source_target_pairs={{0,1},{1,0},{2,3},{3,2},{4,5},{5,4},{6,7},{7,6},{8,9},{9,8},{10,11... | collective-permute-start | bytes 1572872 | tf_op jit(solution)/shard_map/ppermute | solution.py:393
  18.6 20.3 %collective-permute-start.5 = (bf16[512,512]{1,0:T(8,128)(2,1)S(1)}, bf16[512,512]{1,0:T(8,128)(2,1)S(1)}, u32[]{:S(2)}, u32[]{:S(2)}) collective-permute-start(bf16[512,512]{1,0:T(8,128)(2,1)S(1)} %bundle.17.refs_2_.refs_0_), channel_id=1, source_target_pairs={{0,16},{16,0},{1,17},{17,1},{2,18},{18,2},{3,19},{19,3},{4,20},{20... | collective-permute-start | bytes 1572872 | tf_op jit(solution)/shard_map/ppermute | solution.py:393
  26.1 8.5 %collective-permute-start.6 = (bf16[256,512]{1,0:T(8,128)(2,1)S(1)}, bf16[256,512]{1,0:T(8,128)(2,1)S(1)}, u32[]{:S(2)}, u32[]{:S(2)}) collective-permute-start(bf16[256,512]{1,0:T(8,128)(2,1)S(1)} %bundle.18), channel_id=1, source_target_pairs={{0,2},{2,0},{1,3},{3,1},{4,6},{6,4},{5,7},{7,5},{8,10},{10,8},{9,1... | collective-permute-start | bytes 786440 | tf_op jit(solution)/shard_map/ppermute | solution.py:393
  27.7 17.1 %collective-permute-start.15 = (bf16[1360,256]{1,0:T(8,128)(2,1)S(1)}, bf16[1360,256]{1,0:T(8,128)(2,1)S(1)}, u32[]{:S(2)}, u32[]{:S(2)}) collective-permute-start(bf16[1360,256]{1,0:T(8,128)(2,1)S(1)} %after.3), channel_id=1, source_target_pairs={{0,1},{1,0},{2,3},{3,2},{4,5},{5,4},{6,7},{7,6},{8,9},{9,8},{10,11... | collective-permute-start | bytes 2088968 | tf_op jit(solution)/shard_map/ppermute | solution.py:393
  27.8 14.5 %collective-permute-start.9 = (bf16[1088,256]{1,0:T(8,128)(2,1)S(1)}, bf16[1088,256]{1,0:T(8,128)(2,1)S(1)}, u32[]{:S(2)}, u32[]{:S(2)}) collective-permute-start(bf16[1088,256]{1,0:T(8,128)(2,1)S(1)} %bundle.20), channel_id=1, source_target_pairs={{0,2},{1,9},{2,0},{3,11},{4,6},{5,13},{6,4},{7,15},{8,10},{9,1},{1... | collective-permute-start | bytes 1671176 | tf_op jit(solution)/shard_map/ppermute | solution.py:398
  34.7 15.3 %collective-permute-start.11 = (bf16[512,512]{1,0:T(8,128)(2,1)S(1)}, bf16[512,512]{1,0:T(8,128)(2,1)S(1)}, u32[]{:S(2)}, u32[]{:S(2)}) collective-permute-start(bf16[512,512]{1,0:T(8,128)(2,1)S(1)} %bundle.21.refs_1_.refs_0_), channel_id=1, source_target_pairs={{0,16},{16,0},{1,17},{17,1},{2,18},{18,2},{3,19},{19,3},{4,20},{20... | collective-permute-start | bytes 1572872 | tf_op jit(solution)/shard_map/ppermute | solution.py:393
  35.1 14.5 %collective-permute-start.1 = (bf16[256,512]{1,0:T(8,128)(2,1)S(1)}, bf16[256,512]{1,0:T(8,128)(2,1)S(1)}, u32[]{:S(2)}, u32[]{:S(2)}) collective-permute-start(bf16[256,512]{1,0:T(8,128)(2,1)S(1)} %collective-permute-done.refs_2_.refs_0_), channel_id=1, source_target_pairs={{0,4},{4,0},{8,12},{12,8},{1,5},{5,1},{9,13},{13,9},{2,6},{6,2},{1... | collective-permute-start | bytes 786440 | tf_op jit(solution)/shard_map/ppermute | solution.py:393
  40.2 9.4 %collective-permute-start.7 = (bf16[256,512]{1,0:T(8,128)(2,1)S(1)}, bf16[256,512]{1,0:T(8,128)(2,1)S(1)}, u32[]{:S(2)}, u32[]{:S(2)}) collective-permute-start(bf16[256,512]{1,0:T(8,128)(2,1)S(1)} %bundle.19), channel_id=1, source_target_pairs={{0,2},{2,0},{1,3},{3,1},{4,6},{6,4},{5,7},{7,5},{8,10},{10,8},{9,1... | collective-permute-start | bytes 786440 | tf_op jit(solution)/shard_map/ppermute | solution.py:393
  42.3 25.9 %collective-permute-start.20 = (bf16[1024,512]{1,0:T(8,128)(2,1)S(1)}, bf16[1024,512]{1,0:T(8,128)(2,1)S(1)}, u32[]{:S(2)}, u32[]{:S(2)}) collective-permute-start(bf16[1024,512]{1,0:T(8,128)(2,1)S(1)} %bundle.28), channel_id=1, source_target_pairs={{0,1},{1,0},{2,3},{3,2},{4,5},{5,4},{6,7},{7,6},{8,9},{9,8},{10,11... | collective-permute-start | bytes 3145736 | tf_op jit(solution)/shard_map/ppermute | solution.py:393
  44.9 15.1 %collective-permute-start.16 = (bf16[1088,256]{1,0:T(8,128)(2,1)S(1)}, bf16[1088,256]{1,0:T(8,128)(2,1)S(1)}, u32[]{:S(2)}, u32[]{:S(2)}) collective-permute-start(bf16[1088,256]{1,0:T(8,128)(2,1)S(1)} %bundle.24), channel_id=1, source_target_pairs={{0,12},{1,5},{2,14},{3,7},{4,8},{5,1},{6,10},{7,3},{8,4},{9,13},{1... | collective-permute-start | bytes 1671176 | tf_op jit(solution)/shard_map/ppermute | solution.py:398
  50.0 13.8 %collective-permute-start.12 = (bf16[512,512]{1,0:T(8,128)(2,1)S(1)}, bf16[512,512]{1,0:T(8,128)(2,1)S(1)}, u32[]{:S(2)}, u32[]{:S(2)}) collective-permute-start(bf16[512,512]{1,0:T(8,128)(2,1)S(1)} %bundle.22.refs_0_.refs_3_), channel_id=1, source_target_pairs={{0,16},{16,0},{1,17},{17,1},{2,18},{18,2},{3,19},{19,3},{4,20},{20... | collective-permute-start | bytes 1572872 | tf_op jit(solution)/shard_map/ppermute | solution.py:393
  51.8 12.1 %collective-permute-start.14 = (bf16[256,512]{1,0:T(8,128)(2,1)S(1)}, bf16[256,512]{1,0:T(8,128)(2,1)S(1)}, u32[]{:S(2)}, u32[]{:S(2)}) collective-permute-start(bf16[256,512]{1,0:T(8,128)(2,1)S(1)} %collective-permute-done.1.refs_0_), channel_id=1, source_target_pairs={{0,2},{2,0},{1,3},{3,1},{4,6},{6,4},{5,7},{7,5},{8,10},{10,8},{9,1... | collective-permute-start | bytes 786440 | tf_op jit(solution)/shard_map/ppermute | solution.py:393
  53.3 1.4 %collective-permute-start.18 = (bf16[272,256]{1,0:T(8,128)(2,1)S(1)}, bf16[272,256]{1,0:T(8,128)(2,1)S(1)}, u32[]{:S(2)}, u32[]{:S(2)}) collective-permute-start(bf16[272,256]{1,0:T(8,128)(2,1)S(1)} %bundle.26), channel_id=1, source_target_pairs={{0,1},{1,0},{2,3},{3,2},{4,5},{5,4},{6,7},{7,6},{8,9},{9,8},{10,11... | collective-permute-start | bytes 417800 | tf_op jit(solution)/shard_map/ppermute | solution.py:393
  54.8 22.5 %collective-permute-start.23 = (bf16[1024,512]{1,0:T(8,128)(2,1)S(1)}, bf16[1024,512]{1,0:T(8,128)(2,1)S(1)}, u32[]{:S(2)}, u32[]{:S(2)}) collective-permute-start(bf16[1024,512]{1,0:T(8,128)(2,1)S(1)} %bundle.31), channel_id=1, source_target_pairs={{0,1},{1,0},{2,3},{3,2},{4,5},{5,4},{6,7},{7,6},{8,9},{9,8},{10,11... | collective-permute-start | bytes 3145736 | tf_op jit(solution)/shard_map/ppermute | solution.py:393
  60.0 16.4 %collective-permute-start.21 = (bf16[1088,256]{1,0:T(8,128)(2,1)S(1)}, bf16[1088,256]{1,0:T(8,128)(2,1)S(1)}, u32[]{:S(2)}, u32[]{:S(2)}) collective-permute-start(bf16[1088,256]{1,0:T(8,128)(2,1)S(1)} %bundle.29), channel_id=1, source_target_pairs={{0,6},{1,11},{2,4},{3,9},{4,2},{5,15},{6,0},{7,13},{8,14},{9,3},{1... | collective-permute-start | bytes 1671176 | tf_op jit(solution)/shard_map/ppermute | solution.py:398
  63.8 1.6 %collective-permute-start.19 = (bf16[544,256]{1,0:T(8,128)(2,1)S(1)}, bf16[544,256]{1,0:T(8,128)(2,1)S(1)}, u32[]{:S(2)}, u32[]{:S(2)}) collective-permute-start(bf16[544,256]{1,0:T(8,128)(2,1)S(1)} %bundle.27), channel_id=1, source_target_pairs={{0,1},{1,0},{2,3},{3,2},{4,5},{5,4},{6,7},{7,6},{8,9},{9,8},{10,11... | collective-permute-start | bytes 835592 | tf_op jit(solution)/shard_map/ppermute | solution.py:393
  63.9 14.5 %collective-permute-start.13 = (bf16[1024,512]{1,0:T(8,128)(2,1)S(1)}, bf16[1024,512]{1,0:T(8,128)(2,1)S(1)}, u32[]{:S(2)}, u32[]{:S(2)}) collective-permute-start(bf16[1024,512]{1,0:T(8,128)(2,1)S(1)} %bundle.23), channel_id=1, source_target_pairs={{0,1},{1,0},{2,3},{3,2},{4,5},{5,4},{6,7},{7,6},{8,9},{9,8},{10,11... | collective-permute-start | bytes 3145736 | tf_op jit(solution)/shard_map/ppermute | solution.py:393
  65.4 11.0 %collective-permute-start.17 = (bf16[256,512]{1,0:T(8,128)(2,1)S(1)}, bf16[256,512]{1,0:T(8,128)(2,1)S(1)}, u32[]{:S(2)}, u32[]{:S(2)}) collective-permute-start(bf16[256,512]{1,0:T(8,128)(2,1)S(1)} %bundle.25.refs_0_.refs_2_), channel_id=1, source_target_pairs={{0,16},{16,0},{1,17},{17,1},{2,18},{18,2},{3,19},{19,3},{4,20},{20... | collective-permute-start | bytes 786440 | tf_op jit(solution)/shard_map/ppermute | solution.py:393
  76.4 2.0 %collective-permute-start.22 = (bf16[512,512]{1,0:T(8,128)(2,1)S(1)}, bf16[512,512]{1,0:T(8,128)(2,1)S(1)}, u32[]{:S(2)}, u32[]{:S(2)}) collective-permute-start(bf16[512,512]{1,0:T(8,128)(2,1)S(1)} %bundle.30), channel_id=1, source_target_pairs={{0,1},{1,0},{2,3},{3,2},{4,5},{5,4},{6,7},{7,6},{8,9},{9,8},{10,11... | collective-permute-start | bytes 1572872 | tf_op jit(solution)/shard_map/ppermute | solution.py:393
  76.6 3.0 %collective-permute-start.25 = (bf16[544,256]{1,0:T(8,128)(2,1)S(1)}, bf16[544,256]{1,0:T(8,128)(2,1)S(1)}, u32[]{:S(2)}, u32[]{:S(2)}) collective-permute-start(bf16[544,256]{1,0:T(8,128)(2,1)S(1)} %bundle.33), channel_id=1, source_target_pairs={{0,1},{1,0},{2,3},{3,2},{4,5},{5,4},{6,7},{7,6},{8,9},{9,8},{10,11... | collective-permute-start | bytes 835592 | tf_op jit(solution)/shard_map/ppermute | solution.py:393
  77.1 2.4 %collective-permute-start.24 = (bf16[544,256]{1,0:T(8,128)(2,1)S(1)}, bf16[544,256]{1,0:T(8,128)(2,1)S(1)}, u32[]{:S(2)}, u32[]{:S(2)}) collective-permute-start(bf16[544,256]{1,0:T(8,128)(2,1)S(1)} %bundle.32), channel_id=1, source_target_pairs={{0,1},{1,0},{2,3},{3,2},{4,5},{5,4},{6,7},{7,6},{8,9},{9,8},{10,11... | collective-permute-start | bytes 835592 | tf_op jit(solution)/shard_map/ppermute | solution.py:393
